TPU v7x, 128 devices: a whole 4x4x4 slice. The times are simulated.
128 devices in a mesh: scan: 32 (over x, z, core), tile: 4 (over y).
Axes of the slice: x: 4, y: 4, z: 4, core: 2. Of those that a mesh axis runs over, the one named last changes fastest.
Arguments:
- object_slab: float32 [2, 3072, 24576], P(None, 'tile', 'scan'), may hold values from -6 to 6
- probe_field: float32 [2, 512, 512], replicated, may hold values from -3 to 3
- intensities: bfloat16 [32, 4, 6, 512, 512], P('scan', 'tile'), may hold values from 0 to 2
- offsets: int32 [32, 4, 6, 2], P('scan', 'tile'), may hold values from 0 to 767
- live_count: int32 [32, 4], P(None, 'tile'), may hold values from 1 to 6, as said below
Outputs:
- object_grad: float32 [2, 3072, 24576], P(None, 'tile', 'scan')
Inputs may be any that keep to these rules, and one draw needn't show every extreme that they name: The first live_count slots of a group hold its measured positions; some group has all 6 slots live.
All inputs are finite; a program needn't handle non-finite values.
Results may differ from a plain program's by a relative error of at most 0.014.
Values may be sent and summed in bfloat16 or wider, within the bound.
No kernel may reach another device: no remote copies, remote signals or barrier semaphores. Data moves between devices by JAX's collectives and lax.ppermute only.
A program may use at most 128 MiB of HBM per device.

v0:
```python
import math

import jax
import jax.numpy as jnp
from jax import lax
from jax.sharding import PartitionSpec as P

block_rows = 2


def from_behind(value, axis, by):
    peers = lax.axis_size(axis)
    pairs = [(i, i + by) for i in range(peers) if 0 <= i + by < peers]
    return lax.ppermute(value, axis, pairs)


def fourier_tables(side_len):
    across = jnp.arange(side_len, dtype=jnp.int32)
    phase = (across[:, None] * across[None, :] % side_len).astype(jnp.float32) * (
        2.0 * math.pi / side_len
    )
    factor = 1.0 / math.sqrt(side_len)
    return (
        (jnp.cos(phase) * factor).astype(jnp.bfloat16),
        (-jnp.sin(phase) * factor).astype(jnp.bfloat16),
    )


def left_apply(table_re, table_im, part_re, part_im):
    side_len = part_re.shape[-1]
    joined = jnp.concatenate([part_re, part_im], axis=-1)
    with_re = jnp.einsum("ij,bjk->bik", table_re, joined, preferred_element_type=jnp.float32)
    with_im = jnp.einsum("ij,bjk->bik", table_im, joined, preferred_element_type=jnp.float32)
    return (
        with_re[..., :side_len] - with_im[..., side_len:],
        with_re[..., side_len:] + with_im[..., :side_len],
    )


def right_apply(part_re, part_im, table_re, table_im):
    side_len = part_re.shape[-1]
    joined = jnp.concatenate([part_re, part_im], axis=-2)
    with_re = jnp.einsum("bij,jk->bik", joined, table_re, preferred_element_type=jnp.float32)
    with_im = jnp.einsum("bij,jk->bik", joined, table_im, preferred_element_type=jnp.float32)
    return (
        with_re[:, :side_len] - with_im[:, side_len:],
        with_im[:, :side_len] + with_re[:, side_len:],
    )


def transform(exit_waves, measured, tables):
    table_re, table_im = tables
    conj_im = -table_im
    half_re, half_im = left_apply(table_re, table_im, exit_waves[:, 0], exit_waves[:, 1])
    half_re = half_re.astype(jnp.bfloat16)
    half_im = half_im.astype(jnp.bfloat16)
    far_re, far_im = right_apply(half_re, half_im, table_re, table_im)
    misfit = far_re * far_re + far_im * far_im - measured.astype(jnp.float32)
    mis_re = (misfit * far_re).astype(jnp.bfloat16)
    mis_im = (misfit * far_im).astype(jnp.bfloat16)
    back_re, back_im = left_apply(table_re, conj_im, mis_re, mis_im)
    back_re = back_re.astype(jnp.bfloat16)
    back_im = back_im.astype(jnp.bfloat16)
    grad_re, grad_im = right_apply(back_re, back_im, table_re, conj_im)
    return jnp.stack([grad_re, grad_im], axis=1).astype(jnp.bfloat16)


def exit_wave(probe_field, patches):
    probe_re = probe_field[0]
    probe_im = probe_field[1]
    real_part = probe_re * patches[:, 0] - probe_im * patches[:, 1]
    imag_part = probe_re * patches[:, 1] + probe_im * patches[:, 0]
    return jnp.stack([real_part, imag_part], axis=1).astype(jnp.bfloat16)


def object_gradient(probe_field, wave_grads):
    probe_re = probe_field[0]
    probe_im = probe_field[1]
    grad_re = wave_grads[:, 0].astype(jnp.float32)
    grad_im = wave_grads[:, 1].astype(jnp.float32)
    real_part = probe_re * grad_re + probe_im * grad_im
    imag_part = probe_re * grad_im - probe_im * grad_re
    return jnp.stack([real_part, imag_part], axis=1)


def solve_live(exit_waves, measured, live_mask, tables):
    slot_total = exit_waves.shape[0]
    live_int = live_mask.astype(jnp.int32)
    live_sum = jnp.sum(live_int)
    rank_of = jnp.where(
        live_mask, jnp.cumsum(live_int) - 1, live_sum + jnp.cumsum(1 - live_int) - 1
    )
    slot_order = (
        jnp.zeros((slot_total,), jnp.int32).at[rank_of].set(jnp.arange(slot_total, dtype=jnp.int32))
    )
    blocks = (live_sum + block_rows - 1) // block_rows
    results = jnp.zeros(exit_waves.shape, jnp.bfloat16)

    def run_block(block_id, results):
        picked = lax.dynamic_slice(slot_order, (block_id * block_rows,), (block_rows,))
        solved = transform(exit_waves[picked], measured[picked], tables)
        kept_mask = live_mask[picked]
        solved = jnp.where(kept_mask[:, None, None, None], solved, jnp.zeros_like(solved))
        return results.at[picked].set(solved)

    return lax.fori_loop(0, blocks, run_block, results)


def shards(object_slab, probe_field, intensities, offsets, live_count):
    side_len = probe_field.shape[-1]
    tile_len = object_slab.shape[1]
    slot_total = intensities.shape[2]
    below = from_behind(object_slab[:, :side_len, :].astype(jnp.bfloat16), "tile", -1).astype(
        jnp.float32
    )
    taller = jnp.concatenate([object_slab, below], axis=1)
    beside = from_behind(taller[:, :, :side_len].astype(jnp.bfloat16), "scan", -1).astype(
        jnp.float32
    )
    extended = jnp.concatenate([taller, beside], axis=2)
    measured = intensities[0, 0]
    shifts = offsets[0, 0]
    counts_here = live_count[:, 0]
    my_index = lax.axis_index("scan")
    live_total = counts_here[my_index]
    zero_index = jnp.zeros((), jnp.int32)

    def cut_patch(row_at, col_at):
        return lax.dynamic_slice(extended, (zero_index, row_at, col_at), (2, side_len, side_len))

    patches = jax.vmap(cut_patch)(shifts[:, 0], shifts[:, 1])
    exit_waves = exit_wave(probe_field, patches)
    tables = fourier_tables(side_len)
    slot_ids = jnp.arange(slot_total, dtype=jnp.int32)
    live_mask = slot_ids < live_total
    wave_grads = solve_live(exit_waves, measured, live_mask, tables)
    patch_grad = object_gradient(probe_field, wave_grads)
    grown = jnp.zeros((2, tile_len + side_len, tile_len + side_len), jnp.float32)

    def add_one(slot_index, running):
        corner = (zero_index, shifts[slot_index, 0], shifts[slot_index, 1])
        current = lax.dynamic_slice(running, corner, (2, side_len, side_len))
        return lax.dynamic_update_slice(running, current + patch_grad[slot_index], corner)

    grown = lax.fori_loop(0, slot_total, add_one, grown)
    spill = from_behind(grown[:, :, tile_len:].astype(jnp.bfloat16), "scan", 1).astype(jnp.float32)
    narrow = grown[:, :, :tile_len].at[:, :, :side_len].add(spill)
    dropped = from_behind(narrow[:, tile_len:, :].astype(jnp.bfloat16), "tile", 1).astype(
        jnp.float32
    )
    return narrow[:, :tile_len, :].at[:, :side_len, :].add(dropped)


def solution(mesh):
    placed = (
        P(None, "tile", "scan"),
        P(),
        P("scan", "tile", None, None, None),
        P("scan", "tile", None, None),
        P(None, "tile"),
    )
    return jax.shard_map(
        shards, mesh=mesh, in_specs=placed, out_specs=P(None, "tile", "scan"), check_vma=False
    )
```

profile of v0, /device:TPU:22, one launch (start us, length us, event | category | flops | bytes accessed | tf_op | source)
XLA Modules:
  0.0 563.2 jit_solution(3046323554962161020)
XLA Ops:
  4.7 35.7 %collective-permute-done = bf16[2,512,768]{2,1,0:T(8,128)(2,1)S(1)} collective-permute-done((bf16[2,512,768]{2,1,0:T(8,128)(2,1)S(1)}, bf16[2,512,768]{2,1,0:T(8,128)(2,1)S(1)}, u32[]{:S(2)}, u32[]{:S(2)}) %collective-permute-start) | collective-permute-done | bytes 1572896 | tf_op jit(solution)/shard_map/ppermute | solution.py:14
  56.1 20.5 %collective-permute-done.1 = bf16[2,1280,512]{2,1,0:T(8,128)(2,1)} collective-permute-done((bf16[2,1280,512]{2,1,0:T(8,128)(2,1)}, bf16[2,1280,512]{2,1,0:T(8,128)(2,1)}, u32[]{:S(2)}, u32[]{:S(2)}) %collective-permute-start.1) | collective-permute-done | bytes 2621472 | tf_op jit(solution)/shard_map/ppermute | solution.py:14
  79.1 6.2 %pad_maximum_fusion.12 = f32[2,1280,1280]{2,1,0:T(8,128)} fusion(f32[2,1280,512]{2,1,0:T(8,128)S(1)} %convert_element_type.111, f32[2,512,768]{2,1,0:T(8,128)S(1)} %convert_element_type.110, f32[2,768,768]{2,1,0:T(8,128)S(1)} %bitcast.94), kind=kLoop, calls=%fused_computation.133 | loop fusion | flops 6553600 | bytes 26214400 | tf_op jit(solution)/shard_map/concatenate | solution.py:120
  85.3 34.3 %while.30 = (s32[]{:T(128)}, f32[2,1280,1280]{2,1,0:T(8,128)}, s32[6,3]{0,1:T(4,128)S(1)}, f32[6,2,512,512]{3,2,1,0:T(8,128)}, s32[]{:T(128)}) while((s32[]{:T(128)}, f32[2,1280,1280]{2,1,0:T(8,128)}, s32[6,3]{0,1:T(4,128)S(1)}, f32[6,2,512,512]{3,2,1,0:T(8,128)}, s32[]{:T(128)}) %tuple.95), condition=%wide.while_cond.2, body=%wide.while_body.2.sunk | while | flops 2 | bytes 4195945 | solution.py:129
  86.0 5.0 bitcast_dynamic-update-slice_fusion.2
  91.7 5.0 bitcast_dynamic-update-slice_fusion.2
  97.3 5.0 bitcast_dynamic-update-slice_fusion.2
  103.0 5.0 bitcast_dynamic-update-slice_fusion.2
  108.7 5.1 bitcast_dynamic-update-slice_fusion.2
  114.5 5.1 bitcast_dynamic-update-slice_fusion.2
  119.6 5.8 %subtract_convert_fusion = (bf16[6,1,512,512]{3,2,1,0:T(8,128)(2,1)S(1)}, bf16[6,1,512,512]{3,2,1,0:T(8,128)(2,1)S(1)}) fusion(f32[6,2,512,512]{3,2,1,0:T(8,128)} %get-tuple-element.222, f32[512,512]{1,0:T(8,128)S(1)} %copy-done.4, f32[512,512]{1,0:T(8,128)S(1)} %copy-done.3), kind=kLoop, calls=%fused_computation.143 | loop fusion | flops 12582912 | bytes 20971520 | tf_op jit(solution)/shard_map/convert.6
  131.8 72.3 %while.31 = (s32[]{:T(128)}, bf16[6,2,512,512]{3,2,1,0:T(8,128)(2,1)}, s32[]{:T(128)}, s32[6]{0:T(128)S(1)}, bf16[6,2,512,512]{3,2,1,0:T(8,128)(2,1)}, /*index=5...) while((s32[]{:T(128)}, ...), condition=%wide.region_6.7_spmd.clone.clone, body=%wide.region_4.6_spmd.clone.clone.sunk | while | flops 8673821696 | bytes 120590568 | solution.py:106
  140.6 4.9 convolution_bitcast_fusion.8
  146.7 7.2 %fusion.138 = f32[2,1024,512]{1,2,0:T(8,128)} fusion(bf16[2,512,512]{2,1,0:T(8,128)(2,1)S(1)} %get-tuple-element.443, bf16[2,512,512]{2,1,0:T(8,128)(2,1)S(1)} %get-tuple-element.444), kind=kOutput, calls=%fused_computation.49.clone.1 | convolution fusion | flops 1082130432 | bytes 6291456 | tf_op jit(solution)/shard_map/while/body/bij,jk->bik/dot_general | solution.py:43
  154.0 6.9 %fusion.137 = f32[2,1024,512]{1,2,0:T(8,128)} fusion(bf16[2,512,512]{2,1,0:T(8,128)(2,1)S(1)} %get-tuple-element.443, bf16[2,512,512]{2,1,0:T(8,128)(2,1)S(1)} %get-tuple-element.444), kind=kOutput, calls=%fused_computation.48.clone.1 | convolution fusion | flops 1082392576 | bytes 6291456 | tf_op jit(solution)/shard_map/while/body/bij,jk->bik/dot_general | solution.py:44
  168.9 4.9 convolution_bitcast_fusion.11
  173.8 4.9 convolution_bitcast_fusion.10
  179.9 5.0 fusion.141
  192.5 5.2 scatter_fusion
  204.2 6.0 %fusion.102 = (f32[6,1,512,512]{3,2,1,0:T(8,128)S(1)}, f32[6,1,512,512]{3,2,1,0:T(8,128)}) fusion(f32[512,512]{1,0:T(8,128)} %get-tuple-element.326, f32[512,512]{1,0:T(8,128)} %get-tuple-element.325, bf16[6,2,512,512]{3,2,1,0:T(8,128)(2,1)} %get-tuple-element.213), kind=kLoop, calls=%fused_computation.139 | loop fusion | flops 12582912 | bytes 20971520 | tf_op jit(solution)/shard_map/add | solution.py:81
  210.2 8.9 %pad_maximum_fusion.13 = f32[6,2,512,512]{3,2,1,0:T(8,128)} fusion(f32[6,1,512,512]{3,2,1,0:T(8,128)} %get-tuple-element.324, f32[6,1,512,512]{3,2,1,0:T(8,128)S(1)} %get-tuple-element.323), kind=kLoop, calls=%fused_computation.134 | loop fusion | flops 3145728 | bytes 25165824 | tf_op jit(solution)/shard_map/stack | solution.py:83
  219.1 5.6 broadcast_in_dim.13
  224.6 128.2 %while.29 = (s32[]{:T(128)}, f32[2,1280,1280]{2,1,0:T(8,128)}, s32[6,2]{0,1:T(2,128)S(1)}, f32[6,2,512,512]{3,2,1,0:T(8,128)}, s32[]{:T(128)}, /*index=5*/s32[]{:T(128)}, s32[]{:T(128)}) while((s32[]{:T(128)}, f32[2,1280,1280]{2,1,0:T(8,128)}, s32[6,2]{0,1:T(2,128)S(1)}, f32[6,2,512,512]{3,2,1,0:T(8,128)}, s32[]{:T(128)}, ...), condition=%wide.region_8.9_spmd, body=%wide.region_7.8_spmd.sunk | while | flops 524296 | bytes 10485941 | solution.py:145
  231.9 14.5 %dynamic_update_slice.8 = f32[2,1280,1280]{2,1,0:T(8,128)} dynamic-update-slice(f32[2,1280,1280]{2,1,0:T(8,128)} %get-tuple-element.507, f32[2,512,512]{2,1,0:T(8,128)S(1)} %bitcast_add_fusion.2, s32[]{:T(128)} %constant.145.clone.1..sunk, s32[]{:T(128)S(6)} %select_n.178, s32[]{:T(128)S(6)} %select_n.179) | dynamic-update-slice | bytes 4194308 | tf_op jit(solution)/shard_map/while/body/eval_jaxpr/dynamic_update_slice | solution.py:143
  253.7 12.5 %dynamic_update_slice.8 = f32[2,1280,1280]{2,1,0:T(8,128)} dynamic-update-slice(f32[2,1280,1280]{2,1,0:T(8,128)} %get-tuple-element.507, f32[2,512,512]{2,1,0:T(8,128)S(1)} %bitcast_add_fusion.2, s32[]{:T(128)} %constant.145.clone.1..sunk, s32[]{:T(128)S(6)} %select_n.178, s32[]{:T(128)S(6)} %select_n.179) | dynamic-update-slice | bytes 4194308 | tf_op jit(solution)/shard_map/while/body/eval_jaxpr/dynamic_update_slice | solution.py:143
  273.4 14.5 %dynamic_update_slice.8 = f32[2,1280,1280]{2,1,0:T(8,128)} dynamic-update-slice(f32[2,1280,1280]{2,1,0:T(8,128)} %get-tuple-element.507, f32[2,512,512]{2,1,0:T(8,128)S(1)} %bitcast_add_fusion.2, s32[]{:T(128)} %constant.145.clone.1..sunk, s32[]{:T(128)S(6)} %select_n.178, s32[]{:T(128)S(6)} %select_n.179) | dynamic-update-slice | bytes 4194308 | tf_op jit(solution)/shard_map/while/body/eval_jaxpr/dynamic_update_slice | solution.py:143
  295.2 14.5 %dynamic_update_slice.8 = f32[2,1280,1280]{2,1,0:T(8,128)} dynamic-update-slice(f32[2,1280,1280]{2,1,0:T(8,128)} %get-tuple-element.507, f32[2,512,512]{2,1,0:T(8,128)S(1)} %bitcast_add_fusion.2, s32[]{:T(128)} %constant.145.clone.1..sunk, s32[]{:T(128)S(6)} %select_n.178, s32[]{:T(128)S(6)} %select_n.179) | dynamic-update-slice | bytes 4194308 | tf_op jit(solution)/shard_map/while/body/eval_jaxpr/dynamic_update_slice | solution.py:143
  316.9 14.2 %dynamic_update_slice.8 = f32[2,1280,1280]{2,1,0:T(8,128)} dynamic-update-slice(f32[2,1280,1280]{2,1,0:T(8,128)} %get-tuple-element.507, f32[2,512,512]{2,1,0:T(8,128)S(1)} %bitcast_add_fusion.2, s32[]{:T(128)} %constant.145.clone.1..sunk, s32[]{:T(128)S(6)} %select_n.178, s32[]{:T(128)S(6)} %select_n.179) | dynamic-update-slice | bytes 4194308 | tf_op jit(solution)/shard_map/while/body/eval_jaxpr/dynamic_update_slice | solution.py:143
  338.4 14.5 %dynamic_update_slice.8 = f32[2,1280,1280]{2,1,0:T(8,128)} dynamic-update-slice(f32[2,1280,1280]{2,1,0:T(8,128)} %get-tuple-element.507, f32[2,512,512]{2,1,0:T(8,128)S(1)} %bitcast_add_fusion.2, s32[]{:T(128)} %constant.145.clone.1..sunk, s32[]{:T(128)S(6)} %select_n.178, s32[]{:T(128)S(6)} %select_n.179) | dynamic-update-slice | bytes 4194308 | tf_op jit(solution)/shard_map/while/body/eval_jaxpr/dynamic_update_slice | solution.py:143
  362.7 30.4 %collective-permute-done.2 = bf16[2,1280,512]{2,1,0:T(8,128)(2,1)S(1)} collective-permute-done((bf16[2,1280,512]{2,1,0:T(8,128)(2,1)S(1)}, bf16[2,1280,512]{2,1,0:T(8,128)(2,1)S(1)}, u32[]{:S(2)}, u32[]{:S(2)}) %collective-permute-start.2) | collective-permute-done | bytes 2621472 | tf_op jit(solution)/shard_map/ppermute | solution.py:14
  396.7 132.4 %collective-permute-start.3 = (bf16[2,512,768]{2,1,0:T(8,128)(2,1)S(1)}, bf16[2,512,768]{2,1,0:T(8,128)(2,1)S(1)}, u32[]{:S(2)}, u32[]{:S(2)}) collective-permute-start(bf16[2,512,768]{2,1,0:T(8,128)(2,1)S(1)} %slice.342), channel_id=1, source_target_pairs={{0,1},{1,2},{2,3},{4,5},{5,6},{6,7},{8,9},{9,10},{10,11},{12,13},{... | collective-permute-start | bytes 4718600 | tf_op jit(solution)/shard_map/ppermute | solution.py:14
  531.6 29.4 %collective-permute-done.3 = bf16[2,512,768]{2,1,0:T(8,128)(2,1)S(1)} collective-permute-done((bf16[2,512,768]{2,1,0:T(8,128)(2,1)S(1)}, bf16[2,512,768]{2,1,0:T(8,128)(2,1)S(1)}, u32[]{:S(2)}, u32[]{:S(2)}) %collective-permute-start.3) | collective-permute-done | bytes 1572896 | tf_op jit(solution)/shard_map/ppermute | solution.py:14
  (88 shorter events, 98.7 us)
Async XLA Ops:
  0.0 47.2 %copy-start = (s32[32,1]{0,1:T(1,128)S(1)}, s32[32,1]{0,1:T(1,128)}, u32[]{:S(2)}) copy-start(s32[32,1]{0,1:T(1,128)} %param.17) | copy-start | bytes 388
  0.0 40.6 %copy-start.2 = (f32[2,768,768]{2,1,0:T(8,128)S(1)}, f32[2,768,768]{2,1,0:T(8,128)}, u32[]{:S(2)}) copy-start(f32[2,768,768]{2,1,0:T(8,128)} %param.13) | copy-start | bytes 14155780
  2.2 38.2 %collective-permute-start = (bf16[2,512,768]{2,1,0:T(8,128)(2,1)S(1)}, bf16[2,512,768]{2,1,0:T(8,128)(2,1)S(1)}, u32[]{:S(2)}, u32[]{:S(2)}) collective-permute-start(bf16[2,512,768]{2,1,0:T(8,128)(2,1)S(1)} %slice.343), channel_id=1, source_target_pairs={{1,0},{2,1},{3,2},{5,4},{6,5},{7,6},{9,8},{10,9},{11,10},{13,12},{... | collective-permute-start | bytes 4718600 | tf_op jit(solution)/shard_map/ppermute | solution.py:14
  40.6 12.2 %copy-start.5 = (s32[1,1,6,2]{2,3,1,0:T(2,128)S(1)}, s32[1,1,6,2]{2,3,1,0:T(2,128)}, u32[]{:S(2)}) copy-start(s32[1,1,6,2]{2,3,1,0:T(2,128)} %param.16) | copy-start | bytes 148
  42.4 34.2 %collective-permute-start.1 = (bf16[2,1280,512]{2,1,0:T(8,128)(2,1)}, bf16[2,1280,512]{2,1,0:T(8,128)(2,1)}, u32[]{:S(2)}, u32[]{:S(2)}) collective-permute-start(bf16[2,1280,512]{2,1,0:T(8,128)(2,1)} %fusion.104), channel_id=1, source_target_pairs={{4,0},{8,4},{12,8},{16,12},{20,16},{24,20},{28,24},{32,28},{36,32}... | collective-permute-start | bytes 7864328 | tf_op jit(solution)/shard_map/ppermute | solution.py:14
  52.9 26.2 %slice-start = ((s8[4718592]{0:T(1024)(128)(4,1)}), s8[4194304]{0:T(1024)(128)(4,1)S(1)}, s32[]{:S(2)}) async-start(s8[4718592]{0:T(1024)(128)(4,1)} %bitcast.93), calls=%async_computation | async-start | bytes 8388608
  56.1 23.0 %slice-start.1 = ((s8[4718592]{0:T(1024)(128)(4,1)}), s8[524288]{0:T(1024)(128)(4,1)S(1)}, s32[]{:S(2)}) async-start(s8[4718592]{0:T(1024)(128)(4,1)} %bitcast.93), calls=%async_computation.1 | async-start | bytes 1048576
  85.3 34.3 %copy-start.3 = (f32[512,512]{1,0:T(8,128)S(1)}, f32[512,512]{1,0:T(8,128)}, u32[]{:S(2)}) copy-start(f32[512,512]{1,0:T(8,128)} %get-tuple-element.325) | copy-start | bytes 3145732
  85.3 34.3 %copy-start.4 = (f32[512,512]{1,0:T(8,128)S(1)}, f32[512,512]{1,0:T(8,128)}, u32[]{:S(2)}) copy-start(f32[512,512]{1,0:T(8,128)} %get-tuple-element.326) | copy-start | bytes 3145732
  219.1 5.6 copy-start.6
  355.7 37.4 %collective-permute-start.2 = (bf16[2,1280,512]{2,1,0:T(8,128)(2,1)S(1)}, bf16[2,1280,512]{2,1,0:T(8,128)(2,1)S(1)}, u32[]{:S(2)}, u32[]{:S(2)}) collective-permute-start(bf16[2,1280,512]{2,1,0:T(8,128)(2,1)S(1)} %slice.341), channel_id=1, source_target_pairs={{0,4},{4,8},{8,12},{12,16},{16,20},{20,24},{24,28},{28,32},{32,36}... | collective-permute-start | bytes 7864328 | tf_op jit(solution)/shard_map/ppermute | solution.py:14
  396.7 164.3 %collective-permute-start.3 = (bf16[2,512,768]{2,1,0:T(8,128)(2,1)S(1)}, bf16[2,512,768]{2,1,0:T(8,128)(2,1)S(1)}, u32[]{:S(2)}, u32[]{:S(2)}) collective-permute-start(bf16[2,512,768]{2,1,0:T(8,128)(2,1)S(1)} %slice.342), channel_id=1, source_target_pairs={{0,1},{1,2},{2,3},{4,5},{5,6},{6,7},{8,9},{9,10},{10,11},{12,13},{... | collective-permute-start | bytes 4718600 | tf_op jit(solution)/shard_map/ppermute | solution.py:14
  529.1 33.9 %copy-start.1 = (s32[32,1]{0,1:T(1,128)S(1)}, s32[32,1]{0,1:T(1,128)}, u32[]{:S(2)}) copy-start(s32[32,1]{0,1:T(1,128)} %param.17) | copy-start | bytes 388
where the time goes:
time: 573 us; the launch traced here: 563 us
  local copies, waits for them, and re-layouts  160 us (28%)
  starting transfers between devices  143 us (25%)
  waiting for transfers between devices  116 us (20%)
  other arithmetic  71.4 us (12%)
  matrix products  43.5 us (8%)
  loops' own time  28.7 us (5%)
    ppermute x4, starting transfers between devices, from_behind(): return lax.ppermute(value, axis, pairs)  143 us
    ppermute x4, waiting for transfers between devices, from_behind(): return lax.ppermute(value, axis, pairs)  116 us
    dynamic_update_slice x6, local copies, waits for them, and re-layouts, add_one(): lax.dynamic_update_slice(running, current + patch_grad[slot_index], corner)  84.5 us
    gather x18, local copies, waits for them, and re-layouts  34.3 us
    another operation x1, loops' own time, shards(): grown = lax.fori_loop(0, slot_total, add_one, grown)  22 us
    add x6, other arithmetic, add_one(): current + patch_grad[slot_index]  18.2 us
    dot_general x2, matrix products, right_apply(): jnp.einsum('bij,jk->bik', joined, table_re, preferred_element_type=jnp.fl...  12.2 us
    dot_general x2, matrix products, right_apply(): jnp.einsum('bij,jk->bik', joined, table_im, preferred_element_type=jnp.fl...  11.7 us
  transfers between devices with their start and end apart: 4, of which 4 were waited for; matrix products, arithmetic and copies ran while one was open for 3% of the time, Pallas kernels for 0%

commit v1 on v0

v1 whole, which is shorter than its diff:
```python
import functools

import jax
import jax.numpy as jnp
import ml_dtypes
import numpy as np
from jax import lax
from jax.experimental import pallas as pl
from jax.experimental.pallas import tpu as pltpu
from jax.sharding import PartitionSpec as P

W = 512
Q = W // 4
T = 768
E = T + W
NB = E // Q
TB = T // Q
R = 16
f32, bf16 = jnp.float32, jnp.bfloat16


def shifted(value, axis, by):
    n = lax.axis_size(axis)
    return lax.ppermute(value, axis, [(i, i + by) for i in range(n) if 0 <= i + by < n])


def tables():
    k = np.arange(W, dtype=np.int64)
    phase = (k[:, None] * k[None, :] % W).astype(np.float64) * (2.0 * np.pi / W)
    factor = 1.0 / np.sqrt(W)
    re = (np.cos(phase) * factor).astype(np.float32)[:, :Q]
    im = (-np.sin(phase) * factor).astype(np.float32)[:, :Q]
    left = np.stack(
        [
            np.block([[re[j::4], -im[j::4]], [im[j::4], re[j::4]]])
            for j in range(4)
        ]
    ).astype(ml_dtypes.bfloat16)
    pick = np.zeros((W, W), np.float32)
    for j in range(4):
        pick[j * Q + np.arange(Q), 4 * np.arange(Q) + j] = 1.0
    return left, left.transpose(0, 2, 1).copy(), pick.astype(ml_dtypes.bfloat16)


def split4(re, im):
    t0r, t0i, t1r, t1i = re[0] + re[2], im[0] + im[2], re[0] - re[2], im[0] - im[2]
    t2r, t2i, t3r, t3i = re[1] + re[3], im[1] + im[3], re[1] - re[3], im[1] - im[3]
    return (
        (t0r + t2r, t1r + t3i, t0r - t2r, t1r - t3i),
        (t0i + t2i, t1i - t3r, t0i - t2i, t1i + t3r),
    )


def join4(re, im):
    s0r, s0i, s1r, s1i = re[0] + re[2], im[0] + im[2], re[0] - re[2], im[0] - im[2]
    s2r, s2i, s3r, s3i = re[1] + re[3], im[1] + im[3], re[1] - re[3], im[1] - im[3]
    return (
        (s0r + s2r, s1r - s3i, s0r - s2r, s1r + s3i),
        (s0i + s2i, s1i + s3r, s0i - s2i, s1i - s3r),
    )


def lanes(b):
    return pl.ds(b * Q, Q)


def sort_kernel(pick_ref, pick_t_ref, in_ref, out_ref):
    rows = jnp.dot(pick_ref[...], in_ref[0], preferred_element_type=f32).astype(bf16)
    out_ref[0] = jnp.dot(rows, pick_t_ref[...], preferred_element_type=f32).astype(bf16)


def sort_intensities(measured, pick):
    slots = measured.shape[0]
    whole = pl.BlockSpec((W, W), lambda s: (0, 0))
    each = pl.BlockSpec((1, W, W), lambda s: (s, 0, 0))
    return pl.pallas_call(
        sort_kernel,
        grid=(slots,),
        in_specs=[whole, whole, each],
        out_specs=each,
        out_shape=jax.ShapeDtypeStruct(measured.shape, bf16),
        cost_estimate=pl.CostEstimate(
            flops=slots * 4 * W**3, bytes_accessed=slots * 4 * W * W, transcendentals=0
        ),
        compiler_params=pltpu.CompilerParams(vmem_limit_bytes=16 * 2**20),
    )(jnp.asarray(pick), jnp.asarray(pick.T.copy()), measured)


def main_kernel(
    live_ref,
    shift_ref,
    slab_ref,
    right_ref,
    below_ref,
    corner_ref,
    probe_ref,
    meas_ref,
    ga_ref,
    gb_ref,
    local_ref,
    spill_right_ref,
    spill_below_ref,
    spill_corner_ref,
    ext,
    grown,
    half16,
    full32,
    mid,
    out,
    in_sem,
    out_sem,
):
    def slab_copy(p, b):
        return pltpu.make_async_copy(
            slab_ref.at[p, :, lanes(b)], ext.at[p, b, pl.ds(0, T), :], in_sem.at[p, b]
        )

    def local_copy(p, b):
        return pltpu.make_async_copy(
            grown.at[p, b, pl.ds(0, T), :], local_ref.at[p, :, lanes(b)], out_sem.at[p, b]
        )

    for p in range(2):
        for b in range(TB):
            slab_copy(p, b).start()

    def clear(i, carry):
        rows = pl.ds(pl.multiple_of(i * R, R), R)
        for p in range(2):
            for b in range(NB):
                grown[p, b, rows, :] = jnp.zeros((R, Q), f32)
        return carry

    lax.fori_loop(0, E // R, clear, 0)

    def fill_right(i, carry):
        rows = pl.ds(pl.multiple_of(i * R, R), R)
        for p in range(2):
            for b in range(4):
                ext[p, TB + b, rows, :] = right_ref[p, rows, lanes(b)].astype(f32)
        return carry

    lax.fori_loop(0, T // R, fill_right, 0)

    def fill_below(i, carry):
        rows = pl.ds(pl.multiple_of(i * R, R), R)
        there = pl.ds(pl.multiple_of(T + i * R, R), R)
        for p in range(2):
            for b in range(TB):
                ext[p, b, there, :] = below_ref[p, rows, lanes(b)].astype(f32)
            for b in range(4):
                ext[p, TB + b, there, :] = corner_ref[p, rows, lanes(b)].astype(f32)
        return carry

    lax.fori_loop(0, W // R, fill_below, 0)

    for p in range(2):
        for b in range(TB):
            slab_copy(p, b).wait()

    lane = lax.broadcasted_iota(jnp.int32, (R, Q), 1)

    def one_slot(slot, carry):
        row0 = shift_ref[slot, 0]
        col0 = shift_ref[slot, 1]
        block0 = col0 // Q
        by = col0 % Q
        inner = lane < Q - by
        outer = lane < by

        def cut(i, c):
            for b in range(4):
                re, im = [], []
                for q in range(4):
                    rows = pl.ds(row0 + q * Q + i * R, R)
                    here = pl.ds(pl.multiple_of(q * Q + i * R, R), R)
                    part = []
                    for p in range(2):
                        one = pltpu.roll(ext[p, block0 + b, rows, :], Q - by, 1)
                        two = pltpu.roll(ext[p, block0 + b + 1, rows, :], Q - by, 1)
                        part.append(jnp.where(inner, one, two))
                    pr, pi = probe_ref[0, here, lanes(b)], probe_ref[1, here, lanes(b)]
                    re.append(pr * part[0] - pi * part[1])
                    im.append(pr * part[1] + pi * part[0])
                re, im = split4(re, im)
                top = pl.ds(pl.multiple_of(i * R, R), R)
                low = pl.ds(pl.multiple_of(Q + i * R, R), R)
                for j in range(4):
                    half16[j, top, lanes(b)] = re[j].astype(bf16)
                    half16[j, low, lanes(b)] = im[j].astype(bf16)
            return c

        lax.fori_loop(0, Q // R, cut, 0)
        for j in range(4):
            full32[j] = jnp.dot(ga_ref[j], half16[j], preferred_element_type=f32)

        def across(i, c):
            top = pl.ds(pl.multiple_of(i * R, R), R)
            low = pl.ds(pl.multiple_of(Q + i * R, R), R)
            for j in range(4):
                re = [full32[j, top, lanes(q)] for q in range(4)]
                im = [full32[j, low, lanes(q)] for q in range(4)]
                re, im = split4(re, im)
                there = pl.ds(pl.multiple_of(j * Q + i * R, R), R)
                for l in range(4):
                    mid[l, there, lanes(0)] = re[l].astype(bf16)
                    mid[l, there, lanes(1)] = im[l].astype(bf16)
            return c

        lax.fori_loop(0, Q // R, across, 0)
        for l in range(4):
            far = jnp.dot(mid[l], gb_ref[l], preferred_element_type=f32)
            re, im = far[:, :Q], far[:, Q:]
            gap = re * re + im * im - meas_ref[slot, :, lanes(l)].astype(f32)
            misfit = jnp.concatenate([gap * re, gap * im], axis=1).astype(bf16)
            out[l] = jnp.dot(misfit, ga_ref[l], preferred_element_type=f32)

        def back(i, c):
            top = pl.ds(pl.multiple_of(i * R, R), R)
            low = pl.ds(pl.multiple_of(Q + i * R, R), R)
            for j in range(4):
                here = pl.ds(pl.multiple_of(j * Q + i * R, R), R)
                re = [out[l, here, lanes(0)] for l in range(4)]
                im = [out[l, here, lanes(1)] for l in range(4)]
                re, im = join4(re, im)
                for q in range(4):
                    half16[j, top, lanes(q)] = re[q].astype(bf16)
                    half16[j, low, lanes(q)] = im[q].astype(bf16)
            return c

        lax.fori_loop(0, Q // R, back, 0)
        for j in range(4):
            full32[j] = jnp.dot(gb_ref[j], half16[j], preferred_element_type=f32)

        def add(i, c):
            top = pl.ds(pl.multiple_of(i * R, R), R)
            low = pl.ds(pl.multiple_of(Q + i * R, R), R)
            last = [[None, None] for q in range(4)]
            for b in range(5):
                if b < 4:
                    re = [full32[j, top, lanes(b)] for j in range(4)]
                    im = [full32[j, low, lanes(b)] for j in range(4)]
                    re, im = join4(re, im)
                for q in range(4):
                    rows = pl.ds(row0 + q * Q + i * R, R)
                    here = pl.ds(pl.multiple_of(q * Q + i * R, R), R)
                    if b < 4:
                        pr, pi = probe_ref[0, here, lanes(b)], probe_ref[1, here, lanes(b)]
                        both = (pr * re[q] + pi * im[q], pr * im[q] - pi * re[q])
                        both = [pltpu.roll(v, by, 1) for v in both]
                    else:
                        both = [jnp.zeros((R, Q), f32)] * 2
                    for p in range(2):
                        before = last[q][p]
                        if before is None:
                            before = jnp.zeros((R, Q), f32)
                        grown[p, block0 + b, rows, :] += jnp.where(outer, before, both[p])
                        last[q][p] = both[p]
            return c

        lax.fori_loop(0, Q // R, add, 0)
        return carry

    lax.fori_loop(0, live_ref[0], one_slot, 0)

    for p in range(2):
        for b in range(TB):
            local_copy(p, b).start()

    def drain_right(i, carry):
        rows = pl.ds(pl.multiple_of(i * R, R), R)
        for p in range(2):
            for b in range(4):
                spill_right_ref[p, rows, lanes(b)] = grown[p, TB + b, rows, :].astype(bf16)
        return carry

    lax.fori_loop(0, T // R, drain_right, 0)

    def drain_below(i, carry):
        rows = pl.ds(pl.multiple_of(i * R, R), R)
        here = pl.ds(pl.multiple_of(T + i * R, R), R)
        for p in range(2):
            for b in range(TB):
                spill_below_ref[p, rows, lanes(b)] = grown[p, b, here, :].astype(bf16)
            for b in range(4):
                spill_corner_ref[p, rows, lanes(b)] = grown[p, TB + b, here, :].astype(bf16)
        return carry

    lax.fori_loop(0, W // R, drain_below, 0)
    for p in range(2):
        for b in range(TB):
            local_copy(p, b).wait()


def solve(live, shifts, slab, right, below, corner, probe, measured, left, left_t):
    vmem = pl.BlockSpec(memory_space=pltpu.VMEM)
    smem = pl.BlockSpec(memory_space=pltpu.SMEM)
    anywhere = pl.BlockSpec(memory_space=pl.ANY)
    return pl.pallas_call(
        main_kernel,
        in_specs=[smem, smem, anywhere] + [vmem] * 7,
        out_specs=[anywhere, vmem, vmem, vmem],
        out_shape=[
            jax.ShapeDtypeStruct((2, T, T), f32),
            jax.ShapeDtypeStruct((2, T, W), bf16),
            jax.ShapeDtypeStruct((2, W, T), bf16),
            jax.ShapeDtypeStruct((2, W, W), bf16),
        ],
        scratch_shapes=[
            pltpu.VMEM((2, NB, E, Q), f32),
            pltpu.VMEM((2, NB, E, Q), f32),
            pltpu.VMEM((4, 2 * Q, W), bf16),
            pltpu.VMEM((4, 2 * Q, W), f32),
            pltpu.VMEM((4, W, 2 * Q), bf16),
            pltpu.VMEM((4, W, 2 * Q), f32),
            pltpu.SemaphoreType.DMA((2, TB)),
            pltpu.SemaphoreType.DMA((2, TB)),
        ],
        cost_estimate=pl.CostEstimate(
            flops=6 * 2 * W**3, bytes_accessed=20 * 2**20, transcendentals=0
        ),
        compiler_params=pltpu.CompilerParams(vmem_limit_bytes=56 * 2**20),
    )(live, shifts, slab, right, below, corner, probe, measured, left, left_t)


def finish_kernel(local_ref, right_ref, below_ref, out_ref):
    out_ref[...] = local_ref[...]
    out_ref[:, :, :W] += right_ref[...].astype(f32)

    @pl.when(pl.program_id(0) < W // Q)
    def _():
        out_ref[...] += below_ref[...].astype(f32)


def finish(local, right, below):
    return pl.pallas_call(
        finish_kernel,
        grid=(TB,),
        in_specs=[
            pl.BlockSpec((2, Q, T), lambda i: (0, i, 0)),
            pl.BlockSpec((2, Q, W), lambda i: (0, i, 0)),
            pl.BlockSpec((2, Q, T), lambda i: (0, jnp.minimum(i, W // Q - 1), 0)),
        ],
        out_specs=pl.BlockSpec((2, Q, T), lambda i: (0, i, 0)),
        out_shape=jax.ShapeDtypeStruct((2, T, T), f32),
        compiler_params=pltpu.CompilerParams(vmem_limit_bytes=24 * 2**20),
    )(local, right, below)


def shards(slab, probe, intensities, offsets, live_count):
    left, left_t, pick = tables()
    send_below = slab[:, :W, :].astype(bf16)
    send_right = slab[:, :, :W].astype(bf16)
    below = shifted(send_below, "tile", -1)
    right = shifted(send_right, "scan", -1)
    corner = shifted(below[:, :, :W], "scan", -1)
    measured = sort_intensities(intensities[0, 0], pick)
    live = lax.dynamic_slice(live_count[:, 0], (lax.axis_index("scan"),), (1,))
    local, to_right, to_below, to_corner = solve(
        live, offsets[0, 0], slab, right, below, corner, probe, measured,
        jnp.asarray(left), jnp.asarray(left_t),
    )
    from_left = shifted(to_right, "scan", 1)
    from_corner = shifted(to_corner, "scan", 1)
    far_half = shifted(to_below[:, :, W:], "tile", 1)
    near = (to_below[:, :, :W].astype(f32) + from_corner.astype(f32)).astype(bf16)
    near_half = shifted(near, "tile", 1)
    return finish(local, from_left, jnp.concatenate([near_half, far_half], axis=2))


def solution(mesh):
    placed = (
        P(None, "tile", "scan"),
        P(),
        P("scan", "tile", None, None, None),
        P("scan", "tile", None, None),
        P(None, "tile"),
    )
    return jax.shard_map(
        shards, mesh=mesh, in_specs=placed, out_specs=P(None, "tile", "scan"), check_vma=False
    )
```

time: 573 us -> 161 us (0.28); the launches traced: 563 us -> 159 us
  local copies, waits for them, and re-layouts: 160 us -> 9.72 us
  starting transfers between devices: 143 us -> 20.6 us
  other arithmetic: 71.4 us -> 4.35 us
  Pallas kernels: 0 us -> 49.8 us
  matrix products: 43.5 us -> 0 us
  waiting for transfers between devices: 116 us -> 74.8 us
  loops' own time: 28.7 us -> 0 us
    ppermute x4 -> x7, starting transfers between devices: 143 us -> 20.6 us  [shifted(): lax.ppermute(value, axis, [(i, i + by) for i in range(n) if 0 <= i + by <...]
    dynamic_update_slice x6 -> x0, local copies, waits for them, and re-layouts: 84.5 us -> none  [add_one(): lax.dynamic_update_slice(running, current + patch_grad[slot_index], corner)]
    pallas_call x0 -> x3, Pallas kernels: none -> 49.8 us  [the longest x1 41.9 us: solve(): pl.pallas_call(main_kernel, in_specs=[smem, smem, anywhere] + [vmem] * 7,...]
    dot_general x8 -> x0, matrix products: 43.5 us -> none  [the longest x2 12.2 us: right_apply(): jnp.einsum('bij,jk->bik', joined, table_re, preferred_element_type=jnp.fl...]
    gather x22 -> x0, local copies, waits for them, and re-layouts: 41.6 us -> none
    ppermute x4 -> x7, waiting for transfers between devices: 116 us -> 74.8 us  [shifted(): lax.ppermute(value, axis, [(i, i + by) for i in range(n) if 0 <= i + by <...]
    another operation x3 -> x0, loops' own time: 28.7 us -> none  [the longest x1 22 us: shards(): grown = lax.fori_loop(0, slot_total, add_one, grown)]
    add x7 -> x0, other arithmetic: 24.2 us -> none  [the longest x6 18.2 us: add_one(): current + patch_grad[slot_index]]
  transfers between devices with their start and end apart: 4 -> 7, of which waited for: 4 -> 4; matrix products, arithmetic and copies ran while one was open for 3% -> 4% of each run, Pallas kernels for 0% -> 3%
where the time goes in v1:
time: 161 us; the launch traced here: 159 us
  waiting for transfers between devices  74.8 us (46%)
  Pallas kernels  49.8 us (31%)
  starting transfers between devices  20.6 us (13%)
  local copies, waits for them, and re-layouts  9.72 us (6%)
  other arithmetic  4.35 us (3%)
    ppermute x7, waiting for transfers between devices, shifted(): lax.ppermute(value, axis, [(i, i + by) for i in range(n) if 0 <= i + by <...  74.8 us
    pallas_call x1, Pallas kernels, solve(): pl.pallas_call(main_kernel, in_specs=[smem, smem, anywhere] + [vmem] * 7,...  41.9 us
    ppermute x7, starting transfers between devices, shifted(): lax.ppermute(value, axis, [(i, i + by) for i in range(n) if 0 <= i + by <...  20.6 us
    unnamed x16, local copies, waits for them, and re-layouts  4.92 us
    pallas_call x1, Pallas kernels, sort_intensities(): pl.pallas_call(sort_kernel, grid=(slots,), in_specs=[whole, whole, each],...  4.3 us
    pallas_call x1, Pallas kernels, finish(): pl.pallas_call(finish_kernel, grid=(TB,), in_specs=[pl.BlockSpec((2, Q, T...  3.66 us
  transfers between devices with their start and end apart: 7, of which 4 were waited for; matrix products, arithmetic and copies ran while one was open for 4% of the time, Pallas kernels for 3%

profile of v1, /device:TPU:22, one launch (start us, length us, event | category | flops | bytes accessed | tf_op | source)
XLA Modules:
  0.0 159.5 jit_solution(3783286405488251205)
XLA Ops:
  0.0 2.6 %convert.4 = bf16[2,768,768]{2,1,0:T(8,128)(2,1)S(1)} convert(f32[2,768,768]{2,1,0:T(8,128)} %slab_ref.1) | non-fusion elementwise | flops 1179648 | bytes 7077888 | tf_op jit(solution)/shard_map/convert.1
  2.6 0.1 slice.23
  2.7 0.0 copy-start.7
  2.7 0.0 copy-start.3
  2.7 2.6 %collective-permute-start.1 = (bf16[2,512,768]{2,1,0:T(8,128)(2,1)S(1)}, bf16[2,512,768]{2,1,0:T(8,128)(2,1)S(1)}, u32[]{:S(2)}, u32[]{:S(2)}) collective-permute-start(bf16[2,512,768]{2,1,0:T(8,128)(2,1)S(1)} %slice.23), channel_id=1, source_target_pairs={{1,0},{2,1},{3,2},{5,4},{6,5},{7,6},{9,8},{10,9},{11,10},{13,12},{... | collective-permute-start | bytes 4718600 | tf_op jit(solution)/shard_map/ppermute | solution.py:24
  5.4 1.3 slice.22
  6.6 5.4 %collective-permute-start = (bf16[2,768,512]{2,1,0:T(8,128)(2,1)}, bf16[2,768,512]{2,1,0:T(8,128)(2,1)}, u32[]{:S(2)}, u32[]{:S(2)}) collective-permute-start(bf16[2,768,512]{2,1,0:T(8,128)(2,1)} %slice.22), channel_id=1, source_target_pairs={{4,0},{8,4},{12,8},{16,12},{20,16},{24,20},{28,24},{32,28},{36,32}... | collective-permute-start | bytes 4718600 | tf_op jit(solution)/shard_map/ppermute | solution.py:24
  12.0 29.0 %collective-permute-done.1.below_ref = bf16[2,512,768]{2,1,0:T(8,128)(2,1)S(1)} collective-permute-done((bf16[2,512,768]{2,1,0:T(8,128)(2,1)S(1)}, bf16[2,512,768]{2,1,0:T(8,128)(2,1)S(1)}, u32[]{:S(2)}, u32[]{:S(2)}) %collective-permute-start.1) | collective-permute-done | bytes 1572896 | tf_op jit(solution)/shard_map/ppermute | solution.py:24
  41.0 1.2 copy-done.6
  42.2 1.1 slice.24
  43.3 4.8 %collective-permute-start.2 = (bf16[2,512,512]{2,1,0:T(8,128)(2,1)}, bf16[2,512,512]{2,1,0:T(8,128)(2,1)}, u32[]{:S(2)}, u32[]{:S(2)}) collective-permute-start(bf16[2,512,512]{2,1,0:T(8,128)(2,1)} %slice.24), channel_id=1, source_target_pairs={{4,0},{8,4},{12,8},{16,12},{20,16},{24,20},{28,24},{32,28},{36,32}... | collective-permute-start | bytes 3145736 | tf_op jit(solution)/shard_map/ppermute | solution.py:24
  48.1 0.7 copy.10.shift_ref
  48.7 0.6 constant_dynamic-slice_fusion
  49.4 1.0 copy-done.4
  50.4 1.0 copy-done.5
  51.4 4.3 %shard_map.91.meas_ref = bf16[6,512,512]{2,1,0:T(8,128)(2,1)S(1)} custom-call(bf16[512,512]{1,0:T(8,128)(2,1)S(1)} %copy-done.5, bf16[512,512]{1,0:T(8,128)(2,1)S(1)} %copy-done.4, bf16[6,512,512]{2,1,0:T(8,128)(2,1)S(1)} %bitcast.3), custom_call_target="tpu_custom_call" | custom-call | flops 3221225472 | bytes 6291456 | tf_op jit(solution)/shard_map/pallas_call | solution.py:76
  55.8 1.6 %copy-done.2 = bf16[6,512,512]{2,1,0:T(8,128)(2,1)} copy-done((bf16[6,512,512]{2,1,0:T(8,128)(2,1)}, bf16[6,512,512]{2,1,0:T(8,128)(2,1)S(1)}, u32[]{:S(2)}) %copy-start.2) | copy-done | bytes 3145752
  57.4 0.0 collective-permute-done.right_ref
  57.4 3.3 %collective-permute-done.2.corner_ref = bf16[2,512,512]{2,1,0:T(8,128)(2,1)} collective-permute-done((bf16[2,512,512]{2,1,0:T(8,128)(2,1)}, bf16[2,512,512]{2,1,0:T(8,128)(2,1)}, u32[]{:S(2)}, u32[]{:S(2)}) %collective-permute-start.2) | collective-permute-done | bytes 1048608 | tf_op jit(solution)/shard_map/ppermute | solution.py:24
  60.7 41.9 %shard_map.92 = (f32[2,768,768]{2,1,0:T(8,128)}, bf16[2,768,512]{2,1,0:T(8,128)(2,1)}, bf16[2,512,768]{2,1,0:T(8,128)(2,1)}, bf16[2,512,512]{2,1,0:T(8,128)(2,1)}) custom-call(s32[1]{0:T(128)} %bitcast.live_ref, s32[6,2]{1,0:T(8,128)} %copy.10.shift_ref, f32[2,768,768]{2,1,0:T(8,128)} %slab_ref.1, bf16[2,768,512]{2,1,0:T(8,128)(2,1)} %collective-permute-done.right_ref, ...), custom_call_target="tpu_custom_call" | custom-call | flops 1610612736 | bytes 20971520 | tf_op jit(solution)/shard_map/pallas_call | solution.py:299
  102.5 1.9 %collective-permute-start.4 = (bf16[2,512,512]{2,1,0:T(8,128)(2,1)}, bf16[2,512,512]{2,1,0:T(8,128)(2,1)S(1)}, u32[]{:S(2)}, u32[]{:S(2)}) collective-permute-start(bf16[2,512,512]{2,1,0:T(8,128)(2,1)} %get-tuple-element.12), channel_id=1, source_target_pairs={{0,4},{4,8},{8,12},{12,16},{16,20},{20,24},{24,28},{28,32},{32,36}... | collective-permute-start | bytes 3145736 | tf_op jit(solution)/shard_map/ppermute | solution.py:24
  104.5 1.9 %collective-permute-start.3 = (bf16[2,768,512]{2,1,0:T(8,128)(2,1)}, bf16[2,768,512]{2,1,0:T(8,128)(2,1)S(1)}, u32[]{:S(2)}, u32[]{:S(2)}) collective-permute-start(bf16[2,768,512]{2,1,0:T(8,128)(2,1)} %get-tuple-element.10), channel_id=1, source_target_pairs={{0,4},{4,8},{8,12},{12,16},{16,20},{20,24},{24,28},{28,32},{32,36}... | collective-permute-start | bytes 4718600 | tf_op jit(solution)/shard_map/ppermute | solution.py:24
  106.4 14.6 %collective-permute-done.4 = bf16[2,512,512]{2,1,0:T(8,128)(2,1)S(1)} collective-permute-done((bf16[2,512,512]{2,1,0:T(8,128)(2,1)}, bf16[2,512,512]{2,1,0:T(8,128)(2,1)S(1)}, u32[]{:S(2)}, u32[]{:S(2)}) %collective-permute-start.4) | collective-permute-done | bytes 1048608 | tf_op jit(solution)/shard_map/ppermute | solution.py:24
  121.0 1.7 %add_convert_fusion = bf16[2,512,512]{2,1,0:T(8,128)(2,1)S(1)} fusion(bf16[2,512,512]{2,1,0:T(8,128)(2,1)S(1)} %collective-permute-done.4, bf16[2,512,768]{2,1,0:T(8,128)(2,1)} %get-tuple-element.11), kind=kLoop, calls=%fused_computation | loop fusion | flops 2097152 | bytes 3145728 | tf_op jit(solution)/shard_map/convert_element_type | solution.py:366
  122.6 2.1 %collective-permute-start.5 = (bf16[2,512,512]{2,1,0:T(8,128)(2,1)S(1)}, bf16[2,512,512]{2,1,0:T(8,128)(2,1)S(1)}, u32[]{:S(2)}, u32[]{:S(2)}) collective-permute-start(bf16[2,512,512]{2,1,0:T(8,128)(2,1)S(1)} %add_convert_fusion), channel_id=1, source_target_pairs={{0,1},{1,2},{2,3},{4,5},{5,6},{6,7},{8,9},{9,10},{10,11},{12,13},{... | collective-permute-start | bytes 3145736 | tf_op jit(solution)/shard_map/ppermute | solution.py:24
  124.7 1.1 slice.21
  125.8 1.9 %collective-permute-start.6 = (bf16[2,512,256]{2,1,0:T(8,128)(2,1)S(1)}, bf16[2,512,256]{2,1,0:T(8,128)(2,1)S(1)}, u32[]{:S(2)}, u32[]{:S(2)}) collective-permute-start(bf16[2,512,256]{2,1,0:T(8,128)(2,1)S(1)} %slice.21), channel_id=1, source_target_pairs={{0,1},{1,2},{2,3},{4,5},{5,6},{6,7},{8,9},{9,10},{10,11},{12,13},{... | collective-permute-start | bytes 1572872 | tf_op jit(solution)/shard_map/ppermute | solution.py:24
  127.7 28.0 %collective-permute-done.6 = bf16[2,512,256]{2,1,0:T(8,128)(2,1)S(1)} collective-permute-done((bf16[2,512,256]{2,1,0:T(8,128)(2,1)S(1)}, bf16[2,512,256]{2,1,0:T(8,128)(2,1)S(1)}, u32[]{:S(2)}, u32[]{:S(2)}) %collective-permute-start.6) | collective-permute-done | bytes 524320 | tf_op jit(solution)/shard_map/ppermute | solution.py:24
  155.7 0.0 collective-permute-done.5
  155.7 0.1 pad_maximum_fusion.below_ref
  155.8 0.0 collective-permute-done.3.right_ref
  155.8 3.7 %shard_map.93 = f32[2,768,768]{2,1,0:T(8,128)} custom-call(f32[2,768,768]{2,1,0:T(8,128)S(1)} %copy-done.1, bf16[2,768,512]{2,1,0:T(8,128)(2,1)S(1)} %collective-permute-done.3.right_ref, bf16[2,512,768]{2,1,0:T(8,128)(2,1)S(1)} %pad_maximum_fusion.below_ref), custom_call_target="tpu_custom_call" | custom-call | tf_op jit(solution)/shard_map/pallas_call | solution.py:336
  (10 shorter events, 0.0 us)
Async XLA Ops:
  0.0 48.7 %copy-start = (s32[32,1]{0,1:T(1,128)S(1)}, s32[32,1]{0,1:T(1,128)}, u32[]{:S(2)}) copy-start(s32[32,1]{0,1:T(1,128)} %param.13) | copy-start | bytes 388
  2.7 45.4 %copy-start.7 = (s32[1,1,6,2]{2,3,1,0:T(2,128)S(1)}, s32[1,1,6,2]{2,3,1,0:T(2,128)}, u32[]{:S(2)}) copy-start(s32[1,1,6,2]{2,3,1,0:T(2,128)} %param.12) | copy-start | bytes 148
  2.7 46.6 %copy-start.3 = (bf16[1,1,6,512,512]{4,3,2,1,0:T(8,128)(2,1)S(1)}, bf16[1,1,6,512,512]{4,3,2,1,0:T(8,128)(2,1)}, u32[]{:S(2)}) copy-start(bf16[1,1,6,512,512]{4,3,2,1,0:T(8,128)(2,1)} %param.11) | copy-start | bytes 9437188
  2.7 38.3 %collective-permute-start.1 = (bf16[2,512,768]{2,1,0:T(8,128)(2,1)S(1)}, bf16[2,512,768]{2,1,0:T(8,128)(2,1)S(1)}, u32[]{:S(2)}, u32[]{:S(2)}) collective-permute-start(bf16[2,512,768]{2,1,0:T(8,128)(2,1)S(1)} %slice.23), channel_id=1, source_target_pairs={{1,0},{2,1},{3,2},{5,4},{6,5},{7,6},{9,8},{10,9},{11,10},{13,12},{... | collective-permute-start | bytes 4718600 | tf_op jit(solution)/shard_map/ppermute | solution.py:24
  6.6 50.8 %collective-permute-start = (bf16[2,768,512]{2,1,0:T(8,128)(2,1)}, bf16[2,768,512]{2,1,0:T(8,128)(2,1)}, u32[]{:S(2)}, u32[]{:S(2)}) collective-permute-start(bf16[2,768,512]{2,1,0:T(8,128)(2,1)} %slice.22), channel_id=1, source_target_pairs={{4,0},{8,4},{12,8},{16,12},{20,16},{24,20},{28,24},{32,28},{36,32}... | collective-permute-start | bytes 4718600 | tf_op jit(solution)/shard_map/ppermute | solution.py:24
  41.0 1.2 copy-start.6
  43.3 17.4 %collective-permute-start.2 = (bf16[2,512,512]{2,1,0:T(8,128)(2,1)}, bf16[2,512,512]{2,1,0:T(8,128)(2,1)}, u32[]{:S(2)}, u32[]{:S(2)}) collective-permute-start(bf16[2,512,512]{2,1,0:T(8,128)(2,1)} %slice.24), channel_id=1, source_target_pairs={{4,0},{8,4},{12,8},{16,12},{20,16},{24,20},{28,24},{32,28},{36,32}... | collective-permute-start | bytes 3145736 | tf_op jit(solution)/shard_map/ppermute | solution.py:24
  49.4 1.0 copy-start.4
  50.4 1.0 copy-start.5
  55.7 1.6 %copy-start.2 = (bf16[6,512,512]{2,1,0:T(8,128)(2,1)}, bf16[6,512,512]{2,1,0:T(8,128)(2,1)S(1)}, u32[]{:S(2)}) copy-start(bf16[6,512,512]{2,1,0:T(8,128)(2,1)S(1)} %shard_map.91.meas_ref) | copy-start | bytes 9437188
  102.5 18.4 %collective-permute-start.4 = (bf16[2,512,512]{2,1,0:T(8,128)(2,1)}, bf16[2,512,512]{2,1,0:T(8,128)(2,1)S(1)}, u32[]{:S(2)}, u32[]{:S(2)}) collective-permute-start(bf16[2,512,512]{2,1,0:T(8,128)(2,1)} %get-tuple-element.12), channel_id=1, source_target_pairs={{0,4},{4,8},{8,12},{12,16},{16,20},{20,24},{24,28},{28,32},{32,36}... | collective-permute-start | bytes 3145736 | tf_op jit(solution)/shard_map/ppermute | solution.py:24
  104.5 51.3 %collective-permute-start.3 = (bf16[2,768,512]{2,1,0:T(8,128)(2,1)}, bf16[2,768,512]{2,1,0:T(8,128)(2,1)S(1)}, u32[]{:S(2)}, u32[]{:S(2)}) collective-permute-start(bf16[2,768,512]{2,1,0:T(8,128)(2,1)} %get-tuple-element.10), channel_id=1, source_target_pairs={{0,4},{4,8},{8,12},{12,16},{16,20},{20,24},{24,28},{28,32},{32,36}... | collective-permute-start | bytes 4718600 | tf_op jit(solution)/shard_map/ppermute | solution.py:24
  121.0 34.8 %copy-start.1 = (f32[2,768,768]{2,1,0:T(8,128)S(1)}, f32[2,768,768]{2,1,0:T(8,128)}, u32[]{:S(2)}) copy-start(f32[2,768,768]{2,1,0:T(8,128)} %get-tuple-element.9.local_ref) | copy-start | bytes 14155780
  122.6 33.0 %collective-permute-start.5 = (bf16[2,512,512]{2,1,0:T(8,128)(2,1)S(1)}, bf16[2,512,512]{2,1,0:T(8,128)(2,1)S(1)}, u32[]{:S(2)}, u32[]{:S(2)}) collective-permute-start(bf16[2,512,512]{2,1,0:T(8,128)(2,1)S(1)} %add_convert_fusion), channel_id=1, source_target_pairs={{0,1},{1,2},{2,3},{4,5},{5,6},{6,7},{8,9},{9,10},{10,11},{12,13},{... | collective-permute-start | bytes 3145736 | tf_op jit(solution)/shard_map/ppermute | solution.py:24
  125.8 29.9 %collective-permute-start.6 = (bf16[2,512,256]{2,1,0:T(8,128)(2,1)S(1)}, bf16[2,512,256]{2,1,0:T(8,128)(2,1)S(1)}, u32[]{:S(2)}, u32[]{:S(2)}) collective-permute-start(bf16[2,512,256]{2,1,0:T(8,128)(2,1)S(1)} %slice.21), channel_id=1, source_target_pairs={{0,1},{1,2},{2,3},{4,5},{5,6},{6,7},{8,9},{9,10},{10,11},{12,13},{... | collective-permute-start | bytes 1572872 | tf_op jit(solution)/shard_map/ppermute | solution.py:24

commit v2 on v1

--- a/solution.py
+++ b/solution.py
@@ -15,6 +15,7 @@
 E = T + W
 NB = E // Q
 TB = T // Q
+VMEM_MAIN = 48 * 2**20
 R = 16
 f32, bf16 = jnp.float32, jnp.bfloat16
 
@@ -91,15 +92,19 @@
     shift_ref,
     slab_ref,
     right_ref,
-    below_ref,
-    corner_ref,
+    below0_ref,
+    below1_ref,
+    below2_ref,
+    corner0_ref,
+    corner1_ref,
     probe_ref,
     meas_ref,
     ga_ref,
     gb_ref,
     local_ref,
     spill_right_ref,
-    spill_below_ref,
+    spill_near_ref,
+    spill_far_ref,
     spill_corner_ref,
     ext,
     grown,
@@ -110,6 +115,9 @@
     in_sem,
     out_sem,
 ):
+    below_refs = (below0_ref, below1_ref, below2_ref)
+    corner_refs = (corner0_ref, corner1_ref)
+
     def slab_copy(p, b):
         return pltpu.make_async_copy(
             slab_ref.at[p, :, lanes(b)], ext.at[p, b, pl.ds(0, T), :], in_sem.at[p, b]
@@ -146,10 +154,13 @@
         rows = pl.ds(pl.multiple_of(i * R, R), R)
         there = pl.ds(pl.multiple_of(T + i * R, R), R)
         for p in range(2):
-            for b in range(TB):
-                ext[p, b, there, :] = below_ref[p, rows, lanes(b)].astype(f32)
-            for b in range(4):
-                ext[p, TB + b, there, :] = corner_ref[p, rows, lanes(b)].astype(f32)
+            for b in range(2):
+                for piece in range(3):
+                    ext[p, 2 * piece + b, there, :] = below_refs[piece][p, rows, lanes(b)].astype(f32)
+                for piece in range(2):
+                    ext[p, TB + 2 * piece + b, there, :] = corner_refs[piece][
+                        p, rows, lanes(b)
+                    ].astype(f32)
         return carry
 
     lax.fori_loop(0, W // R, fill_below, 0)
@@ -161,8 +172,8 @@
     lane = lax.broadcasted_iota(jnp.int32, (R, Q), 1)
 
     def one_slot(slot, carry):
-        row0 = shift_ref[slot, 0]
-        col0 = shift_ref[slot, 1]
+        row0 = shift_ref[0, slot]
+        col0 = shift_ref[1, slot]
         block0 = col0 // Q
         by = col0 % Q
         inner = lane < Q - by
@@ -267,6 +278,19 @@
         for b in range(TB):
             local_copy(p, b).start()
 
+    def drain_below(i, carry):
+        rows = pl.ds(pl.multiple_of(i * R, R), R)
+        here = pl.ds(pl.multiple_of(T + i * R, R), R)
+        for p in range(2):
+            for b in range(4):
+                spill_near_ref[p, rows, lanes(b)] = grown[p, b, here, :].astype(bf16)
+                spill_corner_ref[p, rows, lanes(b)] = grown[p, TB + b, here, :].astype(bf16)
+            for b in range(2):
+                spill_far_ref[p, rows, lanes(b)] = grown[p, 4 + b, here, :].astype(bf16)
+        return carry
+
+    lax.fori_loop(0, W // R, drain_below, 0)
+
     def drain_right(i, carry):
         rows = pl.ds(pl.multiple_of(i * R, R), R)
         for p in range(2):
@@ -275,18 +299,6 @@
         return carry
 
     lax.fori_loop(0, T // R, drain_right, 0)
-
-    def drain_below(i, carry):
-        rows = pl.ds(pl.multiple_of(i * R, R), R)
-        here = pl.ds(pl.multiple_of(T + i * R, R), R)
-        for p in range(2):
-            for b in range(TB):
-                spill_below_ref[p, rows, lanes(b)] = grown[p, b, here, :].astype(bf16)
-            for b in range(4):
-                spill_corner_ref[p, rows, lanes(b)] = grown[p, TB + b, here, :].astype(bf16)
-        return carry
-
-    lax.fori_loop(0, W // R, drain_below, 0)
     for p in range(2):
         for b in range(TB):
             local_copy(p, b).wait()
@@ -298,12 +310,13 @@
     anywhere = pl.BlockSpec(memory_space=pl.ANY)
     return pl.pallas_call(
         main_kernel,
-        in_specs=[smem, smem, anywhere] + [vmem] * 7,
-        out_specs=[anywhere, vmem, vmem, vmem],
+        in_specs=[smem, smem, anywhere] + [vmem] * 10,
+        out_specs=[anywhere] + [vmem] * 4,
         out_shape=[
             jax.ShapeDtypeStruct((2, T, T), f32),
             jax.ShapeDtypeStruct((2, T, W), bf16),
-            jax.ShapeDtypeStruct((2, W, T), bf16),
+            jax.ShapeDtypeStruct((2, W, W), bf16),
+            jax.ShapeDtypeStruct((2, W, T - W), bf16),
             jax.ShapeDtypeStruct((2, W, W), bf16),
         ],
         scratch_shapes=[
@@ -317,55 +330,78 @@
             pltpu.SemaphoreType.DMA((2, TB)),
         ],
         cost_estimate=pl.CostEstimate(
-            flops=6 * 2 * W**3, bytes_accessed=20 * 2**20, transcendentals=0
+            flops=6 * 4 * W**3, bytes_accessed=20 * 2**20, transcendentals=0
         ),
-        compiler_params=pltpu.CompilerParams(vmem_limit_bytes=56 * 2**20),
-    )(live, shifts, slab, right, below, corner, probe, measured, left, left_t)
-
-
-def finish_kernel(local_ref, right_ref, below_ref, out_ref):
+        compiler_params=pltpu.CompilerParams(vmem_limit_bytes=VMEM_MAIN),
+    )(live, shifts, slab, right, *below, *corner, probe, measured, left, left_t)
+
+
+def add_right_kernel(local_ref, right_ref, out_ref):
     out_ref[...] = local_ref[...]
     out_ref[:, :, :W] += right_ref[...].astype(f32)
 
-    @pl.when(pl.program_id(0) < W // Q)
-    def _():
-        out_ref[...] += below_ref[...].astype(f32)
-
-
-def finish(local, right, below):
+
+def add_right(local, right):
     return pl.pallas_call(
-        finish_kernel,
+        add_right_kernel,
         grid=(TB,),
         in_specs=[
             pl.BlockSpec((2, Q, T), lambda i: (0, i, 0)),
             pl.BlockSpec((2, Q, W), lambda i: (0, i, 0)),
-            pl.BlockSpec((2, Q, T), lambda i: (0, jnp.minimum(i, W // Q - 1), 0)),
         ],
         out_specs=pl.BlockSpec((2, Q, T), lambda i: (0, i, 0)),
         out_shape=jax.ShapeDtypeStruct((2, T, T), f32),
-        compiler_params=pltpu.CompilerParams(vmem_limit_bytes=24 * 2**20),
-    )(local, right, below)
+        input_output_aliases={0: 0},
+        compiler_params=pltpu.CompilerParams(vmem_limit_bytes=16 * 2**20),
+    )(local, right)
+
+
+def add_below_kernel(local_ref, near_ref, far_ref, out_ref):
+    out_ref[:, :, :W] = local_ref[:, :, :W] + near_ref[...].astype(f32)
+    out_ref[:, :, W:] = local_ref[:, :, W:] + far_ref[...].astype(f32)
+
+
+def add_below(local, near, far):
+    return pl.pallas_call(
+        add_below_kernel,
+        grid=(W // Q,),
+        in_specs=[
+            pl.BlockSpec((2, Q, T), lambda i: (0, i, 0)),
+            pl.BlockSpec((2, Q, W), lambda i: (0, i, 0)),
+            pl.BlockSpec((2, Q, T - W), lambda i: (0, i, 0)),
+        ],
+        out_specs=pl.BlockSpec((2, Q, T), lambda i: (0, i, 0)),
+        out_shape=jax.ShapeDtypeStruct((2, T, T), f32),
+        input_output_aliases={0: 0},
+        compiler_params=pltpu.CompilerParams(vmem_limit_bytes=16 * 2**20),
+    )(local, near, far)
 
 
 def shards(slab, probe, intensities, offsets, live_count):
     left, left_t, pick = tables()
-    send_below = slab[:, :W, :].astype(bf16)
-    send_right = slab[:, :, :W].astype(bf16)
-    below = shifted(send_below, "tile", -1)
-    right = shifted(send_right, "scan", -1)
-    corner = shifted(below[:, :, :W], "scan", -1)
+    cols = [slice(piece * 2 * Q, (piece + 1) * 2 * Q) for piece in range(3)]
+    below0 = shifted(slab[:, :W, cols[0]].astype(bf16), "tile", -1)
+    below1 = shifted(slab[:, :W, cols[1]].astype(bf16), "tile", -1)
+    below2 = shifted(slab[:, :W, cols[2]].astype(bf16), "tile", -1)
+    right = shifted(slab[:, :, :W].astype(bf16), "scan", -1)
     measured = sort_intensities(intensities[0, 0], pick)
     live = lax.dynamic_slice(live_count[:, 0], (lax.axis_index("scan"),), (1,))
-    local, to_right, to_below, to_corner = solve(
-        live, offsets[0, 0], slab, right, below, corner, probe, measured,
+    shifts = offsets[0, 0].T
+    below0, measured, live, shifts = lax.optimization_barrier((below0, measured, live, shifts))
+    corner0 = shifted(below0, "scan", -1)
+    corner1 = shifted(below1, "scan", -1)
+    local, to_right, near, far, to_corner = solve(
+        live, shifts, slab, right, (below0, below1, below2), (corner0, corner1), probe, measured,
         jnp.asarray(left), jnp.asarray(left_t),
     )
+    far = shifted(far, "tile", 1)
+    from_corner = shifted(to_corner, "scan", 1)
+    near = (near.astype(f32) + from_corner.astype(f32)).astype(bf16)
+    near, to_right, far = lax.optimization_barrier((near, to_right, far))
+    near = shifted(near, "tile", 1)
     from_left = shifted(to_right, "scan", 1)
-    from_corner = shifted(to_corner, "scan", 1)
-    far_half = shifted(to_below[:, :, W:], "tile", 1)
-    near = (to_below[:, :, :W].astype(f32) + from_corner.astype(f32)).astype(bf16)
-    near_half = shifted(near, "tile", 1)
-    return finish(local, from_left, jnp.concatenate([near_half, far_half], axis=2))
+    local = add_right(local, from_left)
+    return add_below(local, near, far)
 
 
 def solution(mesh):

time: 161 us -> 147 us (0.913)
  waiting for transfers between devices: 74.8 us -> 57.5 us
  Pallas kernels: 49.8 us -> 54.9 us
  starting transfers between devices: 20.6 us -> 24.6 us
  local copies, waits for them, and re-layouts: 9.72 us -> 6.54 us
    ppermute x7 -> x10, waiting for transfers between devices: 74.8 us -> 57.5 us  [shifted(): lax.ppermute(value, axis, [(i, i + by) for i in range(n) if 0 <= i + by <...]
    pallas_call x2 -> x3, Pallas kernels: 45.5 us -> 50.6 us  [the longest x1 40.4 us: solve(): pl.pallas_call(main_kernel, in_specs=[smem, smem, anywhere] + [vmem] * 10...]
    ppermute x7 -> x10, starting transfers between devices: 20.6 us -> 24.6 us  [shifted(): lax.ppermute(value, axis, [(i, i + by) for i in range(n) if 0 <= i + by <...]
    unnamed x16 -> x18, local copies, waits for them, and re-layouts: 4.92 us -> 3.56 us
    slice x4 -> x2, local copies, waits for them, and re-layouts: 3.53 us -> 2.37 us  [the longest x1 1.27 us: shards(): right = shifted(slab[:, :, :W].astype(bf16), 'scan', -1)]
  transfers between devices with their start and end apart: 7 -> 10, of which waited for: 4 -> 7; matrix products, arithmetic and copies ran while one was open for 4% -> 1% of each run, Pallas kernels for 3% -> 7%
where the time goes in v2:
time: 147 us
  waiting for transfers between devices  57.5 us (39%)
  Pallas kernels  54.9 us (37%)
  starting transfers between devices  24.6 us (17%)
  local copies, waits for them, and re-layouts  6.54 us (4%)
  other arithmetic  2.86 us (2%)
    ppermute x10, waiting for transfers between devices, shifted(): lax.ppermute(value, axis, [(i, i + by) for i in range(n) if 0 <= i + by <...  57.5 us
    pallas_call x1, Pallas kernels, solve(): pl.pallas_call(main_kernel, in_specs=[smem, smem, anywhere] + [vmem] * 10...  40.4 us
    ppermute x10, starting transfers between devices, shifted(): lax.ppermute(value, axis, [(i, i + by) for i in range(n) if 0 <= i + by <...  24.6 us
    pallas_call x1, Pallas kernels, add_right(): pl.pallas_call(add_right_kernel, grid=(TB,), in_specs=[pl.BlockSpec((2, Q...  6.06 us
    pallas_call x1, Pallas kernels, sort_intensities(): pl.pallas_call(sort_kernel, grid=(slots,), in_specs=[whole, whole, each],...  4.3 us
    pallas_call x1, Pallas kernels, add_below(): pl.pallas_call(add_below_kernel, grid=(W // Q,), in_specs=[pl.BlockSpec((...  4.21 us
    unnamed x18, local copies, waits for them, and re-layouts  3.56 us
  transfers between devices with their start and end apart: 10, of which 7 were waited for; matrix products, arithmetic and copies ran while one was open for 1% of the time, Pallas kernels for 7%

profile of v2, /device:TPU:22, one launch (start us, length us, event | category | flops | bytes accessed | tf_op | source)
XLA Modules:
  0.0 146.5 jit_solution(7964836362308585521)
XLA Ops:
  0.0 2.6 %convert.6 = bf16[2,768,768]{2,1,0:T(8,128)(2,1)S(1)} convert(f32[2,768,768]{2,1,0:T(8,128)} %slab_ref.1) | non-fusion elementwise | flops 1179648 | bytes 7077888 | tf_op jit(solution)/shard_map/convert.3
  2.6 1.3 slice.21
  3.9 5.8 %collective-permute-start.1 = (bf16[2,768,512]{2,1,0:T(8,128)(2,1)}, bf16[2,768,512]{2,1,0:T(8,128)(2,1)}, u32[]{:S(2)}, u32[]{:S(2)}) collective-permute-start(bf16[2,768,512]{2,1,0:T(8,128)(2,1)} %slice.21), channel_id=1, source_target_pairs={{4,0},{8,4},{12,8},{16,12},{20,16},{24,20},{28,24},{32,28},{36,32}... | collective-permute-start | bytes 4718600 | tf_op jit(solution)/shard_map/ppermute | solution.py:25
  9.6 1.1 fusion
  10.7 2.3 %collective-permute-start = (bf16[2,512,256]{2,1,0:T(8,128)(2,1)}, bf16[2,512,256]{2,1,0:T(8,128)(2,1)S(1)}, u32[]{:S(2)}, u32[]{:S(2)}) collective-permute-start(bf16[2,512,256]{2,1,0:T(8,128)(2,1)} %get-tuple-element.31), channel_id=1, source_target_pairs={{1,0},{2,1},{3,2},{5,4},{6,5},{7,6},{9,8},{10,9},{11,10},{13,12},{... | collective-permute-start | bytes 1572872 | tf_op jit(solution)/shard_map/ppermute | solution.py:25
  13.1 2.4 %collective-permute-start.2 = (bf16[2,512,256]{2,1,0:T(8,128)(2,1)}, bf16[2,512,256]{2,1,0:T(8,128)(2,1)S(1)}, u32[]{:S(2)}, u32[]{:S(2)}) collective-permute-start(bf16[2,512,256]{2,1,0:T(8,128)(2,1)} %get-tuple-element.30), channel_id=1, source_target_pairs={{1,0},{2,1},{3,2},{5,4},{6,5},{7,6},{9,8},{10,9},{11,10},{13,12},{... | collective-permute-start | bytes 1572872 | tf_op jit(solution)/shard_map/ppermute | solution.py:25
  15.5 1.9 %collective-permute-start.3 = (bf16[2,512,256]{2,1,0:T(8,128)(2,1)S(1)}, bf16[2,512,256]{2,1,0:T(8,128)(2,1)S(1)}, u32[]{:S(2)}, u32[]{:S(2)}) collective-permute-start(bf16[2,512,256]{2,1,0:T(8,128)(2,1)S(1)} %get-tuple-element.29), channel_id=1, source_target_pairs={{1,0},{2,1},{3,2},{5,4},{6,5},{7,6},{9,8},{10,9},{11,10},{13,12},{... | collective-permute-start | bytes 1572872 | tf_op jit(solution)/shard_map/ppermute | solution.py:25
  17.4 0.0 copy-done
  17.4 0.6 constant_dynamic-slice_fusion
  18.0 1.9 %copy-done.5 = bf16[1,1,6,512,512]{4,3,2,1,0:T(8,128)(2,1)S(1)} copy-done((bf16[1,1,6,512,512]{4,3,2,1,0:T(8,128)(2,1)S(1)}, bf16[1,1,6,512,512]{4,3,2,1,0:T(8,128)(2,1)}, u32[]{:S(2)}) %copy-start.5) | copy-done | bytes 3145752
  19.9 4.3 %shard_map.91.meas_ref = bf16[6,512,512]{2,1,0:T(8,128)(2,1)S(1)} custom-call(bf16[512,512]{1,0:T(8,128)(2,1)S(1)} %copy-done.7, bf16[512,512]{1,0:T(8,128)(2,1)S(1)} %copy-done.6, bf16[6,512,512]{2,1,0:T(8,128)(2,1)S(1)} %bitcast.6), custom_call_target="tpu_custom_call" | custom-call | flops 3221225472 | bytes 6291456 | tf_op jit(solution)/shard_map/pallas_call | solution.py:77
  24.2 1.6 %copy-done.1 = bf16[6,512,512]{2,1,0:T(8,128)(2,1)} copy-done((bf16[6,512,512]{2,1,0:T(8,128)(2,1)}, bf16[6,512,512]{2,1,0:T(8,128)(2,1)S(1)}, u32[]{:S(2)}) %copy-start.1) | copy-done | bytes 3145752
  25.9 1.8 %collective-permute-done.below0_ref = bf16[2,512,256]{2,1,0:T(8,128)(2,1)S(1)} collective-permute-done((bf16[2,512,256]{2,1,0:T(8,128)(2,1)}, bf16[2,512,256]{2,1,0:T(8,128)(2,1)S(1)}, u32[]{:S(2)}, u32[]{:S(2)}) %collective-permute-start) | collective-permute-done | bytes 524320 | tf_op jit(solution)/shard_map/ppermute | solution.py:25
  27.7 11.2 %collective-permute-done.2.below1_ref = bf16[2,512,256]{2,1,0:T(8,128)(2,1)S(1)} collective-permute-done((bf16[2,512,256]{2,1,0:T(8,128)(2,1)}, bf16[2,512,256]{2,1,0:T(8,128)(2,1)S(1)}, u32[]{:S(2)}, u32[]{:S(2)}) %collective-permute-start.2) | collective-permute-done | bytes 524320 | tf_op jit(solution)/shard_map/ppermute | solution.py:25
  38.9 1.9 %collective-permute-start.5 = (bf16[2,512,256]{2,1,0:T(8,128)(2,1)S(1)}, bf16[2,512,256]{2,1,0:T(8,128)(2,1)S(1)}, u32[]{:S(2)}, u32[]{:S(2)}) collective-permute-start(bf16[2,512,256]{2,1,0:T(8,128)(2,1)S(1)} %collective-permute-done.2.below1_ref), channel_id=1, source_target_pairs={{4,0},{8,4},{12,8},{16,12},{20,16},{24,20},{28,24},{32,28},{36,32}... | collective-permute-start | bytes 1572872 | tf_op jit(solution)/shard_map/ppermute | solution.py:25
  40.8 2.4 %collective-permute-start.4 = (bf16[2,512,256]{2,1,0:T(8,128)(2,1)S(1)}, bf16[2,512,256]{2,1,0:T(8,128)(2,1)S(1)}, u32[]{:S(2)}, u32[]{:S(2)}) collective-permute-start(bf16[2,512,256]{2,1,0:T(8,128)(2,1)S(1)} %collective-permute-done.below0_ref), channel_id=1, source_target_pairs={{4,0},{8,4},{12,8},{16,12},{20,16},{24,20},{28,24},{32,28},{36,32}... | collective-permute-start | bytes 1572872 | tf_op jit(solution)/shard_map/ppermute | solution.py:25
  43.3 2.6 %collective-permute-done.3.below2_ref = bf16[2,512,256]{2,1,0:T(8,128)(2,1)S(1)} collective-permute-done((bf16[2,512,256]{2,1,0:T(8,128)(2,1)S(1)}, bf16[2,512,256]{2,1,0:T(8,128)(2,1)S(1)}, u32[]{:S(2)}, u32[]{:S(2)}) %collective-permute-start.3) | collective-permute-done | bytes 524320 | tf_op jit(solution)/shard_map/ppermute | solution.py:25
  45.9 1.6 %collective-permute-done.5.corner1_ref = bf16[2,512,256]{2,1,0:T(8,128)(2,1)S(1)} collective-permute-done((bf16[2,512,256]{2,1,0:T(8,128)(2,1)S(1)}, bf16[2,512,256]{2,1,0:T(8,128)(2,1)S(1)}, u32[]{:S(2)}, u32[]{:S(2)}) %collective-permute-start.5) | collective-permute-done | bytes 524320 | tf_op jit(solution)/shard_map/ppermute | solution.py:25
  47.5 5.6 %collective-permute-done.4.corner0_ref = bf16[2,512,256]{2,1,0:T(8,128)(2,1)S(1)} collective-permute-done((bf16[2,512,256]{2,1,0:T(8,128)(2,1)S(1)}, bf16[2,512,256]{2,1,0:T(8,128)(2,1)S(1)}, u32[]{:S(2)}, u32[]{:S(2)}) %collective-permute-start.4) | collective-permute-done | bytes 524320 | tf_op jit(solution)/shard_map/ppermute | solution.py:25
  53.1 0.0 collective-permute-done.1.right_ref
  53.2 40.4 %shard_map.92 = (f32[2,768,768]{2,1,0:T(8,128)}, bf16[2,768,512]{2,1,0:T(8,128)(2,1)}, bf16[2,512,512]{2,1,0:T(8,128)(2,1)S(1)}, bf16[2,512,256]{2,1,0:T(8,128)(2,1)S(1)}, bf16[2,512,512]{2,1,0:T(8,128)(2,1)}) custom-call(s32[1]{0:T(128)} %bitcast.1.live_ref, s32[2,6]{1,0:T(2,128)S(1)} %bitcast.5, f32[2,768,768]{2,1,0:T(8,128)} %slab_ref.1, ...), custom_call_target="tpu_custom_call" | custom-call | flops 3221225472 | bytes 20971520 | tf_op jit(solution)/shard_map/pallas_call | solution.py:311
  93.5 2.1 %collective-permute-start.6 = (bf16[2,512,512]{2,1,0:T(8,128)(2,1)}, bf16[2,512,512]{2,1,0:T(8,128)(2,1)S(1)}, u32[]{:S(2)}, u32[]{:S(2)}) collective-permute-start(bf16[2,512,512]{2,1,0:T(8,128)(2,1)} %get-tuple-element.23), channel_id=1, source_target_pairs={{0,4},{4,8},{8,12},{12,16},{16,20},{20,24},{24,28},{28,32},{32,36}... | collective-permute-start | bytes 3145736 | tf_op jit(solution)/shard_map/ppermute | solution.py:25
  95.6 1.9 %collective-permute-start.7 = (bf16[2,512,256]{2,1,0:T(8,128)(2,1)S(1)}, bf16[2,512,256]{2,1,0:T(8,128)(2,1)S(1)}, u32[]{:S(2)}, u32[]{:S(2)}) collective-permute-start(bf16[2,512,256]{2,1,0:T(8,128)(2,1)S(1)} %get-tuple-element.25), channel_id=1, source_target_pairs={{0,1},{1,2},{2,3},{4,5},{5,6},{6,7},{8,9},{9,10},{10,11},{12,13},{... | collective-permute-start | bytes 1572872 | tf_op jit(solution)/shard_map/ppermute | solution.py:25
  97.5 14.6 %collective-permute-done.6 = bf16[2,512,512]{2,1,0:T(8,128)(2,1)S(1)} collective-permute-done((bf16[2,512,512]{2,1,0:T(8,128)(2,1)}, bf16[2,512,512]{2,1,0:T(8,128)(2,1)S(1)}, u32[]{:S(2)}, u32[]{:S(2)}) %collective-permute-start.6) | collective-permute-done | bytes 1048608 | tf_op jit(solution)/shard_map/ppermute | solution.py:25
  112.1 0.3 add_convert_fusion
  112.4 0.0 collective-permute-done.7.far_ref
  112.4 1.9 %collective-permute-start.8 = (bf16[2,768,512]{2,1,0:T(8,128)(2,1)S(1)}, bf16[2,768,512]{2,1,0:T(8,128)(2,1)S(1)}, u32[]{:S(2)}, u32[]{:S(2)}) collective-permute-start(bf16[2,768,512]{2,1,0:T(8,128)(2,1)S(1)} %copy-done.8), channel_id=1, source_target_pairs={{0,4},{4,8},{8,12},{12,16},{16,20},{20,24},{24,28},{28,32},{32,36}... | collective-permute-start | bytes 4718600 | tf_op jit(solution)/shard_map/ppermute | solution.py:25
  114.4 1.9 %collective-permute-start.9 = (bf16[2,512,512]{2,1,0:T(8,128)(2,1)S(1)}, bf16[2,512,512]{2,1,0:T(8,128)(2,1)S(1)}, u32[]{:S(2)}, u32[]{:S(2)}) collective-permute-start(bf16[2,512,512]{2,1,0:T(8,128)(2,1)S(1)} %add_convert_fusion), channel_id=1, source_target_pairs={{0,1},{1,2},{2,3},{4,5},{5,6},{6,7},{8,9},{9,10},{10,11},{12,13},{... | collective-permute-start | bytes 3145736 | tf_op jit(solution)/shard_map/ppermute | solution.py:25
  116.3 20.0 %collective-permute-done.8.right_ref = bf16[2,768,512]{2,1,0:T(8,128)(2,1)S(1)} collective-permute-done((bf16[2,768,512]{2,1,0:T(8,128)(2,1)S(1)}, bf16[2,768,512]{2,1,0:T(8,128)(2,1)S(1)}, u32[]{:S(2)}, u32[]{:S(2)}) %collective-permute-start.8) | collective-permute-done | bytes 1572896 | tf_op jit(solution)/shard_map/ppermute | solution.py:25
  136.3 6.1 %shard_map.93.local_ref = f32[2,768,768]{2,1,0:T(8,128)} custom-call(f32[2,768,768]{2,1,0:T(8,128)} %get-tuple-element.21.local_ref, bf16[2,768,512]{2,1,0:T(8,128)(2,1)S(1)} %collective-permute-done.8.right_ref), custom_call_target="tpu_custom_call", output_to_operand_aliasing={{}: (0, {})} | custom-call | tf_op jit(solution)/shard_map/pallas_call | solution.py:345
  142.3 0.0 collective-permute-done.9.near_ref
  142.3 4.2 %shard_map.94 = f32[2,768,768]{2,1,0:T(8,128)} custom-call(f32[2,768,768]{2,1,0:T(8,128)} %shard_map.93.local_ref, bf16[2,512,512]{2,1,0:T(8,128)(2,1)S(1)} %collective-permute-done.9.near_ref, bf16[2,512,256]{2,1,0:T(8,128)(2,1)S(1)} %collective-permute-done.7.far_ref), custom_call_target="tpu_custom_call", output_to_operand_aliasing={{}: (0, {})} | custom-call | tf_op jit(solution)/shard_map/pallas_call | solution.py:365
  (15 shorter events, 0.0 us)
Async XLA Ops:
  0.0 17.4 %copy-start = (s32[32,1]{0,1:T(1,128)S(1)}, s32[32,1]{0,1:T(1,128)}, u32[]{:S(2)}) copy-start(s32[32,1]{0,1:T(1,128)} %param.13) | copy-start | bytes 388
  3.9 14.2 %copy-start.6 = (bf16[512,512]{1,0:T(8,128)(2,1)S(1)}, bf16[512,512]{1,0:T(8,128)(2,1)}, u32[]{:S(2)}) copy-start(bf16[512,512]{1,0:T(8,128)(2,1)} %constant.20.clone.pick_t_ref) | copy-start | bytes 1572868
  3.9 14.2 %copy-start.7 = (bf16[512,512]{1,0:T(8,128)(2,1)S(1)}, bf16[512,512]{1,0:T(8,128)(2,1)}, u32[]{:S(2)}) copy-start(bf16[512,512]{1,0:T(8,128)(2,1)} %constant.19.clone.pick_ref) | copy-start | bytes 1572868
  3.9 49.3 %collective-permute-start.1 = (bf16[2,768,512]{2,1,0:T(8,128)(2,1)}, bf16[2,768,512]{2,1,0:T(8,128)(2,1)}, u32[]{:S(2)}, u32[]{:S(2)}) collective-permute-start(bf16[2,768,512]{2,1,0:T(8,128)(2,1)} %slice.21), channel_id=1, source_target_pairs={{4,0},{8,4},{12,8},{16,12},{20,16},{24,20},{28,24},{32,28},{36,32}... | collective-permute-start | bytes 4718600 | tf_op jit(solution)/shard_map/ppermute | solution.py:25
  10.7 17.0 %collective-permute-start = (bf16[2,512,256]{2,1,0:T(8,128)(2,1)}, bf16[2,512,256]{2,1,0:T(8,128)(2,1)S(1)}, u32[]{:S(2)}, u32[]{:S(2)}) collective-permute-start(bf16[2,512,256]{2,1,0:T(8,128)(2,1)} %get-tuple-element.31), channel_id=1, source_target_pairs={{1,0},{2,1},{3,2},{5,4},{6,5},{7,6},{9,8},{10,9},{11,10},{13,12},{... | collective-permute-start | bytes 1572872 | tf_op jit(solution)/shard_map/ppermute | solution.py:25
  13.1 25.8 %collective-permute-start.2 = (bf16[2,512,256]{2,1,0:T(8,128)(2,1)}, bf16[2,512,256]{2,1,0:T(8,128)(2,1)S(1)}, u32[]{:S(2)}, u32[]{:S(2)}) collective-permute-start(bf16[2,512,256]{2,1,0:T(8,128)(2,1)} %get-tuple-element.30), channel_id=1, source_target_pairs={{1,0},{2,1},{3,2},{5,4},{6,5},{7,6},{9,8},{10,9},{11,10},{13,12},{... | collective-permute-start | bytes 1572872 | tf_op jit(solution)/shard_map/ppermute | solution.py:25
  15.5 30.4 %collective-permute-start.3 = (bf16[2,512,256]{2,1,0:T(8,128)(2,1)S(1)}, bf16[2,512,256]{2,1,0:T(8,128)(2,1)S(1)}, u32[]{:S(2)}, u32[]{:S(2)}) collective-permute-start(bf16[2,512,256]{2,1,0:T(8,128)(2,1)S(1)} %get-tuple-element.29), channel_id=1, source_target_pairs={{1,0},{2,1},{3,2},{5,4},{6,5},{7,6},{9,8},{10,9},{11,10},{13,12},{... | collective-permute-start | bytes 1572872 | tf_op jit(solution)/shard_map/ppermute | solution.py:25
  18.0 1.9 %copy-start.5 = (bf16[1,1,6,512,512]{4,3,2,1,0:T(8,128)(2,1)S(1)}, bf16[1,1,6,512,512]{4,3,2,1,0:T(8,128)(2,1)}, u32[]{:S(2)}) copy-start(bf16[1,1,6,512,512]{4,3,2,1,0:T(8,128)(2,1)} %param.11) | copy-start | bytes 9437188
  19.9 33.2 %copy-start.2 = (bf16[4,256,256]{2,1,0:T(8,128)(2,1)S(1)}, bf16[4,256,256]{2,1,0:T(8,128)(2,1)}, u32[]{:S(2)}) copy-start(bf16[4,256,256]{2,1,0:T(8,128)(2,1)} %constant.22.clone.gb_ref) | copy-start | bytes 1572868
  19.9 33.2 %copy-start.3 = (bf16[4,256,256]{2,1,0:T(8,128)(2,1)S(1)}, bf16[4,256,256]{2,1,0:T(8,128)(2,1)}, u32[]{:S(2)}) copy-start(bf16[4,256,256]{2,1,0:T(8,128)(2,1)} %constant.21.clone.ga_ref) | copy-start | bytes 1572868
  19.9 33.2 %copy-start.4 = (s32[1,1,6,2]{2,3,1,0:T(2,128)S(1)}, s32[1,1,6,2]{2,3,1,0:T(2,128)}, u32[]{:S(2)}) copy-start(s32[1,1,6,2]{2,3,1,0:T(2,128)} %param.12) | copy-start | bytes 148
  24.2 1.7 %copy-start.1 = (bf16[6,512,512]{2,1,0:T(8,128)(2,1)}, bf16[6,512,512]{2,1,0:T(8,128)(2,1)S(1)}, u32[]{:S(2)}) copy-start(bf16[6,512,512]{2,1,0:T(8,128)(2,1)S(1)} %shard_map.91.meas_ref) | copy-start | bytes 9437188
  38.9 8.6 %collective-permute-start.5 = (bf16[2,512,256]{2,1,0:T(8,128)(2,1)S(1)}, bf16[2,512,256]{2,1,0:T(8,128)(2,1)S(1)}, u32[]{:S(2)}, u32[]{:S(2)}) collective-permute-start(bf16[2,512,256]{2,1,0:T(8,128)(2,1)S(1)} %collective-permute-done.2.below1_ref), channel_id=1, source_target_pairs={{4,0},{8,4},{12,8},{16,12},{20,16},{24,20},{28,24},{32,28},{36,32}... | collective-permute-start | bytes 1572872 | tf_op jit(solution)/shard_map/ppermute | solution.py:25
  40.8 12.3 %collective-permute-start.4 = (bf16[2,512,256]{2,1,0:T(8,128)(2,1)S(1)}, bf16[2,512,256]{2,1,0:T(8,128)(2,1)S(1)}, u32[]{:S(2)}, u32[]{:S(2)}) collective-permute-start(bf16[2,512,256]{2,1,0:T(8,128)(2,1)S(1)} %collective-permute-done.below0_ref), channel_id=1, source_target_pairs={{4,0},{8,4},{12,8},{16,12},{20,16},{24,20},{28,24},{32,28},{36,32}... | collective-permute-start | bytes 1572872 | tf_op jit(solution)/shard_map/ppermute | solution.py:25
  93.5 18.9 %copy-start.8 = (bf16[2,768,512]{2,1,0:T(8,128)(2,1)S(1)}, bf16[2,768,512]{2,1,0:T(8,128)(2,1)}, u32[]{:S(2)}) copy-start(bf16[2,768,512]{2,1,0:T(8,128)(2,1)} %get-tuple-element.26) | copy-start | bytes 4718596
  93.5 18.6 %collective-permute-start.6 = (bf16[2,512,512]{2,1,0:T(8,128)(2,1)}, bf16[2,512,512]{2,1,0:T(8,128)(2,1)S(1)}, u32[]{:S(2)}, u32[]{:S(2)}) collective-permute-start(bf16[2,512,512]{2,1,0:T(8,128)(2,1)} %get-tuple-element.23), channel_id=1, source_target_pairs={{0,4},{4,8},{8,12},{12,16},{16,20},{20,24},{24,28},{28,32},{32,36}... | collective-permute-start | bytes 3145736 | tf_op jit(solution)/shard_map/ppermute | solution.py:25
  95.6 16.8 %collective-permute-start.7 = (bf16[2,512,256]{2,1,0:T(8,128)(2,1)S(1)}, bf16[2,512,256]{2,1,0:T(8,128)(2,1)S(1)}, u32[]{:S(2)}, u32[]{:S(2)}) collective-permute-start(bf16[2,512,256]{2,1,0:T(8,128)(2,1)S(1)} %get-tuple-element.25), channel_id=1, source_target_pairs={{0,1},{1,2},{2,3},{4,5},{5,6},{6,7},{8,9},{9,10},{10,11},{12,13},{... | collective-permute-start | bytes 1572872 | tf_op jit(solution)/shard_map/ppermute | solution.py:25
  112.4 23.8 %collective-permute-start.8 = (bf16[2,768,512]{2,1,0:T(8,128)(2,1)S(1)}, bf16[2,768,512]{2,1,0:T(8,128)(2,1)S(1)}, u32[]{:S(2)}, u32[]{:S(2)}) collective-permute-start(bf16[2,768,512]{2,1,0:T(8,128)(2,1)S(1)} %copy-done.8), channel_id=1, source_target_pairs={{0,4},{4,8},{8,12},{12,16},{16,20},{20,24},{24,28},{28,32},{32,36}... | collective-permute-start | bytes 4718600 | tf_op jit(solution)/shard_map/ppermute | solution.py:25
  114.4 28.0 %collective-permute-start.9 = (bf16[2,512,512]{2,1,0:T(8,128)(2,1)S(1)}, bf16[2,512,512]{2,1,0:T(8,128)(2,1)S(1)}, u32[]{:S(2)}, u32[]{:S(2)}) collective-permute-start(bf16[2,512,512]{2,1,0:T(8,128)(2,1)S(1)} %add_convert_fusion), channel_id=1, source_target_pairs={{0,1},{1,2},{2,3},{4,5},{5,6},{6,7},{8,9},{9,10},{10,11},{12,13},{... | collective-permute-start | bytes 3145736 | tf_op jit(solution)/shard_map/ppermute | solution.py:25

commit v3 on v1

--- a/solution.py
+++ b/solution.py
@@ -15,6 +15,8 @@
 E = T + W
 NB = E // Q
 TB = T // Q
+CUTS = (0, 208, 384, 512)
+F = T - W
 R = 16
 f32, bf16 = jnp.float32, jnp.bfloat16
 
@@ -64,105 +66,148 @@
     return pl.ds(b * Q, Q)
 
 
+def each_rows(count, body):
+    def step(i, carry):
+        body(pl.multiple_of(i * R, R))
+        return carry
+
+    lax.fori_loop(0, count // R, step, 0)
+
+
+VMEM = pl.BlockSpec(memory_space=pltpu.VMEM)
+SMEM = pl.BlockSpec(memory_space=pltpu.SMEM)
+ANY = pl.BlockSpec(memory_space=pl.ANY)
+TILES = jax.ShapeDtypeStruct((2, NB, E, Q), f32)
+
+
+def params(mib):
+    return pltpu.CompilerParams(vmem_limit_bytes=mib * 2**20)
+
+
+def cost():
+    return pl.CostEstimate(flops=1024, bytes_accessed=1024, transcendentals=0)
+
+
+def pack_kernel(slab_ref, *refs):
+    count = len(CUTS) - 1
+    below, right_ref, buf, sem = refs[:count], *refs[count:]
+    cuts = (*CUTS, T)
+
+    def copy(c):
+        rows = pl.ds(cuts[c], cuts[c + 1] - cuts[c])
+        return pltpu.make_async_copy(slab_ref.at[:, rows, :], buf.at[:, rows, :], sem.at[c])
+
+    for c in range(count + 1):
+        copy(c).start()
+    for c in range(count + 1):
+        copy(c).wait()
+
+        def convert(row):
+            here = pl.ds(pl.multiple_of(cuts[c] + row, R), R)
+            for p in range(2):
+                part = buf[p, here, :].astype(bf16)
+                right_ref[p, here, :] = part[:, :W]
+                if c < count:
+                    below[c][p, pl.ds(row, R), :] = part
+
+        each_rows(cuts[c + 1] - cuts[c], convert)
+
+
+def pack(slab):
+    rows = [high - low for low, high in zip(CUTS[:-1], CUTS[1:])]
+    shapes = [(2, r, T) for r in rows] + [(2, T, W)]
+    made = pl.pallas_call(
+        pack_kernel,
+        in_specs=[ANY],
+        out_specs=[VMEM] * len(shapes),
+        out_shape=[jax.ShapeDtypeStruct(shape, bf16) for shape in shapes],
+        scratch_shapes=[pltpu.VMEM((2, T, T), f32), pltpu.SemaphoreType.DMA((len(CUTS),))],
+        cost_estimate=cost(),
+        compiler_params=params(24),
+    )(slab)
+    return made[:-1], made[-1]
+
+
 def sort_kernel(pick_ref, pick_t_ref, in_ref, out_ref):
     rows = jnp.dot(pick_ref[...], in_ref[0], preferred_element_type=f32).astype(bf16)
     out_ref[0] = jnp.dot(rows, pick_t_ref[...], preferred_element_type=f32).astype(bf16)
 
 
 def sort_intensities(measured, pick):
-    slots = measured.shape[0]
     whole = pl.BlockSpec((W, W), lambda s: (0, 0))
     each = pl.BlockSpec((1, W, W), lambda s: (s, 0, 0))
     return pl.pallas_call(
         sort_kernel,
-        grid=(slots,),
+        grid=(measured.shape[0],),
         in_specs=[whole, whole, each],
         out_specs=each,
         out_shape=jax.ShapeDtypeStruct(measured.shape, bf16),
-        cost_estimate=pl.CostEstimate(
-            flops=slots * 4 * W**3, bytes_accessed=slots * 4 * W * W, transcendentals=0
-        ),
-        compiler_params=pltpu.CompilerParams(vmem_limit_bytes=16 * 2**20),
+        cost_estimate=cost(),
+        compiler_params=params(16),
     )(jnp.asarray(pick), jnp.asarray(pick.T.copy()), measured)
 
 
-def main_kernel(
-    live_ref,
-    shift_ref,
-    slab_ref,
-    right_ref,
+def slots_kernel(
+    chunk,
+    meta_ref,
     below_ref,
     corner_ref,
     probe_ref,
     meas_ref,
     ga_ref,
     gb_ref,
-    local_ref,
-    spill_right_ref,
-    spill_below_ref,
-    spill_corner_ref,
+    first_ref,
+    second_ref,
     ext,
     grown,
     half16,
     full32,
     mid,
     out,
-    in_sem,
-    out_sem,
+    sem,
 ):
-    def slab_copy(p, b):
+    def copy(p, b):
         return pltpu.make_async_copy(
-            slab_ref.at[p, :, lanes(b)], ext.at[p, b, pl.ds(0, T), :], in_sem.at[p, b]
+            first_ref.at[p, :, lanes(b)], ext.at[p, b, pl.ds(0, T), :], sem.at[p, b]
         )
 
-    def local_copy(p, b):
-        return pltpu.make_async_copy(
-            grown.at[p, b, pl.ds(0, T), :], local_ref.at[p, :, lanes(b)], out_sem.at[p, b]
-        )
-
-    for p in range(2):
-        for b in range(TB):
-            slab_copy(p, b).start()
-
-    def clear(i, carry):
-        rows = pl.ds(pl.multiple_of(i * R, R), R)
+    def clear(row):
         for p in range(2):
             for b in range(NB):
-                grown[p, b, rows, :] = jnp.zeros((R, Q), f32)
-        return carry
-
-    lax.fori_loop(0, E // R, clear, 0)
-
-    def fill_right(i, carry):
-        rows = pl.ds(pl.multiple_of(i * R, R), R)
-        for p in range(2):
-            for b in range(4):
-                ext[p, TB + b, rows, :] = right_ref[p, rows, lanes(b)].astype(f32)
-        return carry
-
-    lax.fori_loop(0, T // R, fill_right, 0)
-
-    def fill_below(i, carry):
-        rows = pl.ds(pl.multiple_of(i * R, R), R)
-        there = pl.ds(pl.multiple_of(T + i * R, R), R)
+                grown[p, b, pl.ds(row, R), :] = jnp.zeros((R, Q), f32)
+
+    def fill_right(row):
+        for p in range(2):
+            for b in range(4):
+                ext[p, TB + b, pl.ds(row, R), :] = second_ref[p, pl.ds(row, R), lanes(b)].astype(f32)
+
+    if chunk == 0:
+        for p in range(2):
+            for b in range(TB):
+                copy(p, b).start()
+        each_rows(E, clear)
+        each_rows(T, fill_right)
+
+    def fill(row):
+        rows = pl.ds(row, R)
+        there = pl.ds(pl.multiple_of(T + CUTS[chunk] + row, R), R)
         for p in range(2):
             for b in range(TB):
                 ext[p, b, there, :] = below_ref[p, rows, lanes(b)].astype(f32)
             for b in range(4):
                 ext[p, TB + b, there, :] = corner_ref[p, rows, lanes(b)].astype(f32)
-        return carry
-
-    lax.fori_loop(0, W // R, fill_below, 0)
-
-    for p in range(2):
-        for b in range(TB):
-            slab_copy(p, b).wait()
+
+    each_rows(CUTS[chunk + 1] - CUTS[chunk], fill)
+    if chunk == 0:
+        for p in range(2):
+            for b in range(TB):
+                copy(p, b).wait()
 
     lane = lax.broadcasted_iota(jnp.int32, (R, Q), 1)
 
     def one_slot(slot, carry):
-        row0 = shift_ref[slot, 0]
-        col0 = shift_ref[slot, 1]
+        row0 = meta_ref[0, slot]
+        col0 = meta_ref[1, slot]
         block0 = col0 // Q
         by = col0 % Q
         inner = lane < Q - by
@@ -261,111 +306,182 @@
         lax.fori_loop(0, Q // R, add, 0)
         return carry
 
-    lax.fori_loop(0, live_ref[0], one_slot, 0)
-
-    for p in range(2):
-        for b in range(TB):
-            local_copy(p, b).start()
-
-    def drain_right(i, carry):
-        rows = pl.ds(pl.multiple_of(i * R, R), R)
-        for p in range(2):
-            for b in range(4):
-                spill_right_ref[p, rows, lanes(b)] = grown[p, TB + b, rows, :].astype(bf16)
+    def maybe(slot, carry):
+        @pl.when(meta_ref[2, slot] == chunk)
+        def _():
+            one_slot(slot, 0)
+
         return carry
 
-    lax.fori_loop(0, T // R, drain_right, 0)
-
-    def drain_below(i, carry):
-        rows = pl.ds(pl.multiple_of(i * R, R), R)
-        here = pl.ds(pl.multiple_of(T + i * R, R), R)
-        for p in range(2):
-            for b in range(TB):
-                spill_below_ref[p, rows, lanes(b)] = grown[p, b, here, :].astype(bf16)
-            for b in range(4):
-                spill_corner_ref[p, rows, lanes(b)] = grown[p, TB + b, here, :].astype(bf16)
-        return carry
-
-    lax.fori_loop(0, W // R, drain_below, 0)
-    for p in range(2):
-        for b in range(TB):
-            local_copy(p, b).wait()
-
-
-def solve(live, shifts, slab, right, below, corner, probe, measured, left, left_t):
-    vmem = pl.BlockSpec(memory_space=pltpu.VMEM)
-    smem = pl.BlockSpec(memory_space=pltpu.SMEM)
-    anywhere = pl.BlockSpec(memory_space=pl.ANY)
+    lax.fori_loop(0, meta_ref.shape[1], maybe, 0)
+
+
+def solve(chunk, meta, below, corner, probe, measured, left, left_t, first, second):
     return pl.pallas_call(
-        main_kernel,
-        in_specs=[smem, smem, anywhere] + [vmem] * 7,
-        out_specs=[anywhere, vmem, vmem, vmem],
-        out_shape=[
-            jax.ShapeDtypeStruct((2, T, T), f32),
-            jax.ShapeDtypeStruct((2, T, W), bf16),
-            jax.ShapeDtypeStruct((2, W, T), bf16),
-            jax.ShapeDtypeStruct((2, W, W), bf16),
-        ],
+        functools.partial(slots_kernel, chunk),
+        in_specs=[SMEM] + [VMEM] * 6 + [ANY if chunk == 0 else VMEM, VMEM],
+        out_specs=[VMEM, VMEM],
+        out_shape=[TILES, TILES],
+        input_output_aliases={7: 0, 8: 1} if chunk else {},
         scratch_shapes=[
-            pltpu.VMEM((2, NB, E, Q), f32),
-            pltpu.VMEM((2, NB, E, Q), f32),
             pltpu.VMEM((4, 2 * Q, W), bf16),
             pltpu.VMEM((4, 2 * Q, W), f32),
             pltpu.VMEM((4, W, 2 * Q), bf16),
             pltpu.VMEM((4, W, 2 * Q), f32),
             pltpu.SemaphoreType.DMA((2, TB)),
-            pltpu.SemaphoreType.DMA((2, TB)),
         ],
-        cost_estimate=pl.CostEstimate(
-            flops=6 * 2 * W**3, bytes_accessed=20 * 2**20, transcendentals=0
-        ),
-        compiler_params=pltpu.CompilerParams(vmem_limit_bytes=56 * 2**20),
-    )(live, shifts, slab, right, below, corner, probe, measured, left, left_t)
-
-
-def finish_kernel(local_ref, right_ref, below_ref, out_ref):
-    out_ref[...] = local_ref[...]
-    out_ref[:, :, :W] += right_ref[...].astype(f32)
-
-    @pl.when(pl.program_id(0) < W // Q)
-    def _():
-        out_ref[...] += below_ref[...].astype(f32)
-
-
-def finish(local, right, below):
+        cost_estimate=cost(),
+        compiler_params=params(12),
+    )(meta, below, corner, probe, measured, left, left_t, first, second)
+
+
+def drain_kernel(grown, near_ref, far_ref, corner_ref, right_ref):
+    def below(row):
+        rows = pl.ds(row, R)
+        here = pl.ds(pl.multiple_of(T + row, R), R)
+        for p in range(2):
+            for b in range(4):
+                near_ref[p, rows, lanes(b)] = grown[p, b, here, :].astype(bf16)
+                corner_ref[p, rows, lanes(b)] = grown[p, TB + b, here, :].astype(bf16)
+            for b in range(2):
+                far_ref[p, rows, lanes(b)] = grown[p, 4 + b, here, :].astype(bf16)
+
+    def right(row):
+        rows = pl.ds(row, R)
+        for p in range(2):
+            for b in range(4):
+                right_ref[p, rows, lanes(b)] = grown[p, TB + b, rows, :].astype(bf16)
+
+    each_rows(W, below)
+    each_rows(T, right)
+
+
+def drain(grown):
     return pl.pallas_call(
-        finish_kernel,
-        grid=(TB,),
-        in_specs=[
-            pl.BlockSpec((2, Q, T), lambda i: (0, i, 0)),
-            pl.BlockSpec((2, Q, W), lambda i: (0, i, 0)),
-            pl.BlockSpec((2, Q, T), lambda i: (0, jnp.minimum(i, W // Q - 1), 0)),
+        drain_kernel,
+        in_specs=[VMEM],
+        out_specs=[VMEM] * 4,
+        out_shape=[
+            jax.ShapeDtypeStruct((2, W, W), bf16),
+            jax.ShapeDtypeStruct((2, W, F), bf16),
+            jax.ShapeDtypeStruct((2, W, W), bf16),
+            jax.ShapeDtypeStruct((2, T, W), bf16),
         ],
-        out_specs=pl.BlockSpec((2, Q, T), lambda i: (0, i, 0)),
-        out_shape=jax.ShapeDtypeStruct((2, T, T), f32),
-        compiler_params=pltpu.CompilerParams(vmem_limit_bytes=24 * 2**20),
-    )(local, right, below)
+        cost_estimate=cost(),
+        compiler_params=params(4),
+    )(grown)
+
+
+def write_copy(tile, whole_ref, sem, p, b, first, count):
+    rows = pl.ds(first, count)
+    return pltpu.make_async_copy(
+        tile.at[p, b, rows, :], whole_ref.at[p, rows, lanes(b)], sem.at[p, b]
+    )
+
+
+def side_kernel(right_ref, far_ref, grown_in, grown, whole_ref, sem):
+    def done(p, b):
+        if b < 4:
+            return write_copy(grown, whole_ref, sem, p, b, W, T - W)
+        return write_copy(grown, whole_ref, sem, p, b, 0, T)
+
+    def far(row):
+        rows = pl.ds(row, R)
+        for p in range(2):
+            for b in range(2):
+                grown[p, 4 + b, rows, :] += far_ref[p, rows, lanes(b)].astype(f32)
+
+    each_rows(W, far)
+    for p in range(2):
+        for b in range(4, TB):
+            done(p, b).start()
+
+    def right(row):
+        rows = pl.ds(row, R)
+        for p in range(2):
+            for b in range(4):
+                grown[p, b, rows, :] += right_ref[p, rows, lanes(b)].astype(f32)
+
+    each_rows(T, right)
+    for p in range(2):
+        for b in range(4):
+            done(p, b).start()
+    for p in range(2):
+        for b in range(TB):
+            done(p, b).wait()
+
+
+def add_side(right, far, grown):
+    return pl.pallas_call(
+        side_kernel,
+        in_specs=[VMEM] * 3,
+        out_specs=[VMEM, ANY],
+        out_shape=[TILES, jax.ShapeDtypeStruct((2, T, T), f32)],
+        input_output_aliases={2: 0},
+        scratch_shapes=[pltpu.SemaphoreType.DMA((2, TB))],
+        cost_estimate=cost(),
+        compiler_params=params(4),
+    )(right, far, grown)
+
+
+def last_kernel(near_ref, grown_in, whole_in, grown, whole_ref, sem):
+    for b in range(4):
+        for p in range(2):
+
+            def add(row):
+                rows = pl.ds(row, R)
+                grown[p, b, rows, :] += near_ref[p, rows, lanes(b)].astype(f32)
+
+            each_rows(W, add)
+            write_copy(grown, whole_ref, sem, p, b, 0, W).start()
+    for b in range(4):
+        for p in range(2):
+            write_copy(grown, whole_ref, sem, p, b, 0, W).wait()
+
+
+def add_near(near, grown, whole):
+    return pl.pallas_call(
+        last_kernel,
+        in_specs=[VMEM, VMEM, ANY],
+        out_specs=[VMEM, ANY],
+        out_shape=[TILES, jax.ShapeDtypeStruct((2, T, T), f32)],
+        input_output_aliases={1: 0, 2: 1},
+        scratch_shapes=[pltpu.SemaphoreType.DMA((2, 4))],
+        cost_estimate=cost(),
+        compiler_params=params(4),
+    )(near, grown, whole)[1]
 
 
 def shards(slab, probe, intensities, offsets, live_count):
     left, left_t, pick = tables()
-    send_below = slab[:, :W, :].astype(bf16)
-    send_right = slab[:, :, :W].astype(bf16)
-    below = shifted(send_below, "tile", -1)
+    left, left_t = jnp.asarray(left), jnp.asarray(left_t)
+    chunks = range(len(CUTS) - 1)
+    send_below, send_right = pack(slab)
+    below = [shifted(part, "tile", -1) for part in send_below]
     right = shifted(send_right, "scan", -1)
-    corner = shifted(below[:, :, :W], "scan", -1)
+    live = lax.dynamic_slice(live_count[:, 0], (lax.axis_index("scan"),), (1,))
+    shifts = offsets[0, 0].T
+    reach = shifts[0] + (W - T)
+    stage = sum((reach > CUTS[c + 1]).astype(jnp.int32) for c in chunks)
+    stage = jnp.where(jnp.arange(shifts.shape[1], dtype=jnp.int32) < live, stage, len(CUTS))
+    meta = jnp.concatenate([shifts, stage[None]], axis=0)
     measured = sort_intensities(intensities[0, 0], pick)
-    live = lax.dynamic_slice(live_count[:, 0], (lax.axis_index("scan"),), (1,))
-    local, to_right, to_below, to_corner = solve(
-        live, offsets[0, 0], slab, right, below, corner, probe, measured,
-        jnp.asarray(left), jnp.asarray(left_t),
-    )
+    below[0], measured, meta = lax.optimization_barrier((below[0], measured, meta))
+    corner = [shifted(part[:, :, :W], "scan", -1) for part in below]
+    ext, grown = slab, right
+    for c in chunks:
+        ext, grown = solve(
+            c, meta, below[c], corner[c], probe, measured, left, left_t, ext, grown
+        )
+    to_near, to_far, to_corner, to_right = drain(grown)
+    to_far = shifted(to_far, "tile", 1)
+    from_corner = shifted(to_corner, "scan", 1)
+    to_near = (to_near.astype(f32) + from_corner.astype(f32)).astype(bf16)
+    to_near, to_far = lax.optimization_barrier((to_near, to_far))
+    to_near = shifted(to_near, "tile", 1)
     from_left = shifted(to_right, "scan", 1)
-    from_corner = shifted(to_corner, "scan", 1)
-    far_half = shifted(to_below[:, :, W:], "tile", 1)
-    near = (to_below[:, :, :W].astype(f32) + from_corner.astype(f32)).astype(bf16)
-    near_half = shifted(near, "tile", 1)
-    return finish(local, from_left, jnp.concatenate([near_half, far_half], axis=2))
+    grown, whole = add_side(from_left, to_far, grown)
+    return add_near(to_near, grown, whole)
 
 
 def solution(mesh):

time: 161 us -> 141 us (0.88)
  the two profiles are of different devices: /device:TPU:22 before, /device:TPU:12 now
where the time goes in v3:
time: 141 us; the launch traced here: 139 us
  Pallas kernels  49.3 us (35%)
  waiting for transfers between devices  48.9 us (35%)
  starting transfers between devices  28.3 us (20%)
  local copies, waits for them, and re-layouts  11.1 us (8%)
    ppermute x11, waiting for transfers between devices, shifted(): lax.ppermute(value, axis, [(i, i + by) for i in range(n) if 0 <= i + by <...  48.9 us
    pallas_call x3, Pallas kernels, solve(): pl.pallas_call(functools.partial(slots_kernel, chunk), in_specs=[SMEM] +...  37.2 us
    ppermute x11, starting transfers between devices, shifted(): lax.ppermute(value, axis, [(i, i + by) for i in range(n) if 0 <= i + by <...  28.3 us
    unnamed x20, local copies, waits for them, and re-layouts  8.38 us
    pallas_call x1, Pallas kernels, sort_intensities(): pl.pallas_call(sort_kernel, grid=(measured.shape[0],), in_specs=[whole, w...  4.32 us
  transfers between devices with their start and end apart: 11, of which 6 were waited for; matrix products, arithmetic and copies ran while one was open for 3% of the time, Pallas kernels for 23%

profile of v3, /device:TPU:12, one launch (start us, length us, event | category | flops | bytes accessed | tf_op | source)
XLA Modules:
  0.0 138.9 jit_solution(10881374371804153039)
XLA Ops:
  0.0 2.3 %copy-done.2 = f32[2,768,768]{2,1,0:T(8,128)S(1)} copy-done((f32[2,768,768]{2,1,0:T(8,128)S(1)}, f32[2,768,768]{2,1,0:T(8,128)}, u32[]{:S(2)}) %copy-start.2) | copy-done | bytes 4718616
  2.4 2.6 %shard_map.91 = (bf16[2,208,768]{2,1,0:T(8,128)(2,1)}, bf16[2,176,768]{2,1,0:T(8,128)(2,1)}, bf16[2,128,768]{2,1,0:T(8,128)(2,1)}, bf16[2,768,512]{2,1,0:T(8,128)(2,1)}) custom-call(f32[2,768,768]{2,1,0:T(8,128)S(1)} %copy-done.2), custom_call_target="tpu_custom_call" | custom-call | flops 1024 | bytes 1024 | tf_op jit(solution)/shard_map/pallas_call | solution.py:119
  5.0 5.4 %collective-permute-start.6 = (bf16[2,768,512]{2,1,0:T(8,128)(2,1)}, bf16[2,768,512]{2,1,0:T(8,128)(2,1)}, u32[]{:S(2)}, u32[]{:S(2)}) collective-permute-start(bf16[2,768,512]{2,1,0:T(8,128)(2,1)} %get-tuple-element.32), channel_id=1, source_target_pairs={{4,0},{8,4},{12,8},{16,12},{20,16},{24,20},{28,24},{32,28},{36,32}... | collective-permute-start | bytes 4718600 | tf_op jit(solution)/shard_map/ppermute | solution.py:26
  10.4 2.4 %collective-permute-start = (bf16[2,208,768]{2,1,0:T(8,128)(2,1)}, bf16[2,208,768]{2,1,0:T(8,128)(2,1)}, u32[]{:S(2)}, u32[]{:S(2)}) collective-permute-start(bf16[2,208,768]{2,1,0:T(8,128)(2,1)} %get-tuple-element.26), channel_id=1, source_target_pairs={{1,0},{2,1},{3,2},{5,4},{6,5},{7,6},{9,8},{10,9},{11,10},{13,12},{... | collective-permute-start | bytes 1916936 | tf_op jit(solution)/shard_map/ppermute | solution.py:26
  12.7 1.9 %collective-permute-start.3 = (bf16[2,176,768]{2,1,0:T(8,128)(2,1)}, bf16[2,176,768]{2,1,0:T(8,128)(2,1)}, u32[]{:S(2)}, u32[]{:S(2)}) collective-permute-start(bf16[2,176,768]{2,1,0:T(8,128)(2,1)} %get-tuple-element.30), channel_id=1, source_target_pairs={{1,0},{2,1},{3,2},{5,4},{6,5},{7,6},{9,8},{10,9},{11,10},{13,12},{... | collective-permute-start | bytes 1622024 | tf_op jit(solution)/shard_map/ppermute | solution.py:26
  14.7 1.9 %collective-permute-start.1 = (bf16[2,128,768]{2,1,0:T(8,128)(2,1)}, bf16[2,128,768]{2,1,0:T(8,128)(2,1)S(1)}, u32[]{:S(2)}, u32[]{:S(2)}) collective-permute-start(bf16[2,128,768]{2,1,0:T(8,128)(2,1)} %get-tuple-element.28), channel_id=1, source_target_pairs={{1,0},{2,1},{3,2},{5,4},{6,5},{7,6},{9,8},{10,9},{11,10},{13,12},{... | collective-permute-start | bytes 1179656 | tf_op jit(solution)/shard_map/ppermute | solution.py:26
  16.6 4.3 %shard_map.92.meas_ref = bf16[6,512,512]{2,1,0:T(8,128)(2,1)S(1)} custom-call(bf16[512,512]{1,0:T(8,128)(2,1)S(1)} %copy-done.7, bf16[512,512]{1,0:T(8,128)(2,1)S(1)} %copy-done.8, bf16[6,512,512]{2,1,0:T(8,128)(2,1)S(1)} %bitcast.5), custom_call_target="tpu_custom_call" | custom-call | flops 1024 | bytes 1024 | tf_op jit(solution)/shard_map/pallas_call | solution.py:139
  22.3 7.6 %collective-permute-done.below_ref = bf16[2,208,768]{2,1,0:T(8,128)(2,1)} collective-permute-done((bf16[2,208,768]{2,1,0:T(8,128)(2,1)}, bf16[2,208,768]{2,1,0:T(8,128)(2,1)}, u32[]{:S(2)}, u32[]{:S(2)}) %collective-permute-start) | collective-permute-done | bytes 639008 | tf_op jit(solution)/shard_map/ppermute | solution.py:26
  29.9 1.0 slice.15
  30.9 1.9 %collective-permute-start.5 = (bf16[2,208,512]{2,1,0:T(8,128)(2,1)S(1)}, bf16[2,208,512]{2,1,0:T(8,128)(2,1)S(1)}, u32[]{:S(2)}, u32[]{:S(2)}) collective-permute-start(bf16[2,208,512]{2,1,0:T(8,128)(2,1)S(1)} %slice.15), channel_id=1, source_target_pairs={{4,0},{8,4},{12,8},{16,12},{20,16},{24,20},{28,24},{32,28},{36,32}... | collective-permute-start | bytes 1277960 | tf_op jit(solution)/shard_map/ppermute | solution.py:26
  32.9 8.6 %collective-permute-done.3.below_ref = bf16[2,176,768]{2,1,0:T(8,128)(2,1)} collective-permute-done((bf16[2,176,768]{2,1,0:T(8,128)(2,1)}, bf16[2,176,768]{2,1,0:T(8,128)(2,1)}, u32[]{:S(2)}, u32[]{:S(2)}) %collective-permute-start.3) | collective-permute-done | bytes 540704 | tf_op jit(solution)/shard_map/ppermute | solution.py:26
  41.5 1.0 slice.17
  42.5 1.9 %collective-permute-start.4 = (bf16[2,176,512]{2,1,0:T(8,128)(2,1)S(1)}, bf16[2,176,512]{2,1,0:T(8,128)(2,1)S(1)}, u32[]{:S(2)}, u32[]{:S(2)}) collective-permute-start(bf16[2,176,512]{2,1,0:T(8,128)(2,1)S(1)} %slice.17), channel_id=1, source_target_pairs={{4,0},{8,4},{12,8},{16,12},{20,16},{24,20},{28,24},{32,28},{36,32}... | collective-permute-start | bytes 1081352 | tf_op jit(solution)/shard_map/ppermute | solution.py:26
  44.4 1.4 %collective-permute-done.1.below_ref = bf16[2,128,768]{2,1,0:T(8,128)(2,1)S(1)} collective-permute-done((bf16[2,128,768]{2,1,0:T(8,128)(2,1)}, bf16[2,128,768]{2,1,0:T(8,128)(2,1)S(1)}, u32[]{:S(2)}, u32[]{:S(2)}) %collective-permute-start.1) | collective-permute-done | bytes 393248 | tf_op jit(solution)/shard_map/ppermute | solution.py:26
  45.9 5.2 %collective-permute-start.2 = (bf16[2,128,512]{2,1,0:T(8,128)(2,1)S(1)}, bf16[2,128,512]{2,1,0:T(8,128)(2,1)S(1)}, u32[]{:S(2)}, u32[]{:S(2)}) collective-permute-start(bf16[2,128,512]{2,1,0:T(8,128)(2,1)S(1)} %slice.16), channel_id=1, source_target_pairs={{4,0},{8,4},{12,8},{16,12},{20,16},{24,20},{28,24},{32,28},{36,32}... | collective-permute-start | bytes 786440 | tf_op jit(solution)/shard_map/ppermute | solution.py:26
  51.1 1.6 %copy-done.1 = f32[2,512,512]{2,1,0:T(8,128)S(1)} copy-done((f32[2,512,512]{2,1,0:T(8,128)S(1)}, f32[2,512,512]{2,1,0:T(8,128)}, u32[]{:S(2)}) %copy-start.1) | copy-done | bytes 2097176
  52.7 2.3 %copy-done.3 = f32[2,768,768]{2,1,0:T(8,128)S(1)} copy-done((f32[2,768,768]{2,1,0:T(8,128)S(1)}, f32[2,768,768]{2,1,0:T(8,128)}, u32[]{:S(2)}) %copy-start.3) | copy-done | bytes 4718616
  55.1 1.0 copy-done.4
  56.1 1.0 copy-done.5
  57.1 19.3 %shard_map.93 = (f32[2,10,1280,128]{3,2,1,0:T(8,128)S(1)}, f32[2,10,1280,128]{3,2,1,0:T(8,128)S(1)}) custom-call(s32[3,6]{1,0:T(4,128)S(1)} %pad_add_fusion.meta_ref, bf16[2,208,768]{2,1,0:T(8,128)(2,1)} %collective-permute-done.below_ref, bf16[2,208,512]{2,1,0:T(8,128)(2,1)S(1)} %collective-permute-done.5.corner_ref, f32[2,512,512]{2,1,0:T(8,128)S(1)} %copy-done.1, ...), custom_call_target="tpu_custom_call" | custom-call | flops 1024 | bytes 1024 | tf_op jit(solution)/shard_map/pallas_call | solution.py:320
  76.5 6.6 %shard_map.94 = (f32[2,10,1280,128]{3,2,1,0:T(8,128)S(1)}, f32[2,10,1280,128]{3,2,1,0:T(8,128)S(1)}) custom-call(s32[3,6]{1,0:T(4,128)S(1)} %pad_add_fusion.meta_ref, bf16[2,176,768]{2,1,0:T(8,128)(2,1)} %collective-permute-done.3.below_ref, ...), custom_call_target="tpu_custom_call", output_to_operand_aliasing={{0}: (7, {}), {1}: (8, {})} | custom-call | flops 1024 | bytes 1024 | tf_op jit(solution)/shard_map/pallas_call | solution.py:320
  83.1 11.3 %shard_map.95 = (f32[2,10,1280,128]{3,2,1,0:T(8,128)S(1)}, f32[2,10,1280,128]{3,2,1,0:T(8,128)S(1)}) custom-call(s32[3,6]{1,0:T(4,128)S(1)} %pad_add_fusion.meta_ref, bf16[2,128,768]{2,1,0:T(8,128)(2,1)S(1)} %collective-permute-done.1.below_ref, ...), custom_call_target="tpu_custom_call", output_to_operand_aliasing={{0}: (7, {}), {1}: (8, {})} | custom-call | flops 1024 | bytes 1024 | tf_op jit(solution)/shard_map/pallas_call | solution.py:320
  94.4 0.9 shard_map.96
  95.4 1.9 %collective-permute-start.7 = (bf16[2,512,512]{2,1,0:T(8,128)(2,1)S(1)}, bf16[2,512,512]{2,1,0:T(8,128)(2,1)S(1)}, u32[]{:S(2)}, u32[]{:S(2)}) collective-permute-start(bf16[2,512,512]{2,1,0:T(8,128)(2,1)S(1)} %get-tuple-element.39), channel_id=1, source_target_pairs={{0,4},{4,8},{8,12},{12,16},{16,20},{20,24},{24,28},{28,32},{32,36}... | collective-permute-start | bytes 3145736 | tf_op jit(solution)/shard_map/ppermute | solution.py:26
  97.3 1.9 %collective-permute-start.8 = (bf16[2,512,256]{2,1,0:T(8,128)(2,1)S(1)}, bf16[2,512,256]{2,1,0:T(8,128)(2,1)S(1)}, u32[]{:S(2)}, u32[]{:S(2)}) collective-permute-start(bf16[2,512,256]{2,1,0:T(8,128)(2,1)S(1)} %get-tuple-element.40), channel_id=1, source_target_pairs={{0,1},{1,2},{2,3},{4,5},{5,6},{6,7},{8,9},{9,10},{10,11},{12,13},{... | collective-permute-start | bytes 1572872 | tf_op jit(solution)/shard_map/ppermute | solution.py:26
  99.2 1.9 %collective-permute-start.10 = (bf16[2,768,512]{2,1,0:T(8,128)(2,1)S(1)}, bf16[2,768,512]{2,1,0:T(8,128)(2,1)S(1)}, u32[]{:S(2)}, u32[]{:S(2)}) collective-permute-start(bf16[2,768,512]{2,1,0:T(8,128)(2,1)S(1)} %get-tuple-element.42), channel_id=1, source_target_pairs={{0,4},{4,8},{8,12},{12,16},{16,20},{20,24},{24,28},{28,32},{32,36}... | collective-permute-start | bytes 4718600 | tf_op jit(solution)/shard_map/ppermute | solution.py:26
  101.2 12.4 %collective-permute-done.7 = bf16[2,512,512]{2,1,0:T(8,128)(2,1)S(1)} collective-permute-done((bf16[2,512,512]{2,1,0:T(8,128)(2,1)S(1)}, bf16[2,512,512]{2,1,0:T(8,128)(2,1)S(1)}, u32[]{:S(2)}, u32[]{:S(2)}) %collective-permute-start.7) | collective-permute-done | bytes 1048608 | tf_op jit(solution)/shard_map/ppermute | solution.py:26
  113.9 1.9 %collective-permute-start.9 = (bf16[2,512,512]{2,1,0:T(8,128)(2,1)S(1)}, bf16[2,512,512]{2,1,0:T(8,128)(2,1)S(1)}, u32[]{:S(2)}, u32[]{:S(2)}) collective-permute-start(bf16[2,512,512]{2,1,0:T(8,128)(2,1)S(1)} %add_convert_fusion), channel_id=1, source_target_pairs={{0,1},{1,2},{2,3},{4,5},{5,6},{6,7},{8,9},{9,10},{10,11},{12,13},{... | collective-permute-start | bytes 3145736 | tf_op jit(solution)/shard_map/ppermute | solution.py:26
  115.8 14.6 %collective-permute-done.10.right_ref = bf16[2,768,512]{2,1,0:T(8,128)(2,1)S(1)} collective-permute-done((bf16[2,768,512]{2,1,0:T(8,128)(2,1)S(1)}, bf16[2,768,512]{2,1,0:T(8,128)(2,1)S(1)}, u32[]{:S(2)}, u32[]{:S(2)}) %collective-permute-start.10) | collective-permute-done | bytes 1572896 | tf_op jit(solution)/shard_map/ppermute | solution.py:26
  130.5 1.8 %shard_map.97 = (f32[2,10,1280,128]{3,2,1,0:T(8,128)S(1)}, f32[2,768,768]{2,1,0:T(8,128)}) custom-call(bf16[2,768,512]{2,1,0:T(8,128)(2,1)S(1)} %collective-permute-done.10.right_ref, bf16[2,512,256]{2,1,0:T(8,128)(2,1)S(1)} %collective-permute-done.8.far_ref, f32[2,10,1280,128]{3,2,1,0:T(8,128)S(1)} %get-tuple-element.37.grown.grown_in), custom_call_target="tpu_custom_call", output_to_operand_aliasing={{0}: (2, {})} | custom-call | flops 1024 | bytes 1024 | tf_op jit(solution)/shard_map/pallas_call | solution.py:415
  132.3 4.2 %collective-permute-done.9.near_ref = bf16[2,512,512]{2,1,0:T(8,128)(2,1)S(1)} collective-permute-done((bf16[2,512,512]{2,1,0:T(8,128)(2,1)S(1)}, bf16[2,512,512]{2,1,0:T(8,128)(2,1)S(1)}, u32[]{:S(2)}, u32[]{:S(2)}) %collective-permute-start.9) | collective-permute-done | bytes 1048608 | tf_op jit(solution)/shard_map/ppermute | solution.py:26
  136.5 2.4 %shard_map.98 = (f32[2,10,1280,128]{3,2,1,0:T(8,128)S(1)}, f32[2,768,768]{2,1,0:T(8,128)}) custom-call(bf16[2,512,512]{2,1,0:T(8,128)(2,1)S(1)} %collective-permute-done.9.near_ref, f32[2,10,1280,128]{3,2,1,0:T(8,128)S(1)} %get-tuple-element.44.grown_in, f32[2,768,768]{2,1,0:T(8,128)} %get-tuple-element.45.whole_in), custom_call_target="tpu_custom_call", output_to_operand_aliasing={{0}: (1, {}), {1}: (2, {})} | custom-call | flops 1024 | bytes 1024 | tf_op jit(solution)/shard_map/pallas_call | solution.py:443
  (25 shorter events, 1.6 us)
Async XLA Ops:
  0.0 21.0 %copy-start = (s32[32,1]{0,1:T(1,128)S(1)}, s32[32,1]{0,1:T(1,128)}, u32[]{:S(2)}) copy-start(s32[32,1]{0,1:T(1,128)} %param.13) | copy-start | bytes 388
  0.0 2.4 %copy-start.2 = (f32[2,768,768]{2,1,0:T(8,128)S(1)}, f32[2,768,768]{2,1,0:T(8,128)}, u32[]{:S(2)}) copy-start(f32[2,768,768]{2,1,0:T(8,128)} %first_ref.1) | copy-start | bytes 14155780
  2.4 14.2 %copy-start.6 = (bf16[1,1,6,512,512]{4,3,2,1,0:T(8,128)(2,1)S(1)}, bf16[1,1,6,512,512]{4,3,2,1,0:T(8,128)(2,1)}, u32[]{:S(2)}) copy-start(bf16[1,1,6,512,512]{4,3,2,1,0:T(8,128)(2,1)} %param.11) | copy-start | bytes 9437188
  2.4 14.3 %copy-start.7 = (bf16[512,512]{1,0:T(8,128)(2,1)S(1)}, bf16[512,512]{1,0:T(8,128)(2,1)}, u32[]{:S(2)}) copy-start(bf16[512,512]{1,0:T(8,128)(2,1)} %constant.31.clone.pick_ref) | copy-start | bytes 1572868
  2.4 14.3 %copy-start.8 = (bf16[512,512]{1,0:T(8,128)(2,1)S(1)}, bf16[512,512]{1,0:T(8,128)(2,1)}, u32[]{:S(2)}) copy-start(bf16[512,512]{1,0:T(8,128)(2,1)} %constant.32.clone.pick_t_ref) | copy-start | bytes 1572868
  5.0 16.6 %copy-start.9 = (s32[1,1,6,2]{2,3,1,0:T(2,128)S(1)}, s32[1,1,6,2]{2,3,1,0:T(2,128)}, u32[]{:S(2)}) copy-start(s32[1,1,6,2]{2,3,1,0:T(2,128)} %param.12) | copy-start | bytes 148
  5.0 46.1 %collective-permute-start.6 = (bf16[2,768,512]{2,1,0:T(8,128)(2,1)}, bf16[2,768,512]{2,1,0:T(8,128)(2,1)}, u32[]{:S(2)}, u32[]{:S(2)}) collective-permute-start(bf16[2,768,512]{2,1,0:T(8,128)(2,1)} %get-tuple-element.32), channel_id=1, source_target_pairs={{4,0},{8,4},{12,8},{16,12},{20,16},{24,20},{28,24},{32,28},{36,32}... | collective-permute-start | bytes 4718600 | tf_op jit(solution)/shard_map/ppermute | solution.py:26
  10.4 19.5 %collective-permute-start = (bf16[2,208,768]{2,1,0:T(8,128)(2,1)}, bf16[2,208,768]{2,1,0:T(8,128)(2,1)}, u32[]{:S(2)}, u32[]{:S(2)}) collective-permute-start(bf16[2,208,768]{2,1,0:T(8,128)(2,1)} %get-tuple-element.26), channel_id=1, source_target_pairs={{1,0},{2,1},{3,2},{5,4},{6,5},{7,6},{9,8},{10,9},{11,10},{13,12},{... | collective-permute-start | bytes 1916936 | tf_op jit(solution)/shard_map/ppermute | solution.py:26
  12.7 28.8 %collective-permute-start.3 = (bf16[2,176,768]{2,1,0:T(8,128)(2,1)}, bf16[2,176,768]{2,1,0:T(8,128)(2,1)}, u32[]{:S(2)}, u32[]{:S(2)}) collective-permute-start(bf16[2,176,768]{2,1,0:T(8,128)(2,1)} %get-tuple-element.30), channel_id=1, source_target_pairs={{1,0},{2,1},{3,2},{5,4},{6,5},{7,6},{9,8},{10,9},{11,10},{13,12},{... | collective-permute-start | bytes 1622024 | tf_op jit(solution)/shard_map/ppermute | solution.py:26
  14.7 31.2 %collective-permute-start.1 = (bf16[2,128,768]{2,1,0:T(8,128)(2,1)}, bf16[2,128,768]{2,1,0:T(8,128)(2,1)S(1)}, u32[]{:S(2)}, u32[]{:S(2)}) collective-permute-start(bf16[2,128,768]{2,1,0:T(8,128)(2,1)} %get-tuple-element.28), channel_id=1, source_target_pairs={{1,0},{2,1},{3,2},{5,4},{6,5},{7,6},{9,8},{10,9},{11,10},{13,12},{... | collective-permute-start | bytes 1179656 | tf_op jit(solution)/shard_map/ppermute | solution.py:26
  30.9 20.2 %collective-permute-start.5 = (bf16[2,208,512]{2,1,0:T(8,128)(2,1)S(1)}, bf16[2,208,512]{2,1,0:T(8,128)(2,1)S(1)}, u32[]{:S(2)}, u32[]{:S(2)}) collective-permute-start(bf16[2,208,512]{2,1,0:T(8,128)(2,1)S(1)} %slice.15), channel_id=1, source_target_pairs={{4,0},{8,4},{12,8},{16,12},{20,16},{24,20},{28,24},{32,28},{36,32}... | collective-permute-start | bytes 1277960 | tf_op jit(solution)/shard_map/ppermute | solution.py:26
  42.5 34.0 %collective-permute-start.4 = (bf16[2,176,512]{2,1,0:T(8,128)(2,1)S(1)}, bf16[2,176,512]{2,1,0:T(8,128)(2,1)S(1)}, u32[]{:S(2)}, u32[]{:S(2)}) collective-permute-start(bf16[2,176,512]{2,1,0:T(8,128)(2,1)S(1)} %slice.17), channel_id=1, source_target_pairs={{4,0},{8,4},{12,8},{16,12},{20,16},{24,20},{28,24},{32,28},{36,32}... | collective-permute-start | bytes 1081352 | tf_op jit(solution)/shard_map/ppermute | solution.py:26
  45.9 37.3 %collective-permute-start.2 = (bf16[2,128,512]{2,1,0:T(8,128)(2,1)S(1)}, bf16[2,128,512]{2,1,0:T(8,128)(2,1)S(1)}, u32[]{:S(2)}, u32[]{:S(2)}) collective-permute-start(bf16[2,128,512]{2,1,0:T(8,128)(2,1)S(1)} %slice.16), channel_id=1, source_target_pairs={{4,0},{8,4},{12,8},{16,12},{20,16},{24,20},{28,24},{32,28},{36,32}... | collective-permute-start | bytes 786440 | tf_op jit(solution)/shard_map/ppermute | solution.py:26
  51.1 1.6 %copy-start.1 = (f32[2,512,512]{2,1,0:T(8,128)S(1)}, f32[2,512,512]{2,1,0:T(8,128)}, u32[]{:S(2)}) copy-start(f32[2,512,512]{2,1,0:T(8,128)} %probe_ref.5) | copy-start | bytes 6291460
  52.7 2.3 %copy-start.3 = (f32[2,768,768]{2,1,0:T(8,128)S(1)}, f32[2,768,768]{2,1,0:T(8,128)}, u32[]{:S(2)}) copy-start(f32[2,768,768]{2,1,0:T(8,128)} %first_ref.1) | copy-start | bytes 14155780
  55.1 1.0 copy-start.4
  56.1 1.0 copy-start.5
  95.4 18.2 %collective-permute-start.7 = (bf16[2,512,512]{2,1,0:T(8,128)(2,1)S(1)}, bf16[2,512,512]{2,1,0:T(8,128)(2,1)S(1)}, u32[]{:S(2)}, u32[]{:S(2)}) collective-permute-start(bf16[2,512,512]{2,1,0:T(8,128)(2,1)S(1)} %get-tuple-element.39), channel_id=1, source_target_pairs={{0,4},{4,8},{8,12},{12,16},{16,20},{20,24},{24,28},{28,32},{32,36}... | collective-permute-start | bytes 3145736 | tf_op jit(solution)/shard_map/ppermute | solution.py:26
  97.3 16.6 %collective-permute-start.8 = (bf16[2,512,256]{2,1,0:T(8,128)(2,1)S(1)}, bf16[2,512,256]{2,1,0:T(8,128)(2,1)S(1)}, u32[]{:S(2)}, u32[]{:S(2)}) collective-permute-start(bf16[2,512,256]{2,1,0:T(8,128)(2,1)S(1)} %get-tuple-element.40), channel_id=1, source_target_pairs={{0,1},{1,2},{2,3},{4,5},{5,6},{6,7},{8,9},{9,10},{10,11},{12,13},{... | collective-permute-start | bytes 1572872 | tf_op jit(solution)/shard_map/ppermute | solution.py:26
  99.2 31.2 %collective-permute-start.10 = (bf16[2,768,512]{2,1,0:T(8,128)(2,1)S(1)}, bf16[2,768,512]{2,1,0:T(8,128)(2,1)S(1)}, u32[]{:S(2)}, u32[]{:S(2)}) collective-permute-start(bf16[2,768,512]{2,1,0:T(8,128)(2,1)S(1)} %get-tuple-element.42), channel_id=1, source_target_pairs={{0,4},{4,8},{8,12},{12,16},{16,20},{20,24},{24,28},{28,32},{32,36}... | collective-permute-start | bytes 4718600 | tf_op jit(solution)/shard_map/ppermute | solution.py:26
  113.9 22.6 %collective-permute-start.9 = (bf16[2,512,512]{2,1,0:T(8,128)(2,1)S(1)}, bf16[2,512,512]{2,1,0:T(8,128)(2,1)S(1)}, u32[]{:S(2)}, u32[]{:S(2)}) collective-permute-start(bf16[2,512,512]{2,1,0:T(8,128)(2,1)S(1)} %add_convert_fusion), channel_id=1, source_target_pairs={{0,1},{1,2},{2,3},{4,5},{5,6},{6,7},{8,9},{9,10},{10,11},{12,13},{... | collective-permute-start | bytes 3145736 | tf_op jit(solution)/shard_map/ppermute | solution.py:26

commit v4 on v3

--- a/solution.py
+++ b/solution.py
@@ -15,8 +15,8 @@
 E = T + W
 NB = E // Q
 TB = T // Q
-CUTS = (0, 208, 384, 512)
 F = T - W
+SOLVE_MIB = 24
 R = 16
 f32, bf16 = jnp.float32, jnp.bfloat16
 
@@ -88,78 +88,82 @@
     return pl.CostEstimate(flops=1024, bytes_accessed=1024, transcendentals=0)
 
 
-def pack_kernel(slab_ref, *refs):
-    count = len(CUTS) - 1
-    below, right_ref, buf, sem = refs[:count], *refs[count:]
-    cuts = (*CUTS, T)
+def pack_kernel(slab_ref, near_ref, far_ref, right_ref, buf, sem):
+    step = T // 6
 
     def copy(c):
-        rows = pl.ds(cuts[c], cuts[c + 1] - cuts[c])
+        rows = pl.ds(c * step, step)
         return pltpu.make_async_copy(slab_ref.at[:, rows, :], buf.at[:, rows, :], sem.at[c])
 
-    for c in range(count + 1):
+    for c in range(6):
         copy(c).start()
-    for c in range(count + 1):
+    for c in range(6):
         copy(c).wait()
 
         def convert(row):
-            here = pl.ds(pl.multiple_of(cuts[c] + row, R), R)
+            here = pl.ds(pl.multiple_of(c * step + row, R), R)
             for p in range(2):
                 part = buf[p, here, :].astype(bf16)
                 right_ref[p, here, :] = part[:, :W]
-                if c < count:
-                    below[c][p, pl.ds(row, R), :] = part
-
-        each_rows(cuts[c + 1] - cuts[c], convert)
+                if (c + 1) * step <= W:
+                    near_ref[p, here, :] = part[:, :W]
+                    far_ref[p, here, :] = part[:, W:]
+
+        each_rows(step, convert)
 
 
 def pack(slab):
-    rows = [high - low for low, high in zip(CUTS[:-1], CUTS[1:])]
-    shapes = [(2, r, T) for r in rows] + [(2, T, W)]
-    made = pl.pallas_call(
+    return pl.pallas_call(
         pack_kernel,
         in_specs=[ANY],
-        out_specs=[VMEM] * len(shapes),
-        out_shape=[jax.ShapeDtypeStruct(shape, bf16) for shape in shapes],
-        scratch_shapes=[pltpu.VMEM((2, T, T), f32), pltpu.SemaphoreType.DMA((len(CUTS),))],
+        out_specs=[VMEM] * 3,
+        out_shape=[
+            jax.ShapeDtypeStruct((2, W, W), bf16),
+            jax.ShapeDtypeStruct((2, W, F), bf16),
+            jax.ShapeDtypeStruct((2, T, W), bf16),
+        ],
+        scratch_shapes=[pltpu.VMEM((2, T, T), f32), pltpu.SemaphoreType.DMA((6,))],
         cost_estimate=cost(),
-        compiler_params=params(24),
+        compiler_params=params(52),
     )(slab)
-    return made[:-1], made[-1]
-
-
-def sort_kernel(pick_ref, pick_t_ref, in_ref, out_ref):
+
+
+def sort_kernel(pick_ref, pick_t_ref, in_ref, *refs):
+    out_ref = refs[-1]
     rows = jnp.dot(pick_ref[...], in_ref[0], preferred_element_type=f32).astype(bf16)
     out_ref[0] = jnp.dot(rows, pick_t_ref[...], preferred_element_type=f32).astype(bf16)
 
 
-def sort_intensities(measured, pick):
+def sort_intensities(measured, pick, *later):
     whole = pl.BlockSpec((W, W), lambda s: (0, 0))
     each = pl.BlockSpec((1, W, W), lambda s: (s, 0, 0))
     return pl.pallas_call(
         sort_kernel,
         grid=(measured.shape[0],),
-        in_specs=[whole, whole, each],
+        in_specs=[whole, whole, each] + [VMEM] * len(later),
         out_specs=each,
         out_shape=jax.ShapeDtypeStruct(measured.shape, bf16),
-        cost_estimate=cost(),
+        cost_estimate=pl.CostEstimate(
+            flops=24 * W**3, bytes_accessed=24 * W * W, transcendentals=0
+        ),
         compiler_params=params(16),
-    )(jnp.asarray(pick), jnp.asarray(pick.T.copy()), measured)
+    )(jnp.asarray(pick), jnp.asarray(pick.T.copy()), measured, *later)
 
 
 def slots_kernel(
-    chunk,
+    live_ref,
     meta_ref,
-    below_ref,
+    slab_ref,
+    right_ref,
+    near_ref,
+    far_ref,
     corner_ref,
     probe_ref,
     meas_ref,
     ga_ref,
     gb_ref,
-    first_ref,
-    second_ref,
+    grown,
     ext,
-    grown,
     half16,
     full32,
     mid,
@@ -168,8 +172,12 @@
 ):
     def copy(p, b):
         return pltpu.make_async_copy(
-            first_ref.at[p, :, lanes(b)], ext.at[p, b, pl.ds(0, T), :], sem.at[p, b]
+            slab_ref.at[p, :, lanes(b)], ext.at[p, b, pl.ds(0, T), :], sem.at[p, b]
         )
+
+    for p in range(2):
+        for b in range(TB):
+            copy(p, b).start()
 
     def clear(row):
         for p in range(2):
@@ -177,31 +185,27 @@
                 grown[p, b, pl.ds(row, R), :] = jnp.zeros((R, Q), f32)
 
     def fill_right(row):
-        for p in range(2):
-            for b in range(4):
-                ext[p, TB + b, pl.ds(row, R), :] = second_ref[p, pl.ds(row, R), lanes(b)].astype(f32)
-
-    if chunk == 0:
-        for p in range(2):
-            for b in range(TB):
-                copy(p, b).start()
-        each_rows(E, clear)
-        each_rows(T, fill_right)
-
-    def fill(row):
-        rows = pl.ds(row, R)
-        there = pl.ds(pl.multiple_of(T + CUTS[chunk] + row, R), R)
-        for p in range(2):
-            for b in range(TB):
-                ext[p, b, there, :] = below_ref[p, rows, lanes(b)].astype(f32)
-            for b in range(4):
+        rows = pl.ds(row, R)
+        for p in range(2):
+            for b in range(4):
+                ext[p, TB + b, rows, :] = right_ref[p, rows, lanes(b)].astype(f32)
+
+    def fill_below(row):
+        rows = pl.ds(row, R)
+        there = pl.ds(pl.multiple_of(T + row, R), R)
+        for p in range(2):
+            for b in range(4):
+                ext[p, b, there, :] = near_ref[p, rows, lanes(b)].astype(f32)
                 ext[p, TB + b, there, :] = corner_ref[p, rows, lanes(b)].astype(f32)
-
-    each_rows(CUTS[chunk + 1] - CUTS[chunk], fill)
-    if chunk == 0:
-        for p in range(2):
-            for b in range(TB):
-                copy(p, b).wait()
+            for b in range(2):
+                ext[p, 4 + b, there, :] = far_ref[p, rows, lanes(b)].astype(f32)
+
+    each_rows(E, clear)
+    each_rows(T, fill_right)
+    each_rows(W, fill_below)
+    for p in range(2):
+        for b in range(TB):
+            copy(p, b).wait()
 
     lane = lax.broadcasted_iota(jnp.int32, (R, Q), 1)
 
@@ -214,16 +218,20 @@
         outer = lane < by
 
         def cut(i, c):
+            def rolled(q, p, b):
+                rows = pl.ds(row0 + q * Q + i * R, R)
+                return pltpu.roll(ext[p, block0 + b, rows, :], Q - by, 1)
+
+            last = [[rolled(q, p, 0) for p in range(2)] for q in range(4)]
             for b in range(4):
                 re, im = [], []
                 for q in range(4):
-                    rows = pl.ds(row0 + q * Q + i * R, R)
                     here = pl.ds(pl.multiple_of(q * Q + i * R, R), R)
                     part = []
                     for p in range(2):
-                        one = pltpu.roll(ext[p, block0 + b, rows, :], Q - by, 1)
-                        two = pltpu.roll(ext[p, block0 + b + 1, rows, :], Q - by, 1)
-                        part.append(jnp.where(inner, one, two))
+                        after = rolled(q, p, b + 1)
+                        part.append(jnp.where(inner, last[q][p], after))
+                        last[q][p] = after
                     pr, pi = probe_ref[0, here, lanes(b)], probe_ref[1, here, lanes(b)]
                     re.append(pr * part[0] - pi * part[1])
                     im.append(pr * part[1] + pi * part[0])
@@ -235,24 +243,19 @@
                     half16[j, low, lanes(b)] = im[j].astype(bf16)
             return c
 
-        lax.fori_loop(0, Q // R, cut, 0)
+        lax.fori_loop(0, Q // R, cut, 0, unroll=4)
         for j in range(4):
             full32[j] = jnp.dot(ga_ref[j], half16[j], preferred_element_type=f32)
-
-        def across(i, c):
-            top = pl.ds(pl.multiple_of(i * R, R), R)
-            low = pl.ds(pl.multiple_of(Q + i * R, R), R)
-            for j in range(4):
+            for i in range(Q // R):
+                top, low = pl.ds(i * R, R), pl.ds(Q + i * R, R)
                 re = [full32[j, top, lanes(q)] for q in range(4)]
                 im = [full32[j, low, lanes(q)] for q in range(4)]
                 re, im = split4(re, im)
-                there = pl.ds(pl.multiple_of(j * Q + i * R, R), R)
+                there = pl.ds(j * Q + i * R, R)
                 for l in range(4):
                     mid[l, there, lanes(0)] = re[l].astype(bf16)
                     mid[l, there, lanes(1)] = im[l].astype(bf16)
-            return c
-
-        lax.fori_loop(0, Q // R, across, 0)
+
         for l in range(4):
             far = jnp.dot(mid[l], gb_ref[l], preferred_element_type=f32)
             re, im = far[:, :Q], far[:, Q:]
@@ -260,21 +263,16 @@
             misfit = jnp.concatenate([gap * re, gap * im], axis=1).astype(bf16)
             out[l] = jnp.dot(misfit, ga_ref[l], preferred_element_type=f32)
 
-        def back(i, c):
-            top = pl.ds(pl.multiple_of(i * R, R), R)
-            low = pl.ds(pl.multiple_of(Q + i * R, R), R)
-            for j in range(4):
-                here = pl.ds(pl.multiple_of(j * Q + i * R, R), R)
+        for j in range(4):
+            for i in range(Q // R):
+                top, low = pl.ds(i * R, R), pl.ds(Q + i * R, R)
+                here = pl.ds(j * Q + i * R, R)
                 re = [out[l, here, lanes(0)] for l in range(4)]
                 im = [out[l, here, lanes(1)] for l in range(4)]
                 re, im = join4(re, im)
                 for q in range(4):
                     half16[j, top, lanes(q)] = re[q].astype(bf16)
                     half16[j, low, lanes(q)] = im[q].astype(bf16)
-            return c
-
-        lax.fori_loop(0, Q // R, back, 0)
-        for j in range(4):
             full32[j] = jnp.dot(gb_ref[j], half16[j], preferred_element_type=f32)
 
         def add(i, c):
@@ -303,27 +301,20 @@
                         last[q][p] = both[p]
             return c
 
-        lax.fori_loop(0, Q // R, add, 0)
+        lax.fori_loop(0, Q // R, add, 0, unroll=4)
         return carry
 
-    def maybe(slot, carry):
-        @pl.when(meta_ref[2, slot] == chunk)
-        def _():
-            one_slot(slot, 0)
-
-        return carry
-
-    lax.fori_loop(0, meta_ref.shape[1], maybe, 0)
-
-
-def solve(chunk, meta, below, corner, probe, measured, left, left_t, first, second):
-    return pl.pallas_call(
-        functools.partial(slots_kernel, chunk),
-        in_specs=[SMEM] + [VMEM] * 6 + [ANY if chunk == 0 else VMEM, VMEM],
-        out_specs=[VMEM, VMEM],
-        out_shape=[TILES, TILES],
-        input_output_aliases={7: 0, 8: 1} if chunk else {},
+    lax.fori_loop(0, live_ref[0], one_slot, 0)
+
+
+def solve(live, meta, slab, right, near, far, corner, probe, measured, left, left_t):
+    return pl.pallas_call(
+        slots_kernel,
+        in_specs=[SMEM, SMEM, ANY] + [VMEM] * 8,
+        out_specs=VMEM,
+        out_shape=TILES,
         scratch_shapes=[
+            pltpu.VMEM((2, NB, E, Q), f32),
             pltpu.VMEM((4, 2 * Q, W), bf16),
             pltpu.VMEM((4, 2 * Q, W), f32),
             pltpu.VMEM((4, W, 2 * Q), bf16),
@@ -331,29 +322,29 @@
             pltpu.SemaphoreType.DMA((2, TB)),
         ],
         cost_estimate=cost(),
-        compiler_params=params(12),
-    )(meta, below, corner, probe, measured, left, left_t, first, second)
-
-
-def drain_kernel(grown, near_ref, far_ref, corner_ref, right_ref):
-    def below(row):
+        compiler_params=params(SOLVE_MIB),
+    )(live, meta, slab, right, near, far, corner, probe, measured, left, left_t)
+
+
+def drain_kernel(grown, to_near_ref, to_far_ref, to_corner_ref, to_right_ref):
+    def drain_below(row):
         rows = pl.ds(row, R)
         here = pl.ds(pl.multiple_of(T + row, R), R)
         for p in range(2):
             for b in range(4):
-                near_ref[p, rows, lanes(b)] = grown[p, b, here, :].astype(bf16)
-                corner_ref[p, rows, lanes(b)] = grown[p, TB + b, here, :].astype(bf16)
+                to_near_ref[p, rows, lanes(b)] = grown[p, b, here, :].astype(bf16)
+                to_corner_ref[p, rows, lanes(b)] = grown[p, TB + b, here, :].astype(bf16)
             for b in range(2):
-                far_ref[p, rows, lanes(b)] = grown[p, 4 + b, here, :].astype(bf16)
-
-    def right(row):
-        rows = pl.ds(row, R)
-        for p in range(2):
-            for b in range(4):
-                right_ref[p, rows, lanes(b)] = grown[p, TB + b, rows, :].astype(bf16)
-
-    each_rows(W, below)
-    each_rows(T, right)
+                to_far_ref[p, rows, lanes(b)] = grown[p, 4 + b, here, :].astype(bf16)
+
+    def drain_right(row):
+        rows = pl.ds(row, R)
+        for p in range(2):
+            for b in range(4):
+                to_right_ref[p, rows, lanes(b)] = grown[p, TB + b, rows, :].astype(bf16)
+
+    each_rows(W, drain_below)
+    each_rows(T, drain_right)
 
 
 def drain(grown):
@@ -455,33 +446,27 @@
 def shards(slab, probe, intensities, offsets, live_count):
     left, left_t, pick = tables()
     left, left_t = jnp.asarray(left), jnp.asarray(left_t)
-    chunks = range(len(CUTS) - 1)
-    send_below, send_right = pack(slab)
-    below = [shifted(part, "tile", -1) for part in send_below]
-    right = shifted(send_right, "scan", -1)
+    near, far, right = pack(slab)
+    near = shifted(near, "tile", -1)
+    far = shifted(far, "tile", -1)
+    right = shifted(right, "scan", -1)
+    measured = sort_intensities(intensities[0, 0], pick, probe, left, left_t)
     live = lax.dynamic_slice(live_count[:, 0], (lax.axis_index("scan"),), (1,))
     shifts = offsets[0, 0].T
-    reach = shifts[0] + (W - T)
-    stage = sum((reach > CUTS[c + 1]).astype(jnp.int32) for c in chunks)
-    stage = jnp.where(jnp.arange(shifts.shape[1], dtype=jnp.int32) < live, stage, len(CUTS))
-    meta = jnp.concatenate([shifts, stage[None]], axis=0)
-    measured = sort_intensities(intensities[0, 0], pick)
-    below[0], measured, meta = lax.optimization_barrier((below[0], measured, meta))
-    corner = [shifted(part[:, :, :W], "scan", -1) for part in below]
-    ext, grown = slab, right
-    for c in chunks:
-        ext, grown = solve(
-            c, meta, below[c], corner[c], probe, measured, left, left_t, ext, grown
-        )
-    to_near, to_far, to_corner, to_right = drain(grown)
-    to_far = shifted(to_far, "tile", 1)
-    from_corner = shifted(to_corner, "scan", 1)
-    to_near = (to_near.astype(f32) + from_corner.astype(f32)).astype(bf16)
-    to_near, to_far = lax.optimization_barrier((to_near, to_far))
-    to_near = shifted(to_near, "tile", 1)
-    from_left = shifted(to_right, "scan", 1)
-    grown, whole = add_side(from_left, to_far, grown)
-    return add_near(to_near, grown, whole)
+    near, measured, live, shifts = lax.optimization_barrier((near, measured, live, shifts))
+    corner = shifted(near, "scan", -1)
+    grown = solve(
+        live, shifts, slab, right, near, far, corner, probe, measured, left, left_t
+    )
+    near, far, corner, right = drain(grown)
+    far = shifted(far, "tile", 1)
+    corner = shifted(corner, "scan", 1)
+    near = (near.astype(f32) + corner.astype(f32)).astype(bf16)
+    near = shifted(near, "tile", 1)
+    far, right = lax.optimization_barrier((far, right))
+    right = shifted(right, "scan", 1)
+    grown, whole = add_side(right, far, grown)
+    return add_near(near, grown, whole)
 
 
 def solution(mesh):

time: 141 us -> 127 us (0.901)
  the two profiles are of different devices: /device:TPU:12 before, /device:TPU:73 now
where the time goes in v4:
time: 127 us; the launch traced here: 126 us
  waiting for transfers between devices  55.9 us (44%)
  Pallas kernels  38.7 us (30%)
  starting transfers between devices  23.3 us (18%)
  local copies, waits for them, and re-layouts  7.84 us (6%)
    ppermute x8, waiting for transfers between devices, shifted(): lax.ppermute(value, axis, [(i, i + by) for i in range(n) if 0 <= i + by <...  55.9 us
    pallas_call x1, Pallas kernels, solve(): pl.pallas_call(slots_kernel, in_specs=[SMEM, SMEM, ANY] + [VMEM] * 8, out...  25.2 us
    ppermute x8, starting transfers between devices, shifted(): lax.ppermute(value, axis, [(i, i + by) for i in range(n) if 0 <= i + by <...  23.3 us
    unnamed x26, local copies, waits for them, and re-layouts  7.24 us
    pallas_call x1, Pallas kernels, sort_intensities(): pl.pallas_call(sort_kernel, grid=(measured.shape[0],), in_specs=[whole, w...  4.32 us
    pallas_call x1, Pallas kernels, pack(): pl.pallas_call(pack_kernel, in_specs=[ANY], out_specs=[VMEM] * 3, out_sha...  4.06 us
  transfers between devices with their start and end apart: 8, of which 5 were waited for; matrix products, arithmetic and copies ran while one was open for 1% of the time, Pallas kernels for 5%

profile of v4, /device:TPU:73, one launch (start us, length us, event | category | flops | bytes accessed | tf_op | source)
XLA Modules:
  0.0 126.2 jit_solution(14209146096264406530)
XLA Ops:
  0.0 0.0 copy-start
  0.0 4.1 %shard_map.91 = (bf16[2,512,512]{2,1,0:T(8,128)(2,1)}, bf16[2,512,256]{2,1,0:T(8,128)(2,1)S(1)}, bf16[2,768,512]{2,1,0:T(8,128)(2,1)}) custom-call(f32[2,768,768]{2,1,0:T(8,128)} %slab_ref.3), custom_call_target="tpu_custom_call" | custom-call | flops 1024 | bytes 1024 | tf_op jit(solution)/shard_map/pallas_call | solution.py:116
  4.1 0.0 copy-start.7
  4.1 0.8 copy-done.7
  4.9 2.1 %collective-permute-start = (bf16[2,512,512]{2,1,0:T(8,128)(2,1)}, bf16[2,512,512]{2,1,0:T(8,128)(2,1)S(1)}, u32[]{:S(2)}, u32[]{:S(2)}) collective-permute-start(bf16[2,512,512]{2,1,0:T(8,128)(2,1)} %get-tuple-element.21), channel_id=1, source_target_pairs={{1,0},{2,1},{3,2},{5,4},{6,5},{7,6},{9,8},{10,9},{11,10},{13,12},{... | collective-permute-start | bytes 3145736 | tf_op jit(solution)/shard_map/ppermute | solution.py:26
  6.9 2.9 %collective-permute-start.1 = (bf16[2,768,512]{2,1,0:T(8,128)(2,1)}, bf16[2,768,512]{2,1,0:T(8,128)(2,1)}, u32[]{:S(2)}, u32[]{:S(2)}) collective-permute-start(bf16[2,768,512]{2,1,0:T(8,128)(2,1)} %get-tuple-element.24), channel_id=1, source_target_pairs={{4,0},{8,4},{12,8},{16,12},{20,16},{24,20},{28,24},{32,28},{36,32}... | collective-permute-start | bytes 4718600 | tf_op jit(solution)/shard_map/ppermute | solution.py:26
  9.8 0.6 constant_dynamic-slice_fusion
  10.4 1.2 copy-done.2
  11.6 1.3 copy-done.4
  12.9 1.9 %copy-done.6 = bf16[1,1,6,512,512]{4,3,2,1,0:T(8,128)(2,1)S(1)} copy-done((bf16[1,1,6,512,512]{4,3,2,1,0:T(8,128)(2,1)S(1)}, bf16[1,1,6,512,512]{4,3,2,1,0:T(8,128)(2,1)}, u32[]{:S(2)}) %copy-start.6) | copy-done | bytes 3145752
  14.8 1.0 copy-done.9
  15.8 1.0 copy-done.10
  16.9 4.3 %shard_map.92.meas_ref = bf16[6,512,512]{2,1,0:T(8,128)(2,1)S(1)} custom-call(bf16[512,512]{1,0:T(8,128)(2,1)S(1)} %copy-done.10, bf16[512,512]{1,0:T(8,128)(2,1)S(1)} %copy-done.9, bf16[6,512,512]{2,1,0:T(8,128)(2,1)S(1)} %bitcast.8, f32[2,512,512]{2,1,0:T(8,128)S(1)} %copy-done.1, bf16[4,256,256]{2,1,0:T(8,128)(2,1)S(1)} %copy-done.4, ...), custom_call_target="tpu_custom_call" | custom-call | flops 3221225472 | bytes 6291456 | tf_op jit(solution)/shard_map/pallas_call | solution.py:140
  21.2 9.8 %collective-permute-done.near_ref = bf16[2,512,512]{2,1,0:T(8,128)(2,1)S(1)} collective-permute-done((bf16[2,512,512]{2,1,0:T(8,128)(2,1)}, bf16[2,512,512]{2,1,0:T(8,128)(2,1)S(1)}, u32[]{:S(2)}, u32[]{:S(2)}) %collective-permute-start) | collective-permute-done | bytes 1048608 | tf_op jit(solution)/shard_map/ppermute | solution.py:26
  31.0 3.4 %collective-permute-start.3 = (bf16[2,512,512]{2,1,0:T(8,128)(2,1)S(1)}, bf16[2,512,512]{2,1,0:T(8,128)(2,1)S(1)}, u32[]{:S(2)}, u32[]{:S(2)}) collective-permute-start(bf16[2,512,512]{2,1,0:T(8,128)(2,1)S(1)} %collective-permute-done.near_ref), channel_id=1, source_target_pairs={{4,0},{8,4},{12,8},{16,12},{20,16},{24,20},{28,24},{32,28},{36,32}... | collective-permute-start | bytes 3145736 | tf_op jit(solution)/shard_map/ppermute | solution.py:26
  34.5 2.1 %collective-permute-start.2 = (bf16[2,512,256]{2,1,0:T(8,128)(2,1)S(1)}, bf16[2,512,256]{2,1,0:T(8,128)(2,1)S(1)}, u32[]{:S(2)}, u32[]{:S(2)}) collective-permute-start(bf16[2,512,256]{2,1,0:T(8,128)(2,1)S(1)} %copy-done.8), channel_id=1, source_target_pairs={{1,0},{2,1},{3,2},{5,4},{6,5},{7,6},{9,8},{10,9},{11,10},{13,12},{... | collective-permute-start | bytes 1572872 | tf_op jit(solution)/shard_map/ppermute | solution.py:26
  36.5 13.4 %collective-permute-done.2.far_ref = bf16[2,512,256]{2,1,0:T(8,128)(2,1)S(1)} collective-permute-done((bf16[2,512,256]{2,1,0:T(8,128)(2,1)S(1)}, bf16[2,512,256]{2,1,0:T(8,128)(2,1)S(1)}, u32[]{:S(2)}, u32[]{:S(2)}) %collective-permute-start.2) | collective-permute-done | bytes 524320 | tf_op jit(solution)/shard_map/ppermute | solution.py:26
  49.9 0.0 collective-permute-done.1.right_ref
  49.9 0.0 collective-permute-done.3.corner_ref
  49.9 25.2 %shard_map.93.grown.grown_in = f32[2,10,1280,128]{3,2,1,0:T(8,128)S(1)} custom-call(s32[1]{0:T(128)} %bitcast.1.live_ref, s32[2,6]{1,0:T(2,128)S(1)} %bitcast.7, f32[2,768,768]{2,1,0:T(8,128)S(1)} %bitcast.6, bf16[2,768,512]{2,1,0:T(8,128)(2,1)} %collective-permute-done.1.right_ref, bf16[2,512,512]{2,1,0:T(8,128)(2,1)S(1)} %collective-permute-done.near_ref, ...), custom_call_target="tpu_custom_call" | custom-call | flops 1024 | bytes 1024 | tf_op jit(solution)/shard_map/pallas_call | solution.py:311
  75.1 0.9 shard_map.94
  76.1 1.9 %collective-permute-start.4 = (bf16[2,512,512]{2,1,0:T(8,128)(2,1)S(1)}, bf16[2,512,512]{2,1,0:T(8,128)(2,1)S(1)}, u32[]{:S(2)}, u32[]{:S(2)}) collective-permute-start(bf16[2,512,512]{2,1,0:T(8,128)(2,1)S(1)} %get-tuple-element.29), channel_id=1, source_target_pairs={{0,4},{4,8},{8,12},{12,16},{16,20},{20,24},{24,28},{28,32},{32,36}... | collective-permute-start | bytes 3145736 | tf_op jit(solution)/shard_map/ppermute | solution.py:26
  78.0 3.1 %collective-permute-start.6 = (bf16[2,512,256]{2,1,0:T(8,128)(2,1)S(1)}, bf16[2,512,256]{2,1,0:T(8,128)(2,1)S(1)}, u32[]{:S(2)}, u32[]{:S(2)}) collective-permute-start(bf16[2,512,256]{2,1,0:T(8,128)(2,1)S(1)} %get-tuple-element.30), channel_id=1, source_target_pairs={{0,1},{1,2},{2,3},{4,5},{5,6},{6,7},{8,9},{9,10},{10,11},{12,13},{... | collective-permute-start | bytes 1572872 | tf_op jit(solution)/shard_map/ppermute | solution.py:26
  81.1 11.7 %collective-permute-done.6.far_ref = bf16[2,512,256]{2,1,0:T(8,128)(2,1)S(1)} collective-permute-done((bf16[2,512,256]{2,1,0:T(8,128)(2,1)S(1)}, bf16[2,512,256]{2,1,0:T(8,128)(2,1)S(1)}, u32[]{:S(2)}, u32[]{:S(2)}) %collective-permute-start.6) | collective-permute-done | bytes 524320 | tf_op jit(solution)/shard_map/ppermute | solution.py:26
  92.9 3.6 %collective-permute-start.7 = (bf16[2,768,512]{2,1,0:T(8,128)(2,1)S(1)}, bf16[2,768,512]{2,1,0:T(8,128)(2,1)S(1)}, u32[]{:S(2)}, u32[]{:S(2)}) collective-permute-start(bf16[2,768,512]{2,1,0:T(8,128)(2,1)S(1)} %get-tuple-element.32), channel_id=1, source_target_pairs={{0,4},{4,8},{8,12},{12,16},{16,20},{20,24},{24,28},{28,32},{32,36}... | collective-permute-start | bytes 4718600 | tf_op jit(solution)/shard_map/ppermute | solution.py:26
  96.5 0.0 collective-permute-done.4
  96.5 0.3 add_convert_fusion
  96.8 4.1 %collective-permute-start.5 = (bf16[2,512,512]{2,1,0:T(8,128)(2,1)S(1)}, bf16[2,512,512]{2,1,0:T(8,128)(2,1)S(1)}, u32[]{:S(2)}, u32[]{:S(2)}) collective-permute-start(bf16[2,512,512]{2,1,0:T(8,128)(2,1)S(1)} %add_convert_fusion), channel_id=1, source_target_pairs={{0,1},{1,2},{2,3},{4,5},{5,6},{6,7},{8,9},{9,10},{10,11},{12,13},{... | collective-permute-start | bytes 3145736 | tf_op jit(solution)/shard_map/ppermute | solution.py:26
  100.9 12.9 %collective-permute-done.7.right_ref = bf16[2,768,512]{2,1,0:T(8,128)(2,1)S(1)} collective-permute-done((bf16[2,768,512]{2,1,0:T(8,128)(2,1)S(1)}, bf16[2,768,512]{2,1,0:T(8,128)(2,1)S(1)}, u32[]{:S(2)}, u32[]{:S(2)}) %collective-permute-start.7) | collective-permute-done | bytes 1572896 | tf_op jit(solution)/shard_map/ppermute | solution.py:26
  113.9 1.8 %shard_map.95 = (f32[2,10,1280,128]{3,2,1,0:T(8,128)S(1)}, f32[2,768,768]{2,1,0:T(8,128)}) custom-call(bf16[2,768,512]{2,1,0:T(8,128)(2,1)S(1)} %collective-permute-done.7.right_ref, bf16[2,512,256]{2,1,0:T(8,128)(2,1)S(1)} %collective-permute-done.6.far_ref, f32[2,10,1280,128]{3,2,1,0:T(8,128)S(1)} %shard_map.93.grown.grown_in), custom_call_target="tpu_custom_call", output_to_operand_aliasing={{0}: (2, {})} | custom-call | flops 1024 | bytes 1024 | tf_op jit(solution)/shard_map/pallas_call | solution.py:406
  115.7 8.1 %collective-permute-done.5.near_ref = bf16[2,512,512]{2,1,0:T(8,128)(2,1)S(1)} collective-permute-done((bf16[2,512,512]{2,1,0:T(8,128)(2,1)S(1)}, bf16[2,512,512]{2,1,0:T(8,128)(2,1)S(1)}, u32[]{:S(2)}, u32[]{:S(2)}) %collective-permute-start.5) | collective-permute-done | bytes 1048608 | tf_op jit(solution)/shard_map/ppermute | solution.py:26
  123.8 2.4 %shard_map.96 = (f32[2,10,1280,128]{3,2,1,0:T(8,128)S(1)}, f32[2,768,768]{2,1,0:T(8,128)}) custom-call(bf16[2,512,512]{2,1,0:T(8,128)(2,1)S(1)} %collective-permute-done.5.near_ref, f32[2,10,1280,128]{3,2,1,0:T(8,128)S(1)} %get-tuple-element.34.grown_in, f32[2,768,768]{2,1,0:T(8,128)} %get-tuple-element.35.whole_in), custom_call_target="tpu_custom_call", output_to_operand_aliasing={{0}: (1, {}), {1}: (2, {})} | custom-call | flops 1024 | bytes 1024 | tf_op jit(solution)/shard_map/pallas_call | solution.py:434
  (19 shorter events, 0.0 us)
Async XLA Ops:
  0.0 9.8 %copy-start = (s32[32,1]{0,1:T(1,128)S(1)}, s32[32,1]{0,1:T(1,128)}, u32[]{:S(2)}) copy-start(s32[32,1]{0,1:T(1,128)} %param.13) | copy-start | bytes 388
  0.0 10.4 %copy-start.1 = (f32[2,512,512]{2,1,0:T(8,128)S(1)}, f32[2,512,512]{2,1,0:T(8,128)}, u32[]{:S(2)}) copy-start(f32[2,512,512]{2,1,0:T(8,128)} %probe_ref.1) | copy-start | bytes 6291460
  4.1 0.8 copy-start.7
  4.9 26.1 %collective-permute-start = (bf16[2,512,512]{2,1,0:T(8,128)(2,1)}, bf16[2,512,512]{2,1,0:T(8,128)(2,1)S(1)}, u32[]{:S(2)}, u32[]{:S(2)}) collective-permute-start(bf16[2,512,512]{2,1,0:T(8,128)(2,1)} %get-tuple-element.21), channel_id=1, source_target_pairs={{1,0},{2,1},{3,2},{5,4},{6,5},{7,6},{9,8},{10,9},{11,10},{13,12},{... | collective-permute-start | bytes 3145736 | tf_op jit(solution)/shard_map/ppermute | solution.py:26
  6.9 42.9 %collective-permute-start.1 = (bf16[2,768,512]{2,1,0:T(8,128)(2,1)}, bf16[2,768,512]{2,1,0:T(8,128)(2,1)}, u32[]{:S(2)}, u32[]{:S(2)}) collective-permute-start(bf16[2,768,512]{2,1,0:T(8,128)(2,1)} %get-tuple-element.24), channel_id=1, source_target_pairs={{4,0},{8,4},{12,8},{16,12},{20,16},{24,20},{28,24},{32,28},{36,32}... | collective-permute-start | bytes 4718600 | tf_op jit(solution)/shard_map/ppermute | solution.py:26
  10.4 39.5 %slice-start = ((s8[4718592]{0:T(1024)(128)(4,1)}), s8[4194304]{0:T(1024)(128)(4,1)S(1)}, s32[]{:S(2)}) async-start(s8[4718592]{0:T(1024)(128)(4,1)} %bitcast.5), calls=%async_computation | async-start | bytes 8388608
  10.4 1.2 copy-start.2
  11.6 1.3 %copy-start.4 = (bf16[4,256,256]{2,1,0:T(8,128)(2,1)S(1)}, bf16[4,256,256]{2,1,0:T(8,128)(2,1)}, u32[]{:S(2)}) copy-start(bf16[4,256,256]{2,1,0:T(8,128)(2,1)} %constant.19.clone.refs_1_.ga_ref) | copy-start | bytes 1572868
  12.9 1.9 %copy-start.6 = (bf16[1,1,6,512,512]{4,3,2,1,0:T(8,128)(2,1)S(1)}, bf16[1,1,6,512,512]{4,3,2,1,0:T(8,128)(2,1)}, u32[]{:S(2)}) copy-start(bf16[1,1,6,512,512]{4,3,2,1,0:T(8,128)(2,1)} %param.11) | copy-start | bytes 9437188
  14.8 1.0 copy-start.9
  15.8 1.0 copy-start.10
  16.9 17.6 %copy-start.8 = (bf16[2,512,256]{2,1,0:T(8,128)(2,1)S(1)}, bf16[2,512,256]{2,1,0:T(8,128)(2,1)}, u32[]{:S(2)}) copy-start(bf16[2,512,256]{2,1,0:T(8,128)(2,1)} %copy-done.7) | copy-start | bytes 1572868
  16.9 33.0 %slice-start.1 = ((s8[4718592]{0:T(1024)(128)(4,1)}), s8[524288]{0:T(1024)(128)(4,1)S(1)}, s32[]{:S(2)}) async-start(s8[4718592]{0:T(1024)(128)(4,1)} %bitcast.5), calls=%async_computation.1 | async-start | bytes 1048576
  16.9 33.0 %copy-start.3 = (bf16[4,256,256]{2,1,0:T(8,128)(2,1)S(1)}, bf16[4,256,256]{2,1,0:T(8,128)(2,1)}, u32[]{:S(2)}) copy-start(bf16[4,256,256]{2,1,0:T(8,128)(2,1)} %constant.20.clone.refs_2_.gb_ref) | copy-start | bytes 1572868
  16.9 33.1 %copy-start.5 = (s32[1,1,6,2]{2,3,1,0:T(2,128)S(1)}, s32[1,1,6,2]{2,3,1,0:T(2,128)}, u32[]{:S(2)}) copy-start(s32[1,1,6,2]{2,3,1,0:T(2,128)} %param.12) | copy-start | bytes 148
  31.0 18.9 %collective-permute-start.3 = (bf16[2,512,512]{2,1,0:T(8,128)(2,1)S(1)}, bf16[2,512,512]{2,1,0:T(8,128)(2,1)S(1)}, u32[]{:S(2)}, u32[]{:S(2)}) collective-permute-start(bf16[2,512,512]{2,1,0:T(8,128)(2,1)S(1)} %collective-permute-done.near_ref), channel_id=1, source_target_pairs={{4,0},{8,4},{12,8},{16,12},{20,16},{24,20},{28,24},{32,28},{36,32}... | collective-permute-start | bytes 3145736 | tf_op jit(solution)/shard_map/ppermute | solution.py:26
  34.5 15.4 %collective-permute-start.2 = (bf16[2,512,256]{2,1,0:T(8,128)(2,1)S(1)}, bf16[2,512,256]{2,1,0:T(8,128)(2,1)S(1)}, u32[]{:S(2)}, u32[]{:S(2)}) collective-permute-start(bf16[2,512,256]{2,1,0:T(8,128)(2,1)S(1)} %copy-done.8), channel_id=1, source_target_pairs={{1,0},{2,1},{3,2},{5,4},{6,5},{7,6},{9,8},{10,9},{11,10},{13,12},{... | collective-permute-start | bytes 1572872 | tf_op jit(solution)/shard_map/ppermute | solution.py:26
  76.1 20.5 %collective-permute-start.4 = (bf16[2,512,512]{2,1,0:T(8,128)(2,1)S(1)}, bf16[2,512,512]{2,1,0:T(8,128)(2,1)S(1)}, u32[]{:S(2)}, u32[]{:S(2)}) collective-permute-start(bf16[2,512,512]{2,1,0:T(8,128)(2,1)S(1)} %get-tuple-element.29), channel_id=1, source_target_pairs={{0,4},{4,8},{8,12},{12,16},{16,20},{20,24},{24,28},{28,32},{32,36}... | collective-permute-start | bytes 3145736 | tf_op jit(solution)/shard_map/ppermute | solution.py:26
  78.0 14.9 %collective-permute-start.6 = (bf16[2,512,256]{2,1,0:T(8,128)(2,1)S(1)}, bf16[2,512,256]{2,1,0:T(8,128)(2,1)S(1)}, u32[]{:S(2)}, u32[]{:S(2)}) collective-permute-start(bf16[2,512,256]{2,1,0:T(8,128)(2,1)S(1)} %get-tuple-element.30), channel_id=1, source_target_pairs={{0,1},{1,2},{2,3},{4,5},{5,6},{6,7},{8,9},{9,10},{10,11},{12,13},{... | collective-permute-start | bytes 1572872 | tf_op jit(solution)/shard_map/ppermute | solution.py:26
  92.9 21.0 %collective-permute-start.7 = (bf16[2,768,512]{2,1,0:T(8,128)(2,1)S(1)}, bf16[2,768,512]{2,1,0:T(8,128)(2,1)S(1)}, u32[]{:S(2)}, u32[]{:S(2)}) collective-permute-start(bf16[2,768,512]{2,1,0:T(8,128)(2,1)S(1)} %get-tuple-element.32), channel_id=1, source_target_pairs={{0,4},{4,8},{8,12},{12,16},{16,20},{20,24},{24,28},{28,32},{32,36}... | collective-permute-start | bytes 4718600 | tf_op jit(solution)/shard_map/ppermute | solution.py:26
  96.8 27.0 %collective-permute-start.5 = (bf16[2,512,512]{2,1,0:T(8,128)(2,1)S(1)}, bf16[2,512,512]{2,1,0:T(8,128)(2,1)S(1)}, u32[]{:S(2)}, u32[]{:S(2)}) collective-permute-start(bf16[2,512,512]{2,1,0:T(8,128)(2,1)S(1)} %add_convert_fusion), channel_id=1, source_target_pairs={{0,1},{1,2},{2,3},{4,5},{5,6},{6,7},{8,9},{9,10},{10,11},{12,13},{... | collective-permute-start | bytes 3145736 | tf_op jit(solution)/shard_map/ppermute | solution.py:26

commit v5 on v4

--- a/solution.py
+++ b/solution.py
@@ -17,6 +17,7 @@
 TB = T // Q
 F = T - W
 SOLVE_MIB = 24
+PACK_MIB = 52
 R = 16
 f32, bf16 = jnp.float32, jnp.bfloat16
 
@@ -88,43 +89,58 @@
     return pl.CostEstimate(flops=1024, bytes_accessed=1024, transcendentals=0)
 
 
-def pack_kernel(slab_ref, near_ref, far_ref, right_ref, buf, sem):
-    step = T // 6
+def pack_kernel(slab_ref, *refs):
+    outs, halves, (buf, sem, out_sem) = refs[:4], refs[4:8], refs[8:]
+    pieces = 6
+    step = T // pieces
 
     def copy(c):
         rows = pl.ds(c * step, step)
         return pltpu.make_async_copy(slab_ref.at[:, rows, :], buf.at[:, rows, :], sem.at[c])
 
-    for c in range(6):
+    def copies_out(c):
+        rows = pl.ds(c * step, step)
+        return [
+            pltpu.make_async_copy(half.at[:, rows, :], o.at[:, rows, :], out_sem.at[c, k])
+            for k, (half, o) in enumerate(zip(halves, outs))
+            if (c + 1) * step <= o.shape[1]
+        ]
+
+    for c in range(pieces):
         copy(c).start()
-    for c in range(6):
+    for c in range(pieces):
         copy(c).wait()
-
-        def convert(row):
-            here = pl.ds(pl.multiple_of(c * step + row, R), R)
-            for p in range(2):
+        for p in range(2):
+            for row in range(c * step, (c + 1) * step, 2 * R):
+                here = pl.ds(row, 2 * R)
                 part = buf[p, here, :].astype(bf16)
-                right_ref[p, here, :] = part[:, :W]
-                if (c + 1) * step <= W:
-                    near_ref[p, here, :] = part[:, :W]
-                    far_ref[p, here, :] = part[:, W:]
-
-        each_rows(step, convert)
+                if row < W:
+                    halves[0][p, here, :] = part[:, : 2 * Q]
+                    halves[1][p, here, :] = part[:, 2 * Q : W]
+                    halves[2][p, here, :] = part[:, W:]
+                halves[3][p, here, :] = part[:, :W]
+        for one in copies_out(c):
+            one.start()
+    for c in range(pieces):
+        for one in copies_out(c):
+            one.wait()
 
 
 def pack(slab):
+    shapes = [(2, W, 2 * Q)] * 3 + [(2, T, W)]
     return pl.pallas_call(
         pack_kernel,
         in_specs=[ANY],
-        out_specs=[VMEM] * 3,
-        out_shape=[
-            jax.ShapeDtypeStruct((2, W, W), bf16),
-            jax.ShapeDtypeStruct((2, W, F), bf16),
-            jax.ShapeDtypeStruct((2, T, W), bf16),
+        out_specs=[ANY] * 4,
+        out_shape=[jax.ShapeDtypeStruct(shape, bf16) for shape in shapes],
+        scratch_shapes=[pltpu.VMEM(shape, bf16) for shape in shapes]
+        + [
+            pltpu.VMEM((2, T, T), f32),
+            pltpu.SemaphoreType.DMA((6,)),
+            pltpu.SemaphoreType.DMA((6, 4)),
         ],
-        scratch_shapes=[pltpu.VMEM((2, T, T), f32), pltpu.SemaphoreType.DMA((6,))],
         cost_estimate=cost(),
-        compiler_params=params(52),
+        compiler_params=params(PACK_MIB),
     )(slab)
 
 
@@ -155,9 +171,11 @@
     meta_ref,
     slab_ref,
     right_ref,
-    near_ref,
+    near0_ref,
+    near1_ref,
     far_ref,
-    corner_ref,
+    corner0_ref,
+    corner1_ref,
     probe_ref,
     meas_ref,
     ga_ref,
@@ -194,11 +212,12 @@
         rows = pl.ds(row, R)
         there = pl.ds(pl.multiple_of(T + row, R), R)
         for p in range(2):
-            for b in range(4):
-                ext[p, b, there, :] = near_ref[p, rows, lanes(b)].astype(f32)
-                ext[p, TB + b, there, :] = corner_ref[p, rows, lanes(b)].astype(f32)
             for b in range(2):
+                ext[p, b, there, :] = near0_ref[p, rows, lanes(b)].astype(f32)
+                ext[p, 2 + b, there, :] = near1_ref[p, rows, lanes(b)].astype(f32)
                 ext[p, 4 + b, there, :] = far_ref[p, rows, lanes(b)].astype(f32)
+                ext[p, TB + b, there, :] = corner0_ref[p, rows, lanes(b)].astype(f32)
+                ext[p, TB + 2 + b, there, :] = corner1_ref[p, rows, lanes(b)].astype(f32)
 
     each_rows(E, clear)
     each_rows(T, fill_right)
@@ -307,10 +326,10 @@
     lax.fori_loop(0, live_ref[0], one_slot, 0)
 
 
-def solve(live, meta, slab, right, near, far, corner, probe, measured, left, left_t):
+def solve(live, meta, slab, right, below, corner, probe, measured, left, left_t):
     return pl.pallas_call(
         slots_kernel,
-        in_specs=[SMEM, SMEM, ANY] + [VMEM] * 8,
+        in_specs=[SMEM, SMEM, ANY] + [VMEM] * 10,
         out_specs=VMEM,
         out_shape=TILES,
         scratch_shapes=[
@@ -323,7 +342,7 @@
         ],
         cost_estimate=cost(),
         compiler_params=params(SOLVE_MIB),
-    )(live, meta, slab, right, near, far, corner, probe, measured, left, left_t)
+    )(live, meta, slab, right, *below, *corner, probe, measured, left, left_t)
 
 
 def drain_kernel(grown, to_near_ref, to_far_ref, to_corner_ref, to_right_ref):
@@ -446,24 +465,27 @@
 def shards(slab, probe, intensities, offsets, live_count):
     left, left_t, pick = tables()
     left, left_t = jnp.asarray(left), jnp.asarray(left_t)
-    near, far, right = pack(slab)
-    near = shifted(near, "tile", -1)
+    near0, near1, far, right = pack(slab)
+    near0 = shifted(near0, "tile", -1)
+    near1 = shifted(near1, "tile", -1)
     far = shifted(far, "tile", -1)
     right = shifted(right, "scan", -1)
     measured = sort_intensities(intensities[0, 0], pick, probe, left, left_t)
     live = lax.dynamic_slice(live_count[:, 0], (lax.axis_index("scan"),), (1,))
     shifts = offsets[0, 0].T
-    near, measured, live, shifts = lax.optimization_barrier((near, measured, live, shifts))
-    corner = shifted(near, "scan", -1)
+    near0, measured, live, shifts = lax.optimization_barrier((near0, measured, live, shifts))
+    corner0 = shifted(near0, "scan", -1)
+    corner1 = shifted(near1, "scan", -1)
     grown = solve(
-        live, shifts, slab, right, near, far, corner, probe, measured, left, left_t
+        live, shifts, slab, right, (near0, near1, far), (corner0, corner1), probe, measured,
+        left, left_t,
     )
     near, far, corner, right = drain(grown)
     far = shifted(far, "tile", 1)
     corner = shifted(corner, "scan", 1)
     near = (near.astype(f32) + corner.astype(f32)).astype(bf16)
+    near, far = lax.optimization_barrier((near, far))
     near = shifted(near, "tile", 1)
-    far, right = lax.optimization_barrier((far, right))
     right = shifted(right, "scan", 1)
     grown, whole = add_side(right, far, grown)
     return add_near(near, grown, whole)

time: 127 us -> 121 us (0.953)
  the two profiles are of different devices: /device:TPU:73 before, /device:TPU:82 now
where the time goes in v5:
time: 121 us; the launch traced here: 120 us
  waiting for transfers between devices  53.5 us (44%)
  Pallas kernels  39.3 us (32%)
  starting transfers between devices  21.7 us (18%)
  local copies, waits for them, and re-layouts  4.94 us (4%)
    ppermute x10, waiting for transfers between devices, shifted(): lax.ppermute(value, axis, [(i, i + by) for i in range(n) if 0 <= i + by <...  53.5 us
    pallas_call x1, Pallas kernels, solve(): pl.pallas_call(slots_kernel, in_specs=[SMEM, SMEM, ANY] + [VMEM] * 10, ou...  25.8 us
    ppermute x10, starting transfers between devices, shifted(): lax.ppermute(value, axis, [(i, i + by) for i in range(n) if 0 <= i + by <...  21.7 us
    pallas_call x1, Pallas kernels, sort_intensities(): pl.pallas_call(sort_kernel, grid=(measured.shape[0],), in_specs=[whole, w...  4.3 us
    unnamed x20, local copies, waits for them, and re-layouts  4.29 us
    pallas_call x1, Pallas kernels, pack(): pl.pallas_call(pack_kernel, in_specs=[ANY], out_specs=[ANY] * 4, out_shap...  4.1 us
  transfers between devices with their start and end apart: 10, of which 7 were waited for; matrix products, arithmetic and copies ran while one was open for 1% of the time, Pallas kernels for 5%

profile of v5, /device:TPU:82, one launch (start us, length us, event | category | flops | bytes accessed | tf_op | source)
XLA Modules:
  0.0 119.9 jit_solution(10412187283324111424)
XLA Ops:
  0.0 4.1 %shard_map.91 = (bf16[2,512,256]{2,1,0:T(8,128)(2,1)}, bf16[2,512,256]{2,1,0:T(8,128)(2,1)}, bf16[2,512,256]{2,1,0:T(8,128)(2,1)}, bf16[2,768,512]{2,1,0:T(8,128)(2,1)}) custom-call(f32[2,768,768]{2,1,0:T(8,128)} %slab_ref.3), custom_call_target="tpu_custom_call" | custom-call | flops 1024 | bytes 1024 | tf_op jit(solution)/shard_map/pallas_call | solution.py:131
  4.1 1.9 %collective-permute-start.1 = (bf16[2,768,512]{2,1,0:T(8,128)(2,1)}, bf16[2,768,512]{2,1,0:T(8,128)(2,1)}, u32[]{:S(2)}, u32[]{:S(2)}) collective-permute-start(bf16[2,768,512]{2,1,0:T(8,128)(2,1)} %get-tuple-element.25), channel_id=1, source_target_pairs={{4,0},{8,4},{12,8},{16,12},{20,16},{24,20},{28,24},{32,28},{36,32}... | collective-permute-start | bytes 4718600 | tf_op jit(solution)/shard_map/ppermute | solution.py:27
  6.1 2.4 %collective-permute-start = (bf16[2,512,256]{2,1,0:T(8,128)(2,1)}, bf16[2,512,256]{2,1,0:T(8,128)(2,1)}, u32[]{:S(2)}, u32[]{:S(2)}) collective-permute-start(bf16[2,512,256]{2,1,0:T(8,128)(2,1)} %get-tuple-element.22), channel_id=1, source_target_pairs={{1,0},{2,1},{3,2},{5,4},{6,5},{7,6},{9,8},{10,9},{11,10},{13,12},{... | collective-permute-start | bytes 1572872 | tf_op jit(solution)/shard_map/ppermute | solution.py:27
  8.4 2.4 %collective-permute-start.2 = (bf16[2,512,256]{2,1,0:T(8,128)(2,1)}, bf16[2,512,256]{2,1,0:T(8,128)(2,1)}, u32[]{:S(2)}, u32[]{:S(2)}) collective-permute-start(bf16[2,512,256]{2,1,0:T(8,128)(2,1)} %get-tuple-element.27), channel_id=1, source_target_pairs={{1,0},{2,1},{3,2},{5,4},{6,5},{7,6},{9,8},{10,9},{11,10},{13,12},{... | collective-permute-start | bytes 1572872 | tf_op jit(solution)/shard_map/ppermute | solution.py:27
  10.8 1.9 %collective-permute-start.3 = (bf16[2,512,256]{2,1,0:T(8,128)(2,1)}, bf16[2,512,256]{2,1,0:T(8,128)(2,1)}, u32[]{:S(2)}, u32[]{:S(2)}) collective-permute-start(bf16[2,512,256]{2,1,0:T(8,128)(2,1)} %get-tuple-element.28), channel_id=1, source_target_pairs={{1,0},{2,1},{3,2},{5,4},{6,5},{7,6},{9,8},{10,9},{11,10},{13,12},{... | collective-permute-start | bytes 1572872 | tf_op jit(solution)/shard_map/ppermute | solution.py:27
  12.7 0.6 constant_dynamic-slice_fusion
  13.4 0.0 copy-start.5
  13.4 2.0 %copy-done.5 = bf16[1,1,6,512,512]{4,3,2,1,0:T(8,128)(2,1)S(1)} copy-done((bf16[1,1,6,512,512]{4,3,2,1,0:T(8,128)(2,1)S(1)}, bf16[1,1,6,512,512]{4,3,2,1,0:T(8,128)(2,1)}, u32[]{:S(2)}) %copy-start.5) | copy-done | bytes 3145752
  15.4 1.2 copy-done.6
  16.6 1.0 copy-done.7
  17.7 4.3 %shard_map.92.meas_ref = bf16[6,512,512]{2,1,0:T(8,128)(2,1)S(1)} custom-call(bf16[512,512]{1,0:T(8,128)(2,1)S(1)} %copy-done.7, bf16[512,512]{1,0:T(8,128)(2,1)S(1)} %copy-done.6, bf16[6,512,512]{2,1,0:T(8,128)(2,1)S(1)} %bitcast.8, f32[2,512,512]{2,1,0:T(8,128)S(1)} %copy-done.1, bf16[4,256,256]{2,1,0:T(8,128)(2,1)S(1)} %copy-done.3, ...), custom_call_target="tpu_custom_call" | custom-call | flops 3221225472 | bytes 6291456 | tf_op jit(solution)/shard_map/pallas_call | solution.py:156
  22.0 1.0 collective-permute-done.near0_ref
  23.0 1.9 %collective-permute-start.4 = (bf16[2,512,256]{2,1,0:T(8,128)(2,1)}, bf16[2,512,256]{2,1,0:T(8,128)(2,1)S(1)}, u32[]{:S(2)}, u32[]{:S(2)}) collective-permute-start(bf16[2,512,256]{2,1,0:T(8,128)(2,1)} %collective-permute-done.near0_ref), channel_id=1, source_target_pairs={{4,0},{8,4},{12,8},{16,12},{20,16},{24,20},{28,24},{32,28},{36,32}... | collective-permute-start | bytes 1572872 | tf_op jit(solution)/shard_map/ppermute | solution.py:27
  24.9 9.3 %collective-permute-done.2.near1_ref = bf16[2,512,256]{2,1,0:T(8,128)(2,1)} collective-permute-done((bf16[2,512,256]{2,1,0:T(8,128)(2,1)}, bf16[2,512,256]{2,1,0:T(8,128)(2,1)}, u32[]{:S(2)}, u32[]{:S(2)}) %collective-permute-start.2) | collective-permute-done | bytes 524320 | tf_op jit(solution)/shard_map/ppermute | solution.py:27
  34.2 1.9 %collective-permute-start.5 = (bf16[2,512,256]{2,1,0:T(8,128)(2,1)}, bf16[2,512,256]{2,1,0:T(8,128)(2,1)S(1)}, u32[]{:S(2)}, u32[]{:S(2)}) collective-permute-start(bf16[2,512,256]{2,1,0:T(8,128)(2,1)} %collective-permute-done.2.near1_ref), channel_id=1, source_target_pairs={{4,0},{8,4},{12,8},{16,12},{20,16},{24,20},{28,24},{32,28},{36,32}... | collective-permute-start | bytes 1572872 | tf_op jit(solution)/shard_map/ppermute | solution.py:27
  36.1 8.9 %collective-permute-done.3.far_ref = bf16[2,512,256]{2,1,0:T(8,128)(2,1)} collective-permute-done((bf16[2,512,256]{2,1,0:T(8,128)(2,1)}, bf16[2,512,256]{2,1,0:T(8,128)(2,1)}, u32[]{:S(2)}, u32[]{:S(2)}) %collective-permute-start.3) | collective-permute-done | bytes 524320 | tf_op jit(solution)/shard_map/ppermute | solution.py:27
  45.1 0.0 collective-permute-done.4.corner0_ref
  45.1 0.0 collective-permute-done.5.corner1_ref
  45.1 0.0 collective-permute-done.1.right_ref
  45.1 25.8 %shard_map.93.grown.grown_in = f32[2,10,1280,128]{3,2,1,0:T(8,128)S(1)} custom-call(s32[1]{0:T(128)} %bitcast.1.live_ref, s32[2,6]{1,0:T(2,128)S(1)} %bitcast.7, f32[2,768,768]{2,1,0:T(8,128)S(1)} %bitcast.6, bf16[2,768,512]{2,1,0:T(8,128)(2,1)} %collective-permute-done.1.right_ref, bf16[2,512,256]{2,1,0:T(8,128)(2,1)} %collective-permute-done.near0_ref, ...), custom_call_target="tpu_custom_call" | custom-call | flops 1024 | bytes 1024 | tf_op jit(solution)/shard_map/pallas_call | solution.py:330
  70.9 0.9 shard_map.94
  71.8 1.9 %collective-permute-start.6 = (bf16[2,512,512]{2,1,0:T(8,128)(2,1)S(1)}, bf16[2,512,512]{2,1,0:T(8,128)(2,1)S(1)}, u32[]{:S(2)}, u32[]{:S(2)}) collective-permute-start(bf16[2,512,512]{2,1,0:T(8,128)(2,1)S(1)} %get-tuple-element.31), channel_id=1, source_target_pairs={{0,4},{4,8},{8,12},{12,16},{16,20},{20,24},{24,28},{28,32},{32,36}... | collective-permute-start | bytes 3145736 | tf_op jit(solution)/shard_map/ppermute | solution.py:27
  73.8 1.9 %collective-permute-start.7 = (bf16[2,512,256]{2,1,0:T(8,128)(2,1)S(1)}, bf16[2,512,256]{2,1,0:T(8,128)(2,1)S(1)}, u32[]{:S(2)}, u32[]{:S(2)}) collective-permute-start(bf16[2,512,256]{2,1,0:T(8,128)(2,1)S(1)} %get-tuple-element.32), channel_id=1, source_target_pairs={{0,1},{1,2},{2,3},{4,5},{5,6},{6,7},{8,9},{9,10},{10,11},{12,13},{... | collective-permute-start | bytes 1572872 | tf_op jit(solution)/shard_map/ppermute | solution.py:27
  75.7 3.5 %collective-permute-start.9 = (bf16[2,768,512]{2,1,0:T(8,128)(2,1)S(1)}, bf16[2,768,512]{2,1,0:T(8,128)(2,1)S(1)}, u32[]{:S(2)}, u32[]{:S(2)}) collective-permute-start(bf16[2,768,512]{2,1,0:T(8,128)(2,1)S(1)} %get-tuple-element.34), channel_id=1, source_target_pairs={{0,4},{4,8},{8,12},{12,16},{16,20},{20,24},{24,28},{28,32},{32,36}... | collective-permute-start | bytes 4718600 | tf_op jit(solution)/shard_map/ppermute | solution.py:27
  79.2 8.7 %collective-permute-done.6 = bf16[2,512,512]{2,1,0:T(8,128)(2,1)S(1)} collective-permute-done((bf16[2,512,512]{2,1,0:T(8,128)(2,1)S(1)}, bf16[2,512,512]{2,1,0:T(8,128)(2,1)S(1)}, u32[]{:S(2)}, u32[]{:S(2)}) %collective-permute-start.6) | collective-permute-done | bytes 1048608 | tf_op jit(solution)/shard_map/ppermute | solution.py:27
  88.0 0.3 add_convert_fusion
  88.2 1.6 %collective-permute-done.7.far_ref = bf16[2,512,256]{2,1,0:T(8,128)(2,1)S(1)} collective-permute-done((bf16[2,512,256]{2,1,0:T(8,128)(2,1)S(1)}, bf16[2,512,256]{2,1,0:T(8,128)(2,1)S(1)}, u32[]{:S(2)}, u32[]{:S(2)}) %collective-permute-start.7) | collective-permute-done | bytes 524320 | tf_op jit(solution)/shard_map/ppermute | solution.py:27
  89.9 1.9 %collective-permute-start.8 = (bf16[2,512,512]{2,1,0:T(8,128)(2,1)S(1)}, bf16[2,512,512]{2,1,0:T(8,128)(2,1)S(1)}, u32[]{:S(2)}, u32[]{:S(2)}) collective-permute-start(bf16[2,512,512]{2,1,0:T(8,128)(2,1)S(1)} %add_convert_fusion), channel_id=1, source_target_pairs={{0,1},{1,2},{2,3},{4,5},{5,6},{6,7},{8,9},{9,10},{10,11},{12,13},{... | collective-permute-start | bytes 3145736 | tf_op jit(solution)/shard_map/ppermute | solution.py:27
  91.8 13.0 %collective-permute-done.9.right_ref = bf16[2,768,512]{2,1,0:T(8,128)(2,1)S(1)} collective-permute-done((bf16[2,768,512]{2,1,0:T(8,128)(2,1)S(1)}, bf16[2,768,512]{2,1,0:T(8,128)(2,1)S(1)}, u32[]{:S(2)}, u32[]{:S(2)}) %collective-permute-start.9) | collective-permute-done | bytes 1572896 | tf_op jit(solution)/shard_map/ppermute | solution.py:27
  104.8 1.8 %shard_map.95 = (f32[2,10,1280,128]{3,2,1,0:T(8,128)S(1)}, f32[2,768,768]{2,1,0:T(8,128)}) custom-call(bf16[2,768,512]{2,1,0:T(8,128)(2,1)S(1)} %collective-permute-done.9.right_ref, bf16[2,512,256]{2,1,0:T(8,128)(2,1)S(1)} %collective-permute-done.7.far_ref, f32[2,10,1280,128]{3,2,1,0:T(8,128)S(1)} %shard_map.93.grown.grown_in), custom_call_target="tpu_custom_call", output_to_operand_aliasing={{0}: (2, {})} | custom-call | flops 1024 | bytes 1024 | tf_op jit(solution)/shard_map/pallas_call | solution.py:425
  106.6 10.9 %collective-permute-done.8.near_ref = bf16[2,512,512]{2,1,0:T(8,128)(2,1)S(1)} collective-permute-done((bf16[2,512,512]{2,1,0:T(8,128)(2,1)S(1)}, bf16[2,512,512]{2,1,0:T(8,128)(2,1)S(1)}, u32[]{:S(2)}, u32[]{:S(2)}) %collective-permute-start.8) | collective-permute-done | bytes 1048608 | tf_op jit(solution)/shard_map/ppermute | solution.py:27
  117.5 2.4 %shard_map.96 = (f32[2,10,1280,128]{3,2,1,0:T(8,128)S(1)}, f32[2,768,768]{2,1,0:T(8,128)}) custom-call(bf16[2,512,512]{2,1,0:T(8,128)(2,1)S(1)} %collective-permute-done.8.near_ref, f32[2,10,1280,128]{3,2,1,0:T(8,128)S(1)} %get-tuple-element.36.grown_in, f32[2,768,768]{2,1,0:T(8,128)} %get-tuple-element.37.whole_in), custom_call_target="tpu_custom_call", output_to_operand_aliasing={{0}: (1, {}), {1}: (2, {})} | custom-call | flops 1024 | bytes 1024 | tf_op jit(solution)/shard_map/pallas_call | solution.py:453
  (17 shorter events, 0.0 us)
Async XLA Ops:
  0.0 12.7 %copy-start = (s32[32,1]{0,1:T(1,128)S(1)}, s32[32,1]{0,1:T(1,128)}, u32[]{:S(2)}) copy-start(s32[32,1]{0,1:T(1,128)} %param.13) | copy-start | bytes 388
  0.0 13.4 %copy-start.2 = (bf16[4,256,256]{2,1,0:T(8,128)(2,1)S(1)}, bf16[4,256,256]{2,1,0:T(8,128)(2,1)}, u32[]{:S(2)}) copy-start(bf16[4,256,256]{2,1,0:T(8,128)(2,1)} %constant.20.clone.refs_2_.gb_ref) | copy-start | bytes 1572868
  0.0 13.4 %copy-start.3 = (bf16[4,256,256]{2,1,0:T(8,128)(2,1)S(1)}, bf16[4,256,256]{2,1,0:T(8,128)(2,1)}, u32[]{:S(2)}) copy-start(bf16[4,256,256]{2,1,0:T(8,128)(2,1)} %constant.19.clone.refs_1_.ga_ref) | copy-start | bytes 1572868
  0.0 13.4 %copy-start.1 = (f32[2,512,512]{2,1,0:T(8,128)S(1)}, f32[2,512,512]{2,1,0:T(8,128)}, u32[]{:S(2)}) copy-start(f32[2,512,512]{2,1,0:T(8,128)} %probe_ref.1) | copy-start | bytes 6291460
  4.1 40.9 %collective-permute-start.1 = (bf16[2,768,512]{2,1,0:T(8,128)(2,1)}, bf16[2,768,512]{2,1,0:T(8,128)(2,1)}, u32[]{:S(2)}, u32[]{:S(2)}) collective-permute-start(bf16[2,768,512]{2,1,0:T(8,128)(2,1)} %get-tuple-element.25), channel_id=1, source_target_pairs={{4,0},{8,4},{12,8},{16,12},{20,16},{24,20},{28,24},{32,28},{36,32}... | collective-permute-start | bytes 4718600 | tf_op jit(solution)/shard_map/ppermute | solution.py:27
  6.1 16.9 %collective-permute-start = (bf16[2,512,256]{2,1,0:T(8,128)(2,1)}, bf16[2,512,256]{2,1,0:T(8,128)(2,1)}, u32[]{:S(2)}, u32[]{:S(2)}) collective-permute-start(bf16[2,512,256]{2,1,0:T(8,128)(2,1)} %get-tuple-element.22), channel_id=1, source_target_pairs={{1,0},{2,1},{3,2},{5,4},{6,5},{7,6},{9,8},{10,9},{11,10},{13,12},{... | collective-permute-start | bytes 1572872 | tf_op jit(solution)/shard_map/ppermute | solution.py:27
  8.4 25.8 %collective-permute-start.2 = (bf16[2,512,256]{2,1,0:T(8,128)(2,1)}, bf16[2,512,256]{2,1,0:T(8,128)(2,1)}, u32[]{:S(2)}, u32[]{:S(2)}) collective-permute-start(bf16[2,512,256]{2,1,0:T(8,128)(2,1)} %get-tuple-element.27), channel_id=1, source_target_pairs={{1,0},{2,1},{3,2},{5,4},{6,5},{7,6},{9,8},{10,9},{11,10},{13,12},{... | collective-permute-start | bytes 1572872 | tf_op jit(solution)/shard_map/ppermute | solution.py:27
  10.8 34.3 %collective-permute-start.3 = (bf16[2,512,256]{2,1,0:T(8,128)(2,1)}, bf16[2,512,256]{2,1,0:T(8,128)(2,1)}, u32[]{:S(2)}, u32[]{:S(2)}) collective-permute-start(bf16[2,512,256]{2,1,0:T(8,128)(2,1)} %get-tuple-element.28), channel_id=1, source_target_pairs={{1,0},{2,1},{3,2},{5,4},{6,5},{7,6},{9,8},{10,9},{11,10},{13,12},{... | collective-permute-start | bytes 1572872 | tf_op jit(solution)/shard_map/ppermute | solution.py:27
  13.4 31.7 %slice-start = ((s8[4718592]{0:T(1024)(128)(4,1)}), s8[4194304]{0:T(1024)(128)(4,1)S(1)}, s32[]{:S(2)}) async-start(s8[4718592]{0:T(1024)(128)(4,1)} %bitcast.5), calls=%async_computation | async-start | bytes 8388608
  13.4 2.0 %copy-start.5 = (bf16[1,1,6,512,512]{4,3,2,1,0:T(8,128)(2,1)S(1)}, bf16[1,1,6,512,512]{4,3,2,1,0:T(8,128)(2,1)}, u32[]{:S(2)}) copy-start(bf16[1,1,6,512,512]{4,3,2,1,0:T(8,128)(2,1)} %param.11) | copy-start | bytes 9437188
  15.4 1.2 copy-start.6
  16.6 1.0 copy-start.7
  17.7 27.4 %slice-start.1 = ((s8[4718592]{0:T(1024)(128)(4,1)}), s8[524288]{0:T(1024)(128)(4,1)S(1)}, s32[]{:S(2)}) async-start(s8[4718592]{0:T(1024)(128)(4,1)} %bitcast.5), calls=%async_computation.1 | async-start | bytes 1048576
  17.7 27.4 %copy-start.4 = (s32[1,1,6,2]{2,3,1,0:T(2,128)S(1)}, s32[1,1,6,2]{2,3,1,0:T(2,128)}, u32[]{:S(2)}) copy-start(s32[1,1,6,2]{2,3,1,0:T(2,128)} %param.12) | copy-start | bytes 148
  23.0 22.1 %collective-permute-start.4 = (bf16[2,512,256]{2,1,0:T(8,128)(2,1)}, bf16[2,512,256]{2,1,0:T(8,128)(2,1)S(1)}, u32[]{:S(2)}, u32[]{:S(2)}) collective-permute-start(bf16[2,512,256]{2,1,0:T(8,128)(2,1)} %collective-permute-done.near0_ref), channel_id=1, source_target_pairs={{4,0},{8,4},{12,8},{16,12},{20,16},{24,20},{28,24},{32,28},{36,32}... | collective-permute-start | bytes 1572872 | tf_op jit(solution)/shard_map/ppermute | solution.py:27
  34.2 10.8 %collective-permute-start.5 = (bf16[2,512,256]{2,1,0:T(8,128)(2,1)}, bf16[2,512,256]{2,1,0:T(8,128)(2,1)S(1)}, u32[]{:S(2)}, u32[]{:S(2)}) collective-permute-start(bf16[2,512,256]{2,1,0:T(8,128)(2,1)} %collective-permute-done.2.near1_ref), channel_id=1, source_target_pairs={{4,0},{8,4},{12,8},{16,12},{20,16},{24,20},{28,24},{32,28},{36,32}... | collective-permute-start | bytes 1572872 | tf_op jit(solution)/shard_map/ppermute | solution.py:27
  71.8 16.1 %collective-permute-start.6 = (bf16[2,512,512]{2,1,0:T(8,128)(2,1)S(1)}, bf16[2,512,512]{2,1,0:T(8,128)(2,1)S(1)}, u32[]{:S(2)}, u32[]{:S(2)}) collective-permute-start(bf16[2,512,512]{2,1,0:T(8,128)(2,1)S(1)} %get-tuple-element.31), channel_id=1, source_target_pairs={{0,4},{4,8},{8,12},{12,16},{16,20},{20,24},{24,28},{28,32},{32,36}... | collective-permute-start | bytes 3145736 | tf_op jit(solution)/shard_map/ppermute | solution.py:27
  73.8 16.1 %collective-permute-start.7 = (bf16[2,512,256]{2,1,0:T(8,128)(2,1)S(1)}, bf16[2,512,256]{2,1,0:T(8,128)(2,1)S(1)}, u32[]{:S(2)}, u32[]{:S(2)}) collective-permute-start(bf16[2,512,256]{2,1,0:T(8,128)(2,1)S(1)} %get-tuple-element.32), channel_id=1, source_target_pairs={{0,1},{1,2},{2,3},{4,5},{5,6},{6,7},{8,9},{9,10},{10,11},{12,13},{... | collective-permute-start | bytes 1572872 | tf_op jit(solution)/shard_map/ppermute | solution.py:27
  75.7 29.1 %collective-permute-start.9 = (bf16[2,768,512]{2,1,0:T(8,128)(2,1)S(1)}, bf16[2,768,512]{2,1,0:T(8,128)(2,1)S(1)}, u32[]{:S(2)}, u32[]{:S(2)}) collective-permute-start(bf16[2,768,512]{2,1,0:T(8,128)(2,1)S(1)} %get-tuple-element.34), channel_id=1, source_target_pairs={{0,4},{4,8},{8,12},{12,16},{16,20},{20,24},{24,28},{28,32},{32,36}... | collective-permute-start | bytes 4718600 | tf_op jit(solution)/shard_map/ppermute | solution.py:27
  89.9 27.7 %collective-permute-start.8 = (bf16[2,512,512]{2,1,0:T(8,128)(2,1)S(1)}, bf16[2,512,512]{2,1,0:T(8,128)(2,1)S(1)}, u32[]{:S(2)}, u32[]{:S(2)}) collective-permute-start(bf16[2,512,512]{2,1,0:T(8,128)(2,1)S(1)} %add_convert_fusion), channel_id=1, source_target_pairs={{0,1},{1,2},{2,3},{4,5},{5,6},{6,7},{8,9},{9,10},{10,11},{12,13},{... | collective-permute-start | bytes 3145736 | tf_op jit(solution)/shard_map/ppermute | solution.py:27

commit v6 on v5

--- a/solution.py
+++ b/solution.py
@@ -17,6 +17,7 @@
 TB = T // Q
 F = T - W
 SOLVE_MIB = 24
+RP = 2
 PACK_MIB = 52
 R = 16
 f32, bf16 = jnp.float32, jnp.bfloat16
@@ -345,38 +346,37 @@
     )(live, meta, slab, right, *below, *corner, probe, measured, left, left_t)
 
 
-def drain_kernel(grown, to_near_ref, to_far_ref, to_corner_ref, to_right_ref):
-    def drain_below(row):
+def drain_kernel(grown, near0_ref, near1_ref, far_ref, corner0_ref, corner1_ref, *right_refs):
+    def below(row):
         rows = pl.ds(row, R)
         here = pl.ds(pl.multiple_of(T + row, R), R)
         for p in range(2):
+            for b in range(2):
+                near0_ref[p, rows, lanes(b)] = grown[p, b, here, :].astype(bf16)
+                near1_ref[p, rows, lanes(b)] = grown[p, 2 + b, here, :].astype(bf16)
+                far_ref[p, rows, lanes(b)] = grown[p, 4 + b, here, :].astype(bf16)
+                corner0_ref[p, rows, lanes(b)] = grown[p, TB + b, here, :].astype(bf16)
+                corner1_ref[p, rows, lanes(b)] = grown[p, TB + 2 + b, here, :].astype(bf16)
+
+    def right(row):
+        rows = pl.ds(row, R)
+        here = pl.ds(pl.multiple_of(piece * (T // RP) + row, R), R)
+        for p in range(2):
             for b in range(4):
-                to_near_ref[p, rows, lanes(b)] = grown[p, b, here, :].astype(bf16)
-                to_corner_ref[p, rows, lanes(b)] = grown[p, TB + b, here, :].astype(bf16)
-            for b in range(2):
-                to_far_ref[p, rows, lanes(b)] = grown[p, 4 + b, here, :].astype(bf16)
-
-    def drain_right(row):
-        rows = pl.ds(row, R)
-        for p in range(2):
-            for b in range(4):
-                to_right_ref[p, rows, lanes(b)] = grown[p, TB + b, rows, :].astype(bf16)
-
-    each_rows(W, drain_below)
-    each_rows(T, drain_right)
+                right_refs[piece][p, rows, lanes(b)] = grown[p, TB + b, here, :].astype(bf16)
+
+    each_rows(W, below)
+    for piece in range(RP):
+        each_rows(T // RP, right)
 
 
 def drain(grown):
     return pl.pallas_call(
         drain_kernel,
         in_specs=[VMEM],
-        out_specs=[VMEM] * 4,
-        out_shape=[
-            jax.ShapeDtypeStruct((2, W, W), bf16),
-            jax.ShapeDtypeStruct((2, W, F), bf16),
-            jax.ShapeDtypeStruct((2, W, W), bf16),
-            jax.ShapeDtypeStruct((2, T, W), bf16),
-        ],
+        out_specs=[VMEM] * (5 + RP),
+        out_shape=[jax.ShapeDtypeStruct((2, W, 2 * Q), bf16)] * 5
+        + [jax.ShapeDtypeStruct((2, T // RP, W), bf16)] * RP,
         cost_estimate=cost(),
         compiler_params=params(4),
     )(grown)
@@ -389,30 +389,37 @@
     )
 
 
-def side_kernel(right_ref, far_ref, grown_in, grown, whole_ref, sem):
+def side_kernel(*refs):
+    right_refs, (far_ref, near1_ref, grown_in, grown, whole_ref, sem) = refs[:RP], refs[RP:]
+
     def done(p, b):
-        if b < 4:
+        if b < 2:
             return write_copy(grown, whole_ref, sem, p, b, W, T - W)
         return write_copy(grown, whole_ref, sem, p, b, 0, T)
 
-    def far(row):
-        rows = pl.ds(row, R)
-        for p in range(2):
-            for b in range(2):
-                grown[p, 4 + b, rows, :] += far_ref[p, rows, lanes(b)].astype(f32)
-
-    each_rows(W, far)
-    for p in range(2):
-        for b in range(4, TB):
-            done(p, b).start()
+    for part, first in ((far_ref, 4), (near1_ref, 2)):
+
+        def below(row):
+            rows = pl.ds(row, R)
+            for p in range(2):
+                for b in range(2):
+                    grown[p, first + b, rows, :] += part[p, rows, lanes(b)].astype(f32)
+
+        each_rows(W, below)
+        if first == 4:
+            for p in range(2):
+                for b in range(4, TB):
+                    done(p, b).start()
 
     def right(row):
         rows = pl.ds(row, R)
+        here = pl.ds(pl.multiple_of(piece * (T // RP) + row, R), R)
         for p in range(2):
             for b in range(4):
-                grown[p, b, rows, :] += right_ref[p, rows, lanes(b)].astype(f32)
-
-    each_rows(T, right)
+                grown[p, b, here, :] += right_refs[piece][p, rows, lanes(b)].astype(f32)
+
+    for piece in range(RP):
+        each_rows(T // RP, right)
     for p in range(2):
         for b in range(4):
             done(p, b).start()
@@ -421,32 +428,31 @@
             done(p, b).wait()
 
 
-def add_side(right, far, grown):
+def add_side(right, far, near1, grown):
     return pl.pallas_call(
         side_kernel,
-        in_specs=[VMEM] * 3,
+        in_specs=[VMEM] * (3 + RP),
         out_specs=[VMEM, ANY],
         out_shape=[TILES, jax.ShapeDtypeStruct((2, T, T), f32)],
-        input_output_aliases={2: 0},
+        input_output_aliases={2 + RP: 0},
         scratch_shapes=[pltpu.SemaphoreType.DMA((2, TB))],
         cost_estimate=cost(),
         compiler_params=params(4),
-    )(right, far, grown)
+    )(*right, far, near1, grown)
 
 
 def last_kernel(near_ref, grown_in, whole_in, grown, whole_ref, sem):
-    for b in range(4):
-        for p in range(2):
-
-            def add(row):
-                rows = pl.ds(row, R)
-                grown[p, b, rows, :] += near_ref[p, rows, lanes(b)].astype(f32)
-
-            each_rows(W, add)
-            write_copy(grown, whole_ref, sem, p, b, 0, W).start()
-    for b in range(4):
-        for p in range(2):
-            write_copy(grown, whole_ref, sem, p, b, 0, W).wait()
+    for half in range(2):
+        for b in range(2):
+            for p in range(2):
+                for row in range(half * W // 2, (half + 1) * W // 2, 2 * R):
+                    rows = pl.ds(row, 2 * R)
+                    grown[p, b, rows, :] += near_ref[p, rows, lanes(b)].astype(f32)
+                write_copy(grown, whole_ref, sem.at[half], p, b, half * W // 2, W // 2).start()
+    for half in range(2):
+        for b in range(2):
+            for p in range(2):
+                write_copy(grown, whole_ref, sem.at[half], p, b, half * W // 2, W // 2).wait()
 
 
 def add_near(near, grown, whole):
@@ -456,7 +462,7 @@
         out_specs=[VMEM, ANY],
         out_shape=[TILES, jax.ShapeDtypeStruct((2, T, T), f32)],
         input_output_aliases={1: 0, 2: 1},
-        scratch_shapes=[pltpu.SemaphoreType.DMA((2, 4))],
+        scratch_shapes=[pltpu.SemaphoreType.DMA((2, 2, 2))],
         cost_estimate=cost(),
         compiler_params=params(4),
     )(near, grown, whole)[1]
@@ -480,15 +486,19 @@
         live, shifts, slab, right, (near0, near1, far), (corner0, corner1), probe, measured,
         left, left_t,
     )
-    near, far, corner, right = drain(grown)
+    near0, near1, far, corner0, corner1, *right = drain(grown)
+    corner1 = shifted(corner1, "scan", 1)
     far = shifted(far, "tile", 1)
-    corner = shifted(corner, "scan", 1)
-    near = (near.astype(f32) + corner.astype(f32)).astype(bf16)
-    near, far = lax.optimization_barrier((near, far))
-    near = shifted(near, "tile", 1)
-    right = shifted(right, "scan", 1)
-    grown, whole = add_side(right, far, grown)
-    return add_near(near, grown, whole)
+    corner0 = shifted(corner0, "scan", 1)
+    near1 = (near1.astype(f32) + corner1.astype(f32)).astype(bf16)
+    corner0, near1 = lax.optimization_barrier((corner0, near1))
+    near0 = (near0.astype(f32) + corner0.astype(f32)).astype(bf16)
+    near1 = shifted(near1, "tile", 1)
+    right = [shifted(piece, "scan", 1) for piece in right]
+    near0, far = lax.optimization_barrier((near0, far))
+    near0 = shifted(near0, "tile", 1)
+    grown, whole = add_side(right, far, near1, grown)
+    return add_near(near0, grown, whole)
 
 
 def solution(mesh):

time: 121 us -> 118 us (0.975)
  the two profiles are of different devices: /device:TPU:82 before, /device:TPU:22 now
where the time goes in v6:
time: 118 us; the launch traced here: 116 us
  waiting for transfers between devices  39.9 us (34%)
  starting transfers between devices  35.6 us (30%)
  Pallas kernels  34.9 us (30%)
  local copies, waits for them, and re-layouts  4.64 us (4%)
    ppermute x13, waiting for transfers between devices, shifted(): lax.ppermute(value, axis, [(i, i + by) for i in range(n) if 0 <= i + by <...  39.9 us
    ppermute x13, starting transfers between devices, shifted(): lax.ppermute(value, axis, [(i, i + by) for i in range(n) if 0 <= i + by <...  35.6 us
    pallas_call x1, Pallas kernels, solve(): pl.pallas_call(slots_kernel, in_specs=[SMEM, SMEM, ANY] + [VMEM] * 10, ou...  22.1 us
    pallas_call x1, Pallas kernels, sort_intensities(): pl.pallas_call(sort_kernel, grid=(measured.shape[0],), in_specs=[whole, w...  4.3 us
    pallas_call x1, Pallas kernels, pack(): pl.pallas_call(pack_kernel, in_specs=[ANY], out_specs=[ANY] * 4, out_shap...  4.1 us
    unnamed x18, local copies, waits for them, and re-layouts  3.99 us
    pallas_call x1, Pallas kernels, add_side(): pl.pallas_call(side_kernel, in_specs=[VMEM] * (3 + RP), out_specs=[VMEM,...  2.39 us
  transfers between devices with their start and end apart: 13, of which 8 were waited for; matrix products, arithmetic and copies ran while one was open for 1% of the time, Pallas kernels for 6%

profile of v6, /device:TPU:22, one launch (start us, length us, event | category | flops | bytes accessed | tf_op | source)
XLA Modules:
  0.0 115.5 jit_solution(5184409390079345473)
XLA Ops:
  0.0 4.1 %shard_map.91 = (bf16[2,512,256]{2,1,0:T(8,128)(2,1)}, bf16[2,512,256]{2,1,0:T(8,128)(2,1)}, bf16[2,512,256]{2,1,0:T(8,128)(2,1)}, bf16[2,768,512]{2,1,0:T(8,128)(2,1)}) custom-call(f32[2,768,768]{2,1,0:T(8,128)} %slab_ref.3), custom_call_target="tpu_custom_call" | custom-call | flops 1024 | bytes 1024 | tf_op jit(solution)/shard_map/pallas_call | solution.py:132
  4.1 5.7 %collective-permute-start.1 = (bf16[2,768,512]{2,1,0:T(8,128)(2,1)}, bf16[2,768,512]{2,1,0:T(8,128)(2,1)}, u32[]{:S(2)}, u32[]{:S(2)}) collective-permute-start(bf16[2,768,512]{2,1,0:T(8,128)(2,1)} %get-tuple-element.30), channel_id=1, source_target_pairs={{4,0},{8,4},{12,8},{16,12},{20,16},{24,20},{28,24},{32,28},{36,32}... | collective-permute-start | bytes 4718600 | tf_op jit(solution)/shard_map/ppermute | solution.py:28
  9.8 2.4 %collective-permute-start = (bf16[2,512,256]{2,1,0:T(8,128)(2,1)}, bf16[2,512,256]{2,1,0:T(8,128)(2,1)}, u32[]{:S(2)}, u32[]{:S(2)}) collective-permute-start(bf16[2,512,256]{2,1,0:T(8,128)(2,1)} %get-tuple-element.27), channel_id=1, source_target_pairs={{1,0},{2,1},{3,2},{5,4},{6,5},{7,6},{9,8},{10,9},{11,10},{13,12},{... | collective-permute-start | bytes 1572872 | tf_op jit(solution)/shard_map/ppermute | solution.py:28
  12.2 2.4 %collective-permute-start.2 = (bf16[2,512,256]{2,1,0:T(8,128)(2,1)}, bf16[2,512,256]{2,1,0:T(8,128)(2,1)}, u32[]{:S(2)}, u32[]{:S(2)}) collective-permute-start(bf16[2,512,256]{2,1,0:T(8,128)(2,1)} %get-tuple-element.32), channel_id=1, source_target_pairs={{1,0},{2,1},{3,2},{5,4},{6,5},{7,6},{9,8},{10,9},{11,10},{13,12},{... | collective-permute-start | bytes 1572872 | tf_op jit(solution)/shard_map/ppermute | solution.py:28
  14.5 1.9 %collective-permute-start.3 = (bf16[2,512,256]{2,1,0:T(8,128)(2,1)}, bf16[2,512,256]{2,1,0:T(8,128)(2,1)}, u32[]{:S(2)}, u32[]{:S(2)}) collective-permute-start(bf16[2,512,256]{2,1,0:T(8,128)(2,1)} %get-tuple-element.33), channel_id=1, source_target_pairs={{1,0},{2,1},{3,2},{5,4},{6,5},{7,6},{9,8},{10,9},{11,10},{13,12},{... | collective-permute-start | bytes 1572872 | tf_op jit(solution)/shard_map/ppermute | solution.py:28
  16.5 0.6 constant_dynamic-slice_fusion
  17.1 1.9 %copy-done.6 = bf16[1,1,6,512,512]{4,3,2,1,0:T(8,128)(2,1)S(1)} copy-done((bf16[1,1,6,512,512]{4,3,2,1,0:T(8,128)(2,1)S(1)}, bf16[1,1,6,512,512]{4,3,2,1,0:T(8,128)(2,1)}, u32[]{:S(2)}) %copy-start.6) | copy-done | bytes 3145752
  19.0 1.0 copy-done.7
  20.1 1.0 copy-done.8
  21.1 4.3 %shard_map.92.meas_ref = bf16[6,512,512]{2,1,0:T(8,128)(2,1)S(1)} custom-call(bf16[512,512]{1,0:T(8,128)(2,1)S(1)} %copy-done.8, bf16[512,512]{1,0:T(8,128)(2,1)S(1)} %copy-done.7, bf16[6,512,512]{2,1,0:T(8,128)(2,1)S(1)} %bitcast.6, f32[2,512,512]{2,1,0:T(8,128)S(1)} %copy-done.2, bf16[4,256,256]{2,1,0:T(8,128)(2,1)S(1)} %copy-done.4, ...), custom_call_target="tpu_custom_call" | custom-call | flops 3221225472 | bytes 6291456 | tf_op jit(solution)/shard_map/pallas_call | solution.py:157
  25.4 1.4 %collective-permute-done.near0_ref = bf16[2,512,256]{2,1,0:T(8,128)(2,1)} collective-permute-done((bf16[2,512,256]{2,1,0:T(8,128)(2,1)}, bf16[2,512,256]{2,1,0:T(8,128)(2,1)}, u32[]{:S(2)}, u32[]{:S(2)}) %collective-permute-start) | collective-permute-done | bytes 524320 | tf_op jit(solution)/shard_map/ppermute | solution.py:28
  26.9 1.9 %collective-permute-start.4 = (bf16[2,512,256]{2,1,0:T(8,128)(2,1)}, bf16[2,512,256]{2,1,0:T(8,128)(2,1)S(1)}, u32[]{:S(2)}, u32[]{:S(2)}) collective-permute-start(bf16[2,512,256]{2,1,0:T(8,128)(2,1)} %collective-permute-done.near0_ref), channel_id=1, source_target_pairs={{4,0},{8,4},{12,8},{16,12},{20,16},{24,20},{28,24},{32,28},{36,32}... | collective-permute-start | bytes 1572872 | tf_op jit(solution)/shard_map/ppermute | solution.py:28
  28.8 9.3 %collective-permute-done.2.near1_ref = bf16[2,512,256]{2,1,0:T(8,128)(2,1)} collective-permute-done((bf16[2,512,256]{2,1,0:T(8,128)(2,1)}, bf16[2,512,256]{2,1,0:T(8,128)(2,1)}, u32[]{:S(2)}, u32[]{:S(2)}) %collective-permute-start.2) | collective-permute-done | bytes 524320 | tf_op jit(solution)/shard_map/ppermute | solution.py:28
  38.1 1.9 %collective-permute-start.5 = (bf16[2,512,256]{2,1,0:T(8,128)(2,1)}, bf16[2,512,256]{2,1,0:T(8,128)(2,1)S(1)}, u32[]{:S(2)}, u32[]{:S(2)}) collective-permute-start(bf16[2,512,256]{2,1,0:T(8,128)(2,1)} %collective-permute-done.2.near1_ref), channel_id=1, source_target_pairs={{4,0},{8,4},{12,8},{16,12},{20,16},{24,20},{28,24},{32,28},{36,32}... | collective-permute-start | bytes 1572872 | tf_op jit(solution)/shard_map/ppermute | solution.py:28
  40.0 5.1 %collective-permute-done.3.far_ref = bf16[2,512,256]{2,1,0:T(8,128)(2,1)} collective-permute-done((bf16[2,512,256]{2,1,0:T(8,128)(2,1)}, bf16[2,512,256]{2,1,0:T(8,128)(2,1)}, u32[]{:S(2)}, u32[]{:S(2)}) %collective-permute-start.3) | collective-permute-done | bytes 524320 | tf_op jit(solution)/shard_map/ppermute | solution.py:28
  45.1 1.9 %collective-permute-done.5.corner1_ref = bf16[2,512,256]{2,1,0:T(8,128)(2,1)S(1)} collective-permute-done((bf16[2,512,256]{2,1,0:T(8,128)(2,1)}, bf16[2,512,256]{2,1,0:T(8,128)(2,1)S(1)}, u32[]{:S(2)}, u32[]{:S(2)}) %collective-permute-start.5) | collective-permute-done | bytes 524320 | tf_op jit(solution)/shard_map/ppermute | solution.py:28
  47.0 22.1 %shard_map.93.grown.refs_4_ = f32[2,10,1280,128]{3,2,1,0:T(8,128)S(1)} custom-call(s32[1]{0:T(128)} %bitcast.1.live_ref, s32[2,6]{1,0:T(2,128)S(1)} %bitcast.5, f32[2,768,768]{2,1,0:T(8,128)S(1)} %copy-done.1, bf16[2,768,512]{2,1,0:T(8,128)(2,1)} %collective-permute-done.1.right_ref, bf16[2,512,256]{2,1,0:T(8,128)(2,1)} %collective-permute-done.near0_ref, ...), custom_call_target="tpu_custom_call" | custom-call | flops 1024 | bytes 1024 | tf_op jit(solution)/shard_map/pallas_call | solution.py:331
  69.2 0.9 shard_map.94
  70.1 1.9 %collective-permute-start.7 = (bf16[2,512,256]{2,1,0:T(8,128)(2,1)S(1)}, bf16[2,512,256]{2,1,0:T(8,128)(2,1)S(1)}, u32[]{:S(2)}, u32[]{:S(2)}) collective-permute-start(bf16[2,512,256]{2,1,0:T(8,128)(2,1)S(1)} %get-tuple-element.38), channel_id=1, source_target_pairs={{0,4},{4,8},{8,12},{12,16},{16,20},{20,24},{24,28},{28,32},{32,36}... | collective-permute-start | bytes 1572872 | tf_op jit(solution)/shard_map/ppermute | solution.py:28
  72.0 1.9 %collective-permute-start.6 = (bf16[2,512,256]{2,1,0:T(8,128)(2,1)S(1)}, bf16[2,512,256]{2,1,0:T(8,128)(2,1)S(1)}, u32[]{:S(2)}, u32[]{:S(2)}) collective-permute-start(bf16[2,512,256]{2,1,0:T(8,128)(2,1)S(1)} %get-tuple-element.36), channel_id=1, source_target_pairs={{0,4},{4,8},{8,12},{12,16},{16,20},{20,24},{24,28},{28,32},{32,36}... | collective-permute-start | bytes 1572872 | tf_op jit(solution)/shard_map/ppermute | solution.py:28
  74.0 4.9 %collective-permute-start.8 = (bf16[2,512,256]{2,1,0:T(8,128)(2,1)S(1)}, bf16[2,512,256]{2,1,0:T(8,128)(2,1)S(1)}, u32[]{:S(2)}, u32[]{:S(2)}) collective-permute-start(bf16[2,512,256]{2,1,0:T(8,128)(2,1)S(1)} %get-tuple-element.40), channel_id=1, source_target_pairs={{0,1},{1,2},{2,3},{4,5},{5,6},{6,7},{8,9},{9,10},{10,11},{12,13},{... | collective-permute-start | bytes 1572872 | tf_op jit(solution)/shard_map/ppermute | solution.py:28
  78.9 1.9 %collective-permute-start.10 = (bf16[2,384,512]{2,1,0:T(8,128)(2,1)S(1)}, bf16[2,384,512]{2,1,0:T(8,128)(2,1)S(1)}, u32[]{:S(2)}, u32[]{:S(2)}) collective-permute-start(bf16[2,384,512]{2,1,0:T(8,128)(2,1)S(1)} %get-tuple-element.42), channel_id=1, source_target_pairs={{0,4},{4,8},{8,12},{12,16},{16,20},{20,24},{24,28},{28,32},{32,36}... | collective-permute-start | bytes 2359304 | tf_op jit(solution)/shard_map/ppermute | solution.py:28
  80.9 1.9 %collective-permute-start.11 = (bf16[2,384,512]{2,1,0:T(8,128)(2,1)S(1)}, bf16[2,384,512]{2,1,0:T(8,128)(2,1)S(1)}, u32[]{:S(2)}, u32[]{:S(2)}) collective-permute-start(bf16[2,384,512]{2,1,0:T(8,128)(2,1)S(1)} %get-tuple-element.43), channel_id=1, source_target_pairs={{0,4},{4,8},{8,12},{12,16},{16,20},{20,24},{24,28},{28,32},{32,36}... | collective-permute-start | bytes 2359304 | tf_op jit(solution)/shard_map/ppermute | solution.py:28
  82.8 0.1 add_convert_fusion.1
  82.9 5.4 %collective-permute-done.6 = bf16[2,512,256]{2,1,0:T(8,128)(2,1)S(1)} collective-permute-done((bf16[2,512,256]{2,1,0:T(8,128)(2,1)S(1)}, bf16[2,512,256]{2,1,0:T(8,128)(2,1)S(1)}, u32[]{:S(2)}, u32[]{:S(2)}) %collective-permute-start.6) | collective-permute-done | bytes 524320 | tf_op jit(solution)/shard_map/ppermute | solution.py:28
  88.3 4.9 %collective-permute-start.12 = (bf16[2,512,256]{2,1,0:T(8,128)(2,1)S(1)}, bf16[2,512,256]{2,1,0:T(8,128)(2,1)S(1)}, u32[]{:S(2)}, u32[]{:S(2)}) collective-permute-start(bf16[2,512,256]{2,1,0:T(8,128)(2,1)S(1)} %add_convert_fusion.1), channel_id=1, source_target_pairs={{0,1},{1,2},{2,3},{4,5},{5,6},{6,7},{8,9},{9,10},{10,11},{12,13},{... | collective-permute-start | bytes 1572872 | tf_op jit(solution)/shard_map/ppermute | solution.py:28
  93.4 1.9 %collective-permute-start.9 = (bf16[2,512,256]{2,1,0:T(8,128)(2,1)S(1)}, bf16[2,512,256]{2,1,0:T(8,128)(2,1)S(1)}, u32[]{:S(2)}, u32[]{:S(2)}) collective-permute-start(bf16[2,512,256]{2,1,0:T(8,128)(2,1)S(1)} %add_convert_fusion), channel_id=1, source_target_pairs={{0,1},{1,2},{2,3},{4,5},{5,6},{6,7},{8,9},{9,10},{10,11},{12,13},{... | collective-permute-start | bytes 1572872 | tf_op jit(solution)/shard_map/ppermute | solution.py:28
  95.4 1.4 %collective-permute-done.10.refs_0_ = bf16[2,384,512]{2,1,0:T(8,128)(2,1)S(1)} collective-permute-done((bf16[2,384,512]{2,1,0:T(8,128)(2,1)S(1)}, bf16[2,384,512]{2,1,0:T(8,128)(2,1)S(1)}, u32[]{:S(2)}, u32[]{:S(2)}) %collective-permute-start.10) | collective-permute-done | bytes 786464 | tf_op jit(solution)/shard_map/ppermute | solution.py:28
  96.8 8.4 %collective-permute-done.11.refs_1_ = bf16[2,384,512]{2,1,0:T(8,128)(2,1)S(1)} collective-permute-done((bf16[2,384,512]{2,1,0:T(8,128)(2,1)S(1)}, bf16[2,384,512]{2,1,0:T(8,128)(2,1)S(1)}, u32[]{:S(2)}, u32[]{:S(2)}) %collective-permute-start.11) | collective-permute-done | bytes 786464 | tf_op jit(solution)/shard_map/ppermute | solution.py:28
  105.2 2.4 %shard_map.95 = (f32[2,10,1280,128]{3,2,1,0:T(8,128)S(1)}, f32[2,768,768]{2,1,0:T(8,128)}) custom-call(bf16[2,384,512]{2,1,0:T(8,128)(2,1)S(1)} %collective-permute-done.10.refs_0_, bf16[2,384,512]{2,1,0:T(8,128)(2,1)S(1)} %collective-permute-done.11.refs_1_, ...), custom_call_target="tpu_custom_call", output_to_operand_aliasing={{0}: (4, {})} | custom-call | flops 1024 | bytes 1024 | tf_op jit(solution)/shard_map/pallas_call | solution.py:432
  107.6 6.9 %collective-permute-done.9.near_ref = bf16[2,512,256]{2,1,0:T(8,128)(2,1)S(1)} collective-permute-done((bf16[2,512,256]{2,1,0:T(8,128)(2,1)S(1)}, bf16[2,512,256]{2,1,0:T(8,128)(2,1)S(1)}, u32[]{:S(2)}, u32[]{:S(2)}) %collective-permute-start.9) | collective-permute-done | bytes 524320 | tf_op jit(solution)/shard_map/ppermute | solution.py:28
  114.5 1.0 shard_map.96
  (21 shorter events, 0.2 us)
Async XLA Ops:
  0.0 16.5 %copy-start = (s32[32,1]{0,1:T(1,128)S(1)}, s32[32,1]{0,1:T(1,128)}, u32[]{:S(2)}) copy-start(s32[32,1]{0,1:T(1,128)} %param.13) | copy-start | bytes 388
  0.0 17.1 %copy-start.3 = (bf16[4,256,256]{2,1,0:T(8,128)(2,1)S(1)}, bf16[4,256,256]{2,1,0:T(8,128)(2,1)}, u32[]{:S(2)}) copy-start(bf16[4,256,256]{2,1,0:T(8,128)(2,1)} %constant.20.clone.refs_2_.gb_ref) | copy-start | bytes 1572868
  0.0 17.1 %copy-start.4 = (bf16[4,256,256]{2,1,0:T(8,128)(2,1)S(1)}, bf16[4,256,256]{2,1,0:T(8,128)(2,1)}, u32[]{:S(2)}) copy-start(bf16[4,256,256]{2,1,0:T(8,128)(2,1)} %constant.19.clone.refs_1_.ga_ref) | copy-start | bytes 1572868
  0.0 17.1 %copy-start.2 = (f32[2,512,512]{2,1,0:T(8,128)S(1)}, f32[2,512,512]{2,1,0:T(8,128)}, u32[]{:S(2)}) copy-start(f32[2,512,512]{2,1,0:T(8,128)} %probe_ref.1) | copy-start | bytes 6291460
  4.1 42.9 %collective-permute-start.1 = (bf16[2,768,512]{2,1,0:T(8,128)(2,1)}, bf16[2,768,512]{2,1,0:T(8,128)(2,1)}, u32[]{:S(2)}, u32[]{:S(2)}) collective-permute-start(bf16[2,768,512]{2,1,0:T(8,128)(2,1)} %get-tuple-element.30), channel_id=1, source_target_pairs={{4,0},{8,4},{12,8},{16,12},{20,16},{24,20},{28,24},{32,28},{36,32}... | collective-permute-start | bytes 4718600 | tf_op jit(solution)/shard_map/ppermute | solution.py:28
  9.8 17.1 %collective-permute-start = (bf16[2,512,256]{2,1,0:T(8,128)(2,1)}, bf16[2,512,256]{2,1,0:T(8,128)(2,1)}, u32[]{:S(2)}, u32[]{:S(2)}) collective-permute-start(bf16[2,512,256]{2,1,0:T(8,128)(2,1)} %get-tuple-element.27), channel_id=1, source_target_pairs={{1,0},{2,1},{3,2},{5,4},{6,5},{7,6},{9,8},{10,9},{11,10},{13,12},{... | collective-permute-start | bytes 1572872 | tf_op jit(solution)/shard_map/ppermute | solution.py:28
  12.2 25.9 %collective-permute-start.2 = (bf16[2,512,256]{2,1,0:T(8,128)(2,1)}, bf16[2,512,256]{2,1,0:T(8,128)(2,1)}, u32[]{:S(2)}, u32[]{:S(2)}) collective-permute-start(bf16[2,512,256]{2,1,0:T(8,128)(2,1)} %get-tuple-element.32), channel_id=1, source_target_pairs={{1,0},{2,1},{3,2},{5,4},{6,5},{7,6},{9,8},{10,9},{11,10},{13,12},{... | collective-permute-start | bytes 1572872 | tf_op jit(solution)/shard_map/ppermute | solution.py:28
  14.5 30.5 %collective-permute-start.3 = (bf16[2,512,256]{2,1,0:T(8,128)(2,1)}, bf16[2,512,256]{2,1,0:T(8,128)(2,1)}, u32[]{:S(2)}, u32[]{:S(2)}) collective-permute-start(bf16[2,512,256]{2,1,0:T(8,128)(2,1)} %get-tuple-element.33), channel_id=1, source_target_pairs={{1,0},{2,1},{3,2},{5,4},{6,5},{7,6},{9,8},{10,9},{11,10},{13,12},{... | collective-permute-start | bytes 1572872 | tf_op jit(solution)/shard_map/ppermute | solution.py:28
  17.1 1.9 %copy-start.6 = (bf16[1,1,6,512,512]{4,3,2,1,0:T(8,128)(2,1)S(1)}, bf16[1,1,6,512,512]{4,3,2,1,0:T(8,128)(2,1)}, u32[]{:S(2)}) copy-start(bf16[1,1,6,512,512]{4,3,2,1,0:T(8,128)(2,1)} %param.11) | copy-start | bytes 9437188
  19.0 1.0 copy-start.7
  20.1 1.0 copy-start.8
  21.1 25.9 %copy-start.1 = (f32[2,768,768]{2,1,0:T(8,128)S(1)}, f32[2,768,768]{2,1,0:T(8,128)}, u32[]{:S(2)}) copy-start(f32[2,768,768]{2,1,0:T(8,128)} %slab_ref.3) | copy-start | bytes 14155780
  21.1 25.9 %copy-start.5 = (s32[1,1,6,2]{2,3,1,0:T(2,128)S(1)}, s32[1,1,6,2]{2,3,1,0:T(2,128)}, u32[]{:S(2)}) copy-start(s32[1,1,6,2]{2,3,1,0:T(2,128)} %param.12) | copy-start | bytes 148
  26.9 18.2 %collective-permute-start.4 = (bf16[2,512,256]{2,1,0:T(8,128)(2,1)}, bf16[2,512,256]{2,1,0:T(8,128)(2,1)S(1)}, u32[]{:S(2)}, u32[]{:S(2)}) collective-permute-start(bf16[2,512,256]{2,1,0:T(8,128)(2,1)} %collective-permute-done.near0_ref), channel_id=1, source_target_pairs={{4,0},{8,4},{12,8},{16,12},{20,16},{24,20},{28,24},{32,28},{36,32}... | collective-permute-start | bytes 1572872 | tf_op jit(solution)/shard_map/ppermute | solution.py:28
  38.1 8.9 %collective-permute-start.5 = (bf16[2,512,256]{2,1,0:T(8,128)(2,1)}, bf16[2,512,256]{2,1,0:T(8,128)(2,1)S(1)}, u32[]{:S(2)}, u32[]{:S(2)}) collective-permute-start(bf16[2,512,256]{2,1,0:T(8,128)(2,1)} %collective-permute-done.2.near1_ref), channel_id=1, source_target_pairs={{4,0},{8,4},{12,8},{16,12},{20,16},{24,20},{28,24},{32,28},{36,32}... | collective-permute-start | bytes 1572872 | tf_op jit(solution)/shard_map/ppermute | solution.py:28
  70.1 12.7 %collective-permute-start.7 = (bf16[2,512,256]{2,1,0:T(8,128)(2,1)S(1)}, bf16[2,512,256]{2,1,0:T(8,128)(2,1)S(1)}, u32[]{:S(2)}, u32[]{:S(2)}) collective-permute-start(bf16[2,512,256]{2,1,0:T(8,128)(2,1)S(1)} %get-tuple-element.38), channel_id=1, source_target_pairs={{0,4},{4,8},{8,12},{12,16},{16,20},{20,24},{24,28},{28,32},{32,36}... | collective-permute-start | bytes 1572872 | tf_op jit(solution)/shard_map/ppermute | solution.py:28
  72.0 16.3 %collective-permute-start.6 = (bf16[2,512,256]{2,1,0:T(8,128)(2,1)S(1)}, bf16[2,512,256]{2,1,0:T(8,128)(2,1)S(1)}, u32[]{:S(2)}, u32[]{:S(2)}) collective-permute-start(bf16[2,512,256]{2,1,0:T(8,128)(2,1)S(1)} %get-tuple-element.36), channel_id=1, source_target_pairs={{0,4},{4,8},{8,12},{12,16},{16,20},{20,24},{24,28},{28,32},{32,36}... | collective-permute-start | bytes 1572872 | tf_op jit(solution)/shard_map/ppermute | solution.py:28
  74.0 19.5 %collective-permute-start.8 = (bf16[2,512,256]{2,1,0:T(8,128)(2,1)S(1)}, bf16[2,512,256]{2,1,0:T(8,128)(2,1)S(1)}, u32[]{:S(2)}, u32[]{:S(2)}) collective-permute-start(bf16[2,512,256]{2,1,0:T(8,128)(2,1)S(1)} %get-tuple-element.40), channel_id=1, source_target_pairs={{0,1},{1,2},{2,3},{4,5},{5,6},{6,7},{8,9},{9,10},{10,11},{12,13},{... | collective-permute-start | bytes 1572872 | tf_op jit(solution)/shard_map/ppermute | solution.py:28
  78.9 17.8 %collective-permute-start.10 = (bf16[2,384,512]{2,1,0:T(8,128)(2,1)S(1)}, bf16[2,384,512]{2,1,0:T(8,128)(2,1)S(1)}, u32[]{:S(2)}, u32[]{:S(2)}) collective-permute-start(bf16[2,384,512]{2,1,0:T(8,128)(2,1)S(1)} %get-tuple-element.42), channel_id=1, source_target_pairs={{0,4},{4,8},{8,12},{12,16},{16,20},{20,24},{24,28},{28,32},{32,36}... | collective-permute-start | bytes 2359304 | tf_op jit(solution)/shard_map/ppermute | solution.py:28
  80.9 24.3 %collective-permute-start.11 = (bf16[2,384,512]{2,1,0:T(8,128)(2,1)S(1)}, bf16[2,384,512]{2,1,0:T(8,128)(2,1)S(1)}, u32[]{:S(2)}, u32[]{:S(2)}) collective-permute-start(bf16[2,384,512]{2,1,0:T(8,128)(2,1)S(1)} %get-tuple-element.43), channel_id=1, source_target_pairs={{0,4},{4,8},{8,12},{12,16},{16,20},{20,24},{24,28},{28,32},{32,36}... | collective-permute-start | bytes 2359304 | tf_op jit(solution)/shard_map/ppermute | solution.py:28
  88.3 16.9 %collective-permute-start.12 = (bf16[2,512,256]{2,1,0:T(8,128)(2,1)S(1)}, bf16[2,512,256]{2,1,0:T(8,128)(2,1)S(1)}, u32[]{:S(2)}, u32[]{:S(2)}) collective-permute-start(bf16[2,512,256]{2,1,0:T(8,128)(2,1)S(1)} %add_convert_fusion.1), channel_id=1, source_target_pairs={{0,1},{1,2},{2,3},{4,5},{5,6},{6,7},{8,9},{9,10},{10,11},{12,13},{... | collective-permute-start | bytes 1572872 | tf_op jit(solution)/shard_map/ppermute | solution.py:28
  93.4 21.0 %collective-permute-start.9 = (bf16[2,512,256]{2,1,0:T(8,128)(2,1)S(1)}, bf16[2,512,256]{2,1,0:T(8,128)(2,1)S(1)}, u32[]{:S(2)}, u32[]{:S(2)}) collective-permute-start(bf16[2,512,256]{2,1,0:T(8,128)(2,1)S(1)} %add_convert_fusion), channel_id=1, source_target_pairs={{0,1},{1,2},{2,3},{4,5},{5,6},{6,7},{8,9},{9,10},{10,11},{12,13},{... | collective-permute-start | bytes 1572872 | tf_op jit(solution)/shard_map/ppermute | solution.py:28

commit v7 on v6

--- a/solution.py
+++ b/solution.py
@@ -91,7 +91,7 @@
 
 
 def pack_kernel(slab_ref, *refs):
-    outs, halves, (buf, sem, out_sem) = refs[:4], refs[4:8], refs[8:]
+    outs, halves, (buf, sem, out_sem) = refs[: 3 + RP], refs[3 + RP : 6 + 2 * RP], refs[6 + 2 * RP :]
     pieces = 6
     step = T // pieces
 
@@ -101,10 +101,15 @@
 
     def copies_out(c):
         rows = pl.ds(c * step, step)
-        return [
-            pltpu.make_async_copy(half.at[:, rows, :], o.at[:, rows, :], out_sem.at[c, k])
-            for k, (half, o) in enumerate(zip(halves, outs))
-            if (c + 1) * step <= o.shape[1]
+        made = [
+            pltpu.make_async_copy(halves[k].at[:, rows, :], outs[k].at[:, rows, :], out_sem.at[c, k])
+            for k in range(3)
+            if (c + 1) * step <= W
+        ]
+        k, row = 3 + c * step // (T // RP), c * step % (T // RP)
+        rows = pl.ds(row, step)
+        return made + [
+            pltpu.make_async_copy(halves[k].at[:, rows, :], outs[k].at[:, rows, :], out_sem.at[c, 3])
         ]
 
     for c in range(pieces):
@@ -119,7 +124,7 @@
                     halves[0][p, here, :] = part[:, : 2 * Q]
                     halves[1][p, here, :] = part[:, 2 * Q : W]
                     halves[2][p, here, :] = part[:, W:]
-                halves[3][p, here, :] = part[:, :W]
+                halves[3 + row // (T // RP)][p, pl.ds(row % (T // RP), 2 * R), :] = part[:, :W]
         for one in copies_out(c):
             one.start()
     for c in range(pieces):
@@ -128,11 +133,11 @@
 
 
 def pack(slab):
-    shapes = [(2, W, 2 * Q)] * 3 + [(2, T, W)]
+    shapes = [(2, W, 2 * Q)] * 3 + [(2, T // RP, W)] * RP
     return pl.pallas_call(
         pack_kernel,
         in_specs=[ANY],
-        out_specs=[ANY] * 4,
+        out_specs=[ANY] * (3 + RP),
         out_shape=[jax.ShapeDtypeStruct(shape, bf16) for shape in shapes],
         scratch_shapes=[pltpu.VMEM(shape, bf16) for shape in shapes]
         + [
@@ -171,7 +176,6 @@
     live_ref,
     meta_ref,
     slab_ref,
-    right_ref,
     near0_ref,
     near1_ref,
     far_ref,
@@ -181,14 +185,11 @@
     meas_ref,
     ga_ref,
     gb_ref,
-    grown,
-    ext,
-    half16,
-    full32,
-    mid,
-    out,
-    sem,
+    *refs,
 ):
+    right_refs, refs = refs[:RP], refs[RP:]
+    grown, ext, half16, full32, mid, out, sem = refs
+
     def copy(p, b):
         return pltpu.make_async_copy(
             slab_ref.at[p, :, lanes(b)], ext.at[p, b, pl.ds(0, T), :], sem.at[p, b]
@@ -205,9 +206,10 @@
 
     def fill_right(row):
         rows = pl.ds(row, R)
+        here = pl.ds(pl.multiple_of(piece * (T // RP) + row, R), R)
         for p in range(2):
             for b in range(4):
-                ext[p, TB + b, rows, :] = right_ref[p, rows, lanes(b)].astype(f32)
+                ext[p, TB + b, here, :] = right_refs[piece][p, rows, lanes(b)].astype(f32)
 
     def fill_below(row):
         rows = pl.ds(row, R)
@@ -221,7 +223,8 @@
                 ext[p, TB + 2 + b, there, :] = corner1_ref[p, rows, lanes(b)].astype(f32)
 
     each_rows(E, clear)
-    each_rows(T, fill_right)
+    for piece in range(RP):
+        each_rows(T // RP, fill_right)
     each_rows(W, fill_below)
     for p in range(2):
         for b in range(TB):
@@ -330,7 +333,7 @@
 def solve(live, meta, slab, right, below, corner, probe, measured, left, left_t):
     return pl.pallas_call(
         slots_kernel,
-        in_specs=[SMEM, SMEM, ANY] + [VMEM] * 10,
+        in_specs=[SMEM, SMEM, ANY] + [VMEM] * (9 + RP),
         out_specs=VMEM,
         out_shape=TILES,
         scratch_shapes=[
@@ -343,7 +346,7 @@
         ],
         cost_estimate=cost(),
         compiler_params=params(SOLVE_MIB),
-    )(live, meta, slab, right, *below, *corner, probe, measured, left, left_t)
+    )(live, meta, slab, *below, *corner, probe, measured, left, left_t, *right)
 
 
 def drain_kernel(grown, near0_ref, near1_ref, far_ref, corner0_ref, corner1_ref, *right_refs):
@@ -471,11 +474,11 @@
 def shards(slab, probe, intensities, offsets, live_count):
     left, left_t, pick = tables()
     left, left_t = jnp.asarray(left), jnp.asarray(left_t)
-    near0, near1, far, right = pack(slab)
+    near0, near1, far, *right = pack(slab)
     near0 = shifted(near0, "tile", -1)
     near1 = shifted(near1, "tile", -1)
     far = shifted(far, "tile", -1)
-    right = shifted(right, "scan", -1)
+    right = [shifted(piece, "scan", -1) for piece in right]
     measured = sort_intensities(intensities[0, 0], pick, probe, left, left_t)
     live = lax.dynamic_slice(live_count[:, 0], (lax.axis_index("scan"),), (1,))
     shifts = offsets[0, 0].T
@@ -491,6 +494,7 @@
     far = shifted(far, "tile", 1)
     corner0 = shifted(corner0, "scan", 1)
     near1 = (near1.astype(f32) + corner1.astype(f32)).astype(bf16)
+    near1, *right = lax.optimization_barrier((near1, *right))
     corner0, near1 = lax.optimization_barrier((corner0, near1))
     near0 = (near0.astype(f32) + corner0.astype(f32)).astype(bf16)
     near1 = shifted(near1, "tile", 1)

time: 118 us -> 122 us (1.034); the launches traced: 116 us -> 122 us
  starting transfers between devices: 35.6 us -> 59.7 us
  Pallas kernels: 34.9 us -> 20.8 us
  waiting for transfers between devices: 39.9 us -> 35.1 us
    ppermute x13 -> x14, starting transfers between devices: 35.6 us -> 59.7 us  [shifted(): lax.ppermute(value, axis, [(i, i + by) for i in range(n) if 0 <= i + by <...]
    pallas_call x2, Pallas kernels: 26.2 us -> 12.1 us  [the longest x1 7.99 us: solve(): pl.pallas_call(slots_kernel, in_specs=[SMEM, SMEM, ANY] + [VMEM] * (9 + R...]
    ppermute x13 -> x14, waiting for transfers between devices: 39.9 us -> 35.1 us  [shifted(): lax.ppermute(value, axis, [(i, i + by) for i in range(n) if 0 <= i + by <...]
  transfers between devices with their start and end apart: 13 -> 14, of which waited for: 8 -> 8; matrix products, arithmetic and copies ran while one was open for 1% -> 1% of each run, Pallas kernels for 6% -> 5%
where the time goes in v7:
time: 122 us
  starting transfers between devices  59.7 us (49%)
  waiting for transfers between devices  35.1 us (29%)
  Pallas kernels  20.8 us (17%)
  local copies, waits for them, and re-layouts  5.65 us (5%)
    ppermute x14, starting transfers between devices, shifted(): lax.ppermute(value, axis, [(i, i + by) for i in range(n) if 0 <= i + by <...  59.7 us
    ppermute x14, waiting for transfers between devices, shifted(): lax.ppermute(value, axis, [(i, i + by) for i in range(n) if 0 <= i + by <...  35.1 us
    pallas_call x1, Pallas kernels, solve(): pl.pallas_call(slots_kernel, in_specs=[SMEM, SMEM, ANY] + [VMEM] * (9 + R...  7.99 us
    unnamed x18, local copies, waits for them, and re-layouts  5.03 us
    pallas_call x1, Pallas kernels, sort_intensities(): pl.pallas_call(sort_kernel, grid=(measured.shape[0],), in_specs=[whole, w...  4.3 us
    pallas_call x1, Pallas kernels, pack(): pl.pallas_call(pack_kernel, in_specs=[ANY], out_specs=[ANY] * (3 + RP), o...  4.1 us
  transfers between devices with their start and end apart: 14, of which 8 were waited for; matrix products, arithmetic and copies ran while one was open for 1% of the time, Pallas kernels for 5%

profile of v7, /device:TPU:22, one launch (start us, length us, event | category | flops | bytes accessed | tf_op | source)
XLA Modules:
  0.0 121.7 jit_solution(14911662961841230074)
XLA Ops:
  0.0 4.1 %shard_map.91 = (bf16[2,512,256]{2,1,0:T(8,128)(2,1)}, bf16[2,512,256]{2,1,0:T(8,128)(2,1)}, bf16[2,512,256]{2,1,0:T(8,128)(2,1)}, bf16[2,384,512]{2,1,0:T(8,128)(2,1)}, bf16[2,384,512]{2,1,0:T(8,128)(2,1)}) custom-call(f32[2,768,768]{2,1,0:T(8,128)} %slab_ref.3), custom_call_target="tpu_custom_call" | custom-call | flops 1024 | bytes 1024 | tf_op jit(solution)/shard_map/pallas_call | solution.py:137
  4.1 2.4 %collective-permute-start = (bf16[2,512,256]{2,1,0:T(8,128)(2,1)}, bf16[2,512,256]{2,1,0:T(8,128)(2,1)}, u32[]{:S(2)}, u32[]{:S(2)}) collective-permute-start(bf16[2,512,256]{2,1,0:T(8,128)(2,1)} %get-tuple-element.31), channel_id=1, source_target_pairs={{1,0},{2,1},{3,2},{5,4},{6,5},{7,6},{9,8},{10,9},{11,10},{13,12},{... | collective-permute-start | bytes 1572872 | tf_op jit(solution)/shard_map/ppermute | solution.py:28
  6.5 2.4 %collective-permute-start.1 = (bf16[2,512,256]{2,1,0:T(8,128)(2,1)}, bf16[2,512,256]{2,1,0:T(8,128)(2,1)}, u32[]{:S(2)}, u32[]{:S(2)}) collective-permute-start(bf16[2,512,256]{2,1,0:T(8,128)(2,1)} %get-tuple-element.35), channel_id=1, source_target_pairs={{1,0},{2,1},{3,2},{5,4},{6,5},{7,6},{9,8},{10,9},{11,10},{13,12},{... | collective-permute-start | bytes 1572872 | tf_op jit(solution)/shard_map/ppermute | solution.py:28
  8.8 1.9 %collective-permute-start.2 = (bf16[2,512,256]{2,1,0:T(8,128)(2,1)}, bf16[2,512,256]{2,1,0:T(8,128)(2,1)}, u32[]{:S(2)}, u32[]{:S(2)}) collective-permute-start(bf16[2,512,256]{2,1,0:T(8,128)(2,1)} %get-tuple-element.36), channel_id=1, source_target_pairs={{1,0},{2,1},{3,2},{5,4},{6,5},{7,6},{9,8},{10,9},{11,10},{13,12},{... | collective-permute-start | bytes 1572872 | tf_op jit(solution)/shard_map/ppermute | solution.py:28
  10.8 5.1 %collective-permute-start.5 = (bf16[2,384,512]{2,1,0:T(8,128)(2,1)}, bf16[2,384,512]{2,1,0:T(8,128)(2,1)S(1)}, u32[]{:S(2)}, u32[]{:S(2)}) collective-permute-start(bf16[2,384,512]{2,1,0:T(8,128)(2,1)} %get-tuple-element.38), channel_id=1, source_target_pairs={{4,0},{8,4},{12,8},{16,12},{20,16},{24,20},{28,24},{32,28},{36,32}... | collective-permute-start | bytes 2359304 | tf_op jit(solution)/shard_map/ppermute | solution.py:28
  15.9 3.1 %collective-permute-start.6 = (bf16[2,384,512]{2,1,0:T(8,128)(2,1)}, bf16[2,384,512]{2,1,0:T(8,128)(2,1)}, u32[]{:S(2)}, u32[]{:S(2)}) collective-permute-start(bf16[2,384,512]{2,1,0:T(8,128)(2,1)} %get-tuple-element.39), channel_id=1, source_target_pairs={{4,0},{8,4},{12,8},{16,12},{20,16},{24,20},{28,24},{32,28},{36,32}... | collective-permute-start | bytes 2359304 | tf_op jit(solution)/shard_map/ppermute | solution.py:28
  19.7 1.0 copy-done.4
  20.7 1.9 %copy-done.6 = bf16[1,1,6,512,512]{4,3,2,1,0:T(8,128)(2,1)S(1)} copy-done((bf16[1,1,6,512,512]{4,3,2,1,0:T(8,128)(2,1)S(1)}, bf16[1,1,6,512,512]{4,3,2,1,0:T(8,128)(2,1)}, u32[]{:S(2)}) %copy-start.6) | copy-done | bytes 3145752
  22.6 1.0 copy-done.7
  23.6 1.0 copy-done.8
  24.7 4.3 %shard_map.92.meas_ref = bf16[6,512,512]{2,1,0:T(8,128)(2,1)S(1)} custom-call(bf16[512,512]{1,0:T(8,128)(2,1)S(1)} %copy-done.8, bf16[512,512]{1,0:T(8,128)(2,1)S(1)} %copy-done.7, bf16[6,512,512]{2,1,0:T(8,128)(2,1)S(1)} %bitcast.6, f32[2,512,512]{2,1,0:T(8,128)S(1)} %copy-done.2, bf16[4,256,256]{2,1,0:T(8,128)(2,1)S(1)} %copy-done.4, ...), custom_call_target="tpu_custom_call" | custom-call | flops 3221225472 | bytes 6291456 | tf_op jit(solution)/shard_map/pallas_call | solution.py:162
  29.0 1.9 %collective-permute-start.3 = (bf16[2,512,256]{2,1,0:T(8,128)(2,1)}, bf16[2,512,256]{2,1,0:T(8,128)(2,1)S(1)}, u32[]{:S(2)}, u32[]{:S(2)}) collective-permute-start(bf16[2,512,256]{2,1,0:T(8,128)(2,1)} %collective-permute-done.near0_ref), channel_id=1, source_target_pairs={{4,0},{8,4},{12,8},{16,12},{20,16},{24,20},{28,24},{32,28},{36,32}... | collective-permute-start | bytes 1572872 | tf_op jit(solution)/shard_map/ppermute | solution.py:28
  30.9 1.4 %collective-permute-done.1.near1_ref = bf16[2,512,256]{2,1,0:T(8,128)(2,1)} collective-permute-done((bf16[2,512,256]{2,1,0:T(8,128)(2,1)}, bf16[2,512,256]{2,1,0:T(8,128)(2,1)}, u32[]{:S(2)}, u32[]{:S(2)}) %collective-permute-start.1) | collective-permute-done | bytes 524320 | tf_op jit(solution)/shard_map/ppermute | solution.py:28
  32.4 3.6 %collective-permute-start.4 = (bf16[2,512,256]{2,1,0:T(8,128)(2,1)}, bf16[2,512,256]{2,1,0:T(8,128)(2,1)S(1)}, u32[]{:S(2)}, u32[]{:S(2)}) collective-permute-start(bf16[2,512,256]{2,1,0:T(8,128)(2,1)} %collective-permute-done.1.near1_ref), channel_id=1, source_target_pairs={{4,0},{8,4},{12,8},{16,12},{20,16},{24,20},{28,24},{32,28},{36,32}... | collective-permute-start | bytes 1572872 | tf_op jit(solution)/shard_map/ppermute | solution.py:28
  36.0 6.5 %collective-permute-done.2.far_ref = bf16[2,512,256]{2,1,0:T(8,128)(2,1)} collective-permute-done((bf16[2,512,256]{2,1,0:T(8,128)(2,1)}, bf16[2,512,256]{2,1,0:T(8,128)(2,1)}, u32[]{:S(2)}, u32[]{:S(2)}) %collective-permute-start.2) | collective-permute-done | bytes 524320 | tf_op jit(solution)/shard_map/ppermute | solution.py:28
  42.5 2.9 %collective-permute-done.4.corner1_ref = bf16[2,512,256]{2,1,0:T(8,128)(2,1)S(1)} collective-permute-done((bf16[2,512,256]{2,1,0:T(8,128)(2,1)}, bf16[2,512,256]{2,1,0:T(8,128)(2,1)S(1)}, u32[]{:S(2)}, u32[]{:S(2)}) %collective-permute-start.4) | collective-permute-done | bytes 524320 | tf_op jit(solution)/shard_map/ppermute | solution.py:28
  45.3 8.0 %shard_map.93.grown.refs_4_ = f32[2,10,1280,128]{3,2,1,0:T(8,128)S(1)} custom-call(s32[1]{0:T(128)} %bitcast.1.live_ref, s32[2,6]{1,0:T(2,128)S(1)} %bitcast.5, f32[2,768,768]{2,1,0:T(8,128)S(1)} %copy-done.1, bf16[2,512,256]{2,1,0:T(8,128)(2,1)} %collective-permute-done.near0_ref, bf16[2,512,256]{2,1,0:T(8,128)(2,1)} %collective-permute-done.1.near1_ref, ...), custom_call_target="tpu_custom_call" | custom-call | flops 1024 | bytes 1024 | tf_op jit(solution)/shard_map/pallas_call | solution.py:334
  53.3 0.9 shard_map.94
  54.3 18.6 %collective-permute-start.8 = (bf16[2,512,256]{2,1,0:T(8,128)(2,1)S(1)}, bf16[2,512,256]{2,1,0:T(8,128)(2,1)S(1)}, u32[]{:S(2)}, u32[]{:S(2)}) collective-permute-start(bf16[2,512,256]{2,1,0:T(8,128)(2,1)S(1)} %get-tuple-element.43), channel_id=1, source_target_pairs={{0,4},{4,8},{8,12},{12,16},{16,20},{20,24},{24,28},{28,32},{32,36}... | collective-permute-start | bytes 1572872 | tf_op jit(solution)/shard_map/ppermute | solution.py:28
  72.9 1.9 %collective-permute-start.7 = (bf16[2,512,256]{2,1,0:T(8,128)(2,1)S(1)}, bf16[2,512,256]{2,1,0:T(8,128)(2,1)S(1)}, u32[]{:S(2)}, u32[]{:S(2)}) collective-permute-start(bf16[2,512,256]{2,1,0:T(8,128)(2,1)S(1)} %get-tuple-element.41), channel_id=1, source_target_pairs={{0,4},{4,8},{8,12},{12,16},{16,20},{20,24},{24,28},{28,32},{32,36}... | collective-permute-start | bytes 1572872 | tf_op jit(solution)/shard_map/ppermute | solution.py:28
  74.8 5.2 %collective-permute-start.9 = (bf16[2,512,256]{2,1,0:T(8,128)(2,1)S(1)}, bf16[2,512,256]{2,1,0:T(8,128)(2,1)S(1)}, u32[]{:S(2)}, u32[]{:S(2)}) collective-permute-start(bf16[2,512,256]{2,1,0:T(8,128)(2,1)S(1)} %get-tuple-element.48), channel_id=1, source_target_pairs={{0,1},{1,2},{2,3},{4,5},{5,6},{6,7},{8,9},{9,10},{10,11},{12,13},{... | collective-permute-start | bytes 1572872 | tf_op jit(solution)/shard_map/ppermute | solution.py:28
  80.0 0.9 collective-permute-done.8
  81.1 5.5 %collective-permute-done.7 = bf16[2,512,256]{2,1,0:T(8,128)(2,1)S(1)} collective-permute-done((bf16[2,512,256]{2,1,0:T(8,128)(2,1)S(1)}, bf16[2,512,256]{2,1,0:T(8,128)(2,1)S(1)}, u32[]{:S(2)}, u32[]{:S(2)}) %collective-permute-start.7) | collective-permute-done | bytes 524320 | tf_op jit(solution)/shard_map/ppermute | solution.py:28
  86.6 7.8 %collective-permute-start.13 = (bf16[2,512,256]{2,1,0:T(8,128)(2,1)S(1)}, bf16[2,512,256]{2,1,0:T(8,128)(2,1)S(1)}, u32[]{:S(2)}, u32[]{:S(2)}) collective-permute-start(bf16[2,512,256]{2,1,0:T(8,128)(2,1)S(1)} %add_convert_fusion.1), channel_id=1, source_target_pairs={{0,1},{1,2},{2,3},{4,5},{5,6},{6,7},{8,9},{9,10},{10,11},{12,13},{... | collective-permute-start | bytes 1572872 | tf_op jit(solution)/shard_map/ppermute | solution.py:28
  94.4 1.9 %collective-permute-start.11 = (bf16[2,384,512]{2,1,0:T(8,128)(2,1)S(1)}, bf16[2,384,512]{2,1,0:T(8,128)(2,1)S(1)}, u32[]{:S(2)}, u32[]{:S(2)}) collective-permute-start(bf16[2,384,512]{2,1,0:T(8,128)(2,1)S(1)} %get-tuple-element.50), channel_id=1, source_target_pairs={{0,4},{4,8},{8,12},{12,16},{16,20},{20,24},{24,28},{28,32},{32,36}... | collective-permute-start | bytes 2359304 | tf_op jit(solution)/shard_map/ppermute | solution.py:28
  96.3 1.9 %collective-permute-start.12 = (bf16[2,384,512]{2,1,0:T(8,128)(2,1)S(1)}, bf16[2,384,512]{2,1,0:T(8,128)(2,1)S(1)}, u32[]{:S(2)}, u32[]{:S(2)}) collective-permute-start(bf16[2,384,512]{2,1,0:T(8,128)(2,1)S(1)} %get-tuple-element.51), channel_id=1, source_target_pairs={{0,4},{4,8},{8,12},{12,16},{16,20},{20,24},{24,28},{28,32},{32,36}... | collective-permute-start | bytes 2359304 | tf_op jit(solution)/shard_map/ppermute | solution.py:28
  98.4 1.9 %collective-permute-start.10 = (bf16[2,512,256]{2,1,0:T(8,128)(2,1)S(1)}, bf16[2,512,256]{2,1,0:T(8,128)(2,1)S(1)}, u32[]{:S(2)}, u32[]{:S(2)}) collective-permute-start(bf16[2,512,256]{2,1,0:T(8,128)(2,1)S(1)} %add_convert_fusion), channel_id=1, source_target_pairs={{0,1},{1,2},{2,3},{4,5},{5,6},{6,7},{8,9},{9,10},{10,11},{12,13},{... | collective-permute-start | bytes 1572872 | tf_op jit(solution)/shard_map/ppermute | solution.py:28
  100.3 6.2 %collective-permute-done.13.refs_3_ = bf16[2,512,256]{2,1,0:T(8,128)(2,1)S(1)} collective-permute-done((bf16[2,512,256]{2,1,0:T(8,128)(2,1)S(1)}, bf16[2,512,256]{2,1,0:T(8,128)(2,1)S(1)}, u32[]{:S(2)}, u32[]{:S(2)}) %collective-permute-start.13) | collective-permute-done | bytes 524320 | tf_op jit(solution)/shard_map/ppermute | solution.py:28
  106.6 3.2 %collective-permute-done.11.refs_0_ = bf16[2,384,512]{2,1,0:T(8,128)(2,1)S(1)} collective-permute-done((bf16[2,384,512]{2,1,0:T(8,128)(2,1)S(1)}, bf16[2,384,512]{2,1,0:T(8,128)(2,1)S(1)}, u32[]{:S(2)}, u32[]{:S(2)}) %collective-permute-start.11) | collective-permute-done | bytes 786464 | tf_op jit(solution)/shard_map/ppermute | solution.py:28
  109.8 8.4 %collective-permute-done.12.refs_1_ = bf16[2,384,512]{2,1,0:T(8,128)(2,1)S(1)} collective-permute-done((bf16[2,384,512]{2,1,0:T(8,128)(2,1)S(1)}, bf16[2,384,512]{2,1,0:T(8,128)(2,1)S(1)}, u32[]{:S(2)}, u32[]{:S(2)}) %collective-permute-start.12) | collective-permute-done | bytes 786464 | tf_op jit(solution)/shard_map/ppermute | solution.py:28
  118.2 2.4 %shard_map.95 = (f32[2,10,1280,128]{3,2,1,0:T(8,128)S(1)}, f32[2,768,768]{2,1,0:T(8,128)}) custom-call(bf16[2,384,512]{2,1,0:T(8,128)(2,1)S(1)} %collective-permute-done.11.refs_0_, bf16[2,384,512]{2,1,0:T(8,128)(2,1)S(1)} %collective-permute-done.12.refs_1_, ...), custom_call_target="tpu_custom_call", output_to_operand_aliasing={{0}: (4, {})} | custom-call | flops 1024 | bytes 1024 | tf_op jit(solution)/shard_map/pallas_call | solution.py:435
  120.6 1.1 shard_map.96
  (23 shorter events, 0.9 us)
Async XLA Ops:
  0.0 19.0 %copy-start = (s32[32,1]{0,1:T(1,128)S(1)}, s32[32,1]{0,1:T(1,128)}, u32[]{:S(2)}) copy-start(s32[32,1]{0,1:T(1,128)} %param.13) | copy-start | bytes 388
  0.0 19.7 %copy-start.3 = (bf16[4,256,256]{2,1,0:T(8,128)(2,1)S(1)}, bf16[4,256,256]{2,1,0:T(8,128)(2,1)}, u32[]{:S(2)}) copy-start(bf16[4,256,256]{2,1,0:T(8,128)(2,1)} %constant.20.clone.refs_2_.gb_ref) | copy-start | bytes 1572868
  0.0 19.7 %copy-start.2 = (f32[2,512,512]{2,1,0:T(8,128)S(1)}, f32[2,512,512]{2,1,0:T(8,128)}, u32[]{:S(2)}) copy-start(f32[2,512,512]{2,1,0:T(8,128)} %probe_ref.1) | copy-start | bytes 6291460
  4.1 24.9 %collective-permute-start = (bf16[2,512,256]{2,1,0:T(8,128)(2,1)}, bf16[2,512,256]{2,1,0:T(8,128)(2,1)}, u32[]{:S(2)}, u32[]{:S(2)}) collective-permute-start(bf16[2,512,256]{2,1,0:T(8,128)(2,1)} %get-tuple-element.31), channel_id=1, source_target_pairs={{1,0},{2,1},{3,2},{5,4},{6,5},{7,6},{9,8},{10,9},{11,10},{13,12},{... | collective-permute-start | bytes 1572872 | tf_op jit(solution)/shard_map/ppermute | solution.py:28
  6.5 25.9 %collective-permute-start.1 = (bf16[2,512,256]{2,1,0:T(8,128)(2,1)}, bf16[2,512,256]{2,1,0:T(8,128)(2,1)}, u32[]{:S(2)}, u32[]{:S(2)}) collective-permute-start(bf16[2,512,256]{2,1,0:T(8,128)(2,1)} %get-tuple-element.35), channel_id=1, source_target_pairs={{1,0},{2,1},{3,2},{5,4},{6,5},{7,6},{9,8},{10,9},{11,10},{13,12},{... | collective-permute-start | bytes 1572872 | tf_op jit(solution)/shard_map/ppermute | solution.py:28
  8.8 33.6 %collective-permute-start.2 = (bf16[2,512,256]{2,1,0:T(8,128)(2,1)}, bf16[2,512,256]{2,1,0:T(8,128)(2,1)}, u32[]{:S(2)}, u32[]{:S(2)}) collective-permute-start(bf16[2,512,256]{2,1,0:T(8,128)(2,1)} %get-tuple-element.36), channel_id=1, source_target_pairs={{1,0},{2,1},{3,2},{5,4},{6,5},{7,6},{9,8},{10,9},{11,10},{13,12},{... | collective-permute-start | bytes 1572872 | tf_op jit(solution)/shard_map/ppermute | solution.py:28
  10.8 31.7 %collective-permute-start.5 = (bf16[2,384,512]{2,1,0:T(8,128)(2,1)}, bf16[2,384,512]{2,1,0:T(8,128)(2,1)S(1)}, u32[]{:S(2)}, u32[]{:S(2)}) collective-permute-start(bf16[2,384,512]{2,1,0:T(8,128)(2,1)} %get-tuple-element.38), channel_id=1, source_target_pairs={{4,0},{8,4},{12,8},{16,12},{20,16},{24,20},{28,24},{32,28},{36,32}... | collective-permute-start | bytes 2359304 | tf_op jit(solution)/shard_map/ppermute | solution.py:28
  15.9 26.6 %collective-permute-start.6 = (bf16[2,384,512]{2,1,0:T(8,128)(2,1)}, bf16[2,384,512]{2,1,0:T(8,128)(2,1)}, u32[]{:S(2)}, u32[]{:S(2)}) collective-permute-start(bf16[2,384,512]{2,1,0:T(8,128)(2,1)} %get-tuple-element.39), channel_id=1, source_target_pairs={{4,0},{8,4},{12,8},{16,12},{20,16},{24,20},{28,24},{32,28},{36,32}... | collective-permute-start | bytes 2359304 | tf_op jit(solution)/shard_map/ppermute | solution.py:28
  19.7 1.0 copy-start.4
  20.7 1.9 %copy-start.6 = (bf16[1,1,6,512,512]{4,3,2,1,0:T(8,128)(2,1)S(1)}, bf16[1,1,6,512,512]{4,3,2,1,0:T(8,128)(2,1)}, u32[]{:S(2)}) copy-start(bf16[1,1,6,512,512]{4,3,2,1,0:T(8,128)(2,1)} %param.11) | copy-start | bytes 9437188
  22.6 1.0 copy-start.7
  23.6 1.0 copy-start.8
  24.7 20.7 %copy-start.1 = (f32[2,768,768]{2,1,0:T(8,128)S(1)}, f32[2,768,768]{2,1,0:T(8,128)}, u32[]{:S(2)}) copy-start(f32[2,768,768]{2,1,0:T(8,128)} %slab_ref.3) | copy-start | bytes 14155780
  24.7 20.7 %copy-start.5 = (s32[1,1,6,2]{2,3,1,0:T(2,128)S(1)}, s32[1,1,6,2]{2,3,1,0:T(2,128)}, u32[]{:S(2)}) copy-start(s32[1,1,6,2]{2,3,1,0:T(2,128)} %param.12) | copy-start | bytes 148
  29.0 13.5 %collective-permute-start.3 = (bf16[2,512,256]{2,1,0:T(8,128)(2,1)}, bf16[2,512,256]{2,1,0:T(8,128)(2,1)S(1)}, u32[]{:S(2)}, u32[]{:S(2)}) collective-permute-start(bf16[2,512,256]{2,1,0:T(8,128)(2,1)} %collective-permute-done.near0_ref), channel_id=1, source_target_pairs={{4,0},{8,4},{12,8},{16,12},{20,16},{24,20},{28,24},{32,28},{36,32}... | collective-permute-start | bytes 1572872 | tf_op jit(solution)/shard_map/ppermute | solution.py:28
  32.4 13.0 %collective-permute-start.4 = (bf16[2,512,256]{2,1,0:T(8,128)(2,1)}, bf16[2,512,256]{2,1,0:T(8,128)(2,1)S(1)}, u32[]{:S(2)}, u32[]{:S(2)}) collective-permute-start(bf16[2,512,256]{2,1,0:T(8,128)(2,1)} %collective-permute-done.1.near1_ref), channel_id=1, source_target_pairs={{4,0},{8,4},{12,8},{16,12},{20,16},{24,20},{28,24},{32,28},{36,32}... | collective-permute-start | bytes 1572872 | tf_op jit(solution)/shard_map/ppermute | solution.py:28
  54.3 26.6 %collective-permute-start.8 = (bf16[2,512,256]{2,1,0:T(8,128)(2,1)S(1)}, bf16[2,512,256]{2,1,0:T(8,128)(2,1)S(1)}, u32[]{:S(2)}, u32[]{:S(2)}) collective-permute-start(bf16[2,512,256]{2,1,0:T(8,128)(2,1)S(1)} %get-tuple-element.43), channel_id=1, source_target_pairs={{0,4},{4,8},{8,12},{12,16},{16,20},{20,24},{24,28},{28,32},{32,36}... | collective-permute-start | bytes 1572872 | tf_op jit(solution)/shard_map/ppermute | solution.py:28
  72.9 13.7 %collective-permute-start.7 = (bf16[2,512,256]{2,1,0:T(8,128)(2,1)S(1)}, bf16[2,512,256]{2,1,0:T(8,128)(2,1)S(1)}, u32[]{:S(2)}, u32[]{:S(2)}) collective-permute-start(bf16[2,512,256]{2,1,0:T(8,128)(2,1)S(1)} %get-tuple-element.41), channel_id=1, source_target_pairs={{0,4},{4,8},{8,12},{12,16},{16,20},{20,24},{24,28},{28,32},{32,36}... | collective-permute-start | bytes 1572872 | tf_op jit(solution)/shard_map/ppermute | solution.py:28
  74.8 23.6 %collective-permute-start.9 = (bf16[2,512,256]{2,1,0:T(8,128)(2,1)S(1)}, bf16[2,512,256]{2,1,0:T(8,128)(2,1)S(1)}, u32[]{:S(2)}, u32[]{:S(2)}) collective-permute-start(bf16[2,512,256]{2,1,0:T(8,128)(2,1)S(1)} %get-tuple-element.48), channel_id=1, source_target_pairs={{0,1},{1,2},{2,3},{4,5},{5,6},{6,7},{8,9},{9,10},{10,11},{12,13},{... | collective-permute-start | bytes 1572872 | tf_op jit(solution)/shard_map/ppermute | solution.py:28
  86.6 20.0 %collective-permute-start.13 = (bf16[2,512,256]{2,1,0:T(8,128)(2,1)S(1)}, bf16[2,512,256]{2,1,0:T(8,128)(2,1)S(1)}, u32[]{:S(2)}, u32[]{:S(2)}) collective-permute-start(bf16[2,512,256]{2,1,0:T(8,128)(2,1)S(1)} %add_convert_fusion.1), channel_id=1, source_target_pairs={{0,1},{1,2},{2,3},{4,5},{5,6},{6,7},{8,9},{9,10},{10,11},{12,13},{... | collective-permute-start | bytes 1572872 | tf_op jit(solution)/shard_map/ppermute | solution.py:28
  94.4 15.4 %collective-permute-start.11 = (bf16[2,384,512]{2,1,0:T(8,128)(2,1)S(1)}, bf16[2,384,512]{2,1,0:T(8,128)(2,1)S(1)}, u32[]{:S(2)}, u32[]{:S(2)}) collective-permute-start(bf16[2,384,512]{2,1,0:T(8,128)(2,1)S(1)} %get-tuple-element.50), channel_id=1, source_target_pairs={{0,4},{4,8},{8,12},{12,16},{16,20},{20,24},{24,28},{28,32},{32,36}... | collective-permute-start | bytes 2359304 | tf_op jit(solution)/shard_map/ppermute | solution.py:28
  96.3 21.9 %collective-permute-start.12 = (bf16[2,384,512]{2,1,0:T(8,128)(2,1)S(1)}, bf16[2,384,512]{2,1,0:T(8,128)(2,1)S(1)}, u32[]{:S(2)}, u32[]{:S(2)}) collective-permute-start(bf16[2,384,512]{2,1,0:T(8,128)(2,1)S(1)} %get-tuple-element.51), channel_id=1, source_target_pairs={{0,4},{4,8},{8,12},{12,16},{16,20},{20,24},{24,28},{28,32},{32,36}... | collective-permute-start | bytes 2359304 | tf_op jit(solution)/shard_map/ppermute | solution.py:28
  98.4 22.2 %collective-permute-start.10 = (bf16[2,512,256]{2,1,0:T(8,128)(2,1)S(1)}, bf16[2,512,256]{2,1,0:T(8,128)(2,1)S(1)}, u32[]{:S(2)}, u32[]{:S(2)}) collective-permute-start(bf16[2,512,256]{2,1,0:T(8,128)(2,1)S(1)} %add_convert_fusion), channel_id=1, source_target_pairs={{0,1},{1,2},{2,3},{4,5},{5,6},{6,7},{8,9},{9,10},{10,11},{12,13},{... | collective-permute-start | bytes 1572872 | tf_op jit(solution)/shard_map/ppermute | solution.py:28

commit v8 on v7

--- a/solution.py
+++ b/solution.py
@@ -73,7 +73,7 @@
         body(pl.multiple_of(i * R, R))
         return carry
 
-    lax.fori_loop(0, count // R, step, 0)
+    lax.fori_loop(0, count // R, step, 0, unroll=4)
 
 
 VMEM = pl.BlockSpec(memory_space=pltpu.VMEM)
@@ -90,60 +90,54 @@
     return pl.CostEstimate(flops=1024, bytes_accessed=1024, transcendentals=0)
 
 
-def pack_kernel(slab_ref, *refs):
-    outs, halves, (buf, sem, out_sem) = refs[: 3 + RP], refs[3 + RP : 6 + 2 * RP], refs[6 + 2 * RP :]
-    pieces = 6
-    step = T // pieces
+def pack_kernel(first_row, slab_ref, *refs):
+    count = (len(refs) - 3) // 2
+    outs, halves, (buf, sem, out_sem) = refs[:count], refs[count : 2 * count], refs[2 * count :]
+    step = Q
+    width = buf.shape[2]
 
     def copy(c):
+        return pltpu.make_async_copy(
+            slab_ref.at[:, pl.ds(first_row + c * step, step), pl.ds(0, width)],
+            buf.at[:, pl.ds(c * step, step), :],
+            sem.at[c],
+        )
+
+    def copy_out(c, k):
         rows = pl.ds(c * step, step)
-        return pltpu.make_async_copy(slab_ref.at[:, rows, :], buf.at[:, rows, :], sem.at[c])
-
-    def copies_out(c):
-        rows = pl.ds(c * step, step)
-        made = [
-            pltpu.make_async_copy(halves[k].at[:, rows, :], outs[k].at[:, rows, :], out_sem.at[c, k])
-            for k in range(3)
-            if (c + 1) * step <= W
-        ]
-        k, row = 3 + c * step // (T // RP), c * step % (T // RP)
-        rows = pl.ds(row, step)
-        return made + [
-            pltpu.make_async_copy(halves[k].at[:, rows, :], outs[k].at[:, rows, :], out_sem.at[c, 3])
-        ]
-
-    for c in range(pieces):
+        return pltpu.make_async_copy(halves[k].at[:, rows, :], outs[k].at[:, rows, :], out_sem.at[c, k])
+
+    steps = range(buf.shape[1] // step)
+    for c in steps:
         copy(c).start()
-    for c in range(pieces):
+    for c in steps:
         copy(c).wait()
         for p in range(2):
             for row in range(c * step, (c + 1) * step, 2 * R):
                 here = pl.ds(row, 2 * R)
                 part = buf[p, here, :].astype(bf16)
-                if row < W:
-                    halves[0][p, here, :] = part[:, : 2 * Q]
-                    halves[1][p, here, :] = part[:, 2 * Q : W]
-                    halves[2][p, here, :] = part[:, W:]
-                halves[3 + row // (T // RP)][p, pl.ds(row % (T // RP), 2 * R), :] = part[:, :W]
-        for one in copies_out(c):
-            one.start()
-    for c in range(pieces):
-        for one in copies_out(c):
-            one.wait()
-
-
-def pack(slab):
-    shapes = [(2, W, 2 * Q)] * 3 + [(2, T // RP, W)] * RP
+                for k in range(count):
+                    wide = width // count
+                    halves[k][p, here, :] = part[:, k * wide : (k + 1) * wide]
+        for k in range(count):
+            copy_out(c, k).start()
+    for c in steps:
+        for k in range(count):
+            copy_out(c, k).wait()
+
+
+def pack(slab, first_row, rows, width, count):
+    shapes = [(2, rows, width // count)] * count
     return pl.pallas_call(
-        pack_kernel,
+        functools.partial(pack_kernel, first_row),
         in_specs=[ANY],
-        out_specs=[ANY] * (3 + RP),
+        out_specs=[ANY] * count,
         out_shape=[jax.ShapeDtypeStruct(shape, bf16) for shape in shapes],
         scratch_shapes=[pltpu.VMEM(shape, bf16) for shape in shapes]
         + [
-            pltpu.VMEM((2, T, T), f32),
-            pltpu.SemaphoreType.DMA((6,)),
-            pltpu.SemaphoreType.DMA((6, 4)),
+            pltpu.VMEM((2, rows, width), f32),
+            pltpu.SemaphoreType.DMA((rows // Q,)),
+            pltpu.SemaphoreType.DMA((rows // Q, count)),
         ],
         cost_estimate=cost(),
         compiler_params=params(PACK_MIB),
@@ -279,12 +273,18 @@
                     mid[l, there, lanes(0)] = re[l].astype(bf16)
                     mid[l, there, lanes(1)] = im[l].astype(bf16)
 
-        for l in range(4):
-            far = jnp.dot(mid[l], gb_ref[l], preferred_element_type=f32)
+        def finish(l, far):
             re, im = far[:, :Q], far[:, Q:]
             gap = re * re + im * im - meas_ref[slot, :, lanes(l)].astype(f32)
             misfit = jnp.concatenate([gap * re, gap * im], axis=1).astype(bf16)
             out[l] = jnp.dot(misfit, ga_ref[l], preferred_element_type=f32)
+
+        fars = []
+        for l in range(4):
+            fars.append(jnp.dot(mid[l], gb_ref[l], preferred_element_type=f32))
+            if l:
+                finish(l - 1, fars[l - 1])
+        finish(3, fars[3])
 
         for j in range(4):
             for i in range(Q // R):
@@ -474,7 +474,9 @@
 def shards(slab, probe, intensities, offsets, live_count):
     left, left_t, pick = tables()
     left, left_t = jnp.asarray(left), jnp.asarray(left_t)
-    near0, near1, far, *right = pack(slab)
+    near0, near1, far = pack(slab, 0, W, T, 3)
+    right = [pack(slab, piece * (T // RP), T // RP, W, 1)[0] for piece in range(RP)]
+    far, right[1] = lax.optimization_barrier((far, right[1]))
     near0 = shifted(near0, "tile", -1)
     near1 = shifted(near1, "tile", -1)
     far = shifted(far, "tile", -1)
@@ -482,7 +484,8 @@
     measured = sort_intensities(intensities[0, 0], pick, probe, left, left_t)
     live = lax.dynamic_slice(live_count[:, 0], (lax.axis_index("scan"),), (1,))
     shifts = offsets[0, 0].T
-    near0, measured, live, shifts = lax.optimization_barrier((near0, measured, live, shifts))
+    near0, live, shifts = lax.optimization_barrier((near0, live, shifts))
+    near1, measured = lax.optimization_barrier((near1, measured))
     corner0 = shifted(near0, "scan", -1)
     corner1 = shifted(near1, "scan", -1)
     grown = solve(
@@ -494,7 +497,6 @@
     far = shifted(far, "tile", 1)
     corner0 = shifted(corner0, "scan", 1)
     near1 = (near1.astype(f32) + corner1.astype(f32)).astype(bf16)
-    near1, *right = lax.optimization_barrier((near1, *right))
     corner0, near1 = lax.optimization_barrier((corner0, near1))
     near0 = (near0.astype(f32) + corner0.astype(f32)).astype(bf16)
     near1 = shifted(near1, "tile", 1)

time: 122 us -> 121 us (level); the launches traced: 122 us -> 119 us
  starting transfers between devices: 59.7 us -> 39.2 us
  Pallas kernels: 20.8 us -> 39.7 us
  waiting for transfers between devices: 35.1 us -> 31.4 us
  local copies, waits for them, and re-layouts: 5.65 us -> 7.99 us
    ppermute x14, starting transfers between devices: 59.7 us -> 39.2 us  [shifted(): lax.ppermute(value, axis, [(i, i + by) for i in range(n) if 0 <= i + by <...]
    pallas_call x1, Pallas kernels: 7.99 us -> 24.6 us  [solve(): pl.pallas_call(slots_kernel, in_specs=[SMEM, SMEM, ANY] + [VMEM] * (9 + R...]
    ppermute x14, waiting for transfers between devices: 35.1 us -> 31.4 us  [shifted(): lax.ppermute(value, axis, [(i, i + by) for i in range(n) if 0 <= i + by <...]
    pallas_call x1 -> x3, Pallas kernels: 4.1 us -> 7.07 us  [pack(): pl.pallas_call(functools.partial(pack_kernel, first_row), in_specs=[ANY],...]
    unnamed x18 -> x20, local copies, waits for them, and re-layouts: 5.03 us -> 7.38 us
  transfers between devices with their start and end apart: 14 -> 14, of which waited for: 8 -> 7; matrix products, arithmetic and copies ran while one was open for 1% -> 1% of each run, Pallas kernels for 5% -> 9%
where the time goes in v8:
time: 121 us; the launch traced here: 119 us
  Pallas kernels  39.7 us (33%)
  starting transfers between devices  39.2 us (32%)
  waiting for transfers between devices  31.4 us (26%)
  local copies, waits for them, and re-layouts  7.99 us (7%)
    ppermute x14, starting transfers between devices, shifted(): lax.ppermute(value, axis, [(i, i + by) for i in range(n) if 0 <= i + by <...  39.2 us
    ppermute x14, waiting for transfers between devices, shifted(): lax.ppermute(value, axis, [(i, i + by) for i in range(n) if 0 <= i + by <...  31.4 us
    pallas_call x1, Pallas kernels, solve(): pl.pallas_call(slots_kernel, in_specs=[SMEM, SMEM, ANY] + [VMEM] * (9 + R...  24.6 us
    unnamed x20, local copies, waits for them, and re-layouts  7.38 us
    pallas_call x3, Pallas kernels, pack(): pl.pallas_call(functools.partial(pack_kernel, first_row), in_specs=[ANY],...  7.07 us
    pallas_call x1, Pallas kernels, sort_intensities(): pl.pallas_call(sort_kernel, grid=(measured.shape[0],), in_specs=[whole, w...  4.3 us
  transfers between devices with their start and end apart: 14, of which 7 were waited for; matrix products, arithmetic and copies ran while one was open for 1% of the time, Pallas kernels for 9%

profile of v8, /device:TPU:22, one launch (start us, length us, event | category | flops | bytes accessed | tf_op | source)
XLA Modules:
  0.0 118.8 jit_solution(14542817043504750248)
XLA Ops:
  0.0 2.8 %shard_map.91 = (bf16[2,512,256]{2,1,0:T(8,128)(2,1)}, bf16[2,512,256]{2,1,0:T(8,128)(2,1)}, bf16[2,512,256]{2,1,0:T(8,128)(2,1)}) custom-call(f32[2,768,768]{2,1,0:T(8,128)} %slab_ref.7), custom_call_target="tpu_custom_call" | custom-call | flops 1024 | bytes 1024 | tf_op jit(solution)/shard_map/pallas_call | solution.py:131
  2.8 2.4 %collective-permute-start = (bf16[2,512,256]{2,1,0:T(8,128)(2,1)}, bf16[2,512,256]{2,1,0:T(8,128)(2,1)}, u32[]{:S(2)}, u32[]{:S(2)}) collective-permute-start(bf16[2,512,256]{2,1,0:T(8,128)(2,1)} %get-tuple-element.29), channel_id=1, source_target_pairs={{1,0},{2,1},{3,2},{5,4},{6,5},{7,6},{9,8},{10,9},{11,10},{13,12},{... | collective-permute-start | bytes 1572872 | tf_op jit(solution)/shard_map/ppermute | solution.py:28
  5.2 2.5 %collective-permute-start.1 = (bf16[2,512,256]{2,1,0:T(8,128)(2,1)}, bf16[2,512,256]{2,1,0:T(8,128)(2,1)}, u32[]{:S(2)}, u32[]{:S(2)}) collective-permute-start(bf16[2,512,256]{2,1,0:T(8,128)(2,1)} %get-tuple-element.33), channel_id=1, source_target_pairs={{1,0},{2,1},{3,2},{5,4},{6,5},{7,6},{9,8},{10,9},{11,10},{13,12},{... | collective-permute-start | bytes 1572872 | tf_op jit(solution)/shard_map/ppermute | solution.py:28
  7.7 2.2 %shard_map.94 = bf16[2,384,512]{2,1,0:T(8,128)(2,1)} custom-call(f32[2,768,768]{2,1,0:T(8,128)} %slab_ref.7), custom_call_target="tpu_custom_call" | custom-call | flops 1024 | bytes 1024 | tf_op jit(solution)/shard_map/pallas_call | solution.py:131
  9.8 5.1 %collective-permute-start.5 = (bf16[2,384,512]{2,1,0:T(8,128)(2,1)}, bf16[2,384,512]{2,1,0:T(8,128)(2,1)S(1)}, u32[]{:S(2)}, u32[]{:S(2)}) collective-permute-start(bf16[2,384,512]{2,1,0:T(8,128)(2,1)} %shard_map.94), channel_id=1, source_target_pairs={{4,0},{8,4},{12,8},{16,12},{20,16},{24,20},{28,24},{32,28},{36,32}... | collective-permute-start | bytes 2359304 | tf_op jit(solution)/shard_map/ppermute | solution.py:28
  14.9 2.2 %shard_map.93 = bf16[2,384,512]{2,1,0:T(8,128)(2,1)} custom-call(f32[2,768,768]{2,1,0:T(8,128)} %slab_ref.7), custom_call_target="tpu_custom_call" | custom-call | flops 1024 | bytes 1024 | tf_op jit(solution)/shard_map/pallas_call | solution.py:131
  17.1 2.2 %collective-permute-start.2 = (bf16[2,512,256]{2,1,0:T(8,128)(2,1)}, bf16[2,512,256]{2,1,0:T(8,128)(2,1)}, u32[]{:S(2)}, u32[]{:S(2)}) collective-permute-start(bf16[2,512,256]{2,1,0:T(8,128)(2,1)} %get-tuple-element.36), channel_id=1, source_target_pairs={{1,0},{2,1},{3,2},{5,4},{6,5},{7,6},{9,8},{10,9},{11,10},{13,12},{... | collective-permute-start | bytes 1572872 | tf_op jit(solution)/shard_map/ppermute | solution.py:28
  19.3 2.9 %collective-permute-start.6 = (bf16[2,384,512]{2,1,0:T(8,128)(2,1)}, bf16[2,384,512]{2,1,0:T(8,128)(2,1)}, u32[]{:S(2)}, u32[]{:S(2)}) collective-permute-start(bf16[2,384,512]{2,1,0:T(8,128)(2,1)} %shard_map.93), channel_id=1, source_target_pairs={{4,0},{8,4},{12,8},{16,12},{20,16},{24,20},{28,24},{32,28},{36,32}... | collective-permute-start | bytes 2359304 | tf_op jit(solution)/shard_map/ppermute | solution.py:28
  22.8 1.0 copy-done.4
  23.8 1.9 %copy-done.7 = bf16[1,1,6,512,512]{4,3,2,1,0:T(8,128)(2,1)S(1)} copy-done((bf16[1,1,6,512,512]{4,3,2,1,0:T(8,128)(2,1)S(1)}, bf16[1,1,6,512,512]{4,3,2,1,0:T(8,128)(2,1)}, u32[]{:S(2)}) %copy-start.7) | copy-done | bytes 3145752
  25.7 1.0 copy-done.8
  26.8 1.0 copy-done.9
  27.8 4.3 %shard_map.92.meas_ref = bf16[6,512,512]{2,1,0:T(8,128)(2,1)S(1)} custom-call(bf16[512,512]{1,0:T(8,128)(2,1)S(1)} %copy-done.9, bf16[512,512]{1,0:T(8,128)(2,1)S(1)} %copy-done.8, bf16[6,512,512]{2,1,0:T(8,128)(2,1)S(1)} %bitcast.6, f32[2,512,512]{2,1,0:T(8,128)S(1)} %copy-done.2, bf16[4,256,256]{2,1,0:T(8,128)(2,1)S(1)} %copy-done.4, ...), custom_call_target="tpu_custom_call" | custom-call | flops 3221225472 | bytes 6291456 | tf_op jit(solution)/shard_map/pallas_call | solution.py:156
  32.1 1.9 %collective-permute-start.3 = (bf16[2,512,256]{2,1,0:T(8,128)(2,1)}, bf16[2,512,256]{2,1,0:T(8,128)(2,1)S(1)}, u32[]{:S(2)}, u32[]{:S(2)}) collective-permute-start(bf16[2,512,256]{2,1,0:T(8,128)(2,1)} %collective-permute-done.near0_ref), channel_id=1, source_target_pairs={{4,0},{8,4},{12,8},{16,12},{20,16},{24,20},{28,24},{32,28},{36,32}... | collective-permute-start | bytes 1572872 | tf_op jit(solution)/shard_map/ppermute | solution.py:28
  34.1 2.4 %collective-permute-start.4 = (bf16[2,512,256]{2,1,0:T(8,128)(2,1)}, bf16[2,512,256]{2,1,0:T(8,128)(2,1)S(1)}, u32[]{:S(2)}, u32[]{:S(2)}) collective-permute-start(bf16[2,512,256]{2,1,0:T(8,128)(2,1)} %collective-permute-done.1.near1_ref), channel_id=1, source_target_pairs={{4,0},{8,4},{12,8},{16,12},{20,16},{24,20},{28,24},{32,28},{36,32}... | collective-permute-start | bytes 1572872 | tf_op jit(solution)/shard_map/ppermute | solution.py:28
  36.5 4.6 %collective-permute-done.2.far_ref = bf16[2,512,256]{2,1,0:T(8,128)(2,1)} collective-permute-done((bf16[2,512,256]{2,1,0:T(8,128)(2,1)}, bf16[2,512,256]{2,1,0:T(8,128)(2,1)}, u32[]{:S(2)}, u32[]{:S(2)}) %collective-permute-start.2) | collective-permute-done | bytes 524320 | tf_op jit(solution)/shard_map/ppermute | solution.py:28
  41.1 5.5 %collective-permute-done.4.corner1_ref = bf16[2,512,256]{2,1,0:T(8,128)(2,1)S(1)} collective-permute-done((bf16[2,512,256]{2,1,0:T(8,128)(2,1)}, bf16[2,512,256]{2,1,0:T(8,128)(2,1)S(1)}, u32[]{:S(2)}, u32[]{:S(2)}) %collective-permute-start.4) | collective-permute-done | bytes 524320 | tf_op jit(solution)/shard_map/ppermute | solution.py:28
  46.7 2.3 %copy-done.1 = f32[2,768,768]{2,1,0:T(8,128)S(1)} copy-done((f32[2,768,768]{2,1,0:T(8,128)S(1)}, f32[2,768,768]{2,1,0:T(8,128)}, u32[]{:S(2)}) %copy-start.1) | copy-done | bytes 4718616
  49.0 24.6 %shard_map.95.grown.refs_4_ = f32[2,10,1280,128]{3,2,1,0:T(8,128)S(1)} custom-call(s32[1]{0:T(128)} %bitcast.live_ref, s32[2,6]{1,0:T(2,128)S(1)} %bitcast.5, f32[2,768,768]{2,1,0:T(8,128)S(1)} %copy-done.1, bf16[2,512,256]{2,1,0:T(8,128)(2,1)} %collective-permute-done.near0_ref, bf16[2,512,256]{2,1,0:T(8,128)(2,1)} %collective-permute-done.1.near1_ref, ...), custom_call_target="tpu_custom_call" | custom-call | flops 1024 | bytes 1024 | tf_op jit(solution)/shard_map/pallas_call | solution.py:334
  74.3 1.9 %collective-permute-start.8 = (bf16[2,512,256]{2,1,0:T(8,128)(2,1)S(1)}, bf16[2,512,256]{2,1,0:T(8,128)(2,1)S(1)}, u32[]{:S(2)}, u32[]{:S(2)}) collective-permute-start(bf16[2,512,256]{2,1,0:T(8,128)(2,1)S(1)} %get-tuple-element.42), channel_id=1, source_target_pairs={{0,4},{4,8},{8,12},{12,16},{16,20},{20,24},{24,28},{28,32},{32,36}... | collective-permute-start | bytes 1572872 | tf_op jit(solution)/shard_map/ppermute | solution.py:28
  76.2 1.9 %collective-permute-start.7 = (bf16[2,512,256]{2,1,0:T(8,128)(2,1)S(1)}, bf16[2,512,256]{2,1,0:T(8,128)(2,1)S(1)}, u32[]{:S(2)}, u32[]{:S(2)}) collective-permute-start(bf16[2,512,256]{2,1,0:T(8,128)(2,1)S(1)} %get-tuple-element.40), channel_id=1, source_target_pairs={{0,4},{4,8},{8,12},{12,16},{16,20},{20,24},{24,28},{28,32},{32,36}... | collective-permute-start | bytes 1572872 | tf_op jit(solution)/shard_map/ppermute | solution.py:28
  78.1 5.8 %collective-permute-start.9 = (bf16[2,512,256]{2,1,0:T(8,128)(2,1)S(1)}, bf16[2,512,256]{2,1,0:T(8,128)(2,1)S(1)}, u32[]{:S(2)}, u32[]{:S(2)}) collective-permute-start(bf16[2,512,256]{2,1,0:T(8,128)(2,1)S(1)} %get-tuple-element.44), channel_id=1, source_target_pairs={{0,1},{1,2},{2,3},{4,5},{5,6},{6,7},{8,9},{9,10},{10,11},{12,13},{... | collective-permute-start | bytes 1572872 | tf_op jit(solution)/shard_map/ppermute | solution.py:28
  84.0 1.9 %collective-permute-start.11 = (bf16[2,384,512]{2,1,0:T(8,128)(2,1)S(1)}, bf16[2,384,512]{2,1,0:T(8,128)(2,1)S(1)}, u32[]{:S(2)}, u32[]{:S(2)}) collective-permute-start(bf16[2,384,512]{2,1,0:T(8,128)(2,1)S(1)} %get-tuple-element.46), channel_id=1, source_target_pairs={{0,4},{4,8},{8,12},{12,16},{16,20},{20,24},{24,28},{28,32},{32,36}... | collective-permute-start | bytes 2359304 | tf_op jit(solution)/shard_map/ppermute | solution.py:28
  85.9 1.9 %collective-permute-start.12 = (bf16[2,384,512]{2,1,0:T(8,128)(2,1)S(1)}, bf16[2,384,512]{2,1,0:T(8,128)(2,1)S(1)}, u32[]{:S(2)}, u32[]{:S(2)}) collective-permute-start(bf16[2,384,512]{2,1,0:T(8,128)(2,1)S(1)} %get-tuple-element.47), channel_id=1, source_target_pairs={{0,4},{4,8},{8,12},{12,16},{16,20},{20,24},{24,28},{28,32},{32,36}... | collective-permute-start | bytes 2359304 | tf_op jit(solution)/shard_map/ppermute | solution.py:28
  88.0 4.7 %collective-permute-done.7 = bf16[2,512,256]{2,1,0:T(8,128)(2,1)S(1)} collective-permute-done((bf16[2,512,256]{2,1,0:T(8,128)(2,1)S(1)}, bf16[2,512,256]{2,1,0:T(8,128)(2,1)S(1)}, u32[]{:S(2)}, u32[]{:S(2)}) %collective-permute-start.7) | collective-permute-done | bytes 524320 | tf_op jit(solution)/shard_map/ppermute | solution.py:28
  92.7 2.0 %collective-permute-start.13 = (bf16[2,512,256]{2,1,0:T(8,128)(2,1)S(1)}, bf16[2,512,256]{2,1,0:T(8,128)(2,1)S(1)}, u32[]{:S(2)}, u32[]{:S(2)}) collective-permute-start(bf16[2,512,256]{2,1,0:T(8,128)(2,1)S(1)} %add_convert_fusion.1), channel_id=1, source_target_pairs={{0,1},{1,2},{2,3},{4,5},{5,6},{6,7},{8,9},{9,10},{10,11},{12,13},{... | collective-permute-start | bytes 1572872 | tf_op jit(solution)/shard_map/ppermute | solution.py:28
  94.8 1.5 %collective-permute-done.9.refs_2_ = bf16[2,512,256]{2,1,0:T(8,128)(2,1)S(1)} collective-permute-done((bf16[2,512,256]{2,1,0:T(8,128)(2,1)S(1)}, bf16[2,512,256]{2,1,0:T(8,128)(2,1)S(1)}, u32[]{:S(2)}, u32[]{:S(2)}) %collective-permute-start.9) | collective-permute-done | bytes 524320 | tf_op jit(solution)/shard_map/ppermute | solution.py:28
  96.2 4.4 %collective-permute-start.10 = (bf16[2,512,256]{2,1,0:T(8,128)(2,1)S(1)}, bf16[2,512,256]{2,1,0:T(8,128)(2,1)S(1)}, u32[]{:S(2)}, u32[]{:S(2)}) collective-permute-start(bf16[2,512,256]{2,1,0:T(8,128)(2,1)S(1)} %add_convert_fusion), channel_id=1, source_target_pairs={{0,1},{1,2},{2,3},{4,5},{5,6},{6,7},{8,9},{9,10},{10,11},{12,13},{... | collective-permute-start | bytes 1572872 | tf_op jit(solution)/shard_map/ppermute | solution.py:28
  101.1 8.4 %collective-permute-done.12.refs_1_ = bf16[2,384,512]{2,1,0:T(8,128)(2,1)S(1)} collective-permute-done((bf16[2,384,512]{2,1,0:T(8,128)(2,1)S(1)}, bf16[2,384,512]{2,1,0:T(8,128)(2,1)S(1)}, u32[]{:S(2)}, u32[]{:S(2)}) %collective-permute-start.12) | collective-permute-done | bytes 786464 | tf_op jit(solution)/shard_map/ppermute | solution.py:28
  109.5 2.0 %shard_map.97 = (f32[2,10,1280,128]{3,2,1,0:T(8,128)S(1)}, f32[2,768,768]{2,1,0:T(8,128)}) custom-call(bf16[2,384,512]{2,1,0:T(8,128)(2,1)S(1)} %collective-permute-done.11.refs_0_, bf16[2,384,512]{2,1,0:T(8,128)(2,1)S(1)} %collective-permute-done.12.refs_1_, ...), custom_call_target="tpu_custom_call", output_to_operand_aliasing={{0}: (4, {})} | custom-call | flops 1024 | bytes 1024 | tf_op jit(solution)/shard_map/pallas_call | solution.py:435
  111.6 6.2 %collective-permute-done.10.near_ref = bf16[2,512,256]{2,1,0:T(8,128)(2,1)S(1)} collective-permute-done((bf16[2,512,256]{2,1,0:T(8,128)(2,1)S(1)}, bf16[2,512,256]{2,1,0:T(8,128)(2,1)S(1)}, u32[]{:S(2)}, u32[]{:S(2)}) %collective-permute-start.10) | collective-permute-done | bytes 524320 | tf_op jit(solution)/shard_map/ppermute | solution.py:28
  117.8 1.0 shard_map.98
  (27 shorter events, 2.0 us)
Async XLA Ops:
  0.0 22.2 %copy-start = (s32[32,1]{0,1:T(1,128)S(1)}, s32[32,1]{0,1:T(1,128)}, u32[]{:S(2)}) copy-start(s32[32,1]{0,1:T(1,128)} %param.13) | copy-start | bytes 388
  2.8 29.4 %collective-permute-start = (bf16[2,512,256]{2,1,0:T(8,128)(2,1)}, bf16[2,512,256]{2,1,0:T(8,128)(2,1)}, u32[]{:S(2)}, u32[]{:S(2)}) collective-permute-start(bf16[2,512,256]{2,1,0:T(8,128)(2,1)} %get-tuple-element.29), channel_id=1, source_target_pairs={{1,0},{2,1},{3,2},{5,4},{6,5},{7,6},{9,8},{10,9},{11,10},{13,12},{... | collective-permute-start | bytes 1572872 | tf_op jit(solution)/shard_map/ppermute | solution.py:28
  5.1 17.7 %copy-start.2 = (f32[2,512,512]{2,1,0:T(8,128)S(1)}, f32[2,512,512]{2,1,0:T(8,128)}, u32[]{:S(2)}) copy-start(f32[2,512,512]{2,1,0:T(8,128)} %probe_ref.1) | copy-start | bytes 6291460
  5.2 17.6 %copy-start.3 = (bf16[4,256,256]{2,1,0:T(8,128)(2,1)S(1)}, bf16[4,256,256]{2,1,0:T(8,128)(2,1)}, u32[]{:S(2)}) copy-start(bf16[4,256,256]{2,1,0:T(8,128)(2,1)} %constant.20.clone.refs_2_.gb_ref) | copy-start | bytes 1572868
  5.2 28.9 %collective-permute-start.1 = (bf16[2,512,256]{2,1,0:T(8,128)(2,1)}, bf16[2,512,256]{2,1,0:T(8,128)(2,1)}, u32[]{:S(2)}, u32[]{:S(2)}) collective-permute-start(bf16[2,512,256]{2,1,0:T(8,128)(2,1)} %get-tuple-element.33), channel_id=1, source_target_pairs={{1,0},{2,1},{3,2},{5,4},{6,5},{7,6},{9,8},{10,9},{11,10},{13,12},{... | collective-permute-start | bytes 1572872 | tf_op jit(solution)/shard_map/ppermute | solution.py:28
  9.8 31.3 %collective-permute-start.5 = (bf16[2,384,512]{2,1,0:T(8,128)(2,1)}, bf16[2,384,512]{2,1,0:T(8,128)(2,1)S(1)}, u32[]{:S(2)}, u32[]{:S(2)}) collective-permute-start(bf16[2,384,512]{2,1,0:T(8,128)(2,1)} %shard_map.94), channel_id=1, source_target_pairs={{4,0},{8,4},{12,8},{16,12},{20,16},{24,20},{28,24},{32,28},{36,32}... | collective-permute-start | bytes 2359304 | tf_op jit(solution)/shard_map/ppermute | solution.py:28
  17.1 24.0 %collective-permute-start.2 = (bf16[2,512,256]{2,1,0:T(8,128)(2,1)}, bf16[2,512,256]{2,1,0:T(8,128)(2,1)}, u32[]{:S(2)}, u32[]{:S(2)}) collective-permute-start(bf16[2,512,256]{2,1,0:T(8,128)(2,1)} %get-tuple-element.36), channel_id=1, source_target_pairs={{1,0},{2,1},{3,2},{5,4},{6,5},{7,6},{9,8},{10,9},{11,10},{13,12},{... | collective-permute-start | bytes 1572872 | tf_op jit(solution)/shard_map/ppermute | solution.py:28
  19.3 21.8 %collective-permute-start.6 = (bf16[2,384,512]{2,1,0:T(8,128)(2,1)}, bf16[2,384,512]{2,1,0:T(8,128)(2,1)}, u32[]{:S(2)}, u32[]{:S(2)}) collective-permute-start(bf16[2,384,512]{2,1,0:T(8,128)(2,1)} %shard_map.93), channel_id=1, source_target_pairs={{4,0},{8,4},{12,8},{16,12},{20,16},{24,20},{28,24},{32,28},{36,32}... | collective-permute-start | bytes 2359304 | tf_op jit(solution)/shard_map/ppermute | solution.py:28
  22.8 1.0 copy-start.4
  23.8 1.9 %copy-start.7 = (bf16[1,1,6,512,512]{4,3,2,1,0:T(8,128)(2,1)S(1)}, bf16[1,1,6,512,512]{4,3,2,1,0:T(8,128)(2,1)}, u32[]{:S(2)}) copy-start(bf16[1,1,6,512,512]{4,3,2,1,0:T(8,128)(2,1)} %param.11) | copy-start | bytes 9437188
  25.7 1.0 copy-start.8
  26.8 1.0 copy-start.9
  27.8 18.9 %copy-start.5 = (bf16[4,256,256]{2,1,0:T(8,128)(2,1)S(1)}, bf16[4,256,256]{2,1,0:T(8,128)(2,1)}, u32[]{:S(2)}) copy-start(bf16[4,256,256]{2,1,0:T(8,128)(2,1)} %constant.19.clone.refs_1_.ga_ref) | copy-start | bytes 1572868
  27.8 18.9 %copy-start.6 = (s32[1,1,6,2]{2,3,1,0:T(2,128)S(1)}, s32[1,1,6,2]{2,3,1,0:T(2,128)}, u32[]{:S(2)}) copy-start(s32[1,1,6,2]{2,3,1,0:T(2,128)} %param.12) | copy-start | bytes 148
  32.1 9.0 %collective-permute-start.3 = (bf16[2,512,256]{2,1,0:T(8,128)(2,1)}, bf16[2,512,256]{2,1,0:T(8,128)(2,1)S(1)}, u32[]{:S(2)}, u32[]{:S(2)}) collective-permute-start(bf16[2,512,256]{2,1,0:T(8,128)(2,1)} %collective-permute-done.near0_ref), channel_id=1, source_target_pairs={{4,0},{8,4},{12,8},{16,12},{20,16},{24,20},{28,24},{32,28},{36,32}... | collective-permute-start | bytes 1572872 | tf_op jit(solution)/shard_map/ppermute | solution.py:28
  34.1 12.6 %collective-permute-start.4 = (bf16[2,512,256]{2,1,0:T(8,128)(2,1)}, bf16[2,512,256]{2,1,0:T(8,128)(2,1)S(1)}, u32[]{:S(2)}, u32[]{:S(2)}) collective-permute-start(bf16[2,512,256]{2,1,0:T(8,128)(2,1)} %collective-permute-done.1.near1_ref), channel_id=1, source_target_pairs={{4,0},{8,4},{12,8},{16,12},{20,16},{24,20},{28,24},{32,28},{36,32}... | collective-permute-start | bytes 1572872 | tf_op jit(solution)/shard_map/ppermute | solution.py:28
  46.7 2.3 %copy-start.1 = (f32[2,768,768]{2,1,0:T(8,128)S(1)}, f32[2,768,768]{2,1,0:T(8,128)}, u32[]{:S(2)}) copy-start(f32[2,768,768]{2,1,0:T(8,128)} %slab_ref.7) | copy-start | bytes 14155780
  74.3 13.5 %collective-permute-start.8 = (bf16[2,512,256]{2,1,0:T(8,128)(2,1)S(1)}, bf16[2,512,256]{2,1,0:T(8,128)(2,1)S(1)}, u32[]{:S(2)}, u32[]{:S(2)}) collective-permute-start(bf16[2,512,256]{2,1,0:T(8,128)(2,1)S(1)} %get-tuple-element.42), channel_id=1, source_target_pairs={{0,4},{4,8},{8,12},{12,16},{16,20},{20,24},{24,28},{28,32},{32,36}... | collective-permute-start | bytes 1572872 | tf_op jit(solution)/shard_map/ppermute | solution.py:28
  76.2 16.4 %collective-permute-start.7 = (bf16[2,512,256]{2,1,0:T(8,128)(2,1)S(1)}, bf16[2,512,256]{2,1,0:T(8,128)(2,1)S(1)}, u32[]{:S(2)}, u32[]{:S(2)}) collective-permute-start(bf16[2,512,256]{2,1,0:T(8,128)(2,1)S(1)} %get-tuple-element.40), channel_id=1, source_target_pairs={{0,4},{4,8},{8,12},{12,16},{16,20},{20,24},{24,28},{28,32},{32,36}... | collective-permute-start | bytes 1572872 | tf_op jit(solution)/shard_map/ppermute | solution.py:28
  78.1 18.1 %collective-permute-start.9 = (bf16[2,512,256]{2,1,0:T(8,128)(2,1)S(1)}, bf16[2,512,256]{2,1,0:T(8,128)(2,1)S(1)}, u32[]{:S(2)}, u32[]{:S(2)}) collective-permute-start(bf16[2,512,256]{2,1,0:T(8,128)(2,1)S(1)} %get-tuple-element.44), channel_id=1, source_target_pairs={{0,1},{1,2},{2,3},{4,5},{5,6},{6,7},{8,9},{9,10},{10,11},{12,13},{... | collective-permute-start | bytes 1572872 | tf_op jit(solution)/shard_map/ppermute | solution.py:28
  84.0 17.1 %collective-permute-start.11 = (bf16[2,384,512]{2,1,0:T(8,128)(2,1)S(1)}, bf16[2,384,512]{2,1,0:T(8,128)(2,1)S(1)}, u32[]{:S(2)}, u32[]{:S(2)}) collective-permute-start(bf16[2,384,512]{2,1,0:T(8,128)(2,1)S(1)} %get-tuple-element.46), channel_id=1, source_target_pairs={{0,4},{4,8},{8,12},{12,16},{16,20},{20,24},{24,28},{28,32},{32,36}... | collective-permute-start | bytes 2359304 | tf_op jit(solution)/shard_map/ppermute | solution.py:28
  85.9 23.6 %collective-permute-start.12 = (bf16[2,384,512]{2,1,0:T(8,128)(2,1)S(1)}, bf16[2,384,512]{2,1,0:T(8,128)(2,1)S(1)}, u32[]{:S(2)}, u32[]{:S(2)}) collective-permute-start(bf16[2,384,512]{2,1,0:T(8,128)(2,1)S(1)} %get-tuple-element.47), channel_id=1, source_target_pairs={{0,4},{4,8},{8,12},{12,16},{16,20},{20,24},{24,28},{28,32},{32,36}... | collective-permute-start | bytes 2359304 | tf_op jit(solution)/shard_map/ppermute | solution.py:28
  92.7 16.9 %collective-permute-start.13 = (bf16[2,512,256]{2,1,0:T(8,128)(2,1)S(1)}, bf16[2,512,256]{2,1,0:T(8,128)(2,1)S(1)}, u32[]{:S(2)}, u32[]{:S(2)}) collective-permute-start(bf16[2,512,256]{2,1,0:T(8,128)(2,1)S(1)} %add_convert_fusion.1), channel_id=1, source_target_pairs={{0,1},{1,2},{2,3},{4,5},{5,6},{6,7},{8,9},{9,10},{10,11},{12,13},{... | collective-permute-start | bytes 1572872 | tf_op jit(solution)/shard_map/ppermute | solution.py:28
  96.2 21.5 %collective-permute-start.10 = (bf16[2,512,256]{2,1,0:T(8,128)(2,1)S(1)}, bf16[2,512,256]{2,1,0:T(8,128)(2,1)S(1)}, u32[]{:S(2)}, u32[]{:S(2)}) collective-permute-start(bf16[2,512,256]{2,1,0:T(8,128)(2,1)S(1)} %add_convert_fusion), channel_id=1, source_target_pairs={{0,1},{1,2},{2,3},{4,5},{5,6},{6,7},{8,9},{9,10},{10,11},{12,13},{... | collective-permute-start | bytes 1572872 | tf_op jit(solution)/shard_map/ppermute | solution.py:28

commit v9 on v7

--- a/solution.py
+++ b/solution.py
@@ -73,7 +73,7 @@
         body(pl.multiple_of(i * R, R))
         return carry
 
-    lax.fori_loop(0, count // R, step, 0)
+    lax.fori_loop(0, count // R, step, 0, unroll=4)
 
 
 VMEM = pl.BlockSpec(memory_space=pltpu.VMEM)
@@ -279,12 +279,18 @@
                     mid[l, there, lanes(0)] = re[l].astype(bf16)
                     mid[l, there, lanes(1)] = im[l].astype(bf16)
 
-        for l in range(4):
-            far = jnp.dot(mid[l], gb_ref[l], preferred_element_type=f32)
+        def finish(l, far):
             re, im = far[:, :Q], far[:, Q:]
             gap = re * re + im * im - meas_ref[slot, :, lanes(l)].astype(f32)
             misfit = jnp.concatenate([gap * re, gap * im], axis=1).astype(bf16)
             out[l] = jnp.dot(misfit, ga_ref[l], preferred_element_type=f32)
+
+        fars = []
+        for l in range(4):
+            fars.append(jnp.dot(mid[l], gb_ref[l], preferred_element_type=f32))
+            if l:
+                finish(l - 1, fars[l - 1])
+        finish(3, fars[3])
 
         for j in range(4):
             for i in range(Q // R):
@@ -479,10 +485,13 @@
     near1 = shifted(near1, "tile", -1)
     far = shifted(far, "tile", -1)
     right = [shifted(piece, "scan", -1) for piece in right]
-    measured = sort_intensities(intensities[0, 0], pick, probe, left, left_t)
     live = lax.dynamic_slice(live_count[:, 0], (lax.axis_index("scan"),), (1,))
     shifts = offsets[0, 0].T
-    near0, measured, live, shifts = lax.optimization_barrier((near0, measured, live, shifts))
+    near0, live, shifts, intensities = lax.optimization_barrier(
+        (near0, live, shifts, intensities)
+    )
+    measured = sort_intensities(intensities[0, 0], pick, probe, left, left_t)
+    near1, measured = lax.optimization_barrier((near1, measured))
     corner0 = shifted(near0, "scan", -1)
     corner1 = shifted(near1, "scan", -1)
     grown = solve(
@@ -494,7 +503,6 @@
     far = shifted(far, "tile", 1)
     corner0 = shifted(corner0, "scan", 1)
     near1 = (near1.astype(f32) + corner1.astype(f32)).astype(bf16)
-    near1, *right = lax.optimization_barrier((near1, *right))
     corner0, near1 = lax.optimization_barrier((corner0, near1))
     near0 = (near0.astype(f32) + corner0.astype(f32)).astype(bf16)
     near1 = shifted(near1, "tile", 1)

time: 122 us -> 116 us (0.951)
  the two profiles are of different devices: /device:TPU:22 before, /device:TPU:124 now
where the time goes in v9:
time: 116 us; the launch traced here: 115 us
  starting transfers between devices  48.5 us (42%)
  waiting for transfers between devices  40.8 us (35%)
  Pallas kernels  19.6 us (17%)
  local copies, waits for them, and re-layouts  5.64 us (5%)
    ppermute x14, starting transfers between devices, shifted(): lax.ppermute(value, axis, [(i, i + by) for i in range(n) if 0 <= i + by <...  48.5 us
    ppermute x14, waiting for transfers between devices, shifted(): lax.ppermute(value, axis, [(i, i + by) for i in range(n) if 0 <= i + by <...  40.8 us
    pallas_call x1, Pallas kernels, solve(): pl.pallas_call(slots_kernel, in_specs=[SMEM, SMEM, ANY] + [VMEM] * (9 + R...  7.54 us
    unnamed x18, local copies, waits for them, and re-layouts  5.03 us
    pallas_call x1, Pallas kernels, sort_intensities(): pl.pallas_call(sort_kernel, grid=(measured.shape[0],), in_specs=[whole, w...  4.3 us
    pallas_call x1, Pallas kernels, pack(): pl.pallas_call(pack_kernel, in_specs=[ANY], out_specs=[ANY] * (3 + RP), o...  4.1 us
  transfers between devices with their start and end apart: 14, of which 8 were waited for; matrix products, arithmetic and copies ran while one was open for 1% of the time, Pallas kernels for 6%

profile of v9, /device:TPU:124, one launch (start us, length us, event | category | flops | bytes accessed | tf_op | source)
XLA Modules:
  0.0 115.1 jit_solution(7187179318800248208)
XLA Ops:
  0.0 4.1 %shard_map.91 = (bf16[2,512,256]{2,1,0:T(8,128)(2,1)}, bf16[2,512,256]{2,1,0:T(8,128)(2,1)}, bf16[2,512,256]{2,1,0:T(8,128)(2,1)}, bf16[2,384,512]{2,1,0:T(8,128)(2,1)}, bf16[2,384,512]{2,1,0:T(8,128)(2,1)}) custom-call(f32[2,768,768]{2,1,0:T(8,128)} %slab_ref.3), custom_call_target="tpu_custom_call" | custom-call | flops 1024 | bytes 1024 | tf_op jit(solution)/shard_map/pallas_call | solution.py:137
  4.1 3.5 %collective-permute-start = (bf16[2,512,256]{2,1,0:T(8,128)(2,1)}, bf16[2,512,256]{2,1,0:T(8,128)(2,1)}, u32[]{:S(2)}, u32[]{:S(2)}) collective-permute-start(bf16[2,512,256]{2,1,0:T(8,128)(2,1)} %get-tuple-element.30), channel_id=1, source_target_pairs={{1,0},{2,1},{3,2},{5,4},{6,5},{7,6},{9,8},{10,9},{11,10},{13,12},{... | collective-permute-start | bytes 1572872 | tf_op jit(solution)/shard_map/ppermute | solution.py:28
  7.6 2.3 %collective-permute-start.1 = (bf16[2,512,256]{2,1,0:T(8,128)(2,1)}, bf16[2,512,256]{2,1,0:T(8,128)(2,1)}, u32[]{:S(2)}, u32[]{:S(2)}) collective-permute-start(bf16[2,512,256]{2,1,0:T(8,128)(2,1)} %get-tuple-element.34), channel_id=1, source_target_pairs={{1,0},{2,1},{3,2},{5,4},{6,5},{7,6},{9,8},{10,9},{11,10},{13,12},{... | collective-permute-start | bytes 1572872 | tf_op jit(solution)/shard_map/ppermute | solution.py:28
  9.9 2.4 %collective-permute-start.2 = (bf16[2,512,256]{2,1,0:T(8,128)(2,1)}, bf16[2,512,256]{2,1,0:T(8,128)(2,1)}, u32[]{:S(2)}, u32[]{:S(2)}) collective-permute-start(bf16[2,512,256]{2,1,0:T(8,128)(2,1)} %get-tuple-element.37), channel_id=1, source_target_pairs={{1,0},{2,1},{3,2},{5,4},{6,5},{7,6},{9,8},{10,9},{11,10},{13,12},{... | collective-permute-start | bytes 1572872 | tf_op jit(solution)/shard_map/ppermute | solution.py:28
  12.3 1.9 %collective-permute-start.5 = (bf16[2,384,512]{2,1,0:T(8,128)(2,1)}, bf16[2,384,512]{2,1,0:T(8,128)(2,1)S(1)}, u32[]{:S(2)}, u32[]{:S(2)}) collective-permute-start(bf16[2,384,512]{2,1,0:T(8,128)(2,1)} %get-tuple-element.39), channel_id=1, source_target_pairs={{4,0},{8,4},{12,8},{16,12},{20,16},{24,20},{28,24},{32,28},{36,32}... | collective-permute-start | bytes 2359304 | tf_op jit(solution)/shard_map/ppermute | solution.py:28
  14.2 2.4 %collective-permute-start.6 = (bf16[2,384,512]{2,1,0:T(8,128)(2,1)}, bf16[2,384,512]{2,1,0:T(8,128)(2,1)}, u32[]{:S(2)}, u32[]{:S(2)}) collective-permute-start(bf16[2,384,512]{2,1,0:T(8,128)(2,1)} %get-tuple-element.40), channel_id=1, source_target_pairs={{4,0},{8,4},{12,8},{16,12},{20,16},{24,20},{28,24},{32,28},{36,32}... | collective-permute-start | bytes 2359304 | tf_op jit(solution)/shard_map/ppermute | solution.py:28
  17.3 2.1 %collective-permute-done.near0_ref = bf16[2,512,256]{2,1,0:T(8,128)(2,1)} collective-permute-done((bf16[2,512,256]{2,1,0:T(8,128)(2,1)}, bf16[2,512,256]{2,1,0:T(8,128)(2,1)}, u32[]{:S(2)}, u32[]{:S(2)}) %collective-permute-start) | collective-permute-done | bytes 524320 | tf_op jit(solution)/shard_map/ppermute | solution.py:28
  19.4 1.9 %collective-permute-start.3 = (bf16[2,512,256]{2,1,0:T(8,128)(2,1)}, bf16[2,512,256]{2,1,0:T(8,128)(2,1)S(1)}, u32[]{:S(2)}, u32[]{:S(2)}) collective-permute-start(bf16[2,512,256]{2,1,0:T(8,128)(2,1)} %collective-permute-done.near0_ref), channel_id=1, source_target_pairs={{4,0},{8,4},{12,8},{16,12},{20,16},{24,20},{28,24},{32,28},{36,32}... | collective-permute-start | bytes 1572872 | tf_op jit(solution)/shard_map/ppermute | solution.py:28
  21.3 1.0 copy-done.4
  22.4 1.9 %copy-done.6 = bf16[1,1,6,512,512]{4,3,2,1,0:T(8,128)(2,1)S(1)} copy-done((bf16[1,1,6,512,512]{4,3,2,1,0:T(8,128)(2,1)S(1)}, bf16[1,1,6,512,512]{4,3,2,1,0:T(8,128)(2,1)}, u32[]{:S(2)}) %copy-start.6) | copy-done | bytes 3145752
  24.3 1.0 copy-done.7
  25.3 1.0 copy-done.8
  26.4 4.3 %shard_map.92.meas_ref = bf16[6,512,512]{2,1,0:T(8,128)(2,1)S(1)} custom-call(bf16[512,512]{1,0:T(8,128)(2,1)S(1)} %copy-done.8, bf16[512,512]{1,0:T(8,128)(2,1)S(1)} %copy-done.7, bf16[6,512,512]{2,1,0:T(8,128)(2,1)S(1)} %bitcast.6, f32[2,512,512]{2,1,0:T(8,128)S(1)} %copy-done.2, bf16[4,256,256]{2,1,0:T(8,128)(2,1)S(1)} %copy-done.4, ...), custom_call_target="tpu_custom_call" | custom-call | flops 3221225472 | bytes 6291456 | tf_op jit(solution)/shard_map/pallas_call | solution.py:162
  30.7 2.4 %collective-permute-start.4 = (bf16[2,512,256]{2,1,0:T(8,128)(2,1)}, bf16[2,512,256]{2,1,0:T(8,128)(2,1)S(1)}, u32[]{:S(2)}, u32[]{:S(2)}) collective-permute-start(bf16[2,512,256]{2,1,0:T(8,128)(2,1)} %collective-permute-done.1.near1_ref), channel_id=1, source_target_pairs={{4,0},{8,4},{12,8},{16,12},{20,16},{24,20},{28,24},{32,28},{36,32}... | collective-permute-start | bytes 1572872 | tf_op jit(solution)/shard_map/ppermute | solution.py:28
  33.1 7.6 %collective-permute-done.2.far_ref = bf16[2,512,256]{2,1,0:T(8,128)(2,1)} collective-permute-done((bf16[2,512,256]{2,1,0:T(8,128)(2,1)}, bf16[2,512,256]{2,1,0:T(8,128)(2,1)}, u32[]{:S(2)}, u32[]{:S(2)}) %collective-permute-start.2) | collective-permute-done | bytes 524320 | tf_op jit(solution)/shard_map/ppermute | solution.py:28
  40.7 3.0 %collective-permute-done.4.corner1_ref = bf16[2,512,256]{2,1,0:T(8,128)(2,1)S(1)} collective-permute-done((bf16[2,512,256]{2,1,0:T(8,128)(2,1)}, bf16[2,512,256]{2,1,0:T(8,128)(2,1)S(1)}, u32[]{:S(2)}, u32[]{:S(2)}) %collective-permute-start.4) | collective-permute-done | bytes 524320 | tf_op jit(solution)/shard_map/ppermute | solution.py:28
  43.7 7.5 %shard_map.93.grown.refs_4_ = f32[2,10,1280,128]{3,2,1,0:T(8,128)S(1)} custom-call(s32[1]{0:T(128)} %bitcast.live_ref, s32[2,6]{1,0:T(2,128)S(1)} %bitcast.5, f32[2,768,768]{2,1,0:T(8,128)S(1)} %copy-done.1, bf16[2,512,256]{2,1,0:T(8,128)(2,1)} %collective-permute-done.near0_ref, bf16[2,512,256]{2,1,0:T(8,128)(2,1)} %collective-permute-done.1.near1_ref, ...), custom_call_target="tpu_custom_call" | custom-call | flops 1024 | bytes 1024 | tf_op jit(solution)/shard_map/pallas_call | solution.py:340
  51.2 0.6 shard_map.94
  51.9 22.0 %collective-permute-start.8 = (bf16[2,512,256]{2,1,0:T(8,128)(2,1)S(1)}, bf16[2,512,256]{2,1,0:T(8,128)(2,1)S(1)}, u32[]{:S(2)}, u32[]{:S(2)}) collective-permute-start(bf16[2,512,256]{2,1,0:T(8,128)(2,1)S(1)} %get-tuple-element.44), channel_id=1, source_target_pairs={{0,4},{4,8},{8,12},{12,16},{16,20},{20,24},{24,28},{28,32},{32,36}... | collective-permute-start | bytes 1572872 | tf_op jit(solution)/shard_map/ppermute | solution.py:28
  73.9 1.9 %collective-permute-start.7 = (bf16[2,512,256]{2,1,0:T(8,128)(2,1)S(1)}, bf16[2,512,256]{2,1,0:T(8,128)(2,1)S(1)}, u32[]{:S(2)}, u32[]{:S(2)}) collective-permute-start(bf16[2,512,256]{2,1,0:T(8,128)(2,1)S(1)} %get-tuple-element.42), channel_id=1, source_target_pairs={{0,4},{4,8},{8,12},{12,16},{16,20},{20,24},{24,28},{28,32},{32,36}... | collective-permute-start | bytes 1572872 | tf_op jit(solution)/shard_map/ppermute | solution.py:28
  75.8 1.3 %collective-permute-start.9 = (bf16[2,512,256]{2,1,0:T(8,128)(2,1)S(1)}, bf16[2,512,256]{2,1,0:T(8,128)(2,1)S(1)}, u32[]{:S(2)}, u32[]{:S(2)}) collective-permute-start(bf16[2,512,256]{2,1,0:T(8,128)(2,1)S(1)} %get-tuple-element.46), channel_id=1, source_target_pairs={{0,1},{1,2},{2,3},{4,5},{5,6},{6,7},{8,9},{9,10},{10,11},{12,13},{... | collective-permute-start | bytes 1572872 | tf_op jit(solution)/shard_map/ppermute | solution.py:28
  77.1 1.9 %collective-permute-start.11 = (bf16[2,384,512]{2,1,0:T(8,128)(2,1)S(1)}, bf16[2,384,512]{2,1,0:T(8,128)(2,1)S(1)}, u32[]{:S(2)}, u32[]{:S(2)}) collective-permute-start(bf16[2,384,512]{2,1,0:T(8,128)(2,1)S(1)} %get-tuple-element.48), channel_id=1, source_target_pairs={{0,4},{4,8},{8,12},{12,16},{16,20},{20,24},{24,28},{28,32},{32,36}... | collective-permute-start | bytes 2359304 | tf_op jit(solution)/shard_map/ppermute | solution.py:28
  79.0 1.9 %collective-permute-start.12 = (bf16[2,384,512]{2,1,0:T(8,128)(2,1)S(1)}, bf16[2,384,512]{2,1,0:T(8,128)(2,1)S(1)}, u32[]{:S(2)}, u32[]{:S(2)}) collective-permute-start(bf16[2,384,512]{2,1,0:T(8,128)(2,1)S(1)} %get-tuple-element.49), channel_id=1, source_target_pairs={{0,4},{4,8},{8,12},{12,16},{16,20},{20,24},{24,28},{28,32},{32,36}... | collective-permute-start | bytes 2359304 | tf_op jit(solution)/shard_map/ppermute | solution.py:28
  81.1 3.3 %collective-permute-done.7 = bf16[2,512,256]{2,1,0:T(8,128)(2,1)S(1)} collective-permute-done((bf16[2,512,256]{2,1,0:T(8,128)(2,1)S(1)}, bf16[2,512,256]{2,1,0:T(8,128)(2,1)S(1)}, u32[]{:S(2)}, u32[]{:S(2)}) %collective-permute-start.7) | collective-permute-done | bytes 524320 | tf_op jit(solution)/shard_map/ppermute | solution.py:28
  84.4 1.3 %collective-permute-start.13 = (bf16[2,512,256]{2,1,0:T(8,128)(2,1)S(1)}, bf16[2,512,256]{2,1,0:T(8,128)(2,1)S(1)}, u32[]{:S(2)}, u32[]{:S(2)}) collective-permute-start(bf16[2,512,256]{2,1,0:T(8,128)(2,1)S(1)} %add_convert_fusion.1), channel_id=1, source_target_pairs={{0,1},{1,2},{2,3},{4,5},{5,6},{6,7},{8,9},{9,10},{10,11},{12,13},{... | collective-permute-start | bytes 1572872 | tf_op jit(solution)/shard_map/ppermute | solution.py:28
  85.8 6.7 %collective-permute-done.9.refs_2_ = bf16[2,512,256]{2,1,0:T(8,128)(2,1)S(1)} collective-permute-done((bf16[2,512,256]{2,1,0:T(8,128)(2,1)S(1)}, bf16[2,512,256]{2,1,0:T(8,128)(2,1)S(1)}, u32[]{:S(2)}, u32[]{:S(2)}) %collective-permute-start.9) | collective-permute-done | bytes 524320 | tf_op jit(solution)/shard_map/ppermute | solution.py:28
  92.5 1.3 %collective-permute-start.10 = (bf16[2,512,256]{2,1,0:T(8,128)(2,1)S(1)}, bf16[2,512,256]{2,1,0:T(8,128)(2,1)S(1)}, u32[]{:S(2)}, u32[]{:S(2)}) collective-permute-start(bf16[2,512,256]{2,1,0:T(8,128)(2,1)S(1)} %add_convert_fusion), channel_id=1, source_target_pairs={{0,1},{1,2},{2,3},{4,5},{5,6},{6,7},{8,9},{9,10},{10,11},{12,13},{... | collective-permute-start | bytes 1572872 | tf_op jit(solution)/shard_map/ppermute | solution.py:28
  93.8 7.4 %collective-permute-done.12.refs_1_ = bf16[2,384,512]{2,1,0:T(8,128)(2,1)S(1)} collective-permute-done((bf16[2,384,512]{2,1,0:T(8,128)(2,1)S(1)}, bf16[2,384,512]{2,1,0:T(8,128)(2,1)S(1)}, u32[]{:S(2)}, u32[]{:S(2)}) %collective-permute-start.12) | collective-permute-done | bytes 786464 | tf_op jit(solution)/shard_map/ppermute | solution.py:28
  101.2 2.5 %collective-permute-done.13.refs_3_ = bf16[2,512,256]{2,1,0:T(8,128)(2,1)S(1)} collective-permute-done((bf16[2,512,256]{2,1,0:T(8,128)(2,1)S(1)}, bf16[2,512,256]{2,1,0:T(8,128)(2,1)S(1)}, u32[]{:S(2)}, u32[]{:S(2)}) %collective-permute-start.13) | collective-permute-done | bytes 524320 | tf_op jit(solution)/shard_map/ppermute | solution.py:28
  103.7 2.0 %shard_map.95 = (f32[2,10,1280,128]{3,2,1,0:T(8,128)S(1)}, f32[2,768,768]{2,1,0:T(8,128)}) custom-call(bf16[2,384,512]{2,1,0:T(8,128)(2,1)S(1)} %collective-permute-done.11.refs_0_, bf16[2,384,512]{2,1,0:T(8,128)(2,1)S(1)} %collective-permute-done.12.refs_1_, ...), custom_call_target="tpu_custom_call", output_to_operand_aliasing={{0}: (4, {})} | custom-call | flops 1024 | bytes 1024 | tf_op jit(solution)/shard_map/pallas_call | solution.py:441
  105.8 8.2 %collective-permute-done.10.near_ref = bf16[2,512,256]{2,1,0:T(8,128)(2,1)S(1)} collective-permute-done((bf16[2,512,256]{2,1,0:T(8,128)(2,1)S(1)}, bf16[2,512,256]{2,1,0:T(8,128)(2,1)S(1)}, u32[]{:S(2)}, u32[]{:S(2)}) %collective-permute-start.10) | collective-permute-done | bytes 524320 | tf_op jit(solution)/shard_map/ppermute | solution.py:28
  114.0 1.0 shard_map.96
  (23 shorter events, 0.9 us)
Async XLA Ops:
  0.0 16.7 %copy-start = (s32[32,1]{0,1:T(1,128)S(1)}, s32[32,1]{0,1:T(1,128)}, u32[]{:S(2)}) copy-start(s32[32,1]{0,1:T(1,128)} %param.13) | copy-start | bytes 388
  0.0 21.3 %copy-start.3 = (bf16[4,256,256]{2,1,0:T(8,128)(2,1)S(1)}, bf16[4,256,256]{2,1,0:T(8,128)(2,1)}, u32[]{:S(2)}) copy-start(bf16[4,256,256]{2,1,0:T(8,128)(2,1)} %constant.20.clone.refs_2_.gb_ref) | copy-start | bytes 1572868
  0.0 21.3 %copy-start.2 = (f32[2,512,512]{2,1,0:T(8,128)S(1)}, f32[2,512,512]{2,1,0:T(8,128)}, u32[]{:S(2)}) copy-start(f32[2,512,512]{2,1,0:T(8,128)} %probe_ref.1) | copy-start | bytes 6291460
  4.1 15.3 %collective-permute-start = (bf16[2,512,256]{2,1,0:T(8,128)(2,1)}, bf16[2,512,256]{2,1,0:T(8,128)(2,1)}, u32[]{:S(2)}, u32[]{:S(2)}) collective-permute-start(bf16[2,512,256]{2,1,0:T(8,128)(2,1)} %get-tuple-element.30), channel_id=1, source_target_pairs={{1,0},{2,1},{3,2},{5,4},{6,5},{7,6},{9,8},{10,9},{11,10},{13,12},{... | collective-permute-start | bytes 1572872 | tf_op jit(solution)/shard_map/ppermute | solution.py:28
  7.6 23.1 %collective-permute-start.1 = (bf16[2,512,256]{2,1,0:T(8,128)(2,1)}, bf16[2,512,256]{2,1,0:T(8,128)(2,1)}, u32[]{:S(2)}, u32[]{:S(2)}) collective-permute-start(bf16[2,512,256]{2,1,0:T(8,128)(2,1)} %get-tuple-element.34), channel_id=1, source_target_pairs={{1,0},{2,1},{3,2},{5,4},{6,5},{7,6},{9,8},{10,9},{11,10},{13,12},{... | collective-permute-start | bytes 1572872 | tf_op jit(solution)/shard_map/ppermute | solution.py:28
  9.9 30.8 %collective-permute-start.2 = (bf16[2,512,256]{2,1,0:T(8,128)(2,1)}, bf16[2,512,256]{2,1,0:T(8,128)(2,1)}, u32[]{:S(2)}, u32[]{:S(2)}) collective-permute-start(bf16[2,512,256]{2,1,0:T(8,128)(2,1)} %get-tuple-element.37), channel_id=1, source_target_pairs={{1,0},{2,1},{3,2},{5,4},{6,5},{7,6},{9,8},{10,9},{11,10},{13,12},{... | collective-permute-start | bytes 1572872 | tf_op jit(solution)/shard_map/ppermute | solution.py:28
  12.3 28.4 %collective-permute-start.5 = (bf16[2,384,512]{2,1,0:T(8,128)(2,1)}, bf16[2,384,512]{2,1,0:T(8,128)(2,1)S(1)}, u32[]{:S(2)}, u32[]{:S(2)}) collective-permute-start(bf16[2,384,512]{2,1,0:T(8,128)(2,1)} %get-tuple-element.39), channel_id=1, source_target_pairs={{4,0},{8,4},{12,8},{16,12},{20,16},{24,20},{28,24},{32,28},{36,32}... | collective-permute-start | bytes 2359304 | tf_op jit(solution)/shard_map/ppermute | solution.py:28
  14.2 26.5 %collective-permute-start.6 = (bf16[2,384,512]{2,1,0:T(8,128)(2,1)}, bf16[2,384,512]{2,1,0:T(8,128)(2,1)}, u32[]{:S(2)}, u32[]{:S(2)}) collective-permute-start(bf16[2,384,512]{2,1,0:T(8,128)(2,1)} %get-tuple-element.40), channel_id=1, source_target_pairs={{4,0},{8,4},{12,8},{16,12},{20,16},{24,20},{28,24},{32,28},{36,32}... | collective-permute-start | bytes 2359304 | tf_op jit(solution)/shard_map/ppermute | solution.py:28
  19.4 21.3 %collective-permute-start.3 = (bf16[2,512,256]{2,1,0:T(8,128)(2,1)}, bf16[2,512,256]{2,1,0:T(8,128)(2,1)S(1)}, u32[]{:S(2)}, u32[]{:S(2)}) collective-permute-start(bf16[2,512,256]{2,1,0:T(8,128)(2,1)} %collective-permute-done.near0_ref), channel_id=1, source_target_pairs={{4,0},{8,4},{12,8},{16,12},{20,16},{24,20},{28,24},{32,28},{36,32}... | collective-permute-start | bytes 1572872 | tf_op jit(solution)/shard_map/ppermute | solution.py:28
  21.3 1.0 copy-start.4
  22.4 1.9 %copy-start.6 = (bf16[1,1,6,512,512]{4,3,2,1,0:T(8,128)(2,1)S(1)}, bf16[1,1,6,512,512]{4,3,2,1,0:T(8,128)(2,1)}, u32[]{:S(2)}) copy-start(bf16[1,1,6,512,512]{4,3,2,1,0:T(8,128)(2,1)} %param.11) | copy-start | bytes 9437188
  24.3 1.0 copy-start.7
  25.3 1.0 copy-start.8
  26.4 17.3 %copy-start.1 = (f32[2,768,768]{2,1,0:T(8,128)S(1)}, f32[2,768,768]{2,1,0:T(8,128)}, u32[]{:S(2)}) copy-start(f32[2,768,768]{2,1,0:T(8,128)} %slab_ref.3) | copy-start | bytes 14155780
  26.4 17.3 %copy-start.5 = (s32[1,1,6,2]{2,3,1,0:T(2,128)S(1)}, s32[1,1,6,2]{2,3,1,0:T(2,128)}, u32[]{:S(2)}) copy-start(s32[1,1,6,2]{2,3,1,0:T(2,128)} %param.12) | copy-start | bytes 148
  30.7 13.0 %collective-permute-start.4 = (bf16[2,512,256]{2,1,0:T(8,128)(2,1)}, bf16[2,512,256]{2,1,0:T(8,128)(2,1)S(1)}, u32[]{:S(2)}, u32[]{:S(2)}) collective-permute-start(bf16[2,512,256]{2,1,0:T(8,128)(2,1)} %collective-permute-done.1.near1_ref), channel_id=1, source_target_pairs={{4,0},{8,4},{12,8},{16,12},{20,16},{24,20},{28,24},{32,28},{36,32}... | collective-permute-start | bytes 1572872 | tf_op jit(solution)/shard_map/ppermute | solution.py:28
  51.9 29.1 %collective-permute-start.8 = (bf16[2,512,256]{2,1,0:T(8,128)(2,1)S(1)}, bf16[2,512,256]{2,1,0:T(8,128)(2,1)S(1)}, u32[]{:S(2)}, u32[]{:S(2)}) collective-permute-start(bf16[2,512,256]{2,1,0:T(8,128)(2,1)S(1)} %get-tuple-element.44), channel_id=1, source_target_pairs={{0,4},{4,8},{8,12},{12,16},{16,20},{20,24},{24,28},{28,32},{32,36}... | collective-permute-start | bytes 1572872 | tf_op jit(solution)/shard_map/ppermute | solution.py:28
  73.9 10.5 %collective-permute-start.7 = (bf16[2,512,256]{2,1,0:T(8,128)(2,1)S(1)}, bf16[2,512,256]{2,1,0:T(8,128)(2,1)S(1)}, u32[]{:S(2)}, u32[]{:S(2)}) collective-permute-start(bf16[2,512,256]{2,1,0:T(8,128)(2,1)S(1)} %get-tuple-element.42), channel_id=1, source_target_pairs={{0,4},{4,8},{8,12},{12,16},{16,20},{20,24},{24,28},{28,32},{32,36}... | collective-permute-start | bytes 1572872 | tf_op jit(solution)/shard_map/ppermute | solution.py:28
  75.8 16.7 %collective-permute-start.9 = (bf16[2,512,256]{2,1,0:T(8,128)(2,1)S(1)}, bf16[2,512,256]{2,1,0:T(8,128)(2,1)S(1)}, u32[]{:S(2)}, u32[]{:S(2)}) collective-permute-start(bf16[2,512,256]{2,1,0:T(8,128)(2,1)S(1)} %get-tuple-element.46), channel_id=1, source_target_pairs={{0,1},{1,2},{2,3},{4,5},{5,6},{6,7},{8,9},{9,10},{10,11},{12,13},{... | collective-permute-start | bytes 1572872 | tf_op jit(solution)/shard_map/ppermute | solution.py:28
  77.1 16.7 %collective-permute-start.11 = (bf16[2,384,512]{2,1,0:T(8,128)(2,1)S(1)}, bf16[2,384,512]{2,1,0:T(8,128)(2,1)S(1)}, u32[]{:S(2)}, u32[]{:S(2)}) collective-permute-start(bf16[2,384,512]{2,1,0:T(8,128)(2,1)S(1)} %get-tuple-element.48), channel_id=1, source_target_pairs={{0,4},{4,8},{8,12},{12,16},{16,20},{20,24},{24,28},{28,32},{32,36}... | collective-permute-start | bytes 2359304 | tf_op jit(solution)/shard_map/ppermute | solution.py:28
  79.0 22.2 %collective-permute-start.12 = (bf16[2,384,512]{2,1,0:T(8,128)(2,1)S(1)}, bf16[2,384,512]{2,1,0:T(8,128)(2,1)S(1)}, u32[]{:S(2)}, u32[]{:S(2)}) collective-permute-start(bf16[2,384,512]{2,1,0:T(8,128)(2,1)S(1)} %get-tuple-element.49), channel_id=1, source_target_pairs={{0,4},{4,8},{8,12},{12,16},{16,20},{20,24},{24,28},{28,32},{32,36}... | collective-permute-start | bytes 2359304 | tf_op jit(solution)/shard_map/ppermute | solution.py:28
  84.4 19.3 %collective-permute-start.13 = (bf16[2,512,256]{2,1,0:T(8,128)(2,1)S(1)}, bf16[2,512,256]{2,1,0:T(8,128)(2,1)S(1)}, u32[]{:S(2)}, u32[]{:S(2)}) collective-permute-start(bf16[2,512,256]{2,1,0:T(8,128)(2,1)S(1)} %add_convert_fusion.1), channel_id=1, source_target_pairs={{0,1},{1,2},{2,3},{4,5},{5,6},{6,7},{8,9},{9,10},{10,11},{12,13},{... | collective-permute-start | bytes 1572872 | tf_op jit(solution)/shard_map/ppermute | solution.py:28
  92.5 21.5 %collective-permute-start.10 = (bf16[2,512,256]{2,1,0:T(8,128)(2,1)S(1)}, bf16[2,512,256]{2,1,0:T(8,128)(2,1)S(1)}, u32[]{:S(2)}, u32[]{:S(2)}) collective-permute-start(bf16[2,512,256]{2,1,0:T(8,128)(2,1)S(1)} %add_convert_fusion), channel_id=1, source_target_pairs={{0,1},{1,2},{2,3},{4,5},{5,6},{6,7},{8,9},{9,10},{10,11},{12,13},{... | collective-permute-start | bytes 1572872 | tf_op jit(solution)/shard_map/ppermute | solution.py:28

commit v10 on v9

--- a/solution.py
+++ b/solution.py
@@ -503,7 +503,7 @@
     far = shifted(far, "tile", 1)
     corner0 = shifted(corner0, "scan", 1)
     near1 = (near1.astype(f32) + corner1.astype(f32)).astype(bf16)
-    corner0, near1 = lax.optimization_barrier((corner0, near1))
+    near1, right[1] = lax.optimization_barrier((near1, right[1]))
     near0 = (near0.astype(f32) + corner0.astype(f32)).astype(bf16)
     near1 = shifted(near1, "tile", 1)
     right = [shifted(piece, "scan", 1) for piece in right]

time: 116 us -> 116 us (level)
  the two profiles are of different devices: /device:TPU:124 before, /device:TPU:91 now
where the time goes in v10:
time: 116 us; the launch traced here: 115 us
  waiting for transfers between devices  39 us (34%)
  Pallas kernels  36.7 us (32%)
  starting transfers between devices  33.1 us (29%)
  local copies, waits for them, and re-layouts  5.64 us (5%)
    ppermute x14, waiting for transfers between devices, shifted(): lax.ppermute(value, axis, [(i, i + by) for i in range(n) if 0 <= i + by <...  39 us
    ppermute x14, starting transfers between devices, shifted(): lax.ppermute(value, axis, [(i, i + by) for i in range(n) if 0 <= i + by <...  33.1 us
    pallas_call x1, Pallas kernels, solve(): pl.pallas_call(slots_kernel, in_specs=[SMEM, SMEM, ANY] + [VMEM] * (9 + R...  24.6 us
    unnamed x18, local copies, waits for them, and re-layouts  5.03 us
    pallas_call x1, Pallas kernels, sort_intensities(): pl.pallas_call(sort_kernel, grid=(measured.shape[0],), in_specs=[whole, w...  4.3 us
    pallas_call x1, Pallas kernels, pack(): pl.pallas_call(pack_kernel, in_specs=[ANY], out_specs=[ANY] * (3 + RP), o...  4.1 us
  transfers between devices with their start and end apart: 14, of which 8 were waited for; matrix products, arithmetic and copies ran while one was open for 1% of the time, Pallas kernels for 6%

profile of v10, /device:TPU:91, one launch (start us, length us, event | category | flops | bytes accessed | tf_op | source)
XLA Modules:
  0.0 115.0 jit_solution(15321628988004226126)
XLA Ops:
  0.0 4.1 %shard_map.91 = (bf16[2,512,256]{2,1,0:T(8,128)(2,1)}, bf16[2,512,256]{2,1,0:T(8,128)(2,1)}, bf16[2,512,256]{2,1,0:T(8,128)(2,1)}, bf16[2,384,512]{2,1,0:T(8,128)(2,1)}, bf16[2,384,512]{2,1,0:T(8,128)(2,1)}) custom-call(f32[2,768,768]{2,1,0:T(8,128)} %slab_ref.3), custom_call_target="tpu_custom_call" | custom-call | flops 1024 | bytes 1024 | tf_op jit(solution)/shard_map/pallas_call | solution.py:137
  4.1 3.2 %collective-permute-start = (bf16[2,512,256]{2,1,0:T(8,128)(2,1)}, bf16[2,512,256]{2,1,0:T(8,128)(2,1)}, u32[]{:S(2)}, u32[]{:S(2)}) collective-permute-start(bf16[2,512,256]{2,1,0:T(8,128)(2,1)} %get-tuple-element.30), channel_id=1, source_target_pairs={{1,0},{2,1},{3,2},{5,4},{6,5},{7,6},{9,8},{10,9},{11,10},{13,12},{... | collective-permute-start | bytes 1572872 | tf_op jit(solution)/shard_map/ppermute | solution.py:28
  7.3 2.1 %collective-permute-start.1 = (bf16[2,512,256]{2,1,0:T(8,128)(2,1)}, bf16[2,512,256]{2,1,0:T(8,128)(2,1)}, u32[]{:S(2)}, u32[]{:S(2)}) collective-permute-start(bf16[2,512,256]{2,1,0:T(8,128)(2,1)} %get-tuple-element.34), channel_id=1, source_target_pairs={{1,0},{2,1},{3,2},{5,4},{6,5},{7,6},{9,8},{10,9},{11,10},{13,12},{... | collective-permute-start | bytes 1572872 | tf_op jit(solution)/shard_map/ppermute | solution.py:28
  9.4 2.1 %collective-permute-start.2 = (bf16[2,512,256]{2,1,0:T(8,128)(2,1)}, bf16[2,512,256]{2,1,0:T(8,128)(2,1)}, u32[]{:S(2)}, u32[]{:S(2)}) collective-permute-start(bf16[2,512,256]{2,1,0:T(8,128)(2,1)} %get-tuple-element.37), channel_id=1, source_target_pairs={{1,0},{2,1},{3,2},{5,4},{6,5},{7,6},{9,8},{10,9},{11,10},{13,12},{... | collective-permute-start | bytes 1572872 | tf_op jit(solution)/shard_map/ppermute | solution.py:28
  11.5 3.4 %collective-permute-start.5 = (bf16[2,384,512]{2,1,0:T(8,128)(2,1)}, bf16[2,384,512]{2,1,0:T(8,128)(2,1)S(1)}, u32[]{:S(2)}, u32[]{:S(2)}) collective-permute-start(bf16[2,384,512]{2,1,0:T(8,128)(2,1)} %get-tuple-element.39), channel_id=1, source_target_pairs={{4,0},{8,4},{12,8},{16,12},{20,16},{24,20},{28,24},{32,28},{36,32}... | collective-permute-start | bytes 2359304 | tf_op jit(solution)/shard_map/ppermute | solution.py:28
  14.9 1.9 %collective-permute-start.6 = (bf16[2,384,512]{2,1,0:T(8,128)(2,1)}, bf16[2,384,512]{2,1,0:T(8,128)(2,1)}, u32[]{:S(2)}, u32[]{:S(2)}) collective-permute-start(bf16[2,384,512]{2,1,0:T(8,128)(2,1)} %get-tuple-element.40), channel_id=1, source_target_pairs={{4,0},{8,4},{12,8},{16,12},{20,16},{24,20},{28,24},{32,28},{36,32}... | collective-permute-start | bytes 2359304 | tf_op jit(solution)/shard_map/ppermute | solution.py:28
  16.8 0.6 constant_dynamic-slice_fusion
  17.5 4.5 %collective-permute-start.3 = (bf16[2,512,256]{2,1,0:T(8,128)(2,1)}, bf16[2,512,256]{2,1,0:T(8,128)(2,1)S(1)}, u32[]{:S(2)}, u32[]{:S(2)}) collective-permute-start(bf16[2,512,256]{2,1,0:T(8,128)(2,1)} %collective-permute-done.near0_ref), channel_id=1, source_target_pairs={{4,0},{8,4},{12,8},{16,12},{20,16},{24,20},{28,24},{32,28},{36,32}... | collective-permute-start | bytes 1572872 | tf_op jit(solution)/shard_map/ppermute | solution.py:28
  22.0 1.0 copy-done.4
  23.0 1.9 %copy-done.6 = bf16[1,1,6,512,512]{4,3,2,1,0:T(8,128)(2,1)S(1)} copy-done((bf16[1,1,6,512,512]{4,3,2,1,0:T(8,128)(2,1)S(1)}, bf16[1,1,6,512,512]{4,3,2,1,0:T(8,128)(2,1)}, u32[]{:S(2)}) %copy-start.6) | copy-done | bytes 3145752
  24.9 1.0 copy-done.7
  26.0 1.0 copy-done.8
  27.0 4.3 %shard_map.92.meas_ref = bf16[6,512,512]{2,1,0:T(8,128)(2,1)S(1)} custom-call(bf16[512,512]{1,0:T(8,128)(2,1)S(1)} %copy-done.8, bf16[512,512]{1,0:T(8,128)(2,1)S(1)} %copy-done.7, bf16[6,512,512]{2,1,0:T(8,128)(2,1)S(1)} %bitcast.6, f32[2,512,512]{2,1,0:T(8,128)S(1)} %copy-done.2, bf16[4,256,256]{2,1,0:T(8,128)(2,1)S(1)} %copy-done.4, ...), custom_call_target="tpu_custom_call" | custom-call | flops 3221225472 | bytes 6291456 | tf_op jit(solution)/shard_map/pallas_call | solution.py:162
  31.3 1.9 %collective-permute-start.4 = (bf16[2,512,256]{2,1,0:T(8,128)(2,1)}, bf16[2,512,256]{2,1,0:T(8,128)(2,1)S(1)}, u32[]{:S(2)}, u32[]{:S(2)}) collective-permute-start(bf16[2,512,256]{2,1,0:T(8,128)(2,1)} %collective-permute-done.1.near1_ref), channel_id=1, source_target_pairs={{4,0},{8,4},{12,8},{16,12},{20,16},{24,20},{28,24},{32,28},{36,32}... | collective-permute-start | bytes 1572872 | tf_op jit(solution)/shard_map/ppermute | solution.py:28
  33.3 6.6 %collective-permute-done.2.far_ref = bf16[2,512,256]{2,1,0:T(8,128)(2,1)} collective-permute-done((bf16[2,512,256]{2,1,0:T(8,128)(2,1)}, bf16[2,512,256]{2,1,0:T(8,128)(2,1)}, u32[]{:S(2)}, u32[]{:S(2)}) %collective-permute-start.2) | collective-permute-done | bytes 524320 | tf_op jit(solution)/shard_map/ppermute | solution.py:28
  39.9 0.2 collective-permute-done.3.corner0_ref
  40.0 5.6 %collective-permute-done.4.corner1_ref = bf16[2,512,256]{2,1,0:T(8,128)(2,1)S(1)} collective-permute-done((bf16[2,512,256]{2,1,0:T(8,128)(2,1)}, bf16[2,512,256]{2,1,0:T(8,128)(2,1)S(1)}, u32[]{:S(2)}, u32[]{:S(2)}) %collective-permute-start.4) | collective-permute-done | bytes 524320 | tf_op jit(solution)/shard_map/ppermute | solution.py:28
  45.7 24.6 %shard_map.93.grown.refs_4_ = f32[2,10,1280,128]{3,2,1,0:T(8,128)S(1)} custom-call(s32[1]{0:T(128)} %bitcast.live_ref, s32[2,6]{1,0:T(2,128)S(1)} %bitcast.5, f32[2,768,768]{2,1,0:T(8,128)S(1)} %copy-done.1, bf16[2,512,256]{2,1,0:T(8,128)(2,1)} %collective-permute-done.near0_ref, bf16[2,512,256]{2,1,0:T(8,128)(2,1)} %collective-permute-done.1.near1_ref, ...), custom_call_target="tpu_custom_call" | custom-call | flops 1024 | bytes 1024 | tf_op jit(solution)/shard_map/pallas_call | solution.py:340
  70.3 0.6 shard_map.94
  70.9 1.9 %collective-permute-start.11 = (bf16[2,512,256]{2,1,0:T(8,128)(2,1)S(1)}, bf16[2,512,256]{2,1,0:T(8,128)(2,1)S(1)}, u32[]{:S(2)}, u32[]{:S(2)}) collective-permute-start(bf16[2,512,256]{2,1,0:T(8,128)(2,1)S(1)} %get-tuple-element.47), channel_id=1, source_target_pairs={{0,4},{4,8},{8,12},{12,16},{16,20},{20,24},{24,28},{28,32},{32,36}... | collective-permute-start | bytes 1572872 | tf_op jit(solution)/shard_map/ppermute | solution.py:28
  72.9 1.9 %collective-permute-start.7 = (bf16[2,512,256]{2,1,0:T(8,128)(2,1)S(1)}, bf16[2,512,256]{2,1,0:T(8,128)(2,1)S(1)}, u32[]{:S(2)}, u32[]{:S(2)}) collective-permute-start(bf16[2,512,256]{2,1,0:T(8,128)(2,1)S(1)} %get-tuple-element.42), channel_id=1, source_target_pairs={{0,4},{4,8},{8,12},{12,16},{16,20},{20,24},{24,28},{28,32},{32,36}... | collective-permute-start | bytes 1572872 | tf_op jit(solution)/shard_map/ppermute | solution.py:28
  74.8 1.3 %collective-permute-start.8 = (bf16[2,512,256]{2,1,0:T(8,128)(2,1)S(1)}, bf16[2,512,256]{2,1,0:T(8,128)(2,1)S(1)}, u32[]{:S(2)}, u32[]{:S(2)}) collective-permute-start(bf16[2,512,256]{2,1,0:T(8,128)(2,1)S(1)} %get-tuple-element.43), channel_id=1, source_target_pairs={{0,1},{1,2},{2,3},{4,5},{5,6},{6,7},{8,9},{9,10},{10,11},{12,13},{... | collective-permute-start | bytes 1572872 | tf_op jit(solution)/shard_map/ppermute | solution.py:28
  76.1 1.9 %collective-permute-start.10 = (bf16[2,384,512]{2,1,0:T(8,128)(2,1)S(1)}, bf16[2,384,512]{2,1,0:T(8,128)(2,1)S(1)}, u32[]{:S(2)}, u32[]{:S(2)}) collective-permute-start(bf16[2,384,512]{2,1,0:T(8,128)(2,1)S(1)} %get-tuple-element.45), channel_id=1, source_target_pairs={{0,4},{4,8},{8,12},{12,16},{16,20},{20,24},{24,28},{28,32},{32,36}... | collective-permute-start | bytes 2359304 | tf_op jit(solution)/shard_map/ppermute | solution.py:28
  78.0 0.9 collective-permute-done.11
  79.1 1.3 %collective-permute-start.13 = (bf16[2,512,256]{2,1,0:T(8,128)(2,1)S(1)}, bf16[2,512,256]{2,1,0:T(8,128)(2,1)S(1)}, u32[]{:S(2)}, u32[]{:S(2)}) collective-permute-start(bf16[2,512,256]{2,1,0:T(8,128)(2,1)S(1)} %add_convert_fusion), channel_id=1, source_target_pairs={{0,1},{1,2},{2,3},{4,5},{5,6},{6,7},{8,9},{9,10},{10,11},{12,13},{... | collective-permute-start | bytes 1572872 | tf_op jit(solution)/shard_map/ppermute | solution.py:28
  80.4 4.4 %collective-permute-start.12 = (bf16[2,384,512]{2,1,0:T(8,128)(2,1)S(1)}, bf16[2,384,512]{2,1,0:T(8,128)(2,1)S(1)}, u32[]{:S(2)}, u32[]{:S(2)}) collective-permute-start(bf16[2,384,512]{2,1,0:T(8,128)(2,1)S(1)} %get-tuple-element.49), channel_id=1, source_target_pairs={{0,4},{4,8},{8,12},{12,16},{16,20},{20,24},{24,28},{28,32},{32,36}... | collective-permute-start | bytes 2359304 | tf_op jit(solution)/shard_map/ppermute | solution.py:28
  85.0 6.7 %collective-permute-done.8.refs_2_ = bf16[2,512,256]{2,1,0:T(8,128)(2,1)S(1)} collective-permute-done((bf16[2,512,256]{2,1,0:T(8,128)(2,1)S(1)}, bf16[2,512,256]{2,1,0:T(8,128)(2,1)S(1)}, u32[]{:S(2)}, u32[]{:S(2)}) %collective-permute-start.8) | collective-permute-done | bytes 524320 | tf_op jit(solution)/shard_map/ppermute | solution.py:28
  91.6 1.3 %collective-permute-start.9 = (bf16[2,512,256]{2,1,0:T(8,128)(2,1)S(1)}, bf16[2,512,256]{2,1,0:T(8,128)(2,1)S(1)}, u32[]{:S(2)}, u32[]{:S(2)}) collective-permute-start(bf16[2,512,256]{2,1,0:T(8,128)(2,1)S(1)} %add_convert_fusion.1), channel_id=1, source_target_pairs={{0,1},{1,2},{2,3},{4,5},{5,6},{6,7},{8,9},{9,10},{10,11},{12,13},{... | collective-permute-start | bytes 1572872 | tf_op jit(solution)/shard_map/ppermute | solution.py:28
  93.0 9.9 %collective-permute-done.13.refs_3_ = bf16[2,512,256]{2,1,0:T(8,128)(2,1)S(1)} collective-permute-done((bf16[2,512,256]{2,1,0:T(8,128)(2,1)S(1)}, bf16[2,512,256]{2,1,0:T(8,128)(2,1)S(1)}, u32[]{:S(2)}, u32[]{:S(2)}) %collective-permute-start.13) | collective-permute-done | bytes 524320 | tf_op jit(solution)/shard_map/ppermute | solution.py:28
  102.9 2.0 %shard_map.95 = (f32[2,10,1280,128]{3,2,1,0:T(8,128)S(1)}, f32[2,768,768]{2,1,0:T(8,128)}) custom-call(bf16[2,384,512]{2,1,0:T(8,128)(2,1)S(1)} %collective-permute-done.10.refs_0_, bf16[2,384,512]{2,1,0:T(8,128)(2,1)S(1)} %collective-permute-done.12.refs_1_, ...), custom_call_target="tpu_custom_call", output_to_operand_aliasing={{0}: (4, {})} | custom-call | flops 1024 | bytes 1024 | tf_op jit(solution)/shard_map/pallas_call | solution.py:441
  104.9 9.1 %collective-permute-done.9.near_ref = bf16[2,512,256]{2,1,0:T(8,128)(2,1)S(1)} collective-permute-done((bf16[2,512,256]{2,1,0:T(8,128)(2,1)S(1)}, bf16[2,512,256]{2,1,0:T(8,128)(2,1)S(1)}, u32[]{:S(2)}, u32[]{:S(2)}) %collective-permute-start.9) | collective-permute-done | bytes 524320 | tf_op jit(solution)/shard_map/ppermute | solution.py:28
  114.0 1.0 shard_map.96
  (23 shorter events, 0.4 us)
Async XLA Ops:
  0.0 16.8 %copy-start = (s32[32,1]{0,1:T(1,128)S(1)}, s32[32,1]{0,1:T(1,128)}, u32[]{:S(2)}) copy-start(s32[32,1]{0,1:T(1,128)} %param.13) | copy-start | bytes 388
  0.0 22.0 %copy-start.3 = (bf16[4,256,256]{2,1,0:T(8,128)(2,1)S(1)}, bf16[4,256,256]{2,1,0:T(8,128)(2,1)}, u32[]{:S(2)}) copy-start(bf16[4,256,256]{2,1,0:T(8,128)(2,1)} %constant.20.clone.refs_2_.gb_ref) | copy-start | bytes 1572868
  0.0 22.0 %copy-start.2 = (f32[2,512,512]{2,1,0:T(8,128)S(1)}, f32[2,512,512]{2,1,0:T(8,128)}, u32[]{:S(2)}) copy-start(f32[2,512,512]{2,1,0:T(8,128)} %probe_ref.1) | copy-start | bytes 6291460
  4.1 13.3 %collective-permute-start = (bf16[2,512,256]{2,1,0:T(8,128)(2,1)}, bf16[2,512,256]{2,1,0:T(8,128)(2,1)}, u32[]{:S(2)}, u32[]{:S(2)}) collective-permute-start(bf16[2,512,256]{2,1,0:T(8,128)(2,1)} %get-tuple-element.30), channel_id=1, source_target_pairs={{1,0},{2,1},{3,2},{5,4},{6,5},{7,6},{9,8},{10,9},{11,10},{13,12},{... | collective-permute-start | bytes 1572872 | tf_op jit(solution)/shard_map/ppermute | solution.py:28
  7.3 24.0 %collective-permute-start.1 = (bf16[2,512,256]{2,1,0:T(8,128)(2,1)}, bf16[2,512,256]{2,1,0:T(8,128)(2,1)}, u32[]{:S(2)}, u32[]{:S(2)}) collective-permute-start(bf16[2,512,256]{2,1,0:T(8,128)(2,1)} %get-tuple-element.34), channel_id=1, source_target_pairs={{1,0},{2,1},{3,2},{5,4},{6,5},{7,6},{9,8},{10,9},{11,10},{13,12},{... | collective-permute-start | bytes 1572872 | tf_op jit(solution)/shard_map/ppermute | solution.py:28
  9.4 30.5 %collective-permute-start.2 = (bf16[2,512,256]{2,1,0:T(8,128)(2,1)}, bf16[2,512,256]{2,1,0:T(8,128)(2,1)}, u32[]{:S(2)}, u32[]{:S(2)}) collective-permute-start(bf16[2,512,256]{2,1,0:T(8,128)(2,1)} %get-tuple-element.37), channel_id=1, source_target_pairs={{1,0},{2,1},{3,2},{5,4},{6,5},{7,6},{9,8},{10,9},{11,10},{13,12},{... | collective-permute-start | bytes 1572872 | tf_op jit(solution)/shard_map/ppermute | solution.py:28
  11.5 28.4 %collective-permute-start.5 = (bf16[2,384,512]{2,1,0:T(8,128)(2,1)}, bf16[2,384,512]{2,1,0:T(8,128)(2,1)S(1)}, u32[]{:S(2)}, u32[]{:S(2)}) collective-permute-start(bf16[2,384,512]{2,1,0:T(8,128)(2,1)} %get-tuple-element.39), channel_id=1, source_target_pairs={{4,0},{8,4},{12,8},{16,12},{20,16},{24,20},{28,24},{32,28},{36,32}... | collective-permute-start | bytes 2359304 | tf_op jit(solution)/shard_map/ppermute | solution.py:28
  14.9 25.0 %collective-permute-start.6 = (bf16[2,384,512]{2,1,0:T(8,128)(2,1)}, bf16[2,384,512]{2,1,0:T(8,128)(2,1)}, u32[]{:S(2)}, u32[]{:S(2)}) collective-permute-start(bf16[2,384,512]{2,1,0:T(8,128)(2,1)} %get-tuple-element.40), channel_id=1, source_target_pairs={{4,0},{8,4},{12,8},{16,12},{20,16},{24,20},{28,24},{32,28},{36,32}... | collective-permute-start | bytes 2359304 | tf_op jit(solution)/shard_map/ppermute | solution.py:28
  17.5 22.6 %collective-permute-start.3 = (bf16[2,512,256]{2,1,0:T(8,128)(2,1)}, bf16[2,512,256]{2,1,0:T(8,128)(2,1)S(1)}, u32[]{:S(2)}, u32[]{:S(2)}) collective-permute-start(bf16[2,512,256]{2,1,0:T(8,128)(2,1)} %collective-permute-done.near0_ref), channel_id=1, source_target_pairs={{4,0},{8,4},{12,8},{16,12},{20,16},{24,20},{28,24},{32,28},{36,32}... | collective-permute-start | bytes 1572872 | tf_op jit(solution)/shard_map/ppermute | solution.py:28
  22.0 1.0 copy-start.4
  23.0 1.9 %copy-start.6 = (bf16[1,1,6,512,512]{4,3,2,1,0:T(8,128)(2,1)S(1)}, bf16[1,1,6,512,512]{4,3,2,1,0:T(8,128)(2,1)}, u32[]{:S(2)}) copy-start(bf16[1,1,6,512,512]{4,3,2,1,0:T(8,128)(2,1)} %param.11) | copy-start | bytes 9437188
  24.9 1.0 copy-start.7
  26.0 1.0 copy-start.8
  27.0 18.6 %copy-start.1 = (f32[2,768,768]{2,1,0:T(8,128)S(1)}, f32[2,768,768]{2,1,0:T(8,128)}, u32[]{:S(2)}) copy-start(f32[2,768,768]{2,1,0:T(8,128)} %slab_ref.3) | copy-start | bytes 14155780
  27.0 18.6 %copy-start.5 = (s32[1,1,6,2]{2,3,1,0:T(2,128)S(1)}, s32[1,1,6,2]{2,3,1,0:T(2,128)}, u32[]{:S(2)}) copy-start(s32[1,1,6,2]{2,3,1,0:T(2,128)} %param.12) | copy-start | bytes 148
  31.3 14.3 %collective-permute-start.4 = (bf16[2,512,256]{2,1,0:T(8,128)(2,1)}, bf16[2,512,256]{2,1,0:T(8,128)(2,1)S(1)}, u32[]{:S(2)}, u32[]{:S(2)}) collective-permute-start(bf16[2,512,256]{2,1,0:T(8,128)(2,1)} %collective-permute-done.1.near1_ref), channel_id=1, source_target_pairs={{4,0},{8,4},{12,8},{16,12},{20,16},{24,20},{28,24},{32,28},{36,32}... | collective-permute-start | bytes 1572872 | tf_op jit(solution)/shard_map/ppermute | solution.py:28
  70.9 8.0 %collective-permute-start.11 = (bf16[2,512,256]{2,1,0:T(8,128)(2,1)S(1)}, bf16[2,512,256]{2,1,0:T(8,128)(2,1)S(1)}, u32[]{:S(2)}, u32[]{:S(2)}) collective-permute-start(bf16[2,512,256]{2,1,0:T(8,128)(2,1)S(1)} %get-tuple-element.47), channel_id=1, source_target_pairs={{0,4},{4,8},{8,12},{12,16},{16,20},{20,24},{24,28},{28,32},{32,36}... | collective-permute-start | bytes 1572872 | tf_op jit(solution)/shard_map/ppermute | solution.py:28
  72.9 11.9 %collective-permute-start.7 = (bf16[2,512,256]{2,1,0:T(8,128)(2,1)S(1)}, bf16[2,512,256]{2,1,0:T(8,128)(2,1)S(1)}, u32[]{:S(2)}, u32[]{:S(2)}) collective-permute-start(bf16[2,512,256]{2,1,0:T(8,128)(2,1)S(1)} %get-tuple-element.42), channel_id=1, source_target_pairs={{0,4},{4,8},{8,12},{12,16},{16,20},{20,24},{24,28},{28,32},{32,36}... | collective-permute-start | bytes 1572872 | tf_op jit(solution)/shard_map/ppermute | solution.py:28
  74.8 16.8 %collective-permute-start.8 = (bf16[2,512,256]{2,1,0:T(8,128)(2,1)S(1)}, bf16[2,512,256]{2,1,0:T(8,128)(2,1)S(1)}, u32[]{:S(2)}, u32[]{:S(2)}) collective-permute-start(bf16[2,512,256]{2,1,0:T(8,128)(2,1)S(1)} %get-tuple-element.43), channel_id=1, source_target_pairs={{0,1},{1,2},{2,3},{4,5},{5,6},{6,7},{8,9},{9,10},{10,11},{12,13},{... | collective-permute-start | bytes 1572872 | tf_op jit(solution)/shard_map/ppermute | solution.py:28
  76.1 16.9 %collective-permute-start.10 = (bf16[2,384,512]{2,1,0:T(8,128)(2,1)S(1)}, bf16[2,384,512]{2,1,0:T(8,128)(2,1)S(1)}, u32[]{:S(2)}, u32[]{:S(2)}) collective-permute-start(bf16[2,384,512]{2,1,0:T(8,128)(2,1)S(1)} %get-tuple-element.45), channel_id=1, source_target_pairs={{0,4},{4,8},{8,12},{12,16},{16,20},{20,24},{24,28},{28,32},{32,36}... | collective-permute-start | bytes 2359304 | tf_op jit(solution)/shard_map/ppermute | solution.py:28
  79.1 23.8 %collective-permute-start.13 = (bf16[2,512,256]{2,1,0:T(8,128)(2,1)S(1)}, bf16[2,512,256]{2,1,0:T(8,128)(2,1)S(1)}, u32[]{:S(2)}, u32[]{:S(2)}) collective-permute-start(bf16[2,512,256]{2,1,0:T(8,128)(2,1)S(1)} %add_convert_fusion), channel_id=1, source_target_pairs={{0,1},{1,2},{2,3},{4,5},{5,6},{6,7},{8,9},{9,10},{10,11},{12,13},{... | collective-permute-start | bytes 1572872 | tf_op jit(solution)/shard_map/ppermute | solution.py:28
  80.4 22.5 %collective-permute-start.12 = (bf16[2,384,512]{2,1,0:T(8,128)(2,1)S(1)}, bf16[2,384,512]{2,1,0:T(8,128)(2,1)S(1)}, u32[]{:S(2)}, u32[]{:S(2)}) collective-permute-start(bf16[2,384,512]{2,1,0:T(8,128)(2,1)S(1)} %get-tuple-element.49), channel_id=1, source_target_pairs={{0,4},{4,8},{8,12},{12,16},{16,20},{20,24},{24,28},{28,32},{32,36}... | collective-permute-start | bytes 2359304 | tf_op jit(solution)/shard_map/ppermute | solution.py:28
  91.6 22.4 %collective-permute-start.9 = (bf16[2,512,256]{2,1,0:T(8,128)(2,1)S(1)}, bf16[2,512,256]{2,1,0:T(8,128)(2,1)S(1)}, u32[]{:S(2)}, u32[]{:S(2)}) collective-permute-start(bf16[2,512,256]{2,1,0:T(8,128)(2,1)S(1)} %add_convert_fusion.1), channel_id=1, source_target_pairs={{0,1},{1,2},{2,3},{4,5},{5,6},{6,7},{8,9},{9,10},{10,11},{12,13},{... | collective-permute-start | bytes 1572872 | tf_op jit(solution)/shard_map/ppermute | solution.py:28

commit v11 on v10

--- a/solution.py
+++ b/solution.py
@@ -504,10 +504,10 @@
     corner0 = shifted(corner0, "scan", 1)
     near1 = (near1.astype(f32) + corner1.astype(f32)).astype(bf16)
     near1, right[1] = lax.optimization_barrier((near1, right[1]))
-    near0 = (near0.astype(f32) + corner0.astype(f32)).astype(bf16)
     near1 = shifted(near1, "tile", 1)
     right = [shifted(piece, "scan", 1) for piece in right]
-    near0, far = lax.optimization_barrier((near0, far))
+    far, near0 = lax.optimization_barrier((far, near0))
+    near0 = (near0.astype(f32) + corner0.astype(f32)).astype(bf16)
     near0 = shifted(near0, "tile", 1)
     grown, whole = add_side(right, far, near1, grown)
     return add_near(near0, grown, whole)

time: 116 us -> 115 us (level)
  the two profiles are of different devices: /device:TPU:91 before, /device:TPU:18 now
where the time goes in v11:
time: 115 us; the launch traced here: 113 us
  starting transfers between devices  39.4 us (34%)
  Pallas kernels  36.8 us (32%)
  waiting for transfers between devices  30.5 us (27%)
  local copies, waits for them, and re-layouts  5.64 us (5%)
    ppermute x14, starting transfers between devices, shifted(): lax.ppermute(value, axis, [(i, i + by) for i in range(n) if 0 <= i + by <...  39.4 us
    ppermute x14, waiting for transfers between devices, shifted(): lax.ppermute(value, axis, [(i, i + by) for i in range(n) if 0 <= i + by <...  30.5 us
    pallas_call x1, Pallas kernels, solve(): pl.pallas_call(slots_kernel, in_specs=[SMEM, SMEM, ANY] + [VMEM] * (9 + R...  24.7 us
    unnamed x18, local copies, waits for them, and re-layouts  5.03 us
    pallas_call x1, Pallas kernels, sort_intensities(): pl.pallas_call(sort_kernel, grid=(measured.shape[0],), in_specs=[whole, w...  4.3 us
    pallas_call x1, Pallas kernels, pack(): pl.pallas_call(pack_kernel, in_specs=[ANY], out_specs=[ANY] * (3 + RP), o...  4.1 us
  transfers between devices with their start and end apart: 14, of which 9 were waited for; matrix products, arithmetic and copies ran while one was open for 1% of the time, Pallas kernels for 6%

profile of v11, /device:TPU:18, one launch (start us, length us, event | category | flops | bytes accessed | tf_op | source)
XLA Modules:
  0.0 112.8 jit_solution(3784067350684319568)
XLA Ops:
  0.0 4.1 %shard_map.91 = (bf16[2,512,256]{2,1,0:T(8,128)(2,1)}, bf16[2,512,256]{2,1,0:T(8,128)(2,1)}, bf16[2,512,256]{2,1,0:T(8,128)(2,1)}, bf16[2,384,512]{2,1,0:T(8,128)(2,1)}, bf16[2,384,512]{2,1,0:T(8,128)(2,1)}) custom-call(f32[2,768,768]{2,1,0:T(8,128)} %slab_ref.3), custom_call_target="tpu_custom_call" | custom-call | flops 1024 | bytes 1024 | tf_op jit(solution)/shard_map/pallas_call | solution.py:137
  4.1 2.4 %collective-permute-start = (bf16[2,512,256]{2,1,0:T(8,128)(2,1)}, bf16[2,512,256]{2,1,0:T(8,128)(2,1)}, u32[]{:S(2)}, u32[]{:S(2)}) collective-permute-start(bf16[2,512,256]{2,1,0:T(8,128)(2,1)} %get-tuple-element.30), channel_id=1, source_target_pairs={{1,0},{2,1},{3,2},{5,4},{6,5},{7,6},{9,8},{10,9},{11,10},{13,12},{... | collective-permute-start | bytes 1572872 | tf_op jit(solution)/shard_map/ppermute | solution.py:28
  6.5 2.4 %collective-permute-start.1 = (bf16[2,512,256]{2,1,0:T(8,128)(2,1)}, bf16[2,512,256]{2,1,0:T(8,128)(2,1)}, u32[]{:S(2)}, u32[]{:S(2)}) collective-permute-start(bf16[2,512,256]{2,1,0:T(8,128)(2,1)} %get-tuple-element.34), channel_id=1, source_target_pairs={{1,0},{2,1},{3,2},{5,4},{6,5},{7,6},{9,8},{10,9},{11,10},{13,12},{... | collective-permute-start | bytes 1572872 | tf_op jit(solution)/shard_map/ppermute | solution.py:28
  8.8 1.9 %collective-permute-start.2 = (bf16[2,512,256]{2,1,0:T(8,128)(2,1)}, bf16[2,512,256]{2,1,0:T(8,128)(2,1)}, u32[]{:S(2)}, u32[]{:S(2)}) collective-permute-start(bf16[2,512,256]{2,1,0:T(8,128)(2,1)} %get-tuple-element.37), channel_id=1, source_target_pairs={{1,0},{2,1},{3,2},{5,4},{6,5},{7,6},{9,8},{10,9},{11,10},{13,12},{... | collective-permute-start | bytes 1572872 | tf_op jit(solution)/shard_map/ppermute | solution.py:28
  10.8 4.8 %collective-permute-start.5 = (bf16[2,384,512]{2,1,0:T(8,128)(2,1)}, bf16[2,384,512]{2,1,0:T(8,128)(2,1)S(1)}, u32[]{:S(2)}, u32[]{:S(2)}) collective-permute-start(bf16[2,384,512]{2,1,0:T(8,128)(2,1)} %get-tuple-element.39), channel_id=1, source_target_pairs={{4,0},{8,4},{12,8},{16,12},{20,16},{24,20},{28,24},{32,28},{36,32}... | collective-permute-start | bytes 2359304 | tf_op jit(solution)/shard_map/ppermute | solution.py:28
  15.6 3.1 %collective-permute-start.6 = (bf16[2,384,512]{2,1,0:T(8,128)(2,1)}, bf16[2,384,512]{2,1,0:T(8,128)(2,1)}, u32[]{:S(2)}, u32[]{:S(2)}) collective-permute-start(bf16[2,384,512]{2,1,0:T(8,128)(2,1)} %get-tuple-element.40), channel_id=1, source_target_pairs={{4,0},{8,4},{12,8},{16,12},{20,16},{24,20},{28,24},{32,28},{36,32}... | collective-permute-start | bytes 2359304 | tf_op jit(solution)/shard_map/ppermute | solution.py:28
  19.4 1.8 %collective-permute-done.near0_ref = bf16[2,512,256]{2,1,0:T(8,128)(2,1)} collective-permute-done((bf16[2,512,256]{2,1,0:T(8,128)(2,1)}, bf16[2,512,256]{2,1,0:T(8,128)(2,1)}, u32[]{:S(2)}, u32[]{:S(2)}) %collective-permute-start) | collective-permute-done | bytes 524320 | tf_op jit(solution)/shard_map/ppermute | solution.py:28
  21.1 3.3 %collective-permute-start.3 = (bf16[2,512,256]{2,1,0:T(8,128)(2,1)}, bf16[2,512,256]{2,1,0:T(8,128)(2,1)S(1)}, u32[]{:S(2)}, u32[]{:S(2)}) collective-permute-start(bf16[2,512,256]{2,1,0:T(8,128)(2,1)} %collective-permute-done.near0_ref), channel_id=1, source_target_pairs={{4,0},{8,4},{12,8},{16,12},{20,16},{24,20},{28,24},{32,28},{36,32}... | collective-permute-start | bytes 1572872 | tf_op jit(solution)/shard_map/ppermute | solution.py:28
  24.5 1.0 copy-done.4
  25.5 1.9 %copy-done.6 = bf16[1,1,6,512,512]{4,3,2,1,0:T(8,128)(2,1)S(1)} copy-done((bf16[1,1,6,512,512]{4,3,2,1,0:T(8,128)(2,1)S(1)}, bf16[1,1,6,512,512]{4,3,2,1,0:T(8,128)(2,1)}, u32[]{:S(2)}) %copy-start.6) | copy-done | bytes 3145752
  27.4 1.0 copy-done.7
  28.5 1.0 copy-done.8
  29.5 4.3 %shard_map.92.meas_ref = bf16[6,512,512]{2,1,0:T(8,128)(2,1)S(1)} custom-call(bf16[512,512]{1,0:T(8,128)(2,1)S(1)} %copy-done.8, bf16[512,512]{1,0:T(8,128)(2,1)S(1)} %copy-done.7, bf16[6,512,512]{2,1,0:T(8,128)(2,1)S(1)} %bitcast.6, f32[2,512,512]{2,1,0:T(8,128)S(1)} %copy-done.2, bf16[4,256,256]{2,1,0:T(8,128)(2,1)S(1)} %copy-done.4, ...), custom_call_target="tpu_custom_call" | custom-call | flops 3221225472 | bytes 6291456 | tf_op jit(solution)/shard_map/pallas_call | solution.py:162
  33.8 4.6 %collective-permute-start.4 = (bf16[2,512,256]{2,1,0:T(8,128)(2,1)}, bf16[2,512,256]{2,1,0:T(8,128)(2,1)S(1)}, u32[]{:S(2)}, u32[]{:S(2)}) collective-permute-start(bf16[2,512,256]{2,1,0:T(8,128)(2,1)} %collective-permute-done.1.near1_ref), channel_id=1, source_target_pairs={{4,0},{8,4},{12,8},{16,12},{20,16},{24,20},{28,24},{32,28},{36,32}... | collective-permute-start | bytes 1572872 | tf_op jit(solution)/shard_map/ppermute | solution.py:28
  38.4 4.0 %collective-permute-done.2.far_ref = bf16[2,512,256]{2,1,0:T(8,128)(2,1)} collective-permute-done((bf16[2,512,256]{2,1,0:T(8,128)(2,1)}, bf16[2,512,256]{2,1,0:T(8,128)(2,1)}, u32[]{:S(2)}, u32[]{:S(2)}) %collective-permute-start.2) | collective-permute-done | bytes 524320 | tf_op jit(solution)/shard_map/ppermute | solution.py:28
  42.5 3.0 %collective-permute-done.4.corner1_ref = bf16[2,512,256]{2,1,0:T(8,128)(2,1)S(1)} collective-permute-done((bf16[2,512,256]{2,1,0:T(8,128)(2,1)}, bf16[2,512,256]{2,1,0:T(8,128)(2,1)S(1)}, u32[]{:S(2)}, u32[]{:S(2)}) %collective-permute-start.4) | collective-permute-done | bytes 524320 | tf_op jit(solution)/shard_map/ppermute | solution.py:28
  45.4 24.7 %shard_map.93.grown.refs_4_ = f32[2,10,1280,128]{3,2,1,0:T(8,128)S(1)} custom-call(s32[1]{0:T(128)} %bitcast.live_ref, s32[2,6]{1,0:T(2,128)S(1)} %bitcast.5, f32[2,768,768]{2,1,0:T(8,128)S(1)} %copy-done.1, bf16[2,512,256]{2,1,0:T(8,128)(2,1)} %collective-permute-done.near0_ref, bf16[2,512,256]{2,1,0:T(8,128)(2,1)} %collective-permute-done.1.near1_ref, ...), custom_call_target="tpu_custom_call" | custom-call | flops 1024 | bytes 1024 | tf_op jit(solution)/shard_map/pallas_call | solution.py:340
  70.7 1.9 %collective-permute-start.7 = (bf16[2,512,256]{2,1,0:T(8,128)(2,1)S(1)}, bf16[2,512,256]{2,1,0:T(8,128)(2,1)S(1)}, u32[]{:S(2)}, u32[]{:S(2)}) collective-permute-start(bf16[2,512,256]{2,1,0:T(8,128)(2,1)S(1)} %get-tuple-element.41), channel_id=1, source_target_pairs={{0,1},{1,2},{2,3},{4,5},{5,6},{6,7},{8,9},{9,10},{10,11},{12,13},{... | collective-permute-start | bytes 1572872 | tf_op jit(solution)/shard_map/ppermute | solution.py:28
  72.7 1.9 %collective-permute-start.11 = (bf16[2,512,256]{2,1,0:T(8,128)(2,1)S(1)}, bf16[2,512,256]{2,1,0:T(8,128)(2,1)S(1)}, u32[]{:S(2)}, u32[]{:S(2)}) collective-permute-start(bf16[2,512,256]{2,1,0:T(8,128)(2,1)S(1)} %get-tuple-element.47), channel_id=1, source_target_pairs={{0,4},{4,8},{8,12},{12,16},{16,20},{20,24},{24,28},{28,32},{32,36}... | collective-permute-start | bytes 1572872 | tf_op jit(solution)/shard_map/ppermute | solution.py:28
  74.6 1.9 %collective-permute-start.8 = (bf16[2,512,256]{2,1,0:T(8,128)(2,1)S(1)}, bf16[2,512,256]{2,1,0:T(8,128)(2,1)S(1)}, u32[]{:S(2)}, u32[]{:S(2)}) collective-permute-start(bf16[2,512,256]{2,1,0:T(8,128)(2,1)S(1)} %get-tuple-element.44), channel_id=1, source_target_pairs={{0,4},{4,8},{8,12},{12,16},{16,20},{20,24},{24,28},{28,32},{32,36}... | collective-permute-start | bytes 1572872 | tf_op jit(solution)/shard_map/ppermute | solution.py:28
  76.5 5.3 %collective-permute-start.10 = (bf16[2,384,512]{2,1,0:T(8,128)(2,1)S(1)}, bf16[2,384,512]{2,1,0:T(8,128)(2,1)S(1)}, u32[]{:S(2)}, u32[]{:S(2)}) collective-permute-start(bf16[2,384,512]{2,1,0:T(8,128)(2,1)S(1)} %get-tuple-element.45), channel_id=1, source_target_pairs={{0,4},{4,8},{8,12},{12,16},{16,20},{20,24},{24,28},{28,32},{32,36}... | collective-permute-start | bytes 2359304 | tf_op jit(solution)/shard_map/ppermute | solution.py:28
  81.9 3.5 %collective-permute-done.7.refs_2_ = bf16[2,512,256]{2,1,0:T(8,128)(2,1)S(1)} collective-permute-done((bf16[2,512,256]{2,1,0:T(8,128)(2,1)S(1)}, bf16[2,512,256]{2,1,0:T(8,128)(2,1)S(1)}, u32[]{:S(2)}, u32[]{:S(2)}) %collective-permute-start.7) | collective-permute-done | bytes 524320 | tf_op jit(solution)/shard_map/ppermute | solution.py:28
  85.4 1.9 %collective-permute-done.11 = bf16[2,512,256]{2,1,0:T(8,128)(2,1)S(1)} collective-permute-done((bf16[2,512,256]{2,1,0:T(8,128)(2,1)S(1)}, bf16[2,512,256]{2,1,0:T(8,128)(2,1)S(1)}, u32[]{:S(2)}, u32[]{:S(2)}) %collective-permute-start.11) | collective-permute-done | bytes 524320 | tf_op jit(solution)/shard_map/ppermute | solution.py:28
  87.4 1.9 %collective-permute-start.13 = (bf16[2,512,256]{2,1,0:T(8,128)(2,1)S(1)}, bf16[2,512,256]{2,1,0:T(8,128)(2,1)S(1)}, u32[]{:S(2)}, u32[]{:S(2)}) collective-permute-start(bf16[2,512,256]{2,1,0:T(8,128)(2,1)S(1)} %add_convert_fusion), channel_id=1, source_target_pairs={{0,1},{1,2},{2,3},{4,5},{5,6},{6,7},{8,9},{9,10},{10,11},{12,13},{... | collective-permute-start | bytes 1572872 | tf_op jit(solution)/shard_map/ppermute | solution.py:28
  89.3 1.9 %collective-permute-start.12 = (bf16[2,384,512]{2,1,0:T(8,128)(2,1)S(1)}, bf16[2,384,512]{2,1,0:T(8,128)(2,1)S(1)}, u32[]{:S(2)}, u32[]{:S(2)}) collective-permute-start(bf16[2,384,512]{2,1,0:T(8,128)(2,1)S(1)} %get-tuple-element.49), channel_id=1, source_target_pairs={{0,4},{4,8},{8,12},{12,16},{16,20},{20,24},{24,28},{28,32},{32,36}... | collective-permute-start | bytes 2359304 | tf_op jit(solution)/shard_map/ppermute | solution.py:28
  91.3 1.6 %collective-permute-done.8 = bf16[2,512,256]{2,1,0:T(8,128)(2,1)S(1)} collective-permute-done((bf16[2,512,256]{2,1,0:T(8,128)(2,1)S(1)}, bf16[2,512,256]{2,1,0:T(8,128)(2,1)S(1)}, u32[]{:S(2)}, u32[]{:S(2)}) %collective-permute-start.8) | collective-permute-done | bytes 524320 | tf_op jit(solution)/shard_map/ppermute | solution.py:28
  93.0 1.9 %collective-permute-start.9 = (bf16[2,512,256]{2,1,0:T(8,128)(2,1)S(1)}, bf16[2,512,256]{2,1,0:T(8,128)(2,1)S(1)}, u32[]{:S(2)}, u32[]{:S(2)}) collective-permute-start(bf16[2,512,256]{2,1,0:T(8,128)(2,1)S(1)} %add_convert_fusion.1), channel_id=1, source_target_pairs={{0,1},{1,2},{2,3},{4,5},{5,6},{6,7},{8,9},{9,10},{10,11},{12,13},{... | collective-permute-start | bytes 1572872 | tf_op jit(solution)/shard_map/ppermute | solution.py:28
  94.9 6.4 %collective-permute-done.10.refs_0_ = bf16[2,384,512]{2,1,0:T(8,128)(2,1)S(1)} collective-permute-done((bf16[2,384,512]{2,1,0:T(8,128)(2,1)S(1)}, bf16[2,384,512]{2,1,0:T(8,128)(2,1)S(1)}, u32[]{:S(2)}, u32[]{:S(2)}) %collective-permute-start.10) | collective-permute-done | bytes 786464 | tf_op jit(solution)/shard_map/ppermute | solution.py:28
  101.3 2.9 %collective-permute-done.13.refs_3_ = bf16[2,512,256]{2,1,0:T(8,128)(2,1)S(1)} collective-permute-done((bf16[2,512,256]{2,1,0:T(8,128)(2,1)S(1)}, bf16[2,512,256]{2,1,0:T(8,128)(2,1)S(1)}, u32[]{:S(2)}, u32[]{:S(2)}) %collective-permute-start.13) | collective-permute-done | bytes 524320 | tf_op jit(solution)/shard_map/ppermute | solution.py:28
  104.1 5.6 %collective-permute-done.12.refs_1_ = bf16[2,384,512]{2,1,0:T(8,128)(2,1)S(1)} collective-permute-done((bf16[2,384,512]{2,1,0:T(8,128)(2,1)S(1)}, bf16[2,384,512]{2,1,0:T(8,128)(2,1)S(1)}, u32[]{:S(2)}, u32[]{:S(2)}) %collective-permute-start.12) | collective-permute-done | bytes 786464 | tf_op jit(solution)/shard_map/ppermute | solution.py:28
  109.7 2.0 %shard_map.95 = (f32[2,10,1280,128]{3,2,1,0:T(8,128)S(1)}, f32[2,768,768]{2,1,0:T(8,128)}) custom-call(bf16[2,384,512]{2,1,0:T(8,128)(2,1)S(1)} %collective-permute-done.10.refs_0_, bf16[2,384,512]{2,1,0:T(8,128)(2,1)S(1)} %collective-permute-done.12.refs_1_, ...), custom_call_target="tpu_custom_call", output_to_operand_aliasing={{0}: (4, {})} | custom-call | flops 1024 | bytes 1024 | tf_op jit(solution)/shard_map/pallas_call | solution.py:441
  111.8 1.1 shard_map.96
  (23 shorter events, 1.6 us)
Async XLA Ops:
  0.0 18.7 %copy-start = (s32[32,1]{0,1:T(1,128)S(1)}, s32[32,1]{0,1:T(1,128)}, u32[]{:S(2)}) copy-start(s32[32,1]{0,1:T(1,128)} %param.13) | copy-start | bytes 388
  0.0 24.5 %copy-start.3 = (bf16[4,256,256]{2,1,0:T(8,128)(2,1)S(1)}, bf16[4,256,256]{2,1,0:T(8,128)(2,1)}, u32[]{:S(2)}) copy-start(bf16[4,256,256]{2,1,0:T(8,128)(2,1)} %constant.20.clone.refs_2_.gb_ref) | copy-start | bytes 1572868
  0.0 24.5 %copy-start.2 = (f32[2,512,512]{2,1,0:T(8,128)S(1)}, f32[2,512,512]{2,1,0:T(8,128)}, u32[]{:S(2)}) copy-start(f32[2,512,512]{2,1,0:T(8,128)} %probe_ref.1) | copy-start | bytes 6291460
  4.1 17.0 %collective-permute-start = (bf16[2,512,256]{2,1,0:T(8,128)(2,1)}, bf16[2,512,256]{2,1,0:T(8,128)(2,1)}, u32[]{:S(2)}, u32[]{:S(2)}) collective-permute-start(bf16[2,512,256]{2,1,0:T(8,128)(2,1)} %get-tuple-element.30), channel_id=1, source_target_pairs={{1,0},{2,1},{3,2},{5,4},{6,5},{7,6},{9,8},{10,9},{11,10},{13,12},{... | collective-permute-start | bytes 1572872 | tf_op jit(solution)/shard_map/ppermute | solution.py:28
  6.5 27.3 %collective-permute-start.1 = (bf16[2,512,256]{2,1,0:T(8,128)(2,1)}, bf16[2,512,256]{2,1,0:T(8,128)(2,1)}, u32[]{:S(2)}, u32[]{:S(2)}) collective-permute-start(bf16[2,512,256]{2,1,0:T(8,128)(2,1)} %get-tuple-element.34), channel_id=1, source_target_pairs={{1,0},{2,1},{3,2},{5,4},{6,5},{7,6},{9,8},{10,9},{11,10},{13,12},{... | collective-permute-start | bytes 1572872 | tf_op jit(solution)/shard_map/ppermute | solution.py:28
  8.8 33.6 %collective-permute-start.2 = (bf16[2,512,256]{2,1,0:T(8,128)(2,1)}, bf16[2,512,256]{2,1,0:T(8,128)(2,1)}, u32[]{:S(2)}, u32[]{:S(2)}) collective-permute-start(bf16[2,512,256]{2,1,0:T(8,128)(2,1)} %get-tuple-element.37), channel_id=1, source_target_pairs={{1,0},{2,1},{3,2},{5,4},{6,5},{7,6},{9,8},{10,9},{11,10},{13,12},{... | collective-permute-start | bytes 1572872 | tf_op jit(solution)/shard_map/ppermute | solution.py:28
  10.8 31.7 %collective-permute-start.5 = (bf16[2,384,512]{2,1,0:T(8,128)(2,1)}, bf16[2,384,512]{2,1,0:T(8,128)(2,1)S(1)}, u32[]{:S(2)}, u32[]{:S(2)}) collective-permute-start(bf16[2,384,512]{2,1,0:T(8,128)(2,1)} %get-tuple-element.39), channel_id=1, source_target_pairs={{4,0},{8,4},{12,8},{16,12},{20,16},{24,20},{28,24},{32,28},{36,32}... | collective-permute-start | bytes 2359304 | tf_op jit(solution)/shard_map/ppermute | solution.py:28
  15.6 26.9 %collective-permute-start.6 = (bf16[2,384,512]{2,1,0:T(8,128)(2,1)}, bf16[2,384,512]{2,1,0:T(8,128)(2,1)}, u32[]{:S(2)}, u32[]{:S(2)}) collective-permute-start(bf16[2,384,512]{2,1,0:T(8,128)(2,1)} %get-tuple-element.40), channel_id=1, source_target_pairs={{4,0},{8,4},{12,8},{16,12},{20,16},{24,20},{28,24},{32,28},{36,32}... | collective-permute-start | bytes 2359304 | tf_op jit(solution)/shard_map/ppermute | solution.py:28
  21.1 21.3 %collective-permute-start.3 = (bf16[2,512,256]{2,1,0:T(8,128)(2,1)}, bf16[2,512,256]{2,1,0:T(8,128)(2,1)S(1)}, u32[]{:S(2)}, u32[]{:S(2)}) collective-permute-start(bf16[2,512,256]{2,1,0:T(8,128)(2,1)} %collective-permute-done.near0_ref), channel_id=1, source_target_pairs={{4,0},{8,4},{12,8},{16,12},{20,16},{24,20},{28,24},{32,28},{36,32}... | collective-permute-start | bytes 1572872 | tf_op jit(solution)/shard_map/ppermute | solution.py:28
  24.5 1.0 copy-start.4
  25.5 1.9 %copy-start.6 = (bf16[1,1,6,512,512]{4,3,2,1,0:T(8,128)(2,1)S(1)}, bf16[1,1,6,512,512]{4,3,2,1,0:T(8,128)(2,1)}, u32[]{:S(2)}) copy-start(bf16[1,1,6,512,512]{4,3,2,1,0:T(8,128)(2,1)} %param.11) | copy-start | bytes 9437188
  27.4 1.0 copy-start.7
  28.5 1.0 copy-start.8
  29.5 15.9 %copy-start.1 = (f32[2,768,768]{2,1,0:T(8,128)S(1)}, f32[2,768,768]{2,1,0:T(8,128)}, u32[]{:S(2)}) copy-start(f32[2,768,768]{2,1,0:T(8,128)} %slab_ref.3) | copy-start | bytes 14155780
  29.5 15.9 %copy-start.5 = (s32[1,1,6,2]{2,3,1,0:T(2,128)S(1)}, s32[1,1,6,2]{2,3,1,0:T(2,128)}, u32[]{:S(2)}) copy-start(s32[1,1,6,2]{2,3,1,0:T(2,128)} %param.12) | copy-start | bytes 148
  33.8 11.6 %collective-permute-start.4 = (bf16[2,512,256]{2,1,0:T(8,128)(2,1)}, bf16[2,512,256]{2,1,0:T(8,128)(2,1)S(1)}, u32[]{:S(2)}, u32[]{:S(2)}) collective-permute-start(bf16[2,512,256]{2,1,0:T(8,128)(2,1)} %collective-permute-done.1.near1_ref), channel_id=1, source_target_pairs={{4,0},{8,4},{12,8},{16,12},{20,16},{24,20},{28,24},{32,28},{36,32}... | collective-permute-start | bytes 1572872 | tf_op jit(solution)/shard_map/ppermute | solution.py:28
  70.7 14.6 %collective-permute-start.7 = (bf16[2,512,256]{2,1,0:T(8,128)(2,1)S(1)}, bf16[2,512,256]{2,1,0:T(8,128)(2,1)S(1)}, u32[]{:S(2)}, u32[]{:S(2)}) collective-permute-start(bf16[2,512,256]{2,1,0:T(8,128)(2,1)S(1)} %get-tuple-element.41), channel_id=1, source_target_pairs={{0,1},{1,2},{2,3},{4,5},{5,6},{6,7},{8,9},{9,10},{10,11},{12,13},{... | collective-permute-start | bytes 1572872 | tf_op jit(solution)/shard_map/ppermute | solution.py:28
  72.7 14.6 %collective-permute-start.11 = (bf16[2,512,256]{2,1,0:T(8,128)(2,1)S(1)}, bf16[2,512,256]{2,1,0:T(8,128)(2,1)S(1)}, u32[]{:S(2)}, u32[]{:S(2)}) collective-permute-start(bf16[2,512,256]{2,1,0:T(8,128)(2,1)S(1)} %get-tuple-element.47), channel_id=1, source_target_pairs={{0,4},{4,8},{8,12},{12,16},{16,20},{20,24},{24,28},{28,32},{32,36}... | collective-permute-start | bytes 1572872 | tf_op jit(solution)/shard_map/ppermute | solution.py:28
  74.6 18.3 %collective-permute-start.8 = (bf16[2,512,256]{2,1,0:T(8,128)(2,1)S(1)}, bf16[2,512,256]{2,1,0:T(8,128)(2,1)S(1)}, u32[]{:S(2)}, u32[]{:S(2)}) collective-permute-start(bf16[2,512,256]{2,1,0:T(8,128)(2,1)S(1)} %get-tuple-element.44), channel_id=1, source_target_pairs={{0,4},{4,8},{8,12},{12,16},{16,20},{20,24},{24,28},{28,32},{32,36}... | collective-permute-start | bytes 1572872 | tf_op jit(solution)/shard_map/ppermute | solution.py:28
  76.5 24.8 %collective-permute-start.10 = (bf16[2,384,512]{2,1,0:T(8,128)(2,1)S(1)}, bf16[2,384,512]{2,1,0:T(8,128)(2,1)S(1)}, u32[]{:S(2)}, u32[]{:S(2)}) collective-permute-start(bf16[2,384,512]{2,1,0:T(8,128)(2,1)S(1)} %get-tuple-element.45), channel_id=1, source_target_pairs={{0,4},{4,8},{8,12},{12,16},{16,20},{20,24},{24,28},{28,32},{32,36}... | collective-permute-start | bytes 2359304 | tf_op jit(solution)/shard_map/ppermute | solution.py:28
  87.4 16.8 %collective-permute-start.13 = (bf16[2,512,256]{2,1,0:T(8,128)(2,1)S(1)}, bf16[2,512,256]{2,1,0:T(8,128)(2,1)S(1)}, u32[]{:S(2)}, u32[]{:S(2)}) collective-permute-start(bf16[2,512,256]{2,1,0:T(8,128)(2,1)S(1)} %add_convert_fusion), channel_id=1, source_target_pairs={{0,1},{1,2},{2,3},{4,5},{5,6},{6,7},{8,9},{9,10},{10,11},{12,13},{... | collective-permute-start | bytes 1572872 | tf_op jit(solution)/shard_map/ppermute | solution.py:28
  89.3 20.4 %collective-permute-start.12 = (bf16[2,384,512]{2,1,0:T(8,128)(2,1)S(1)}, bf16[2,384,512]{2,1,0:T(8,128)(2,1)S(1)}, u32[]{:S(2)}, u32[]{:S(2)}) collective-permute-start(bf16[2,384,512]{2,1,0:T(8,128)(2,1)S(1)} %get-tuple-element.49), channel_id=1, source_target_pairs={{0,4},{4,8},{8,12},{12,16},{16,20},{20,24},{24,28},{28,32},{32,36}... | collective-permute-start | bytes 2359304 | tf_op jit(solution)/shard_map/ppermute | solution.py:28
  93.0 18.8 %collective-permute-start.9 = (bf16[2,512,256]{2,1,0:T(8,128)(2,1)S(1)}, bf16[2,512,256]{2,1,0:T(8,128)(2,1)S(1)}, u32[]{:S(2)}, u32[]{:S(2)}) collective-permute-start(bf16[2,512,256]{2,1,0:T(8,128)(2,1)S(1)} %add_convert_fusion.1), channel_id=1, source_target_pairs={{0,1},{1,2},{2,3},{4,5},{5,6},{6,7},{8,9},{9,10},{10,11},{12,13},{... | collective-permute-start | bytes 1572872 | tf_op jit(solution)/shard_map/ppermute | solution.py:28
